TPU v7x, 32 devices: a whole 2x2x4 slice. The times are simulated.
32 devices in a mesh: tok: 16 (over z, y, x), rep: 2 (over core).
Axes of the slice: x: 2, y: 2, z: 4, core: 2. Of those that a mesh axis runs over, the one named last changes fastest.
Arguments:
- tokens: bfloat16 [2, 4096, 1024], P('rep', 'tok'), may hold values from -6 to 6
- cotangent: bfloat16 [2, 4096, 1024], P('rep', 'tok'), may hold values from -6 to 6
- lengths: int32 [2, 16], P('rep'), may hold values from 1 to 3586, as said below
- up_weight: float32 [1024, 3072], P(('tok', 'rep')), may hold values from -0.1875 to 0.1875
- value_weight: float32 [1024, 512], P(('tok', 'rep')), may hold values from -0.1875 to 0.1875
- expand_weight: float32 [512, 3072], P(('tok', 'rep')), may hold values from -0.25 to 0.25
- down_weight: float32 [3072, 1024], P(('tok', 'rep')), may hold values from -0.109375 to 0.109375
- norm_params: float32 [2, 1024], P(None, ('tok', 'rep')), may hold values from -3 to 3
- state_params: float32 [2, 512, 512], P(None, 'tok'), may hold values from -0.02 to 0.02
- state_poles: float32 [2, 512, 512], P(None, 'tok'), may hold values from -9 to 1
- up_mean: float32 [1024, 3072], P(('tok', 'rep')), may hold values from -20 to 20
- up_square: float32 [1024, 3072], P(('tok', 'rep')), may hold values from 0.49152 to 8.02816
- value_mean: float32 [1024, 512], P(('tok', 'rep')), may hold values from -32 to 32
- value_square: float32 [1024, 512], P(('tok', 'rep')), may hold values from 1.2288 to 19.6608
- expand_mean: float32 [512, 3072], P(('tok', 'rep')), may hold values from -24 to 24
- expand_square: float32 [512, 3072], P(('tok', 'rep')), may hold values from 0.589824 to 9.4208
- down_mean: float32 [3072, 1024], P(('tok', 'rep')), may hold values from -40 to 40
- down_square: float32 [3072, 1024], P(('tok', 'rep')), may hold values from 1.72032 to 27.8528
- norm_mean: float32 [2, 1024], P(None, ('tok', 'rep')), may hold values from -40 to 40
- norm_square: float32 [2, 1024], P(None, ('tok', 'rep')), may hold values from 2.12992 to 33.5872
- state_mean: float32 [2, 512, 512], P(None, 'tok')
- state_square: float32 [2, 512, 512], P(None, 'tok')
Outputs:
- layer_out: bfloat16 [2, 4096, 1024], P('rep', 'tok')
- token_grad: float32 [2, 4096, 1024], P('rep', 'tok')
- up_next: float32 [1024, 3072], P(('tok', 'rep'))
- up_mean_next: float32 [1024, 3072], P(('tok', 'rep'))
- up_square_next: float32 [1024, 3072], P(('tok', 'rep'))
- value_next: float32 [1024, 512], P(('tok', 'rep'))
- value_mean_next: float32 [1024, 512], P(('tok', 'rep'))
- value_square_next: float32 [1024, 512], P(('tok', 'rep'))
- expand_next: float32 [512, 3072], P(('tok', 'rep'))
- expand_mean_next: float32 [512, 3072], P(('tok', 'rep'))
- expand_square_next: float32 [512, 3072], P(('tok', 'rep'))
- down_next: float32 [3072, 1024], P(('tok', 'rep'))
- down_mean_next: float32 [3072, 1024], P(('tok', 'rep'))
- down_square_next: float32 [3072, 1024], P(('tok', 'rep'))
- norm_next: float32 [2, 1024], P(None, ('tok', 'rep'))
- norm_mean_next: float32 [2, 1024], P(None, ('tok', 'rep'))
- norm_square_next: float32 [2, 1024], P(None, ('tok', 'rep'))
- state_next: float32 [2, 512, 512], P(None, 'tok')
- state_mean_next: float32 [2, 512, 512], P(None, 'tok')
- state_square_next: float32 [2, 512, 512], P(None, 'tok')
Inputs may be any that keep to these rules, and one draw needn't show every extreme that they name: `lengths`: each row sums to 4096; a group's items lie end to end in its tokens in the order given; each group has one item of exactly 3586 tokens.
All inputs are finite; a program needn't handle non-finite values.
Results may differ from a plain program's by a relative error of at most 0.005.
Values may be sent and summed in bfloat16 or wider, within the bound.
No kernel may reach another device: no remote copies, remote signals or barrier semaphores. Data moves between devices by JAX's collectives and lax.ppermute only.
A program may use at most 256 MiB of HBM per device.

v0:
```python
import functools

import jax
import jax.numpy as jnp
from jax import lax
from jax.experimental import pallas as pl
from jax.experimental.pallas import tpu as pltpu
from jax.sharding import PartitionSpec as P

BLOCK = 128
STEP = 5


epsilon_norm = 1e-05
epsilon_adam = 1e-08
beta_first = 0.9
beta_second = 0.999


def gelu_curve(values):
    return jax.nn.gelu(values, approximate=True)


def layer_norm(rows, norm_weights):
    average = jnp.mean(rows, axis=-1, keepdims=True)
    centered = rows - average
    variance = jnp.mean(centered * centered, axis=-1, keepdims=True)
    return centered * lax.rsqrt(variance + epsilon_norm) * norm_weights[0] + norm_weights[1]


def pieces_of(lengths_row, length):
    blocks = length // BLOCK
    items = lengths_row.shape[0]
    ends = jnp.cumsum(lengths_row, dtype=jnp.int32)
    heads = BLOCK * jnp.arange(blocks, dtype=jnp.int32)
    head_rank = jnp.arange(blocks, dtype=jnp.int32) + jnp.sum(
        (ends[None, :] < heads[:, None]).astype(jnp.int32), axis=1
    )
    end_rank = jnp.arange(items, dtype=jnp.int32) + jnp.sum(
        (heads[None, :] <= ends[:, None]).astype(jnp.int32), axis=1
    )
    places = jnp.arange(blocks + items, dtype=jnp.int32)[:, None]
    starts = jnp.sum(jnp.where(head_rank[None, :] == places, heads[None, :], 0), axis=1) + jnp.sum(
        jnp.where(end_rank[None, :] == places, ends[None, :], 0), axis=1
    )
    stops = jnp.concatenate([starts[1:], jnp.full((1,), length, jnp.int32)])
    owner = starts // BLOCK
    segment = jnp.sum((ends[None, :] <= starts[:, None]).astype(jnp.int32), axis=1)
    positions = owner[:, None] * BLOCK + jnp.arange(BLOCK, dtype=jnp.int32)[None, :]
    mask = (positions >= starts[:, None]) & (positions < stops[:, None])
    pick = owner[:, None] == jnp.arange(blocks, dtype=jnp.int32)[None, :]
    follows = (segment[1:] == segment[:-1]) & (owner[1:] != owner[:-1])
    follows = jnp.concatenate([jnp.zeros((1,), bool), follows])
    return (
        pick.astype(jnp.bfloat16),
        mask.astype(jnp.bfloat16),
        follows.astype(jnp.float32),
    )


def powers_of(poles):
    decay_rate = jnp.exp(poles[0])[:, None, :]
    frequency = poles[1][:, None, :]
    lags = jnp.array([0, 1, 2, 3, 4, 5, 6, 7, 8, 16, 32, 64, 128, 128, 128, 128], jnp.float32)
    lags = lags[None, :, None]
    magnitude = jnp.exp(-decay_rate * lags)
    phase = frequency * lags
    return jnp.concatenate([magnitude * jnp.cos(phase), magnitude * jnp.sin(phase)], axis=2)


def cmul(ar, ai, br, bi):
    return ar * br - ai * bi, ar * bi + ai * br


def fill_tables(c, states, low_ref, up_ref, down_ref):
    for lane in range(0, states, 128):
        re_lanes = pl.ds(lane, 128)
        im_lanes = pl.ds(states + lane, 128)
        base = low_ref[c, 0:8, re_lanes], low_ref[c, 0:8, im_lanes]
        for ref, forward in ((up_ref, True), (down_ref, False)):
            if forward:
                re, im = base
            else:
                re = jnp.concatenate([base[0][7 - k : 8 - k] for k in range(8)], axis=0)
                im = jnp.concatenate([base[1][7 - k : 8 - k] for k in range(8)], axis=0)
            for k in range(4):
                nr, ni = cmul(
                    re,
                    im,
                    low_ref[c, 8 + k : 9 + k, re_lanes],
                    low_ref[c, 8 + k : 9 + k, im_lanes],
                )
                if forward:
                    re = jnp.concatenate([re, nr], axis=0)
                    im = jnp.concatenate([im, ni], axis=0)
                else:
                    re = jnp.concatenate([nr, re], axis=0)
                    im = jnp.concatenate([ni, im], axis=0)
            ref[c, :, re_lanes] = re.astype(jnp.bfloat16)
            ref[c, :, im_lanes] = im.astype(jnp.bfloat16)


def nt(a, b):
    return lax.dot_general(a, b, (((1,), (1,)), ((), ())), preferred_element_type=jnp.float32)


def nn(a, b):
    return lax.dot_general(a, b, (((1,), (0,)), ((), ())), preferred_element_type=jnp.float32)


def tn(a, b):
    return lax.dot_general(a, b, (((0,), (0,)), ((), ())), preferred_element_type=jnp.float32)


def split_rows(row):
    high = row.astype(jnp.bfloat16)
    rest = (row - high.astype(jnp.float32)).astype(jnp.bfloat16)
    return high, rest


def toeplitz(kernel_row):
    spread = jnp.broadcast_to(kernel_row, (BLOCK, BLOCK))
    rolled = pltpu.roll(spread, 0, 1, stride=1, stride_axis=0)
    rows = lax.broadcasted_iota(jnp.int32, (BLOCK, BLOCK), 0)
    columns = lax.broadcasted_iota(jnp.int32, (BLOCK, BLOCK), 1)
    return jnp.where(columns >= rows, rolled, 0.0)


def put_rows(ref, c, places, group, block):
    for k in range(ref.shape[0]):
        ref[k, pl.ds(c, places, stride=group), :] = block[:, 128 * k : 128 * (k + 1)]


def get_rows(ref, c, places, group):
    chunks = [ref[k, pl.ds(c, places, stride=group), :] for k in range(ref.shape[0])]
    return jnp.concatenate([chunk.astype(jnp.bfloat16) for chunk in chunks], axis=1)


def get_step(ref, rows, half):
    count = ref.shape[0] // 2
    return jnp.concatenate([ref[half * count + k, rows, :] for k in range(count)], axis=1)


def put_step(ref, rows, half, block):
    count = ref.shape[0] // 2
    for k in range(count):
        ref[half * count + k, rows, :] = block[:, 128 * k : 128 * (k + 1)]


def forward_kernel(
    active, follows_ref, pick_ref, mask_ref, values_ref, low_ref, lam_ref, coef_ref,
    out_ref, start_ref, taps_ref, up_ref, down_ref, work_ref,
):
    places = pick_ref.shape[0]
    group, states = coef_ref.shape[0], coef_ref.shape[1] // 2
    if active < group:
        work_ref[...] = jnp.zeros_like(work_ref)
    mask = mask_ref[...]
    pick = pick_ref[...]
    for c in range(active):
        fill_tables(c, states, low_ref, up_ref, down_ref)
        spread = nn(pick, values_ref[c]).astype(jnp.bfloat16) * mask
        put_rows(work_ref, c, places, group, nn(spread, down_ref[c]))
    lam_re, lam_im = lam_ref[0, :, :states], lam_ref[0, :, states:]
    far_re, far_im = lam_ref[1, :, :states], lam_ref[1, :, states:]
    coef_re, coef_im = coef_ref[:, :states], coef_ref[:, states:]
    mix_re, mix_im = cmul(coef_re, coef_im, lam_re, lam_im)

    def advance(p, carry):
        re, im = carry
        rows = pl.ds(pl.multiple_of(p * group, group), group)
        keep = follows_ref[p]
        re, im = re * keep, im * keep
        start_ref[rows, :states] = re
        start_ref[rows, states:] = im
        far = cmul(re, im, far_re, far_im)
        new_re = far[0] + get_step(work_ref, rows, 0)
        new_im = far[1] + get_step(work_ref, rows, 1)
        mixed = cmul(re, im, mix_re, mix_im)
        put_step(work_ref, rows, 0, mixed[0])
        put_step(work_ref, rows, 1, -mixed[1])
        return new_re, new_im

    zero = jnp.zeros((group, states), jnp.float32)
    lax.fori_loop(0, places, advance, (zero, zero), unroll=4)
    for c in range(active):
        row = jnp.concatenate([coef_ref[c : c + 1, :states], -coef_ref[c : c + 1, states:]], axis=1)
        high, rest = split_rows(row)
        rows = jnp.concatenate([high, rest, jnp.zeros((14, 2 * states), jnp.bfloat16)], axis=0)
        mixed = get_rows(work_ref, c, places, group)
        carried = nt(jnp.concatenate([mixed, rows], axis=0), up_ref[c])
        kernel_row = carried[places : places + 1] + carried[places + 1 : places + 2]
        taps = toeplitz(kernel_row).astype(jnp.bfloat16)
        taps_ref[c] = taps
        spread = nn(pick, values_ref[c]).astype(jnp.bfloat16) * mask
        result = (carried[:places] + nn(spread, taps)).astype(jnp.bfloat16) * mask
        out_ref[c] = tn(pick, result).astype(jnp.bfloat16)


def backward_kernel(
    active, follows_ref, pick_ref, mask_ref, values_ref, grads_ref, low_ref, lam_ref, coef_ref,
    start_ref, taps_ref, out_ref, sum_ref, up_ref, down_ref, work_ref,
):
    places = pick_ref.shape[0]
    group, states = coef_ref.shape[0], coef_ref.shape[1] // 2
    if active < group:
        work_ref[...] = jnp.zeros_like(work_ref)
        sum_ref[...] = jnp.zeros_like(sum_ref)
    mask = mask_ref[...]
    pick = pick_ref[...]
    rows = lax.broadcasted_iota(jnp.int32, (BLOCK, BLOCK), 0)
    columns = lax.broadcasted_iota(jnp.int32, (BLOCK, BLOCK), 1)
    turn = (rows + columns == BLOCK - 1).astype(jnp.bfloat16)
    for c in range(active):
        fill_tables(c, states, low_ref, up_ref, down_ref)
        values = nn(pick, values_ref[c]).astype(jnp.bfloat16) * mask
        grads = nn(pick, grads_ref[c]).astype(jnp.bfloat16) * mask
        pairs = tn(nn(values, turn).astype(jnp.bfloat16), grads)
        skewed = pltpu.roll(pairs, 1, 1, stride=1, stride_axis=0)
        lag_sum = jnp.sum(jnp.where(columns <= rows, skewed, 0.0), axis=0, keepdims=True)
        high, rest = split_rows(lag_sum)
        extra = jnp.concatenate([high, rest, jnp.zeros((14, BLOCK), jnp.bfloat16)], axis=0)
        folded = nn(jnp.concatenate([grads, extra], axis=0), up_ref[c])
        put_rows(work_ref, c, places, group, folded[:places])
        sum_ref[c : c + 1, :] = folded[places : places + 1] + folded[places + 1 : places + 2]
    lam_re, lam_im = lam_ref[0, :, :states], lam_ref[0, :, states:]
    far_re, far_im = lam_ref[1, :, :states], lam_ref[1, :, states:]
    coef_re, coef_im = coef_ref[:, :states], coef_ref[:, states:]

    def retreat(step, carry):
        re, im, total_re, total_im = carry
        p = places - 1 - step
        rows = pl.ds(pl.multiple_of(p * group, group), group)
        near = cmul(get_step(work_ref, rows, 0), get_step(work_ref, rows, 1), lam_re, lam_im)
        begin = start_ref[rows, :states], start_ref[rows, states:]
        product = cmul(begin[0], begin[1], near[0], near[1])
        mixed = cmul(re, im, coef_re, coef_im)
        put_step(work_ref, rows, 0, mixed[0])
        put_step(work_ref, rows, 1, -mixed[1])
        keep = follows_ref[p]
        far = cmul(re, im, far_re, far_im)
        return (
            (near[0] + far[0]) * keep,
            (near[1] + far[1]) * keep,
            total_re + product[0],
            total_im + product[1],
        )

    zero = jnp.zeros((group, states), jnp.float32)
    _, _, total_re, total_im = lax.fori_loop(0, places, retreat, (zero, zero, zero, zero), unroll=4)
    sum_ref[:, :states] = sum_ref[:, :states] + total_re
    sum_ref[:, states:] = -(sum_ref[:, states:] + total_im)
    for c in range(active):
        mixed = get_rows(work_ref, c, places, group)
        grads = nn(pick, grads_ref[c]).astype(jnp.bfloat16) * mask
        result = nt(mixed, down_ref[c]) + nt(grads, taps_ref[c])
        out_ref[c] = tn(pick, result.astype(jnp.bfloat16) * mask).astype(jnp.bfloat16)


def whole(shape):
    return pl.BlockSpec(shape, lambda i: (0,) * len(shape))


def mixer_specs(active, group, blocks, places, states):
    return [
        pl.BlockSpec(memory_space=pltpu.SMEM),
        whole((places, blocks)),
        whole((places, BLOCK)),
        pl.BlockSpec((active, blocks, BLOCK), lambda i: (i, 0, 0)),
    ], [
        pl.BlockSpec((active, 16, 2 * states), lambda i: (i, 0, 0)),
        pl.BlockSpec((2, group, 2 * states), lambda i: (0, i, 0)),
        pl.BlockSpec((group, 2 * states), lambda i: (i, 0)),
    ]


def scratches(active, group, places, states):
    return [
        pltpu.VMEM((active, BLOCK, 2 * states), jnp.bfloat16),
        pltpu.VMEM((active, BLOCK, 2 * states), jnp.bfloat16),
        pltpu.VMEM((2 * states // 128, places * group, 128), jnp.float32),
    ]


def mix_forward(values, pieces, powers, lams, coefs):
    channels, blocks = values.shape[0], values.shape[1]
    pick, mask, follows = pieces
    places, states = pick.shape[0], coefs.shape[1] // 2
    group, active = 8, min(8, channels)
    spare = max(0, group - channels)
    lams = jnp.pad(lams, ((0, 0), (0, spare), (0, 0)))
    coefs = jnp.pad(coefs, ((0, spare), (0, 0)))
    first, last = mixer_specs(active, group, blocks, places, states)
    table = 2 * channels * places * BLOCK * 2 * states * 2
    return pl.pallas_call(
        functools.partial(forward_kernel, active),
        grid=(channels // active,),
        in_specs=first + last,
        out_specs=[
            pl.BlockSpec((active, blocks, BLOCK), lambda i: (i, 0, 0)),
            pl.BlockSpec((places * group, 2 * states), lambda i: (i, 0)),
            pl.BlockSpec((active, BLOCK, BLOCK), lambda i: (i, 0, 0)),
        ],
        out_shape=[
            jax.ShapeDtypeStruct((channels, blocks, BLOCK), jnp.bfloat16),
            jax.ShapeDtypeStruct((places * (channels + spare), 2 * states), jnp.float32),
            jax.ShapeDtypeStruct((channels, BLOCK, BLOCK), jnp.bfloat16),
        ],
        scratch_shapes=scratches(active, group, places, states),
        compiler_params=pltpu.CompilerParams(vmem_limit_bytes=48 * 2**20),
        cost_estimate=pl.CostEstimate(flops=20 * table, bytes_accessed=16 * 2**20, transcendentals=0),
        name="mix_forward",
    )(follows, pick, mask, values, powers, lams, coefs)


def mix_backward(values, grads, pieces, powers, lams, coefs, starts, taps):
    channels, blocks = values.shape[0], values.shape[1]
    pick, mask, follows = pieces
    places, states = pick.shape[0], coefs.shape[1] // 2
    group, active = 8, min(8, channels)
    spare = max(0, group - channels)
    lams = jnp.pad(lams, ((0, 0), (0, spare), (0, 0)))
    coefs = jnp.pad(coefs, ((0, spare), (0, 0)))
    first, last = mixer_specs(active, group, blocks, places, states)
    table = 2 * channels * places * BLOCK * 2 * states * 2
    result, sums = pl.pallas_call(
        functools.partial(backward_kernel, active),
        grid=(channels // active,),
        in_specs=first
        + [pl.BlockSpec((active, blocks, BLOCK), lambda i: (i, 0, 0))]
        + last
        + [
            pl.BlockSpec((places * group, 2 * states), lambda i: (i, 0)),
            pl.BlockSpec((active, BLOCK, BLOCK), lambda i: (i, 0, 0)),
        ],
        out_specs=[
            pl.BlockSpec((active, blocks, BLOCK), lambda i: (i, 0, 0)),
            pl.BlockSpec((group, 2 * states), lambda i: (i, 0)),
        ],
        out_shape=[
            jax.ShapeDtypeStruct((channels, blocks, BLOCK), jnp.bfloat16),
            jax.ShapeDtypeStruct((channels + spare, 2 * states), jnp.float32),
        ],
        scratch_shapes=scratches(active, group, places, states),
        compiler_params=pltpu.CompilerParams(vmem_limit_bytes=48 * 2**20),
        cost_estimate=pl.CostEstimate(flops=20 * table, bytes_accessed=16 * 2**20, transcendentals=0),
        name="mix_backward",
    )(follows, pick, mask, values, grads, powers, lams, coefs, starts, taps)
    return result, sums[:channels]


def mixer_inputs(poles, params):
    table = powers_of(poles)
    lams = jnp.stack([table[:, 1], table[:, 12]])
    coefs = jnp.concatenate([params[0], params[1]], axis=1)
    return table, lams, coefs


def adam_step(weight, gradient, first_moment, second, step_value, step_rate, decay_rate):
    first_new = beta_first * first_moment + (1.0 - beta_first) * gradient
    second_new = beta_second * second + (1.0 - beta_second) * gradient * gradient
    first_hat = first_new / (1.0 - jnp.power(beta_first, step_value))
    second_hat = second_new / (1.0 - jnp.power(beta_second, step_value))
    weight_new = weight - step_rate * (
        first_hat / (jnp.sqrt(second_hat) + epsilon_adam) + decay_rate * weight
    )
    return (weight_new, first_new, second_new)


def per_device(
    tokens,
    cotangent,
    lengths,
    up_weight,
    value_weight,
    expand_weight,
    down_weight,
    norm_params,
    state_params,
    state_poles,
    up_mean,
    up_square,
    value_mean,
    value_square,
    expand_mean,
    expand_square,
    down_mean,
    down_square,
    norm_mean,
    norm_square,
    state_mean,
    state_square,
):
    up_full, value_full, expand_full, down_full, norm_full = (
        lax.all_gather(up_weight.astype(jnp.bfloat16), ("tok", "rep"), axis=0, tiled=True),
        lax.all_gather(value_weight.astype(jnp.bfloat16), ("tok", "rep"), axis=0, tiled=True),
        lax.all_gather(expand_weight.astype(jnp.bfloat16), ("tok", "rep"), axis=0, tiled=True),
        lax.all_gather(down_weight.astype(jnp.bfloat16), ("tok", "rep"), axis=0, tiled=True),
        lax.all_gather(norm_params.astype(jnp.bfloat16), ("tok", "rep"), axis=1, tiled=True),
    )
    token_rows = tokens[0].astype(jnp.float32)
    normalized_rows, norm_back = jax.vjp(layer_norm, token_rows, norm_full.astype(jnp.float32))
    normed_low = normalized_rows.astype(jnp.bfloat16)
    up_pre = jnp.dot(normed_low, up_full, preferred_element_type=jnp.float32)
    upper, upper_back = jax.vjp(gelu_curve, up_pre)
    value_preactivation = jnp.einsum(
        "td,dc->ct", normed_low, value_full, preferred_element_type=jnp.float32
    )
    value_act, value_back = jax.vjp(gelu_curve, value_preactivation)
    channel_values = lax.all_to_all(
        value_act.astype(jnp.bfloat16), "tok", split_axis=0, concat_axis=1, tiled=True
    )
    channels, length = channel_values.shape
    blocked = (channels, length // BLOCK, BLOCK)
    pieces = pieces_of(lengths[0], length)
    powers, lams, coefs = mixer_inputs(state_poles, state_params)
    channel_values = channel_values.reshape(blocked)
    state_out, starts, taps = mix_forward(channel_values, pieces, powers, lams, coefs)
    token_states = lax.all_to_all(
        state_out.reshape(channels, length), "tok", split_axis=1, concat_axis=0, tiled=True
    )
    expanded = jnp.einsum(
        "ct,ch->th", token_states, expand_full, preferred_element_type=jnp.float32
    )
    gated_low = (upper * expanded).astype(jnp.bfloat16)
    layer_rows = token_rows + jnp.dot(gated_low, down_full, preferred_element_type=jnp.float32)
    layer_out = layer_rows.astype(jnp.bfloat16)[None]
    grad_rows = cotangent[0]
    down_grad = jnp.einsum("th,td->hd", gated_low, grad_rows, preferred_element_type=jnp.float32)
    gated_grad = jnp.einsum("td,hd->th", grad_rows, down_full, preferred_element_type=jnp.float32)
    expanded_grad = (gated_grad * upper).astype(jnp.bfloat16)
    upper_grad = gated_grad * expanded
    expand_grad = jnp.einsum(
        "ct,th->ch", token_states, expanded_grad, preferred_element_type=jnp.float32
    )
    state_grad = jnp.einsum(
        "th,ch->ct", expanded_grad, expand_full, preferred_element_type=jnp.float32
    ).astype(jnp.bfloat16)
    channel_grad = lax.all_to_all(state_grad, "tok", split_axis=0, concat_axis=1, tiled=True)
    value_grad_channels, param_grad = mix_backward(
        channel_values, channel_grad.reshape(blocked), pieces, powers, lams, coefs, starts, taps
    )
    states = param_grad.shape[1] // 2
    param_grad = jnp.stack([param_grad[:, :states], param_grad[:, states:]])
    param_sum = lax.psum(param_grad, "rep")
    value_grad = lax.all_to_all(
        value_grad_channels.reshape(channels, length),
        "tok",
        split_axis=1,
        concat_axis=0,
        tiled=True,
    )
    value_pre_grad = value_back(value_grad.astype(jnp.float32))[0].astype(jnp.bfloat16)
    up_pre_grad = upper_back(upper_grad)[0].astype(jnp.bfloat16)
    up_grad = jnp.einsum("td,th->dh", normed_low, up_pre_grad, preferred_element_type=jnp.float32)
    value_w_grad = jnp.einsum(
        "td,ct->dc", normed_low, value_pre_grad, preferred_element_type=jnp.float32
    )
    normed_grad = jnp.einsum("th,dh->td", up_pre_grad, up_full, preferred_element_type=jnp.float32)
    normed_grad = normed_grad + jnp.einsum(
        "ct,dc->td", value_pre_grad, value_full, preferred_element_type=jnp.float32
    )
    row_grad, norm_grad = norm_back(normed_grad)
    token_grad = (row_grad + grad_rows.astype(jnp.float32))[None]
    expand_sum, down_sum = (
        lax.psum_scatter(expand_grad, ("tok", "rep"), scatter_dimension=0, tiled=True),
        lax.psum_scatter(down_grad, ("tok", "rep"), scatter_dimension=0, tiled=True),
    )
    up_sum, value_sum, norm_sum = (
        lax.psum_scatter(up_grad, ("tok", "rep"), scatter_dimension=0, tiled=True),
        lax.psum_scatter(value_w_grad, ("tok", "rep"), scatter_dimension=0, tiled=True),
        lax.psum_scatter(norm_grad, ("tok", "rep"), scatter_dimension=1, tiled=True),
    )
    step_value = jnp.float32(STEP)
    up_next, up_mean_next, up_square_next = adam_step(
        up_weight, up_sum, up_mean, up_square, step_value, 0.08, 0.1
    )
    value_next, value_mean_next, value_square_next = adam_step(
        value_weight, value_sum, value_mean, value_square, step_value, 0.08, 0.1
    )
    expand_next, expand_mean_next, expand_square_next = adam_step(
        expand_weight, expand_sum, expand_mean, expand_square, step_value, 0.08, 0.1
    )
    down_next, down_mean_next, down_square_next = adam_step(
        down_weight, down_sum, down_mean, down_square, step_value, 0.08, 0.1
    )
    norm_next, norm_mean_next, norm_square_next = adam_step(
        norm_params, norm_sum, norm_mean, norm_square, step_value, 1.0, 0.0
    )
    state_next, state_mean_next, state_square_next = adam_step(
        state_params, param_sum, state_mean, state_square, step_value, 0.006, 0.0
    )
    return (
        layer_out,
        token_grad,
        up_next,
        up_mean_next,
        up_square_next,
        value_next,
        value_mean_next,
        value_square_next,
        expand_next,
        expand_mean_next,
        expand_square_next,
        down_next,
        down_mean_next,
        down_square_next,
        norm_next,
        norm_mean_next,
        norm_square_next,
        state_next,
        state_mean_next,
        state_square_next,
    )


def solution(mesh):
    placed = (
        P("rep", "tok", None),
        P("rep", "tok", None),
        P("rep", None),
        P(("tok", "rep"), None),
        P(("tok", "rep"), None),
        P(("tok", "rep"), None),
        P(("tok", "rep"), None),
        P(None, ("tok", "rep")),
        P(None, "tok", None),
        P(None, "tok", None),
        P(("tok", "rep"), None),
        P(("tok", "rep"), None),
        P(("tok", "rep"), None),
        P(("tok", "rep"), None),
        P(("tok", "rep"), None),
        P(("tok", "rep"), None),
        P(("tok", "rep"), None),
        P(("tok", "rep"), None),
        P(None, ("tok", "rep")),
        P(None, ("tok", "rep")),
        P(None, "tok", None),
        P(None, "tok", None),
    )
    return jax.shard_map(
        per_device,
        mesh=mesh,
        in_specs=placed,
        out_specs=(
            P("rep", "tok", None),
            P("rep", "tok", None),
            P(("tok", "rep"), None),
            P(("tok", "rep"), None),
            P(("tok", "rep"), None),
            P(("tok", "rep"), None),
            P(("tok", "rep"), None),
            P(("tok", "rep"), None),
            P(("tok", "rep"), None),
            P(("tok", "rep"), None),
            P(("tok", "rep"), None),
            P(("tok", "rep"), None),
            P(("tok", "rep"), None),
            P(("tok", "rep"), None),
            P(None, ("tok", "rep")),
            P(None, ("tok", "rep")),
            P(None, ("tok", "rep")),
            P(None, "tok", None),
            P(None, "tok", None),
            P(None, "tok", None),
        ),
        check_vma=False,
    )
```

profile of v0, /device:TPU:0, one launch (start us, length us, event | category | flops | bytes accessed | tf_op | source)
XLA Modules:
  0.0 1092.7 jit_solution(1094379529066625816)
XLA Ops:
  7.2 1.5 convert_element_type.93
  8.8 1.6 convert_element_type.95
  10.4 1.7 convert_element_type.86
  12.2 1.7 convert_element_type.97
  13.9 0.8 copy.86
  14.9 0.2 convert_reduce_fusion.2
  15.4 0.7 convert_bitcast_fusion.1
  16.1 43.0 %all-gather = bf16[32,32,2]{1,2,0:T(2,128)(2,1)S(1)} all-gather(bf16[1,32,2]{1,2,0:T(2,128)(2,1)S(1)} %convert_bitcast_fusion.1), channel_id=1, replica_groups=mesh['tok'=16,'rep'=2] {'tok','rep'}, dimensions={0}, use_global_device_ids=true | all-gather | bytes 4224 | tf_op jit(solution)/shard_map/all_gather | solution.py:399
  59.5 0.9 slice_bitcast_fusion.3
  60.4 0.9 negate_bitcast_fusion
  61.3 4.5 fusion.23
  66.0 0.3 fusion.21
  66.3 1.5 pad_maximum_fusion
  68.0 2.6 multiply_convert_fusion.2
  70.5 0.8 copy.87
  71.4 4.5 all-to-all-start
  76.0 2.8 copy.89.low_ref
  79.0 8.0 all-to-all-done
  87.2 27.9 %mix_forward.1 = (bf16[32,32,128]{2,1,0:T(8,128)(2,1)S(1)}, f32[1536,1024]{1,0:T(8,128)}, bf16[32,128,128]{2,1,0:T(8,128)(2,1)S(1)}) custom-call(f32[48]{0:T(128)S(1)} %add_convert_fusion.follows_ref, bf16[48,32]{1,0:T(8,128)(2,1)S(1)} %fusion.47.pick_ref, bf16[48,128]{1,0:T(8,128)(2,1)S(1)} %fusion.49.mask_ref, ...), custom_call_target="tpu_custom_call" | custom-call | flops 16106127360 | bytes 16777216 | tf_op jit(solution)/shard_map/mix_forward/pallas_call | solution.py:295
  115.1 1.0 copy-done
  116.3 17.1 %all_to_all.64 = bf16[32,16,256]{2,0,1:T(8,128)(2,1)} all-to-all(bf16[32,16,256]{2,0,1:T(8,128)(2,1)S(1)} %copy.90), channel_id=1, replica_groups=mesh['tok'=16,'rep'=2] {'tok'}, dimensions={1} | all-to-all | bytes 524288 | tf_op jit(solution)/shard_map/all_to_all | solution.py:419
  133.4 0.5 all-gather.10.cloned.1.call-done
  133.9 4.8 fusion.68
  138.6 66.2 %all-gather.6.cloned.1.call-done = bf16[1024,3072]{1,0:T(8,128)(2,1)} async-done(((bf16[32,3072]{1,0:T(8,128)(2,1)}), bf16[1024,3072]{1,0:T(8,128)(2,1)}) %all-gather.6.cloned.1.call-update) | async-done | bytes 6291472 | tf_op jit(solution)/shard_map/all_gather | solution.py:395
  204.8 6.4 fusion.58
  211.1 65.0 %all-gather.12.cloned.1.call-done = bf16[3072,1024]{1,0:T(8,128)(2,1)} async-done(((bf16[96,1024]{1,0:T(8,128)(2,1)}), bf16[3072,1024]{1,0:T(8,128)(2,1)}) %all-gather.12.cloned.1.call-update) | async-done | bytes 6291472 | tf_op jit(solution)/shard_map/all_gather | solution.py:398
  276.1 10.5 multiply_convert_fusion
  286.7 1.2 copy-done.11
  287.9 1.0 fusion.17
  289.0 14.2 %all_to_all.65 = bf16[16,32,256]{2,1,0:T(8,128)(2,1)S(1)} all-to-all(bf16[16,32,256]{2,1,0:T(8,128)(2,1)S(1)} %bitcast.123), channel_id=1, replica_groups=mesh['tok'=16,'rep'=2] {'tok'}, dimensions={0} | all-to-all | bytes 524288 | tf_op jit(solution)/shard_map/all_to_all | solution.py:439
  303.5 1.2 copy-done.1
  304.7 37.2 %mix_backward.1 = (bf16[32,32,128]{2,1,0:T(8,128)(2,1)S(1)}, f32[32,1024]{1,0:T(8,128)S(1)}) custom-call(f32[48]{0:T(128)S(1)} %add_convert_fusion.follows_ref, bf16[48,32]{1,0:T(8,128)(2,1)S(1)} %fusion.47.pick_ref, bf16[48,128]{1,0:T(8,128)(2,1)S(1)} %fusion.49.mask_ref, bf16[32,32,128]{2,1,0:T(8,128)(2,1)S(1)} %reshape.190.values_ref, ...), custom_call_target="tpu_custom_call" | custom-call | flops 16106127360 | bytes 16777216 | tf_op jit(solution)/shard_map/mix_backward/pallas_call | solution.py:326
  342.1 0.8 copy.94
  342.9 3.7 all-to-all-start.3
  346.6 6.1 fusion.69
  352.8 0.7 pad_maximum_fusion.3
  353.5 2.4 all-to-all-done.3
  356.0 0.2 copy.95
  356.2 0.4 fusion.31
  356.6 1.8 fusion.60
  358.4 1.1 fusion.20
  359.6 1.1 copy.97
  360.7 1.9 fusion.53
  362.7 5.1 fusion.70
  367.9 1.3 copy-done.10
  369.2 6.5 fusion.55
  375.8 0.3 reduce-scatter.14.cloned.1.call-start
  376.0 0.8 copy-done.7
  376.8 7.8 fusion.32
  384.6 5.9 fusion.14
  390.6 1.8 multiply_subtract_fusion.3
  392.4 0.7 negate_multiply_fusion
  393.1 1.4 add_bitcast_fusion
  394.5 115.6 %reduce-scatter.16.cloned.1.call-done = f32[32,2]{1,0:T(8,128)} async-done(((f32[1024,2]{1,0:T(8,128)}), f32[32,2]{1,0:T(8,128)}) %reduce-scatter.16.cloned.1.call-update) | async-done | bytes 272
  510.1 0.8 copy.98
  510.9 1.3 add_subtract_fusion
  512.2 132.9 %reduce-scatter.10.cloned.1.call-done = f32[32,512]{1,0:T(8,128)} async-done(((f32[1024,512]{1,0:T(8,128)}), f32[32,512]{1,0:T(8,128)}) %reduce-scatter.10.cloned.1.call-update) | async-done | bytes 65552 | tf_op jit(solution)/shard_map/reduce_scatter | solution.py:471
  645.1 1.6 multiply_subtract_fusion.4
  646.7 114.3 %reduce-scatter.12.cloned.1.call-done = f32[16,3072]{1,0:T(8,128)} async-done(((f32[512,3072]{1,0:T(8,128)}), f32[16,3072]{1,0:T(8,128)}) %reduce-scatter.12.cloned.1.call-update) | async-done | bytes 196624 | tf_op jit(solution)/shard_map/reduce_scatter | solution.py:466
  761.0 2.0 multiply_subtract_fusion.2
  763.0 159.7 %reduce-scatter.8.cloned.1.call-done = f32[32,3072]{1,0:T(8,128)} async-done(((f32[1024,3072]{1,0:T(8,128)}), f32[32,3072]{1,0:T(8,128)}) %reduce-scatter.8.cloned.1.call-update) | async-done | bytes 393232 | tf_op jit(solution)/shard_map/reduce_scatter | solution.py:470
  922.8 2.3 multiply_subtract_fusion.1
  925.1 158.4 %reduce-scatter.14.cloned.1.call-done = f32[96,1024]{1,0:T(8,128)} async-done(((f32[3072,1024]{1,0:T(8,128)}), f32[96,1024]{1,0:T(8,128)}) %reduce-scatter.14.cloned.1.call-update) | async-done | bytes 393232 | tf_op jit(solution)/shard_map/reduce_scatter | solution.py:467
  1083.5 2.2 multiply_subtract_fusion
  (111 shorter events, 3.1 us)
Async XLA Ops:
  7.2 60.8 %all-gather.8.cloned.1.call-start = ((), (), s32[]{:S(2)}) async-start(), calls=%async_computation.10 | async-start | bytes 1081344 | tf_op jit(solution)/shard_map/all_gather | solution.py:396
  8.7 125.1 %all-gather.10.cloned.1.call-start = ((), (), s32[]{:S(2)}) async-start(), calls=%async_computation.11 | async-start | bytes 3244032 | tf_op jit(solution)/shard_map/all_gather | solution.py:397
  10.4 194.4 %all-gather.6.cloned.1.call-start = ((), (), s32[]{:S(2)}) async-start(), calls=%async_computation.9 | async-start | bytes 6488064 | tf_op jit(solution)/shard_map/all_gather | solution.py:395
  12.1 264.0 %all-gather.12.cloned.1.call-start = ((), (), s32[]{:S(2)}) async-start(), calls=%async_computation.12 | async-start | bytes 6488064 | tf_op jit(solution)/shard_map/all_gather | solution.py:398
  13.9 52.0 %copy-start.2 = (bf16[1,256,1024]{2,1,0:T(8,128)(2,1)S(1)}, bf16[1,256,1024]{2,1,0:T(8,128)(2,1)}, u32[]{:S(2)}) copy-start(bf16[1,256,1024]{2,1,0:T(8,128)(2,1)} %param.23) | copy-start | bytes 1572868
  66.3 1.7 copy-start.27
  67.8 8.1 copy-start.22
  71.4 15.6 %all-to-all-start = ((bf16[16,32,256]{2,1,0:T(8,128)(2,1)}), bf16[16,32,256]{2,1,0:T(8,128)(2,1)S(1)}, u32[]{:S(2)}, u32[]{:S(2)}) async-start(bf16[16,32,256]{2,1,0:T(8,128)(2,1)} %bitcast.8), calls=%async_computation | async-start | bytes 524288 | tf_op jit(solution)/shard_map/all_to_all | solution.py:410
  115.1 1.0 copy-start
  133.9 70.9 %copy-start.3 = (bf16[1,256,1024]{2,1,0:T(8,128)(2,1)S(1)}, bf16[1,256,1024]{2,1,0:T(8,128)(2,1)}, u32[]{:S(2)}) copy-start(bf16[1,256,1024]{2,1,0:T(8,128)(2,1)} %param.23) | copy-start | bytes 1572868
  133.9 70.9 %copy-start.23 = (f32[256]{0:T(256)S(1)}, f32[256]{0:T(256)}, u32[]{:S(2)}) copy-start(f32[256]{0:T(256)} %copy-done.22) | copy-start | bytes 3076
  276.1 11.8 %copy-start.5 = (bf16[512,3072]{1,0:T(8,128)(2,1)S(1)}, bf16[512,3072]{1,0:T(8,128)(2,1)}, u32[]{:S(2)}) copy-start(bf16[512,3072]{1,0:T(8,128)(2,1)} %all-gather.10.cloned.1.call-done) | copy-start | bytes 9437188
  286.7 1.2 copy-start.11
  303.5 1.2 copy-start.1
  342.9 13.0 %all-to-all-start.3 = ((bf16[32,16,256]{2,0,1:T(8,128)(2,1)}), bf16[32,16,256]{2,0,1:T(8,128)(2,1)S(1)}, u32[]{:S(2)}, u32[]{:S(2)}) async-start(bf16[32,16,256]{2,0,1:T(8,128)(2,1)} %copy.94), calls=%async_computation.3 | async-start | bytes 524288 | tf_op jit(solution)/shard_map/all_to_all | solution.py:446
  346.6 44.0 %all-reduce.4.cloned.1.call-start = ((), (), s32[]{:S(2)}) async-start(), calls=%async_computation.17 | async-start | bytes 262144 | tf_op jit(solution)/shard_map/psum | solution.py:445
  346.6 9.5 copy-start.15
  352.7 3.8 copy-start.4
  352.7 3.8 copy-start.12
  353.5 156.6 %reduce-scatter.16.cloned.1.call-start = ((), (), s32[]{:S(2)}) async-start(), calls=%async_computation.18 | async-start | bytes 540672
  355.9 2.5 copy-start.28
  356.0 2.5 copy-start.24
  358.4 4.2 copy-start.25
  359.5 3.2 copy-start.6
  360.6 284.5 %reduce-scatter.10.cloned.1.call-start = ((), (), s32[]{:S(2)}) async-start(), calls=%async_computation.14 | async-start | bytes 2162688 | tf_op jit(solution)/shard_map/reduce_scatter | solution.py:471
  362.6 398.4 %reduce-scatter.12.cloned.1.call-start = ((), (), s32[]{:S(2)}) async-start(), calls=%async_computation.15 | async-start | bytes 6488064 | tf_op jit(solution)/shard_map/reduce_scatter | solution.py:466
  367.8 1.4 copy-start.10
  367.9 554.9 %reduce-scatter.8.cloned.1.call-start = ((), (), s32[]{:S(2)}) async-start(), calls=%async_computation.13 | async-start | bytes 12976128 | tf_op jit(solution)/shard_map/reduce_scatter | solution.py:470
  375.7 1.0 copy-start.7
  375.8 707.7 %reduce-scatter.14.cloned.1.call-start = ((), (), s32[]{:S(2)}) async-start(), calls=%async_computation.16 | async-start | bytes 12976128 | tf_op jit(solution)/shard_map/reduce_scatter | solution.py:467
  384.6 6.0 copy-start.14
  384.6 6.0 copy-start.20
  384.6 6.0 copy-start.21
  384.6 8.5 copy-start.26
  390.5 254.6 %copy-start.19 = (f32[32,512]{1,0:T(8,128)S(1)}, f32[32,512]{1,0:T(8,128)}, u32[]{:S(2)}) copy-start(f32[32,512]{1,0:T(8,128)} %param.27) | copy-start | bytes 196612
  390.5 370.5 %copy-start.13 = (f32[16,3072]{1,0:T(8,128)S(1)}, f32[16,3072]{1,0:T(8,128)}, u32[]{:S(2)}) copy-start(f32[16,3072]{1,0:T(8,128)} %param.28) | copy-start | bytes 589828
  390.5 532.2 %copy-start.8 = (f32[32,3072]{1,0:T(8,128)S(1)}, f32[32,3072]{1,0:T(8,128)}, u32[]{:S(2)}) copy-start(f32[32,3072]{1,0:T(8,128)} %param.26) | copy-start | bytes 1179652
  390.5 532.2 %copy-start.16 = (f32[32,3072]{1,0:T(8,128)S(1)}, f32[32,3072]{1,0:T(8,128)}, u32[]{:S(2)}) copy-start(f32[32,3072]{1,0:T(8,128)} %param.34) | copy-start | bytes 1179652
  393.1 690.4 %copy-start.9 = (f32[96,1024]{1,0:T(8,128)S(1)}, f32[96,1024]{1,0:T(8,128)}, u32[]{:S(2)}) copy-start(f32[96,1024]{1,0:T(8,128)} %param.29) | copy-start | bytes 1179652
  394.5 689.0 %copy-start.17 = (f32[96,1024]{1,0:T(8,128)S(1)}, f32[96,1024]{1,0:T(8,128)}, u32[]{:S(2)}) copy-start(f32[96,1024]{1,0:T(8,128)} %param.40) | copy-start | bytes 1179652
  394.5 689.0 %copy-start.18 = (f32[96,1024]{1,0:T(8,128)S(1)}, f32[96,1024]{1,0:T(8,128)}, u32[]{:S(2)}) copy-start(f32[96,1024]{1,0:T(8,128)} %param.39) | copy-start | bytes 1179652
Sparse Core Ops, SparseCore 0:
  11.5 56.4 all-gather.7
  71.4 62.4 all-gather.9
  137.3 67.4 all-gather.5
  208.1 68.0 all-gather.11
  353.6 19.1 all-reduce.3
  374.9 135.1 reduce-scatter.15
  512.4 132.6 reduce-scatter.9
  650.8 110.2 reduce-scatter.11
  768.1 154.6 reduce-scatter.7
  928.6 154.7 reduce-scatter.13
where the time goes:
time: 1100 us; the launch traced here: 1090 us
  waiting for transfers between devices  823 us (75%)
  blocking collectives  74.4 us (7%)
  Pallas kernels  65.2 us (6%)
  matrix products  60.4 us (5%)
  other arithmetic  31.1 us (3%)
  local copies, waits for them, and re-layouts  14.8 us (1%)
  between operations  14.8 us (1%)
    reduce_scatter x1, waiting for transfers between devices, per_device(): lax.psum_scatter(up_grad, ('tok', 'rep'), scatter_dimension=0, tiled=True)  160 us
    reduce_scatter x1, waiting for transfers between devices, per_device(): lax.psum_scatter(down_grad, ('tok', 'rep'), scatter_dimension=0, tiled=True)  158 us
    reduce_scatter x1, waiting for transfers between devices, per_device(): lax.psum_scatter(value_w_grad, ('tok', 'rep'), scatter_dimension=0, tiled...  133 us
    unnamed x11, waiting for transfers between devices  116 us
    reduce_scatter x1, waiting for transfers between devices, per_device(): lax.psum_scatter(expand_grad, ('tok', 'rep'), scatter_dimension=0, tiled=...  114 us
    all_gather x1, waiting for transfers between devices, per_device(): lax.all_gather(up_weight.astype(jnp.bfloat16), ('tok', 'rep'), axis=0, ti...  66.2 us
    all_gather x1, waiting for transfers between devices, per_device(): lax.all_gather(down_weight.astype(jnp.bfloat16), ('tok', 'rep'), axis=0,...  65 us
    all_gather x1, blocking collectives, per_device(): lax.all_gather(norm_params.astype(jnp.bfloat16), ('tok', 'rep'), axis=1,...  43 us
  transfers between devices with their start and end apart: 12, of which 11 were waited for; matrix products, arithmetic and copies ran while one was open for 8% of the time, Pallas kernels for 3%

commit v1 on v0

--- a/solution.py
+++ b/solution.py
@@ -19,13 +19,6 @@
 
 def gelu_curve(values):
     return jax.nn.gelu(values, approximate=True)
-
-
-def layer_norm(rows, norm_weights):
-    average = jnp.mean(rows, axis=-1, keepdims=True)
-    centered = rows - average
-    variance = jnp.mean(centered * centered, axis=-1, keepdims=True)
-    return centered * lax.rsqrt(variance + epsilon_norm) * norm_weights[0] + norm_weights[1]
 
 
 def pieces_of(lengths_row, length):
@@ -96,8 +89,11 @@
                 else:
                     re = jnp.concatenate([nr, re], axis=0)
                     im = jnp.concatenate([ni, im], axis=0)
-            ref[c, :, re_lanes] = re.astype(jnp.bfloat16)
-            ref[c, :, im_lanes] = im.astype(jnp.bfloat16)
+            for lanes, entries in ((re_lanes, re), (im_lanes, im)):
+                high, rest = split_rows(entries)
+                ref[c, 0, :, lanes] = high
+                if ref.shape[1] > 1:
+                    ref[c, 1, :, lanes] = rest
 
 
 def nt(a, b):
@@ -133,7 +129,7 @@
 
 def get_rows(ref, c, places, group):
     chunks = [ref[k, pl.ds(c, places, stride=group), :] for k in range(ref.shape[0])]
-    return jnp.concatenate([chunk.astype(jnp.bfloat16) for chunk in chunks], axis=1)
+    return jnp.concatenate(chunks, axis=1)
 
 
 def get_step(ref, rows, half):
@@ -149,8 +145,9 @@
 
 def forward_kernel(
     active, follows_ref, pick_ref, mask_ref, values_ref, low_ref, lam_ref, coef_ref,
-    out_ref, start_ref, taps_ref, up_ref, down_ref, work_ref,
+    out_ref, start_ref, taps_ref, token_ref, up_ref, down_ref, work_ref,
 ):
+    token_ref[...] = jnp.zeros_like(token_ref)
     places = pick_ref.shape[0]
     group, states = coef_ref.shape[0], coef_ref.shape[1] // 2
     if active < group:
@@ -160,7 +157,7 @@
     for c in range(active):
         fill_tables(c, states, low_ref, up_ref, down_ref)
         spread = nn(pick, values_ref[c]).astype(jnp.bfloat16) * mask
-        put_rows(work_ref, c, places, group, nn(spread, down_ref[c]))
+        put_rows(work_ref, c, places, group, nn(spread, down_ref[c, 0]) + nn(spread, down_ref[c, 1]))
     lam_re, lam_im = lam_ref[0, :, :states], lam_ref[0, :, states:]
     far_re, far_im = lam_ref[1, :, :states], lam_ref[1, :, states:]
     coef_re, coef_im = coef_ref[:, :states], coef_ref[:, states:]
@@ -187,20 +184,26 @@
         row = jnp.concatenate([coef_ref[c : c + 1, :states], -coef_ref[c : c + 1, states:]], axis=1)
         high, rest = split_rows(row)
         rows = jnp.concatenate([high, rest, jnp.zeros((14, 2 * states), jnp.bfloat16)], axis=0)
-        mixed = get_rows(work_ref, c, places, group)
-        carried = nt(jnp.concatenate([mixed, rows], axis=0), up_ref[c])
+        mixed = split_rows(get_rows(work_ref, c, places, group))
+        stack = jnp.concatenate([mixed[0], rows, mixed[1]], axis=0)
+        carried = nt(stack, up_ref[c, 0])
+        finer = nt(stack[: places + 16], up_ref[c, 1])
+        carried = jnp.concatenate(
+            [carried[:places] + carried[places + 16 :], carried[places : places + 16]], axis=0
+        ) + finer
         kernel_row = carried[places : places + 1] + carried[places + 1 : places + 2]
-        taps = toeplitz(kernel_row).astype(jnp.bfloat16)
-        taps_ref[c] = taps
+        taps = split_rows(toeplitz(kernel_row))
+        taps_ref[c] = taps[0]
         spread = nn(pick, values_ref[c]).astype(jnp.bfloat16) * mask
-        result = (carried[:places] + nn(spread, taps)).astype(jnp.bfloat16) * mask
+        result = (carried[:places] + nn(spread, taps[0]) + nn(spread, taps[1])).astype(jnp.bfloat16) * mask
         out_ref[c] = tn(pick, result).astype(jnp.bfloat16)
 
 
 def backward_kernel(
     active, follows_ref, pick_ref, mask_ref, values_ref, grads_ref, low_ref, lam_ref, coef_ref,
-    start_ref, taps_ref, out_ref, sum_ref, up_ref, down_ref, work_ref,
+    start_ref, taps_ref, out_ref, sum_ref, token_ref, up_ref, down_ref, work_ref,
 ):
+    token_ref[...] = jnp.zeros_like(token_ref)
     places = pick_ref.shape[0]
     group, states = coef_ref.shape[0], coef_ref.shape[1] // 2
     if active < group:
@@ -220,7 +223,7 @@
         lag_sum = jnp.sum(jnp.where(columns <= rows, skewed, 0.0), axis=0, keepdims=True)
         high, rest = split_rows(lag_sum)
         extra = jnp.concatenate([high, rest, jnp.zeros((14, BLOCK), jnp.bfloat16)], axis=0)
-        folded = nn(jnp.concatenate([grads, extra], axis=0), up_ref[c])
+        folded = nn(jnp.concatenate([grads, extra], axis=0), up_ref[c, 0])
         put_rows(work_ref, c, places, group, folded[:places])
         sum_ref[c : c + 1, :] = folded[places : places + 1] + folded[places + 1 : places + 2]
     lam_re, lam_im = lam_ref[0, :, :states], lam_ref[0, :, states:]
@@ -251,9 +254,9 @@
     sum_ref[:, :states] = sum_ref[:, :states] + total_re
     sum_ref[:, states:] = -(sum_ref[:, states:] + total_im)
     for c in range(active):
-        mixed = get_rows(work_ref, c, places, group)
+        mixed = get_rows(work_ref, c, places, group).astype(jnp.bfloat16)
         grads = nn(pick, grads_ref[c]).astype(jnp.bfloat16) * mask
-        result = nt(mixed, down_ref[c]) + nt(grads, taps_ref[c])
+        result = nt(mixed, down_ref[c, 0]) + nt(grads, taps_ref[c])
         out_ref[c] = tn(pick, result.astype(jnp.bfloat16) * mask).astype(jnp.bfloat16)
 
 
@@ -261,92 +264,150 @@
     return pl.BlockSpec(shape, lambda i: (0,) * len(shape))
 
 
-def mixer_specs(active, group, blocks, places, states):
+def part(shape, place, dim=0):
+    index = tuple(place if k == dim else 0 for k in range(len(shape)))
+    return pl.BlockSpec(shape, lambda i: index)
+
+
+class Parts:
+    def __init__(self, kernel, name, inputs, results, scratch, parts, flops):
+        self.kernel, self.name, self.inputs, self.results = kernel, name, inputs, results
+        self.scratch, self.parts, self.flops = scratch, parts, flops
+        self.done, self.outs, self.waits = 0, [], []
+
+    def run(self, *waits):
+        self.waits += waits
+        if self.done < self.parts - 1:
+            return self.call()
+        return None
+
+    def last(self, *waits):
+        self.waits += waits
+        return self.call()
+
+    def call(self):
+        k = self.done
+        operands = [array for array, _ in self.inputs]
+        specs = [spec(k) for _, spec in self.inputs]
+        count, waits, before = len(operands), self.waits, list(self.outs)
+
+        def body(*refs):
+            self.kernel(*refs[:count], *refs[count + len(waits) + len(before) :])
+
+        token = jax.ShapeDtypeStruct((8, 128), jnp.float32)
+        *self.outs, token = pl.pallas_call(
+            body,
+            grid=(1,),
+            in_specs=specs + [pl.BlockSpec(memory_space=pl.ANY)] * (len(waits) + len(before)),
+            out_specs=[spec(k) for _, spec in self.results] + [whole((8, 128))],
+            out_shape=[shape for shape, _ in self.results] + [token],
+            input_output_aliases={count + len(waits) + n: n for n in range(len(before))},
+            scratch_shapes=self.scratch,
+            compiler_params=pltpu.CompilerParams(vmem_limit_bytes=48 * 2**20),
+            cost_estimate=pl.CostEstimate(
+                flops=self.flops, bytes_accessed=4 * 2**20, transcendentals=0
+            ),
+            name=self.name,
+        )(*operands, *waits, *before)
+        self.done, self.waits = k + 1, []
+        return token
+
+
+def scratches(active, group, places, states, tables):
     return [
-        pl.BlockSpec(memory_space=pltpu.SMEM),
-        whole((places, blocks)),
-        whole((places, BLOCK)),
-        pl.BlockSpec((active, blocks, BLOCK), lambda i: (i, 0, 0)),
-    ], [
-        pl.BlockSpec((active, 16, 2 * states), lambda i: (i, 0, 0)),
-        pl.BlockSpec((2, group, 2 * states), lambda i: (0, i, 0)),
-        pl.BlockSpec((group, 2 * states), lambda i: (i, 0)),
-    ]
-
-
-def scratches(active, group, places, states):
-    return [
-        pltpu.VMEM((active, BLOCK, 2 * states), jnp.bfloat16),
-        pltpu.VMEM((active, BLOCK, 2 * states), jnp.bfloat16),
+        pltpu.VMEM((active, tables, BLOCK, 2 * states), jnp.bfloat16),
+        pltpu.VMEM((active, tables, BLOCK, 2 * states), jnp.bfloat16),
         pltpu.VMEM((2 * states // 128, places * group, 128), jnp.float32),
     ]
+
+
+def padded(values, lams, coefs):
+    channels = values.shape[0]
+    group, active = 8, min(8, channels)
+    spare = max(0, group - channels)
+    lams = jnp.pad(lams, ((0, 0), (0, spare), (0, 0)))
+    coefs = jnp.pad(coefs, ((0, spare), (0, 0)))
+    return group, active, spare, lams, coefs
 
 
 def mix_forward(values, pieces, powers, lams, coefs):
     channels, blocks = values.shape[0], values.shape[1]
     pick, mask, follows = pieces
     places, states = pick.shape[0], coefs.shape[1] // 2
-    group, active = 8, min(8, channels)
-    spare = max(0, group - channels)
-    lams = jnp.pad(lams, ((0, 0), (0, spare), (0, 0)))
-    coefs = jnp.pad(coefs, ((0, spare), (0, 0)))
-    first, last = mixer_specs(active, group, blocks, places, states)
-    table = 2 * channels * places * BLOCK * 2 * states * 2
-    return pl.pallas_call(
+    group, active, spare, lams, coefs = padded(values, lams, coefs)
+    full = lambda shape: lambda k: whole(shape)
+    inputs = [
+        (follows, lambda k: pl.BlockSpec(memory_space=pltpu.SMEM)),
+        (pick, full((places, blocks))),
+        (mask, full((places, BLOCK))),
+        (values, lambda k: part((active, blocks, BLOCK), k)),
+        (powers, lambda k: part((active, 16, 2 * states), k)),
+        (lams, lambda k: part((2, group, 2 * states), k, 1)),
+        (coefs, lambda k: part((group, 2 * states), k)),
+    ]
+    f32 = jnp.float32
+    results = [
+        (
+            jax.ShapeDtypeStruct((channels, blocks, BLOCK), jnp.bfloat16),
+            lambda k: part((active, blocks, BLOCK), k),
+        ),
+        (
+            jax.ShapeDtypeStruct((places * (channels + spare), 2 * states), f32),
+            lambda k: part((places * group, 2 * states), k),
+        ),
+        (
+            jax.ShapeDtypeStruct((channels, BLOCK, BLOCK), jnp.bfloat16),
+            lambda k: part((active, BLOCK, BLOCK), k),
+        ),
+    ]
+    return Parts(
         functools.partial(forward_kernel, active),
-        grid=(channels // active,),
-        in_specs=first + last,
-        out_specs=[
-            pl.BlockSpec((active, blocks, BLOCK), lambda i: (i, 0, 0)),
-            pl.BlockSpec((places * group, 2 * states), lambda i: (i, 0)),
-            pl.BlockSpec((active, BLOCK, BLOCK), lambda i: (i, 0, 0)),
-        ],
-        out_shape=[
-            jax.ShapeDtypeStruct((channels, blocks, BLOCK), jnp.bfloat16),
-            jax.ShapeDtypeStruct((places * (channels + spare), 2 * states), jnp.float32),
-            jax.ShapeDtypeStruct((channels, BLOCK, BLOCK), jnp.bfloat16),
-        ],
-        scratch_shapes=scratches(active, group, places, states),
-        compiler_params=pltpu.CompilerParams(vmem_limit_bytes=48 * 2**20),
-        cost_estimate=pl.CostEstimate(flops=20 * table, bytes_accessed=16 * 2**20, transcendentals=0),
-        name="mix_forward",
-    )(follows, pick, mask, values, powers, lams, coefs)
+        "mix_forward",
+        inputs,
+        results,
+        scratches(active, group, places, states, 2),
+        channels // active,
+        8 * 10**9,
+    )
 
 
 def mix_backward(values, grads, pieces, powers, lams, coefs, starts, taps):
     channels, blocks = values.shape[0], values.shape[1]
     pick, mask, follows = pieces
     places, states = pick.shape[0], coefs.shape[1] // 2
-    group, active = 8, min(8, channels)
-    spare = max(0, group - channels)
-    lams = jnp.pad(lams, ((0, 0), (0, spare), (0, 0)))
-    coefs = jnp.pad(coefs, ((0, spare), (0, 0)))
-    first, last = mixer_specs(active, group, blocks, places, states)
-    table = 2 * channels * places * BLOCK * 2 * states * 2
-    result, sums = pl.pallas_call(
+    group, active, spare, lams, coefs = padded(values, lams, coefs)
+    full = lambda shape: lambda k: whole(shape)
+    inputs = [
+        (follows, lambda k: pl.BlockSpec(memory_space=pltpu.SMEM)),
+        (pick, full((places, blocks))),
+        (mask, full((places, BLOCK))),
+        (values, lambda k: part((active, blocks, BLOCK), k)),
+        (grads, lambda k: part((active, blocks, BLOCK), k)),
+        (powers, lambda k: part((active, 16, 2 * states), k)),
+        (lams, lambda k: part((2, group, 2 * states), k, 1)),
+        (coefs, lambda k: part((group, 2 * states), k)),
+        (starts, lambda k: part((places * group, 2 * states), k)),
+        (taps, lambda k: part((active, BLOCK, BLOCK), k)),
+    ]
+    results = [
+        (
+            jax.ShapeDtypeStruct((channels, blocks, BLOCK), jnp.bfloat16),
+            lambda k: part((active, blocks, BLOCK), k),
+        ),
+        (
+            jax.ShapeDtypeStruct((channels + spare, 2 * states), jnp.float32),
+            lambda k: part((group, 2 * states), k),
+        ),
+    ]
+    return Parts(
         functools.partial(backward_kernel, active),
-        grid=(channels // active,),
-        in_specs=first
-        + [pl.BlockSpec((active, blocks, BLOCK), lambda i: (i, 0, 0))]
-        + last
-        + [
-            pl.BlockSpec((places * group, 2 * states), lambda i: (i, 0)),
-            pl.BlockSpec((active, BLOCK, BLOCK), lambda i: (i, 0, 0)),
-        ],
-        out_specs=[
-            pl.BlockSpec((active, blocks, BLOCK), lambda i: (i, 0, 0)),
-            pl.BlockSpec((group, 2 * states), lambda i: (i, 0)),
-        ],
-        out_shape=[
-            jax.ShapeDtypeStruct((channels, blocks, BLOCK), jnp.bfloat16),
-            jax.ShapeDtypeStruct((channels + spare, 2 * states), jnp.float32),
-        ],
-        scratch_shapes=scratches(active, group, places, states),
-        compiler_params=pltpu.CompilerParams(vmem_limit_bytes=48 * 2**20),
-        cost_estimate=pl.CostEstimate(flops=20 * table, bytes_accessed=16 * 2**20, transcendentals=0),
-        name="mix_backward",
-    )(follows, pick, mask, values, grads, powers, lams, coefs, starts, taps)
-    return result, sums[:channels]
+        "mix_backward",
+        inputs,
+        results,
+        scratches(active, group, places, states, 1),
+        channels // active,
+        107 * 10**8,
+    )
 
 
 def mixer_inputs(poles, params):
@@ -367,7 +428,131 @@
     return (weight_new, first_new, second_new)
 
 
+class Cube:
+    def __init__(self, tok_size):
+        self.size = 2 * tok_size
+        bits = tok_size.bit_length() - 1
+        across = bits // 3
+        self.xs = [1 + k for k in range(across)]
+        self.ys = [1 + across + k for k in range(across)]
+        self.zs = [1 + k for k in range(2 * across, bits)]
+        self.place = lax.axis_index("tok") * 2 + lax.axis_index("rep")
+
+    def bit(self, b):
+        return lax.rem(lax.div(self.place, 1 << b), 2)
+
+    def swap(self, block, b):
+        pairs = [(i, i ^ (1 << b)) for i in range(self.size)]
+        return lax.ppermute(block, ("tok", "rep"), pairs)
+
+    def halves(self, block, have, b):
+        above = 1 << sum(1 for k in have if k > b)
+        split = block.reshape((above, 2, -1) + block.shape[1:])
+        index = self.bit(b)
+        mine = lax.dynamic_index_in_dim(split, index, 1, keepdims=False)
+        other = lax.dynamic_index_in_dim(split, 1 - index, 1, keepdims=False)
+        shape = (-1,) + block.shape[1:]
+        return mine.reshape(shape), other.reshape(shape)
+
+    def split(self, block):
+        stack = block.reshape((self.size, -1) + block.shape[1:])
+        return self.halves(stack, range(self.size.bit_length() - 1), 0)
+
+    def merge(self, mine, other):
+        swapped = self.bit(0) == 1
+        first, second = jnp.where(swapped, other, mine), jnp.where(swapped, mine, other)
+        pair = jnp.stack([first, second], axis=1)
+        return pair.reshape((-1,) + pair.shape[3:])
+
+
+class Gather:
+    def __init__(self, cube, shard, order):
+        self.cube, self.order, self.have = cube, list(order), []
+        self.block = shard[None]
+
+    def send(self, *waits):
+        self.arriving = self.cube.swap(after(self.block, *waits), self.order[0])
+
+    def take(self, *waits):
+        b = self.order.pop(0)
+        other = after(self.arriving, *waits)
+        above = 1 << sum(1 for k in self.have if k > b)
+        shape = (above, 1, -1) + self.block.shape[1:]
+        mine, other = self.block.reshape(shape), other.reshape(shape)
+        joined = jnp.where(
+            self.cube.bit(b) == 1,
+            jnp.concatenate([other, mine], axis=1),
+            jnp.concatenate([mine, other], axis=1),
+        )
+        self.have.append(b)
+        self.block = joined.reshape((1 << len(self.have),) + self.block.shape[1:])
+
+    def rest(self, *waits):
+        if self.order:
+            self.take(*waits)
+        while self.order:
+            self.send()
+            self.take()
+
+    def both(self):
+        return self.block, self.cube.swap(self.block, 0)
+
+
+class Scatter:
+    def __init__(self, cube, keep, send, order, have, wide=()):
+        self.cube, self.order, self.have = cube, list(order), list(have)
+        self.keep, self.sent, self.wide = keep, send, wide
+        self.going = False
+
+    def send(self, *waits):
+        self.arriving = self.cube.swap(after(self.sent, *waits), self.order[0])
+        self.going = True
+
+    def take(self, *waits):
+        b, self.going = self.order.pop(0), False
+        self.have.remove(b)
+        total = self.keep + after(self.arriving, *waits).astype(jnp.float32)
+        if not self.order:
+            self.keep, self.sent = total, total
+            return
+        self.keep, sent = self.cube.halves(total, self.have, self.order[0])
+        self.sent = sent if self.order[0] in self.wide else sent.astype(jnp.bfloat16)
+
+    def rest(self):
+        while self.order:
+            if not self.going:
+                self.send()
+            self.take()
+        return self.keep[0]
+
+
+def after(block, *waits):
+    return lax.optimization_barrier((block, *waits))[0] if waits else block
+
+
+def products(cube, lefts, rights, first, have):
+    sides = [cube.halves(left, have, first) for left in lefts]
+
+    def product(side):
+        parts = []
+        for pair, right in zip(sides, rights):
+            left = pair[side]
+            parts.append(dot(left.reshape((-1, left.shape[2])), right, 1, 1))
+        shape = (-1, lefts[0].shape[1], rights[0].shape[0])
+        return (parts[0] + parts[1]).reshape(shape)
+
+    send = product(1).astype(jnp.bfloat16)
+    return product(0), send
+
+
+def dot(a, b, a_dim, b_dim):
+    return lax.dot_general(
+        a, b, (((a_dim,), (b_dim,)), ((), ())), preferred_element_type=jnp.float32
+    )
+
+
 def per_device(
+    tok_size,
     tokens,
     cotangent,
     lengths,
@@ -391,58 +576,175 @@
     state_mean,
     state_square,
 ):
-    up_full, value_full, expand_full, down_full, norm_full = (
-        lax.all_gather(up_weight.astype(jnp.bfloat16), ("tok", "rep"), axis=0, tiled=True),
-        lax.all_gather(value_weight.astype(jnp.bfloat16), ("tok", "rep"), axis=0, tiled=True),
-        lax.all_gather(expand_weight.astype(jnp.bfloat16), ("tok", "rep"), axis=0, tiled=True),
-        lax.all_gather(down_weight.astype(jnp.bfloat16), ("tok", "rep"), axis=0, tiled=True),
-        lax.all_gather(norm_params.astype(jnp.bfloat16), ("tok", "rep"), axis=1, tiled=True),
-    )
+    low = jnp.bfloat16
+    cube = Cube(tok_size)
+    xs, ys, zs = cube.xs, cube.ys, cube.zs
+    down_zs, tok_bits = zs[::-1], xs + ys + zs
+    nz, nx = len(zs), len(xs)
+
+    def flat(block):
+        return block.reshape((-1,) + block.shape[2:])
+
+    def dots(lefts, rights, left_dim, right_dim):
+        return dot(flat(lefts[0]), flat(rights[0]), left_dim, right_dim) + dot(
+            flat(lefts[1]), flat(rights[1]), left_dim, right_dim
+        )
+
+    inner = value_weight.shape[1]
+    norm_columns = jnp.pad(norm_params.T, ((0, 0), (0, 126)))
+    packed = jnp.concatenate([value_weight, norm_columns], axis=1).astype(low)
+    pack = Gather(cube, packed, xs + ys + down_zs)
+    up = Gather(cube, up_weight.astype(low), down_zs + xs + ys)
+    down = Gather(cube, down_weight.astype(low), down_zs + ys + xs)
+    expand = Gather(cube, expand_weight.astype(low), xs + ys + down_zs)
+
+    grad_rows = cotangent[0]
     token_rows = tokens[0].astype(jnp.float32)
-    normalized_rows, norm_back = jax.vjp(layer_norm, token_rows, norm_full.astype(jnp.float32))
-    normed_low = normalized_rows.astype(jnp.bfloat16)
-    up_pre = jnp.dot(normed_low, up_full, preferred_element_type=jnp.float32)
-    upper, upper_back = jax.vjp(gelu_curve, up_pre)
-    value_preactivation = jnp.einsum(
-        "td,dc->ct", normed_low, value_full, preferred_element_type=jnp.float32
-    )
+    width = token_rows.shape[1]
+    average = jnp.mean(token_rows, axis=1)
+    centered = token_rows - average[:, None]
+    scale = lax.rsqrt(jnp.mean(centered * centered, axis=1) + epsilon_norm)
+    hats = [
+        (part.astype(jnp.float32) - average) * scale for part in cube.split(tokens[0].T)
+    ]
+
+    up.send()
+    down.send()
+    expand.send()
+    for _ in range(2 * nx):
+        pack.send()
+        pack.take()
+    up.take()
+    down.take()
+    for _ in range(nz):
+        pack.send(up.block, down.block)
+        pack.take()
+    up.send(pack.block)
+    down.send(pack.block)
+    expand.take(pack.block)
+    if expand.order:
+        expand.send()
+    packs = pack.both()
+    values = [pack[:, :, :inner] for pack in packs]
+    gains = [pack[:, :, inner : inner + 1].astype(jnp.float32) for pack in packs]
+    shifts = [pack[:, :, inner + 1 : inner + 2].astype(jnp.float32) for pack in packs]
+    normed = [(h * g + b).astype(low) for h, g, b in zip(hats, gains, shifts)]
+    value_preactivation = dots(values, normed, 0, 0)
     value_act, value_back = jax.vjp(gelu_curve, value_preactivation)
-    channel_values = lax.all_to_all(
-        value_act.astype(jnp.bfloat16), "tok", split_axis=0, concat_axis=1, tiled=True
-    )
+    value_low = value_act.astype(low)
+    channel_values = lax.all_to_all(value_low, "tok", split_axis=0, concat_axis=1, tiled=True)
+
+    for _ in range(nz - 2):
+        up.take(value_low)
+        down.take(value_low)
+        up.send()
+        down.send()
+    for _ in range(2 * nx - 2):
+        expand.take(value_low)
+        expand.send()
+    poles, coefs = lax.optimization_barrier((state_poles, state_params, value_low))[:2]
     channels, length = channel_values.shape
     blocked = (channels, length // BLOCK, BLOCK)
     pieces = pieces_of(lengths[0], length)
-    powers, lams, coefs = mixer_inputs(state_poles, state_params)
+    powers, lams, coefs = mixer_inputs(poles, coefs)
     channel_values = channel_values.reshape(blocked)
-    state_out, starts, taps = mix_forward(channel_values, pieces, powers, lams, coefs)
+    grad_columns = grad_rows.T
+    normed_swapped = cube.swap(normed[1], 0)
+    columns_swapped = cube.swap(grad_columns, 0)
+    mixer = mix_forward(channel_values, pieces, powers, lams, coefs)
+
+    def run(*waits):
+        token = mixer.run(*waits)
+        return [] if token is None else [token]
+
+    up.take(channel_values)
+    down.take(channel_values)
+    expand.take(channel_values)
+    up.send()
+    down.send()
+    expand.send()
+    token = run(up.block, down.block, expand.block)
+    for _ in range(nx):
+        up.take(*token)
+        down.take(*token)
+        up.send()
+        down.send()
+    token = run(up.block, down.block)
+    expand.take(*token)
+    if expand.order:
+        expand.send()
+    token = run(*token, expand.block, normed_swapped, columns_swapped)
+    mixer.last()
+    state_out, starts, taps = mixer.outs
     token_states = lax.all_to_all(
         state_out.reshape(channels, length), "tok", split_axis=1, concat_axis=0, tiled=True
     )
-    expanded = jnp.einsum(
-        "ct,ch->th", token_states, expand_full, preferred_element_type=jnp.float32
-    )
-    gated_low = (upper * expanded).astype(jnp.bfloat16)
-    layer_rows = token_rows + jnp.dot(gated_low, down_full, preferred_element_type=jnp.float32)
-    layer_out = layer_rows.astype(jnp.bfloat16)[None]
-    grad_rows = cotangent[0]
-    down_grad = jnp.einsum("th,td->hd", gated_low, grad_rows, preferred_element_type=jnp.float32)
-    gated_grad = jnp.einsum("td,hd->th", grad_rows, down_full, preferred_element_type=jnp.float32)
-    expanded_grad = (gated_grad * upper).astype(jnp.bfloat16)
-    upper_grad = gated_grad * expanded
-    expand_grad = jnp.einsum(
-        "ct,th->ch", token_states, expanded_grad, preferred_element_type=jnp.float32
-    )
-    state_grad = jnp.einsum(
-        "th,ch->ct", expanded_grad, expand_full, preferred_element_type=jnp.float32
-    ).astype(jnp.bfloat16)
+    state_sides = cube.split(token_states)
+    expand.rest(token_states)
+    up.rest(token_states)
+    down.rest(token_states)
+    ups, downs, expands = up.both(), down.both(), expand.both()
+
+    upper, upper_back = jax.vjp(gelu_curve, dots(ups, normed, 0, 0))
+    gated_grad = cube.merge(
+        *[dot(flat(down), grad_rows, 1, 1).reshape(down.shape[:2] + (-1,)) for down in downs]
+    )
+    expanded = dots(expands, state_sides, 0, 0)
+    expanded_grad = (gated_grad * upper).astype(low)
+    state_grad = cube.merge(
+        *[
+            dot(flat(expand), expanded_grad, 1, 0).astype(low).reshape(expand.shape[:2] + (-1,))
+            for expand in expands
+        ]
+    )
     channel_grad = lax.all_to_all(state_grad, "tok", split_axis=0, concat_axis=1, tiled=True)
-    value_grad_channels, param_grad = mix_backward(
+    gated = (upper * expanded).astype(low)
+    gated_sides = cube.split(gated)
+    up_pre_grad = upper_back(gated_grad * expanded)[0].astype(low)
+
+    def both(block):
+        return block, cube.swap(block, 0)
+
+    def scatter(lefts, rights, order):
+        keep, send = products(cube, lefts, rights, order[0], tok_bits)
+        sums = Scatter(cube, keep, send, order, tok_bits)
+        sums.send()
+        return sums
+
+    down_sums = scatter(
+        (gated_sides[0], cube.swap(gated_sides[1], 0)),
+        (grad_columns, columns_swapped),
+        xs + ys + zs,
+    )
+    up_sums = scatter((normed[0], normed_swapped), both(up_pre_grad), ys + xs + zs)
+    expand_sums = scatter(
+        (state_sides[0], cube.swap(state_sides[1], 0)), both(expanded_grad), zs + ys + xs
+    )
+    layer_out = (token_rows + dots(gated_sides, downs, 0, 0)).astype(low)[None]
+
+    mixer = mix_backward(
         channel_values, channel_grad.reshape(blocked), pieces, powers, lams, coefs, starts, taps
     )
+    token = run(up_sums.sent, down_sums.sent, expand_sums.sent)
+    token = run()
+    expand_sums.take(*token)
+    expand_sums.send()
+    token = run(expand_sums.sent)
+    for _ in range(nx):
+        up_sums.take(*token)
+        down_sums.take(*token)
+        up_sums.send()
+        down_sums.send()
+    expand_sums.take(*token)
+    expand_sums.send()
+    mixer.last(up_sums.sent, down_sums.sent, expand_sums.sent)
+    value_grad_channels, param_grad = mixer.outs
     states = param_grad.shape[1] // 2
-    param_grad = jnp.stack([param_grad[:, :states], param_grad[:, states:]])
-    param_sum = lax.psum(param_grad, "rep")
+    param_grad = jnp.stack([param_grad[:channels, :states], param_grad[:channels, states:]])
+    param_sum = param_grad + cube.swap(param_grad, 0)
+    for sums in (up_sums, down_sums, expand_sums):
+        sums.arriving = after(sums.arriving, value_grad_channels)
+    value_grad_channels = after(value_grad_channels, up_sums.arriving, down_sums.arriving)
     value_grad = lax.all_to_all(
         value_grad_channels.reshape(channels, length),
         "tok",
@@ -450,27 +752,48 @@
         concat_axis=0,
         tiled=True,
     )
-    value_pre_grad = value_back(value_grad.astype(jnp.float32))[0].astype(jnp.bfloat16)
-    up_pre_grad = upper_back(upper_grad)[0].astype(jnp.bfloat16)
-    up_grad = jnp.einsum("td,th->dh", normed_low, up_pre_grad, preferred_element_type=jnp.float32)
-    value_w_grad = jnp.einsum(
-        "td,ct->dc", normed_low, value_pre_grad, preferred_element_type=jnp.float32
-    )
-    normed_grad = jnp.einsum("th,dh->td", up_pre_grad, up_full, preferred_element_type=jnp.float32)
-    normed_grad = normed_grad + jnp.einsum(
-        "ct,dc->td", value_pre_grad, value_full, preferred_element_type=jnp.float32
-    )
-    row_grad, norm_grad = norm_back(normed_grad)
-    token_grad = (row_grad + grad_rows.astype(jnp.float32))[None]
-    expand_sum, down_sum = (
-        lax.psum_scatter(expand_grad, ("tok", "rep"), scatter_dimension=0, tiled=True),
-        lax.psum_scatter(down_grad, ("tok", "rep"), scatter_dimension=0, tiled=True),
-    )
-    up_sum, value_sum, norm_sum = (
-        lax.psum_scatter(up_grad, ("tok", "rep"), scatter_dimension=0, tiled=True),
-        lax.psum_scatter(value_w_grad, ("tok", "rep"), scatter_dimension=0, tiled=True),
-        lax.psum_scatter(norm_grad, ("tok", "rep"), scatter_dimension=1, tiled=True),
-    )
+    value_pre_grad = value_back(value_grad.astype(jnp.float32))[0].astype(low)
+    ups_grads = [dot(flat(up), up_pre_grad, 1, 0) for up in ups]
+    normed_grads = [
+        (g + dot(flat(value), value_pre_grad, 1, 0)).reshape(h.shape)
+        for g, value, h in zip(ups_grads, values, hats)
+    ]
+    packed_grads = []
+    for side, h, g in zip(normed, hats, normed_grads):
+        weight_grad = dot(flat(side), value_pre_grad, 1, 1).reshape(side.shape[:2] + (-1,))
+        norm_grad = jnp.stack([jnp.sum(g * h, axis=2), jnp.sum(g, axis=2)], axis=2)
+        norm_grad = jnp.pad(norm_grad, ((0, 0), (0, 0), (0, 126)))
+        packed_grads.append(jnp.concatenate([weight_grad, norm_grad], axis=2))
+    packed_sums = Scatter(
+        cube, packed_grads[0], packed_grads[1].astype(low), [0] + tok_bits, [0] + tok_bits, ys + zs
+    )
+    for sums in (up_sums, down_sums):
+        sums.take()
+        sums.send()
+    expand_sums.take(value_pre_grad)
+    if expand_sums.order:
+        expand_sums.send()
+    packed_sums.send()
+    packed_sums.take(up_sums.arriving, down_sums.arriving)
+    for sums in (up_sums, down_sums, expand_sums):
+        if sums.order:
+            sums.take(value_pre_grad)
+        if sums.order:
+            sums.send()
+    packed_sums.send()
+    packed_sums.take()
+    packed_sums.send(up_sums.arriving, down_sums.arriving)
+    packed_sum = packed_sums.rest()
+    up_sum, down_sum, expand_sum = [
+        sums.rest() for sums in (up_sums, down_sums, expand_sums)
+    ]
+    value_sum = packed_sum[:, :inner]
+    norm_sum = packed_sum[:, inner : inner + 2].T
+    hat_grads = [g * gain for g, gain in zip(normed_grads, gains)]
+    hat_mean = sum(jnp.sum(d, axis=(0, 1)) for d in hat_grads) / width
+    hat_product = sum(jnp.sum(d * h, axis=(0, 1)) for d, h in zip(hat_grads, hats)) / width
+    row_grads = [(d - hat_mean - h * hat_product) * scale for d, h in zip(hat_grads, hats)]
+    token_grad = (cube.merge(*row_grads).T + grad_rows.astype(jnp.float32))[None]
     step_value = jnp.float32(STEP)
     up_next, up_mean_next, up_square_next = adam_step(
         up_weight, up_sum, up_mean, up_square, step_value, 0.08, 0.1
@@ -540,7 +863,7 @@
         P(None, "tok", None),
     )
     return jax.shard_map(
-        per_device,
+        functools.partial(per_device, mesh.shape["tok"]),
         mesh=mesh,
         in_specs=placed,
         out_specs=(

time: 1100 us -> 420 us (0.38)
  waiting for transfers between devices: 823 us -> 81.6 us
  blocking collectives: 74.4 us -> 0 us
  starting transfers between devices: 8.88 us -> 61.2 us
  local copies, waits for them, and re-layouts: 14.8 us -> 48.4 us
  other arithmetic: 31.1 us -> 56.5 us
  Pallas kernels: 65.2 us -> 87.8 us
  matrix products: 60.4 us -> 75.6 us
  between operations: 14.8 us -> 2.62 us
    reduce_scatter x4 -> x0, waiting for transfers between devices: 565 us -> none  [the longest x1 160 us: per_device(): lax.psum_scatter(up_grad, ('tok', 'rep'), scatter_dimension=0, tiled=True)]
    all_gather x4 -> x0, waiting for transfers between devices: 132 us -> none  [the longest x1 66.2 us: per_device(): lax.all_gather(up_weight.astype(jnp.bfloat16), ('tok', 'rep'), axis=0, ti...]
    unnamed x11 -> x0, waiting for transfers between devices: 116 us -> none
    ppermute x0 -> x44, waiting for transfers between devices: none -> 67 us  [swap(): return lax.ppermute(block, ('tok', 'rep'), pairs)]
    all_gather x1 -> x0, blocking collectives: 43 us -> none  [per_device(): lax.all_gather(norm_params.astype(jnp.bfloat16), ('tok', 'rep'), axis=1,...]
    ppermute x0 -> x44, starting transfers between devices: none -> 41.7 us  [swap(): return lax.ppermute(block, ('tok', 'rep'), pairs)]
    all_to_all x2 -> x0, blocking collectives: 31.4 us -> none  [the longest x1 17.1 us: per_device(): lax.all_to_all(state_out.reshape(channels, length), 'tok', split_axis=1,...]
    pallas_call x2 -> x8, Pallas kernels: 65.2 us -> 87.8 us  [call(): pl.pallas_call(body, grid=(1,), in_specs=specs + [pl.BlockSpec(memory_spa...]
  transfers between devices with their start and end apart: 12 -> 48, of which waited for: 11 -> 18; matrix products, arithmetic and copies ran while one was open for 8% -> 37% of each run, Pallas kernels for 3% -> 21%
where the time goes in v1:
time: 420 us; the launch traced here: 414 us
  Pallas kernels  87.8 us (21%)
  waiting for transfers between devices  81.6 us (19%)
  matrix products  75.6 us (18%)
  starting transfers between devices  61.2 us (15%)
  other arithmetic  56.5 us (13%)
  local copies, waits for them, and re-layouts  48.4 us (12%)
    pallas_call x8, Pallas kernels, call(): pl.pallas_call(body, grid=(1,), in_specs=specs + [pl.BlockSpec(memory_spa...  87.8 us
    dot_general x30, matrix products, dot(): lax.dot_general(a, b, (((a_dim,), (b_dim,)), ((), ())), preferred_element...  75.6 us
    ppermute x44, waiting for transfers between devices, swap(): return lax.ppermute(block, ('tok', 'rep'), pairs)  67 us
    ppermute x44, starting transfers between devices, swap(): return lax.ppermute(block, ('tok', 'rep'), pairs)  41.7 us
    unnamed x214, local copies, waits for them, and re-layouts  18.1 us
    select_n x23, other arithmetic, take(): jnp.where(self.cube.bit(b) == 1, jnp.concatenate([other, mine], axis=1),...  18.1 us
    add x13, other arithmetic, take(): total = self.keep + after(self.arriving, *waits).astype(jnp.float32)  12.7 us
  transfers between devices with their start and end apart: 48, of which 18 were waited for; matrix products, arithmetic and copies ran while one was open for 37% of the time, Pallas kernels for 21%

profile of v1, /device:TPU:0, one launch (start us, length us, event | category | flops | bytes accessed | tf_op | source)
XLA Modules:
  0.0 413.8 jit_solution(8070936722406903955)
XLA Ops:
  1.7 3.0 collective-permute-start.10
  7.5 3.1 collective-permute-start
  15.4 3.1 collective-permute-done.2
  18.6 6.0 %collective-permute-done = bf16[1,32,3072]{2,1,0:T(8,128)(2,1)S(1)} collective-permute-done((bf16[1,32,3072]{2,1,0:T(8,128)(2,1)S(1)}, bf16[1,32,3072]{2,1,0:T(8,128)(2,1)S(1)}, u32[]{:S(2)}, u32[]{:S(2)}) %collective-permute-start) | collective-permute-done | bytes 196640 | tf_op jit(solution)/shard_map/ppermute | solution.py:446
  25.4 2.2 collective-permute-done.3
  31.3 6.8 %collective-permute-done.4 = bf16[4,32,640]{2,1,0:T(8,128)(2,1)S(1)} collective-permute-done((bf16[4,32,640]{2,1,0:T(8,128)(2,1)S(1)}, bf16[4,32,640]{2,1,0:T(8,128)(2,1)S(1)}, u32[]{:S(2)}, u32[]{:S(2)}) %collective-permute-start.4) | collective-permute-done | bytes 163872 | tf_op jit(solution)/shard_map/ppermute | solution.py:446
  39.9 5.4 %collective-permute-done.5 = bf16[8,32,640]{2,1,0:T(8,128)(2,1)S(1)} collective-permute-done((bf16[8,32,640]{2,1,0:T(8,128)(2,1)S(1)}, bf16[8,32,640]{2,1,0:T(8,128)(2,1)S(1)}, u32[]{:S(2)}, u32[]{:S(2)}) %collective-permute-start.5) | collective-permute-done | bytes 327712 | tf_op jit(solution)/shard_map/ppermute | solution.py:446
  52.8 2.3 multiply_convert_fusion.1
  55.1 5.3 %all-to-all-start = ((bf16[16,32,256]{2,1,0:T(8,128)(2,1)}), bf16[16,32,256]{2,1,0:T(8,128)(2,1)S(1)}, u32[]{:S(2)}, u32[]{:S(2)}) async-start(bf16[16,32,256]{2,1,0:T(8,128)(2,1)} %bitcast.21), calls=%async_computation | async-start | bytes 524288 | tf_op jit(solution)/shard_map/all_to_all | solution.py:635
  60.5 3.9 fusion.16
  64.6 2.6 copy.375.refs_4_.refs_5_
  67.2 5.9 %all-to-all-done = bf16[16,32,256]{2,1,0:T(8,128)(2,1)S(1)} async-done(((bf16[16,32,256]{2,1,0:T(8,128)(2,1)}), bf16[16,32,256]{2,1,0:T(8,128)(2,1)S(1)}, u32[]{:S(2)}, u32[]{:S(2)}) %all-to-all-start) | async-done | bytes 262176 | tf_op jit(solution)/shard_map/all_to_all | solution.py:635
  81.9 11.0 %mix_forward.4 = (bf16[32,32,128]{2,1,0:T(8,128)(2,1)S(1)}, f32[1536,1024]{1,0:T(8,128)}, bf16[32,128,128]{2,1,0:T(8,128)(2,1)S(1)}, f32[8,128]{1,0:T(8,128)}) custom-call(f32[48]{0:T(128)S(1)} %add_convert_fusion.3.refs_0_, bf16[48,32]{1,0:T(8,128)(2,1)S(1)} %fusion.85.refs_1_, bf16[48,128]{1,0:T(8,128)(2,1)S(1)} %fusion.87.refs_2_, ...), custom_call_target="tpu_custom_call" | custom-call | flops 8000000000 | bytes 4194304 | tf_op jit(solution)/shard_map/mix_forward/pallas_call | solution.py:298
  92.8 3.8 collective-permute-done.8
  101.8 11.4 %mix_forward.5 = (bf16[32,32,128]{2,1,0:T(8,128)(2,1)S(1)}, f32[1536,1024]{1,0:T(8,128)}, bf16[32,128,128]{2,1,0:T(8,128)(2,1)S(1)}, f32[8,128]{1,0:T(8,128)S(1)}) custom-call(f32[48]{0:T(128)S(1)} %add_convert_fusion.3.refs_0_, bf16[48,32]{1,0:T(8,128)(2,1)S(1)} %fusion.85.refs_1_, ...), custom_call_target="tpu_custom_call", output_to_operand_aliasing={{0}: (9, {}), {1}: (10, {}), {2}: (11, {})} | custom-call | flops 8000000000 | bytes 4194304 | tf_op jit(solution)/shard_map/mix_forward/pallas_call | solution.py:298
  114.0 11.2 %mix_forward.6 = (bf16[32,32,128]{2,1,0:T(8,128)(2,1)S(1)}, f32[1536,1024]{1,0:T(8,128)}, bf16[32,128,128]{2,1,0:T(8,128)(2,1)S(1)}, f32[8,128]{1,0:T(8,128)}) custom-call(f32[48]{0:T(128)S(1)} %add_convert_fusion.3.refs_0_, bf16[48,32]{1,0:T(8,128)(2,1)S(1)} %fusion.85.refs_1_, ...), custom_call_target="tpu_custom_call", output_to_operand_aliasing={{0}: (11, {}), {1}: (12, {}), {2}: (13, {})} | custom-call | flops 8000000000 | bytes 4194304 | tf_op jit(solution)/shard_map/mix_forward/pallas_call | solution.py:298
  125.2 10.7 %mix_forward.7 = (bf16[32,32,128]{2,1,0:T(8,128)(2,1)S(1)}, f32[1536,1024]{1,0:T(8,128)}, bf16[32,128,128]{2,1,0:T(8,128)(2,1)S(1)}, f32[8,128]{1,0:T(8,128)}) custom-call(f32[48]{0:T(128)S(1)} %add_convert_fusion.3.refs_0_, bf16[48,32]{1,0:T(8,128)(2,1)S(1)} %fusion.85.refs_1_, ...), custom_call_target="tpu_custom_call", output_to_operand_aliasing={{0}: (7, {}), {1}: (8, {}), {2}: (9, {})} | custom-call | flops 8000000000 | bytes 4194304 | tf_op jit(solution)/shard_map/mix_forward/pallas_call | solution.py:298
  141.1 4.2 %all-to-all-start.1 = ((bf16[32,16,256]{2,0,1:T(8,128)(2,1)}), bf16[32,16,256]{2,0,1:T(8,128)(2,1)}, u32[]{:S(2)}, u32[]{:S(2)}) async-start(bf16[32,16,256]{2,0,1:T(8,128)(2,1)} %copy.382), calls=%async_computation.1 | async-start | bytes 524288 | tf_op jit(solution)/shard_map/all_to_all | solution.py:679
  149.0 2.8 maximum_select_fusion.4
  151.8 4.2 %all-to-all-done.1 = bf16[32,16,256]{2,0,1:T(8,128)(2,1)} async-done(((bf16[32,16,256]{2,0,1:T(8,128)(2,1)}), bf16[32,16,256]{2,0,1:T(8,128)(2,1)}, u32[]{:S(2)}, u32[]{:S(2)}) %all-to-all-start.1) | async-done | bytes 262176 | tf_op jit(solution)/shard_map/all_to_all | solution.py:679
  155.9 2.3 maximum_select_fusion.1
  158.3 2.2 copy.392
  160.4 2.5 maximum_select_fusion
  176.8 3.0 fusion.36
  179.8 2.9 fusion.105
  182.7 2.1 convolution_add_fusion.2
  184.8 3.0 select_bitcast_fusion.1
  188.4 7.0 %fusion.9 = (bf16[3072,256]{1,0:T(8,128)(2,1)}, bf16[3072,256]{1,0:T(8,128)(2,1)}, bf16[3072,256]{1,0:T(8,128)(2,1)S(1)}) fusion(f32[3072,256]{1,0:T(8,128)S(1)} %convolution_add_fusion.2, f32[16,2,96,256]{3,2,1,0:T(8,128)S(1)} %copy.396, f32[3072,256]{1,0:T(8,128)S(1)} %fusion.105, bf16[16,32,3072]{2,1,0:T(8,128)(2,1)} %collective-permute-done.17, ...), kind=kOutput, calls=%fused_computation.17 | convolution fusion | flops 826540032 | bytes 17563648 | tf_op jit(solution)/shard_map/dot_general | solution.py:549
  195.4 4.2 %fusion.113 = f32[512,256]{1,0:T(8,128)} fusion(bf16[512,3072]{1,0:T(8,128)(2,1)} %bitcast.57, bf16[3072,256]{1,0:T(8,128)(2,1)} %get-tuple-element.300), kind=kOutput, calls=%fused_computation.301 | convolution fusion | flops 805306368 | bytes 5242880 | tf_op jit(solution)/shard_map/dot_general | solution.py:549
  203.4 2.5 broadcast_select_fusion.3
  206.7 6.3 %all-to-all-start.2 = ((bf16[16,32,256]{2,1,0:T(8,128)(2,1)}), bf16[16,32,256]{2,1,0:T(8,128)(2,1)}, u32[]{:S(2)}, u32[]{:S(2)}) async-start(bf16[16,32,256]{2,1,0:T(8,128)(2,1)} %bitcast.92), calls=%async_computation.2 | async-start | bytes 524288 | tf_op jit(solution)/shard_map/all_to_all | solution.py:700
  213.0 3.7 fusion.108
  216.7 3.8 fusion.109
  220.5 2.3 fusion.32
  222.8 2.9 fusion.107
  225.8 4.0 fusion.14
  229.7 2.3 fusion.30
  232.0 3.2 fusion.110
  235.3 3.2 fusion.111
  240.9 3.9 add_convert_fusion
  248.7 2.1 fusion.1
  253.6 2.2 fusion.2
  257.3 11.2 %mix_backward.4 = (bf16[32,32,128]{2,1,0:T(8,128)(2,1)S(1)}, f32[32,1024]{1,0:T(8,128)S(1)}, f32[8,128]{1,0:T(8,128)}) custom-call(f32[48]{0:T(128)S(1)} %add_convert_fusion.3.refs_0_, bf16[48,32]{1,0:T(8,128)(2,1)S(1)} %fusion.85.refs_1_, bf16[48,128]{1,0:T(8,128)(2,1)S(1)} %copy-done.13, bf16[32,32,128]{2,1,0:T(8,128)(2,1)S(1)} %copy-done.6, ...), custom_call_target="tpu_custom_call" | custom-call | flops 10700000256 | bytes 4194304 | tf_op jit(solution)/shard_map/mix_backward/pallas_call | solution.py:298
  268.5 3.9 convolution_add_fusion.1
  274.0 10.4 %mix_backward.5 = (bf16[32,32,128]{2,1,0:T(8,128)(2,1)S(1)}, f32[32,1024]{1,0:T(8,128)S(1)}, f32[8,128]{1,0:T(8,128)}) custom-call(f32[48]{0:T(128)S(1)} %add_convert_fusion.3.refs_0_, bf16[48,32]{1,0:T(8,128)(2,1)S(1)} %fusion.85.refs_1_, bf16[48,128]{1,0:T(8,128)(2,1)S(1)} %copy-done.13, ...), custom_call_target="tpu_custom_call", output_to_operand_aliasing={{0}: (10, {}), {1}: (11, {})} | custom-call | flops 10700000256 | bytes 4194304 | tf_op jit(solution)/shard_map/mix_backward/pallas_call | solution.py:298
  284.6 2.4 collective-permute-start.29
  287.1 10.6 %mix_backward.6 = (bf16[32,32,128]{2,1,0:T(8,128)(2,1)S(1)}, f32[32,1024]{1,0:T(8,128)S(1)}, f32[8,128]{1,0:T(8,128)}) custom-call(f32[48]{0:T(128)S(1)} %add_convert_fusion.3.refs_0_, bf16[48,32]{1,0:T(8,128)(2,1)S(1)} %fusion.85.refs_1_, bf16[48,128]{1,0:T(8,128)(2,1)S(1)} %copy-done.13, ...), custom_call_target="tpu_custom_call", output_to_operand_aliasing={{0}: (11, {}), {1}: (12, {})} | custom-call | flops 10700000256 | bytes 4194304 | tf_op jit(solution)/shard_map/mix_backward/pallas_call | solution.py:298
  297.7 2.3 convert_add_fusion
  300.7 4.0 collective-permute-done.29
  307.9 11.2 %mix_backward.7 = (bf16[32,32,128]{2,1,0:T(8,128)(2,1)S(1)}, f32[32,1024]{1,0:T(8,128)S(1)}, f32[8,128]{1,0:T(8,128)}) custom-call(f32[48]{0:T(128)S(1)} %add_convert_fusion.3.refs_0_, bf16[48,32]{1,0:T(8,128)(2,1)S(1)} %fusion.85.refs_1_, bf16[48,128]{1,0:T(8,128)(2,1)S(1)} %copy-done.13, ...), custom_call_target="tpu_custom_call", output_to_operand_aliasing={{0}: (13, {}), {1}: (14, {})} | custom-call | flops 10700000256 | bytes 4194304 | tf_op jit(solution)/shard_map/mix_backward/pallas_call | solution.py:298
  319.2 4.1 collective-permute-done.41
  327.9 3.8 all-to-all-start.3
  337.5 4.6 %all-to-all-done.3 = bf16[32,16,256]{2,0,1:T(8,128)(2,1)S(1)} async-done(((bf16[32,16,256]{2,0,1:T(8,128)(2,1)}), bf16[32,16,256]{2,0,1:T(8,128)(2,1)S(1)}, u32[]{:S(2)}, u32[]{:S(2)}) %all-to-all-start.3) | async-done | bytes 262176 | tf_op jit(solution)/shard_map/all_to_all | solution.py:748
  345.2 3.6 multiply_reduce_fusion
  349.4 2.2 bitcast_add_fusion.2
  351.6 2.5 copy.419
  367.8 2.2 collective-permute-start.37
  370.1 5.0 %collective-permute-done.36 = bf16[8,32,640]{2,1,0:T(8,128)(2,1)S(1)} collective-permute-done((bf16[8,32,640]{2,1,0:T(8,128)(2,1)S(1)}, bf16[8,32,640]{2,1,0:T(8,128)(2,1)S(1)}, u32[]{:S(2)}, u32[]{:S(2)}) %collective-permute-start.36) | collective-permute-done | bytes 327712 | tf_op jit(solution)/shard_map/ppermute | solution.py:446
  375.2 4.4 %collective-permute-done.37 = bf16[1,96,1024]{2,1,0:T(8,128)(2,1)S(1)} collective-permute-done((bf16[1,96,1024]{2,1,0:T(8,128)(2,1)S(1)}, bf16[1,96,1024]{2,1,0:T(8,128)(2,1)S(1)}, u32[]{:S(2)}, u32[]{:S(2)}) %collective-permute-start.37) | collective-permute-done | bytes 196640 | tf_op jit(solution)/shard_map/ppermute | solution.py:446
  382.4 5.9 %collective-permute-done.38 = f32[4,32,640]{2,1,0:T(8,128)S(1)} collective-permute-done((f32[4,32,640]{2,1,0:T(8,128)S(1)}, f32[4,32,640]{2,1,0:T(8,128)S(1)}, u32[]{:S(2)}, u32[]{:S(2)}) %collective-permute-start.38) | collective-permute-done | bytes 327712 | tf_op jit(solution)/shard_map/ppermute | solution.py:446
  389.1 2.1 multiply_subtract_fusion.1
  391.6 3.2 collective-permute-done.39
  396.9 2.1 multiply_subtract_fusion
  399.0 11.4 %collective-permute-done.40 = f32[1,32,640]{1,2,0:T(8,128)S(1)} collective-permute-done((f32[1,32,640]{1,2,0:T(8,128)S(1)}, f32[1,32,640]{1,2,0:T(8,128)S(1)}, u32[]{:S(2)}, u32[]{:S(2)}) %collective-permute-start.40) | collective-permute-done | bytes 81952 | tf_op jit(solution)/shard_map/ppermute | solution.py:446
  (433 shorter events, 117.6 us)
Async XLA Ops:
  1.7 44.1 %collective-permute-start.10 = (bf16[1,16,3072]{2,1,0:T(8,128)(2,1)S(1)}, bf16[1,16,3072]{2,1,0:T(8,128)(2,1)S(1)}, u32[]{:S(2)}, u32[]{:S(2)}) collective-permute-start(bf16[1,16,3072]{2,1,0:T(8,128)(2,1)S(1)} %get-tuple-element.329), channel_id=1, source_target_pairs={{0,2},{1,3},{2,0},{3,1},{4,6},{5,7},{6,4},{7,5},{8,10},{9,11},{10,... | collective-permute-start | bytes 294920 | tf_op jit(solution)/shard_map/ppermute | solution.py:446
  6.4 7.1 %collective-permute-start.1 = (bf16[1,32,640]{2,1,0:T(8,128)(2,1)S(1)}, bf16[1,32,640]{2,1,0:T(8,128)(2,1)S(1)}, u32[]{:S(2)}, u32[]{:S(2)}) collective-permute-start(bf16[1,32,640]{2,1,0:T(8,128)(2,1)S(1)} %get-tuple-element.343), channel_id=1, source_target_pairs={{0,2},{1,3},{2,0},{3,1},{4,6},{5,7},{6,4},{7,5},{8,10},{9,11},{10,... | collective-permute-start | bytes 122888 | tf_op jit(solution)/shard_map/ppermute | solution.py:446
  7.5 17.1 %collective-permute-start = (bf16[1,32,3072]{2,1,0:T(8,128)(2,1)S(1)}, bf16[1,32,3072]{2,1,0:T(8,128)(2,1)S(1)}, u32[]{:S(2)}, u32[]{:S(2)}) collective-permute-start(bf16[1,32,3072]{2,1,0:T(8,128)(2,1)S(1)} %get-tuple-element.318), channel_id=1, source_target_pairs={{0,16},{1,17},{2,18},{3,19},{4,20},{5,21},{6,22},{7,23},{8,24},{9,... | collective-permute-start | bytes 589832 | tf_op jit(solution)/shard_map/ppermute | solution.py:446
  10.7 16.9 %collective-permute-start.3 = (bf16[1,96,1024]{2,1,0:T(8,128)(2,1)S(1)}, bf16[1,96,1024]{2,1,0:T(8,128)(2,1)S(1)}, u32[]{:S(2)}, u32[]{:S(2)}) collective-permute-start(bf16[1,96,1024]{2,1,0:T(8,128)(2,1)S(1)} %get-tuple-element.316), channel_id=1, source_target_pairs={{0,16},{1,17},{2,18},{3,19},{4,20},{5,21},{6,22},{7,23},{8,24},{9,... | collective-permute-start | bytes 589832 | tf_op jit(solution)/shard_map/ppermute | solution.py:446
  11.8 101.6 %collective-permute-start.16 = (bf16[1024,256]{1,0:T(8,128)(2,1)}, bf16[1024,256]{1,0:T(8,128)(2,1)S(1)}, u32[]{:S(2)}, u32[]{:S(2)}) collective-permute-start(bf16[1024,256]{1,0:T(8,128)(2,1)} %bitcast.53), channel_id=1, source_target_pairs={{0,1},{1,0},{2,3},{3,2},{4,5},{5,4},{6,7},{7,6},{8,9},{9,8},{10,11... | collective-permute-start | bytes 1572872 | tf_op jit(solution)/shard_map/ppermute | solution.py:446
  12.8 15.7 %copy-start.74 = (f32[32,512]{1,0:T(8,128)S(1)}, f32[32,512]{1,0:T(8,128)}, u32[]{:S(2)}) copy-start(f32[32,512]{1,0:T(8,128)} %param.27) | copy-start | bytes 196612
  12.8 39.0 %copy-start.92 = (f32[256]{0:T(256)}, f32[256]{0:T(256)S(1)}, u32[]{:S(2)}) copy-start(f32[256]{0:T(256)S(1)} %broadcast_multiply_fusion) | copy-start | bytes 3076
  13.1 38.7 %copy-start.94 = (f32[256]{0:T(256)}, f32[256]{0:T(256)S(1)}, u32[]{:S(2)}) copy-start(f32[256]{0:T(256)S(1)} %add_rsqrt_fusion) | copy-start | bytes 3076
  13.4 68.4 %copy-start.11 = (bf16[48,128]{1,0:T(8,128)(2,1)}, bf16[48,128]{1,0:T(8,128)(2,1)S(1)}, u32[]{:S(2)}) copy-start(bf16[48,128]{1,0:T(8,128)(2,1)S(1)} %fusion.87.refs_2_) | copy-start | bytes 36868
  13.5 5.0 %collective-permute-start.2 = (bf16[2,32,640]{2,1,0:T(8,128)(2,1)S(1)}, bf16[2,32,640]{2,1,0:T(8,128)(2,1)S(1)}, u32[]{:S(2)}, u32[]{:S(2)}) collective-permute-start(bf16[2,32,640]{2,1,0:T(8,128)(2,1)S(1)} %maximum_select_fusion.21), channel_id=1, source_target_pairs={{0,4},{1,5},{2,6},{3,7},{4,0},{5,1},{6,2},{7,3},{8,12},{9,13},{10,... | collective-permute-start | bytes 245768 | tf_op jit(solution)/shard_map/ppermute | solution.py:446
  28.4 9.7 %collective-permute-start.4 = (bf16[4,32,640]{2,1,0:T(8,128)(2,1)S(1)}, bf16[4,32,640]{2,1,0:T(8,128)(2,1)S(1)}, u32[]{:S(2)}, u32[]{:S(2)}) collective-permute-start(bf16[4,32,640]{2,1,0:T(8,128)(2,1)S(1)} %bitcast.514), channel_id=1, source_target_pairs={{0,16},{1,17},{2,18},{3,19},{4,20},{5,21},{6,22},{7,23},{8,24},{9,... | collective-permute-start | bytes 491528 | tf_op jit(solution)/shard_map/ppermute | solution.py:446
  29.6 22.3 %copy-start.23 = (bf16[1024,256]{1,0:T(8,128)(2,1)}, bf16[1024,256]{1,0:T(8,128)(2,1)S(1)}, u32[]{:S(2)}) copy-start(bf16[1024,256]{1,0:T(8,128)(2,1)S(1)} %copy.370) | copy-start | bytes 1572868
  38.2 7.1 %collective-permute-start.5 = (bf16[8,32,640]{2,1,0:T(8,128)(2,1)S(1)}, bf16[8,32,640]{2,1,0:T(8,128)(2,1)S(1)}, u32[]{:S(2)}, u32[]{:S(2)}) collective-permute-start(bf16[8,32,640]{2,1,0:T(8,128)(2,1)S(1)} %bitcast.536), channel_id=1, source_target_pairs={{0,8},{1,9},{2,10},{3,11},{4,12},{5,13},{6,14},{7,15},{8,0},{9,1},... | collective-permute-start | bytes 983048 | tf_op jit(solution)/shard_map/ppermute | solution.py:446
  45.5 6.1 %collective-permute-start.7 = (bf16[16,32,640]{2,1,0:T(8,128)(2,1)S(1)}, bf16[16,32,640]{2,1,0:T(8,128)(2,1)S(1)}, u32[]{:S(2)}, u32[]{:S(2)}) collective-permute-start(bf16[16,32,640]{2,1,0:T(8,128)(2,1)S(1)} %bitcast.491), channel_id=1, source_target_pairs={{0,1},{1,0},{2,3},{3,2},{4,5},{5,4},{6,7},{7,6},{8,9},{9,8},{10,11... | collective-permute-start | bytes 1966088 | tf_op jit(solution)/shard_map/ppermute | solution.py:446
  46.6 26.8 %collective-permute-start.11 = (bf16[2,16,3072]{2,1,0:T(8,128)(2,1)}, bf16[2,16,3072]{2,1,0:T(8,128)(2,1)}, u32[]{:S(2)}, u32[]{:S(2)}) collective-permute-start(bf16[2,16,3072]{2,1,0:T(8,128)(2,1)} %maximum_select_fusion.18), channel_id=1, source_target_pairs={{0,4},{1,5},{2,6},{3,7},{4,0},{5,1},{6,2},{7,3},{8,12},{9,13},{10,... | collective-permute-start | bytes 589832 | tf_op jit(solution)/shard_map/ppermute | solution.py:446
  48.1 28.1 %collective-permute-start.6 = (bf16[2,32,3072]{2,1,0:T(8,128)(2,1)}, bf16[2,32,3072]{2,1,0:T(8,128)(2,1)S(1)}, u32[]{:S(2)}, u32[]{:S(2)}) collective-permute-start(bf16[2,32,3072]{2,1,0:T(8,128)(2,1)} %maximum_select_fusion.11), channel_id=1, source_target_pairs={{0,8},{1,9},{2,10},{3,11},{4,12},{5,13},{6,14},{7,15},{8,0},{9,1},... | collective-permute-start | bytes 1179656 | tf_op jit(solution)/shard_map/ppermute | solution.py:446
  48.9 30.0 %collective-permute-start.9 = (bf16[2,96,1024]{2,1,0:T(8,128)(2,1)}, bf16[2,96,1024]{2,1,0:T(8,128)(2,1)}, u32[]{:S(2)}, u32[]{:S(2)}) collective-permute-start(bf16[2,96,1024]{2,1,0:T(8,128)(2,1)} %maximum_select_fusion.12), channel_id=1, source_target_pairs={{0,8},{1,9},{2,10},{3,11},{4,12},{5,13},{6,14},{7,15},{8,0},{9,1},... | collective-permute-start | bytes 1179656 | tf_op jit(solution)/shard_map/ppermute | solution.py:446
  52.8 60.6 %collective-permute-start.15 = (bf16[16,32,256]{2,1,0:T(8,128)(2,1)}, bf16[16,32,256]{2,1,0:T(8,128)(2,1)}, u32[]{:S(2)}, u32[]{:S(2)}) collective-permute-start(bf16[16,32,256]{2,1,0:T(8,128)(2,1)} %fusion.54), channel_id=1, source_target_pairs={{0,1},{1,0},{2,3},{3,2},{4,5},{5,4},{6,7},{7,6},{8,9},{9,8},{10,11... | collective-permute-start | bytes 786440 | tf_op jit(solution)/shard_map/ppermute | solution.py:446
  55.1 18.0 %all-to-all-start = ((bf16[16,32,256]{2,1,0:T(8,128)(2,1)}), bf16[16,32,256]{2,1,0:T(8,128)(2,1)S(1)}, u32[]{:S(2)}, u32[]{:S(2)}) async-start(bf16[16,32,256]{2,1,0:T(8,128)(2,1)} %bitcast.21), calls=%async_computation | async-start | bytes 524288 | tf_op jit(solution)/shard_map/all_to_all | solution.py:635
  64.6 17.2 %copy-start.8 = (f32[32,1024]{1,0:T(8,128)}, f32[32,1024]{1,0:T(8,128)S(1)}, u32[]{:S(2)}) copy-start(f32[32,1024]{1,0:T(8,128)S(1)} %pad_maximum_fusion.5.refs_6_.refs_7_) | copy-start | bytes 393220
  74.5 38.7 %collective-permute-start.14 = (bf16[4,16,3072]{2,1,0:T(8,128)(2,1)S(1)}, bf16[4,16,3072]{2,1,0:T(8,128)(2,1)S(1)}, u32[]{:S(2)}, u32[]{:S(2)}) collective-permute-start(bf16[4,16,3072]{2,1,0:T(8,128)(2,1)S(1)} %bitcast.451), channel_id=1, source_target_pairs={{0,16},{1,17},{2,18},{3,19},{4,20},{5,21},{6,22},{7,23},{8,24},{9,... | collective-permute-start | bytes 1179656 | tf_op jit(solution)/shard_map/ppermute | solution.py:446
  78.3 18.3 %collective-permute-start.8 = (bf16[4,32,3072]{2,1,0:T(8,128)(2,1)S(1)}, bf16[4,32,3072]{2,1,0:T(8,128)(2,1)S(1)}, u32[]{:S(2)}, u32[]{:S(2)}) collective-permute-start(bf16[4,32,3072]{2,1,0:T(8,128)(2,1)S(1)} %bitcast.444), channel_id=1, source_target_pairs={{0,2},{1,3},{2,0},{3,1},{4,6},{5,7},{6,4},{7,5},{8,10},{9,11},{10,... | collective-permute-start | bytes 2359304 | tf_op jit(solution)/shard_map/ppermute | solution.py:446
  80.1 18.8 %collective-permute-start.13 = (bf16[4,96,1024]{2,1,0:T(8,128)(2,1)S(1)}, bf16[4,96,1024]{2,1,0:T(8,128)(2,1)S(1)}, u32[]{:S(2)}, u32[]{:S(2)}) collective-permute-start(bf16[4,96,1024]{2,1,0:T(8,128)(2,1)S(1)} %bitcast.455), channel_id=1, source_target_pairs={{0,4},{1,5},{2,6},{3,7},{4,0},{5,1},{6,2},{7,3},{8,12},{9,13},{10,... | collective-permute-start | bytes 2359304 | tf_op jit(solution)/shard_map/ppermute | solution.py:446
  99.4 56.5 %collective-permute-start.20 = (bf16[8,96,1024]{2,1,0:T(8,128)(2,1)S(1)}, bf16[8,96,1024]{2,1,0:T(8,128)(2,1)}, u32[]{:S(2)}, u32[]{:S(2)}) collective-permute-start(bf16[8,96,1024]{2,1,0:T(8,128)(2,1)S(1)} %bitcast.448), channel_id=1, source_target_pairs={{0,2},{1,3},{2,0},{3,1},{4,6},{5,7},{6,4},{7,5},{8,10},{9,11},{10,... | collective-permute-start | bytes 4718600 | tf_op jit(solution)/shard_map/ppermute | solution.py:446
  100.2 60.2 %collective-permute-start.12 = (bf16[8,32,3072]{2,1,0:T(8,128)(2,1)}, bf16[8,32,3072]{2,1,0:T(8,128)(2,1)}, u32[]{:S(2)}, u32[]{:S(2)}) collective-permute-start(bf16[8,32,3072]{2,1,0:T(8,128)(2,1)} %bitcast.45.refs_7_), channel_id=1, source_target_pairs={{0,4},{1,5},{2,6},{3,7},{4,0},{5,1},{6,2},{7,3},{8,12},{9,13},{10,... | collective-permute-start | bytes 4718600 | tf_op jit(solution)/shard_map/ppermute | solution.py:446
  141.1 14.9 %all-to-all-start.1 = ((bf16[32,16,256]{2,0,1:T(8,128)(2,1)}), bf16[32,16,256]{2,0,1:T(8,128)(2,1)}, u32[]{:S(2)}, u32[]{:S(2)}) async-start(bf16[32,16,256]{2,0,1:T(8,128)(2,1)} %copy.382), calls=%async_computation.1 | async-start | bytes 524288 | tf_op jit(solution)/shard_map/all_to_all | solution.py:679
  147.2 19.3 %collective-permute-start.18 = (bf16[8,16,3072]{2,1,0:T(8,128)(2,1)}, bf16[8,16,3072]{2,1,0:T(8,128)(2,1)}, u32[]{:S(2)}, u32[]{:S(2)}) collective-permute-start(bf16[8,16,3072]{2,1,0:T(8,128)(2,1)} %bitcast.461), channel_id=1, source_target_pairs={{0,8},{1,9},{2,10},{3,11},{4,12},{5,13},{6,14},{7,15},{8,0},{9,1},... | collective-permute-start | bytes 2359304 | tf_op jit(solution)/shard_map/ppermute | solution.py:446
  160.4 24.4 %collective-permute-start.21 = (bf16[16,96,1024]{2,1,0:T(8,128)(2,1)}, bf16[16,96,1024]{2,1,0:T(8,128)(2,1)}, u32[]{:S(2)}, u32[]{:S(2)}) collective-permute-start(bf16[16,96,1024]{2,1,0:T(8,128)(2,1)} %bitcast.78), channel_id=1, source_target_pairs={{0,1},{1,0},{2,3},{3,2},{4,5},{5,4},{6,7},{7,6},{8,9},{9,8},{10,11... | collective-permute-start | bytes 9437192 | tf_op jit(solution)/shard_map/ppermute | solution.py:446
  164.9 23.5 %collective-permute-start.17 = (bf16[16,32,3072]{2,1,0:T(8,128)(2,1)}, bf16[16,32,3072]{2,1,0:T(8,128)(2,1)}, u32[]{:S(2)}, u32[]{:S(2)}) collective-permute-start(bf16[16,32,3072]{2,1,0:T(8,128)(2,1)} %bitcast.59), channel_id=1, source_target_pairs={{0,1},{1,0},{2,3},{3,2},{4,5},{5,4},{6,7},{7,6},{8,9},{9,8},{10,11... | collective-permute-start | bytes 9437192 | tf_op jit(solution)/shard_map/ppermute | solution.py:446
  168.3 14.4 %collective-permute-start.19 = (bf16[16,16,3072]{2,1,0:T(8,128)(2,1)S(1)}, bf16[16,16,3072]{2,1,0:T(8,128)(2,1)}, u32[]{:S(2)}, u32[]{:S(2)}) collective-permute-start(bf16[16,16,3072]{2,1,0:T(8,128)(2,1)S(1)} %bitcast.464), channel_id=1, source_target_pairs={{0,1},{1,0},{2,3},{3,2},{4,5},{5,4},{6,7},{7,6},{8,9},{9,8},{10,11... | collective-permute-start | bytes 4718600 | tf_op jit(solution)/shard_map/ppermute | solution.py:446
  172.3 2.9 collective-permute-start.24
  199.6 47.9 %collective-permute-start.22 = (bf16[3072,256]{1,0:T(8,128)(2,1)}, bf16[3072,256]{1,0:T(8,128)(2,1)}, u32[]{:S(2)}, u32[]{:S(2)}) collective-permute-start(bf16[3072,256]{1,0:T(8,128)(2,1)} %get-tuple-element.300), channel_id=1, source_target_pairs={{0,1},{1,0},{2,3},{3,2},{4,5},{5,4},{6,7},{7,6},{8,9},{9,8},{10,11... | collective-permute-start | bytes 4718600 | tf_op jit(solution)/shard_map/ppermute | solution.py:446
  201.6 50.8 %collective-permute-start.25 = (bf16[3072,256]{1,0:T(8,128)(2,1)}, bf16[3072,256]{1,0:T(8,128)(2,1)S(1)}, u32[]{:S(2)}, u32[]{:S(2)}) collective-permute-start(bf16[3072,256]{1,0:T(8,128)(2,1)} %get-tuple-element.301), channel_id=1, source_target_pairs={{0,1},{1,0},{2,3},{3,2},{4,5},{5,4},{6,7},{7,6},{8,9},{9,8},{10,11... | collective-permute-start | bytes 4718600 | tf_op jit(solution)/shard_map/ppermute | solution.py:446
  206.7 31.8 %all-to-all-start.2 = ((bf16[16,32,256]{2,1,0:T(8,128)(2,1)}), bf16[16,32,256]{2,1,0:T(8,128)(2,1)}, u32[]{:S(2)}, u32[]{:S(2)}) async-start(bf16[16,32,256]{2,1,0:T(8,128)(2,1)} %bitcast.92), calls=%async_computation.2 | async-start | bytes 524288 | tf_op jit(solution)/shard_map/all_to_all | solution.py:700
  222.8 16.9 %collective-permute-start.27 = (bf16[16,96,256]{2,1,0:T(8,128)(2,1)}, bf16[16,96,256]{2,1,0:T(8,128)(2,1)}, u32[]{:S(2)}, u32[]{:S(2)}) collective-permute-start(bf16[16,96,256]{2,1,0:T(8,128)(2,1)} %bitcast.115), channel_id=1, source_target_pairs={{0,1},{1,0},{2,3},{3,2},{4,5},{5,4},{6,7},{7,6},{8,9},{9,8},{10,11... | collective-permute-start | bytes 2359304 | tf_op jit(solution)/shard_map/ppermute | solution.py:446
  244.8 52.9 %collective-permute-start.28 = (bf16[8,96,1024]{2,1,0:T(8,128)(2,1)}, bf16[8,96,1024]{2,1,0:T(8,128)(2,1)}, u32[]{:S(2)}, u32[]{:S(2)}) collective-permute-start(bf16[8,96,1024]{2,1,0:T(8,128)(2,1)} %bitcast.118.refs_11_), channel_id=1, source_target_pairs={{0,2},{1,3},{2,0},{3,1},{4,6},{5,7},{6,4},{7,5},{8,10},{9,11},{10,... | collective-permute-start | bytes 4718600 | tf_op jit(solution)/shard_map/ppermute | solution.py:446
  250.8 54.6 %collective-permute-start.23 = (bf16[8,32,3072]{2,1,0:T(8,128)(2,1)S(1)}, bf16[8,32,3072]{2,1,0:T(8,128)(2,1)}, u32[]{:S(2)}, u32[]{:S(2)}) collective-permute-start(bf16[8,32,3072]{2,1,0:T(8,128)(2,1)S(1)} %bitcast.458), channel_id=1, source_target_pairs={{0,4},{1,5},{2,6},{3,7},{4,0},{5,1},{6,2},{7,3},{8,12},{9,13},{10,... | collective-permute-start | bytes 4718600 | tf_op jit(solution)/shard_map/ppermute | solution.py:446
  255.7 28.7 %collective-permute-start.26 = (bf16[8,16,3072]{2,1,0:T(8,128)(2,1)S(1)}, bf16[8,16,3072]{2,1,0:T(8,128)(2,1)S(1)}, u32[]{:S(2)}, u32[]{:S(2)}) collective-permute-start(bf16[8,16,3072]{2,1,0:T(8,128)(2,1)S(1)} %bitcast.462), channel_id=1, source_target_pairs={{0,8},{1,9},{2,10},{3,11},{4,12},{5,13},{6,14},{7,15},{8,0},{9,1},... | collective-permute-start | bytes 2359304 | tf_op jit(solution)/shard_map/ppermute | solution.py:446
  284.6 20.1 %collective-permute-start.29 = (bf16[4,16,3072]{2,1,0:T(8,128)(2,1)S(1)}, bf16[4,16,3072]{2,1,0:T(8,128)(2,1)S(1)}, u32[]{:S(2)}, u32[]{:S(2)}) collective-permute-start(bf16[4,16,3072]{2,1,0:T(8,128)(2,1)S(1)} %fusion.61.refs_10_), channel_id=1, source_target_pairs={{0,16},{1,17},{2,18},{3,19},{4,20},{5,21},{6,22},{7,23},{8,24},{9,... | collective-permute-start | bytes 1179656 | tf_op jit(solution)/shard_map/ppermute | solution.py:446
  300.1 23.2 %collective-permute-start.31 = (bf16[4,96,1024]{2,1,0:T(8,128)(2,1)S(1)}, bf16[4,96,1024]{2,1,0:T(8,128)(2,1)}, u32[]{:S(2)}, u32[]{:S(2)}) collective-permute-start(bf16[4,96,1024]{2,1,0:T(8,128)(2,1)S(1)} %fusion.21.refs_11_), channel_id=1, source_target_pairs={{0,4},{1,5},{2,6},{3,7},{4,0},{5,1},{6,2},{7,3},{8,12},{9,13},{10,... | collective-permute-start | bytes 2359304 | tf_op jit(solution)/shard_map/ppermute | solution.py:446
  304.8 18.4 %collective-permute-start.41 = (bf16[2,16,3072]{2,1,0:T(8,128)(2,1)S(1)}, bf16[2,16,3072]{2,1,0:T(8,128)(2,1)S(1)}, u32[]{:S(2)}, u32[]{:S(2)}) collective-permute-start(bf16[2,16,3072]{2,1,0:T(8,128)(2,1)S(1)} %fusion.72.refs_12_), channel_id=1, source_target_pairs={{0,4},{1,5},{2,6},{3,7},{4,0},{5,1},{6,2},{7,3},{8,12},{9,13},{10,... | collective-permute-start | bytes 589832 | tf_op jit(solution)/shard_map/ppermute | solution.py:446
  307.5 19.5 %collective-permute-start.30 = (bf16[4,32,3072]{2,1,0:T(8,128)(2,1)S(1)}, bf16[4,32,3072]{2,1,0:T(8,128)(2,1)}, u32[]{:S(2)}, u32[]{:S(2)}) collective-permute-start(bf16[4,32,3072]{2,1,0:T(8,128)(2,1)S(1)} %fusion.20.refs_10_), channel_id=1, source_target_pairs={{0,2},{1,3},{2,0},{3,1},{4,6},{5,7},{6,4},{7,5},{8,10},{9,11},{10,... | collective-permute-start | bytes 2359304 | tf_op jit(solution)/shard_map/ppermute | solution.py:446
  323.3 2.9 collective-permute-start.43
  325.7 36.0 %collective-permute-start.35 = (bf16[2,96,1024]{2,1,0:T(8,128)(2,1)}, bf16[2,96,1024]{2,1,0:T(8,128)(2,1)}, u32[]{:S(2)}, u32[]{:S(2)}) collective-permute-start(bf16[2,96,1024]{2,1,0:T(8,128)(2,1)} %fusion.63), channel_id=1, source_target_pairs={{0,8},{1,9},{2,10},{3,11},{4,12},{5,13},{6,14},{7,15},{8,0},{9,1},... | collective-permute-start | bytes 1179656 | tf_op jit(solution)/shard_map/ppermute | solution.py:446
  327.9 14.1 %all-to-all-start.3 = ((bf16[32,16,256]{2,0,1:T(8,128)(2,1)}), bf16[32,16,256]{2,0,1:T(8,128)(2,1)S(1)}, u32[]{:S(2)}, u32[]{:S(2)}) async-start(bf16[32,16,256]{2,0,1:T(8,128)(2,1)} %copy.405), calls=%async_computation.3 | async-start | bytes 524288 | tf_op jit(solution)/shard_map/all_to_all | solution.py:748
  335.4 18.7 %collective-permute-start.32 = (bf16[2,32,3072]{2,1,0:T(8,128)(2,1)}, bf16[2,32,3072]{2,1,0:T(8,128)(2,1)}, u32[]{:S(2)}, u32[]{:S(2)}) collective-permute-start(bf16[2,32,3072]{2,1,0:T(8,128)(2,1)} %fusion.62), channel_id=1, source_target_pairs={{0,8},{1,9},{2,10},{3,11},{4,12},{5,13},{6,14},{7,15},{8,0},{9,1},... | collective-permute-start | bytes 1179656 | tf_op jit(solution)/shard_map/ppermute | solution.py:446
  357.1 18.1 %collective-permute-start.33 = (bf16[1,32,3072]{2,1,0:T(8,128)(2,1)}, bf16[1,32,3072]{2,1,0:T(8,128)(2,1)}, u32[]{:S(2)}, u32[]{:S(2)}) collective-permute-start(bf16[1,32,3072]{2,1,0:T(8,128)(2,1)} %dynamic-slice_convert_fusion.3), channel_id=1, source_target_pairs={{0,16},{1,17},{2,18},{3,19},{4,20},{5,21},{6,22},{7,23},{8,24},{9,... | collective-permute-start | bytes 589832 | tf_op jit(solution)/shard_map/ppermute | solution.py:446
  361.4 2.4 collective-permute-start.34
  361.7 8.4 %collective-permute-start.42 = (bf16[1,16,3072]{2,1,0:T(8,128)(2,1)S(1)}, bf16[1,16,3072]{2,1,0:T(8,128)(2,1)S(1)}, u32[]{:S(2)}, u32[]{:S(2)}) collective-permute-start(bf16[1,16,3072]{2,1,0:T(8,128)(2,1)S(1)} %dynamic-slice_convert_fusion.5), channel_id=1, source_target_pairs={{0,2},{1,3},{2,0},{3,1},{4,6},{5,7},{6,4},{7,5},{8,10},{9,11},{10,... | collective-permute-start | bytes 294920 | tf_op jit(solution)/shard_map/ppermute | solution.py:446
  365.2 9.8 %collective-permute-start.36 = (bf16[8,32,640]{2,1,0:T(8,128)(2,1)S(1)}, bf16[8,32,640]{2,1,0:T(8,128)(2,1)S(1)}, u32[]{:S(2)}, u32[]{:S(2)}) collective-permute-start(bf16[8,32,640]{2,1,0:T(8,128)(2,1)S(1)} %fusion.66), channel_id=1, source_target_pairs={{0,2},{1,3},{2,0},{3,1},{4,6},{5,7},{6,4},{7,5},{8,10},{9,11},{10,... | collective-permute-start | bytes 983048 | tf_op jit(solution)/shard_map/ppermute | solution.py:446
  367.8 13.7 %copy-start.58 = (f32[16,3072]{1,0:T(8,128)S(1)}, f32[16,3072]{1,0:T(8,128)}, u32[]{:S(2)}) copy-start(f32[16,3072]{1,0:T(8,128)} %param.28) | copy-start | bytes 589828
  367.8 13.7 %copy-start.80 = (f32[16,3072]{1,0:T(8,128)S(1)}, f32[16,3072]{1,0:T(8,128)}, u32[]{:S(2)}) copy-start(f32[16,3072]{1,0:T(8,128)} %param.38) | copy-start | bytes 589828
  367.8 13.7 %copy-start.81 = (f32[16,3072]{1,0:T(8,128)S(1)}, f32[16,3072]{1,0:T(8,128)}, u32[]{:S(2)}) copy-start(f32[16,3072]{1,0:T(8,128)} %param.37) | copy-start | bytes 589828
  367.8 11.8 %collective-permute-start.37 = (bf16[1,96,1024]{2,1,0:T(8,128)(2,1)S(1)}, bf16[1,96,1024]{2,1,0:T(8,128)(2,1)S(1)}, u32[]{:S(2)}, u32[]{:S(2)}) collective-permute-start(bf16[1,96,1024]{2,1,0:T(8,128)(2,1)S(1)} %dynamic-slice_convert_fusion.2), channel_id=1, source_target_pairs={{0,16},{1,17},{2,18},{3,19},{4,20},{5,21},{6,22},{7,23},{8,24},{9,... | collective-permute-start | bytes 589832 | tf_op jit(solution)/shard_map/ppermute | solution.py:446
  375.2 13.9 %copy-start.41 = (f32[2,32,3072]{2,1,0:T(8,128)S(1)}, f32[2,32,3072]{2,1,0:T(8,128)}, u32[]{:S(2)}) copy-start(f32[2,32,3072]{2,1,0:T(8,128)} %copy-done.40) | copy-start | bytes 2359300
  375.2 13.9 %copy-start.46 = (f32[32,3072]{1,0:T(8,128)S(1)}, f32[32,3072]{1,0:T(8,128)}, u32[]{:S(2)}) copy-start(f32[32,3072]{1,0:T(8,128)} %param.26) | copy-start | bytes 1179652
  375.2 13.9 %copy-start.64 = (f32[32,3072]{1,0:T(8,128)S(1)}, f32[32,3072]{1,0:T(8,128)}, u32[]{:S(2)}) copy-start(f32[32,3072]{1,0:T(8,128)} %param.34) | copy-start | bytes 1179652
  375.2 13.9 %copy-start.65 = (f32[32,3072]{1,0:T(8,128)S(1)}, f32[32,3072]{1,0:T(8,128)}, u32[]{:S(2)}) copy-start(f32[32,3072]{1,0:T(8,128)} %param.33) | copy-start | bytes 1179652
  379.7 8.7 %collective-permute-start.38 = (f32[4,32,640]{2,1,0:T(8,128)S(1)}, f32[4,32,640]{2,1,0:T(8,128)S(1)}, u32[]{:S(2)}, u32[]{:S(2)}) collective-permute-start(f32[4,32,640]{2,1,0:T(8,128)S(1)} %dynamic-slice_bitcast_fusion), channel_id=1, source_target_pairs={{0,4},{1,5},{2,6},{3,7},{4,0},{5,1},{6,2},{7,3},{8,12},{9,13},{10,... | collective-permute-start | bytes 983048 | tf_op jit(solution)/shard_map/ppermute | solution.py:446
  389.1 5.6 %collective-permute-start.39 = (f32[2,32,640]{2,1,0:T(8,128)}, f32[2,32,640]{2,1,0:T(8,128)}, u32[]{:S(2)}, u32[]{:S(2)}) collective-permute-start(f32[2,32,640]{2,1,0:T(8,128)} %get-tuple-element.319), channel_id=1, source_target_pairs={{0,8},{1,9},{2,10},{3,11},{4,12},{5,13},{6,14},{7,15},{8,0},{9,1},... | collective-permute-start | bytes 491528 | tf_op jit(solution)/shard_map/ppermute | solution.py:446
  396.0 14.5 %copy-start.53 = (f32[32,512]{0,1:T(8,128)S(1)}, f32[32,512]{0,1:T(8,128)}, u32[]{:S(2)}) copy-start(f32[32,512]{0,1:T(8,128)} %copy.418) | copy-start | bytes 196612
  396.0 14.5 %copy-start.54 = (f32[32,512]{0,1:T(8,128)S(1)}, f32[32,512]{0,1:T(8,128)}, u32[]{:S(2)}) copy-start(f32[32,512]{0,1:T(8,128)} %copy.416) | copy-start | bytes 196612
  396.0 14.5 %copy-start.55 = (f32[32,512]{0,1:T(8,128)S(1)}, f32[32,512]{0,1:T(8,128)}, u32[]{:S(2)}) copy-start(f32[32,512]{0,1:T(8,128)} %copy.408) | copy-start | bytes 196612
  396.0 14.4 %collective-permute-start.40 = (f32[1,32,640]{1,2,0:T(8,128)S(1)}, f32[1,32,640]{1,2,0:T(8,128)S(1)}, u32[]{:S(2)}, u32[]{:S(2)}) collective-permute-start(f32[1,32,640]{1,2,0:T(8,128)S(1)} %constant_dynamic-slice_fusion), channel_id=1, source_target_pairs={{0,16},{1,17},{2,18},{3,19},{4,20},{5,21},{6,22},{7,23},{8,24},{9,... | collective-permute-start | bytes 245768 | tf_op jit(solution)/shard_map/ppermute | solution.py:446
  (88 other events, 410.2 us)

commit v2 on v1

--- a/solution.py
+++ b/solution.py
@@ -442,7 +442,10 @@
         return lax.rem(lax.div(self.place, 1 << b), 2)
 
     def swap(self, block, b):
-        pairs = [(i, i ^ (1 << b)) for i in range(self.size)]
+        return self.trade(block, 1 << b)
+
+    def trade(self, block, mask):
+        pairs = [(i, i ^ mask) for i in range(self.size)]
         return lax.ppermute(block, ("tok", "rep"), pairs)
 
     def halves(self, block, have, b):
@@ -468,30 +471,43 @@
 class Gather:
     def __init__(self, cube, shard, order):
         self.cube, self.order, self.have = cube, list(order), []
-        self.block = shard[None]
+        self.block, self.going = shard[None], False
 
     def send(self, *waits):
-        self.arriving = self.cube.swap(after(self.block, *waits), self.order[0])
-
-    def take(self, *waits):
-        b = self.order.pop(0)
-        other = after(self.arriving, *waits)
+        if self.order and not self.going:
+            self.arriving = self.cube.swap(after(self.block, *waits), self.order[0])
+            self.going = True
+
+    def join(self, mine, other, b):
         above = 1 << sum(1 for k in self.have if k > b)
-        shape = (above, 1, -1) + self.block.shape[1:]
-        mine, other = self.block.reshape(shape), other.reshape(shape)
+        shape = (above, 1, -1) + mine.shape[1:]
+        first, second = mine.reshape(shape), other.reshape(shape)
         joined = jnp.where(
             self.cube.bit(b) == 1,
-            jnp.concatenate([other, mine], axis=1),
-            jnp.concatenate([mine, other], axis=1),
+            jnp.concatenate([second, first], axis=1),
+            jnp.concatenate([first, second], axis=1),
         )
-        self.have.append(b)
-        self.block = joined.reshape((1 << len(self.have),) + self.block.shape[1:])
-
-    def rest(self, *waits):
+        return joined.reshape((2 * mine.shape[0],) + mine.shape[1:])
+
+    def take(self, *waits):
+        self.send()
         if self.order:
-            self.take(*waits)
+            b, self.going = self.order.pop(0), False
+            self.block = self.join(self.block, after(self.arriving, *waits), b)
+            self.have.append(b)
+
+    def direct(self, bits):
+        masks = [sum(1 << b for k, b in enumerate(bits) if n >> k & 1) for n in range(1 << len(bits))]
+        blocks = {m: self.cube.trade(self.block, m) if m else self.block for m in masks}
+        for b in bits:
+            blocks = {
+                m: self.join(blocks[m], blocks[m | 1 << b], b) for m in blocks if not m >> b & 1
+            }
+            self.have.append(b)
+        self.block = blocks[0]
+
+    def rest(self):
         while self.order:
-            self.send()
             self.take()
 
     def both(self):
@@ -505,10 +521,14 @@
         self.going = False
 
     def send(self, *waits):
-        self.arriving = self.cube.swap(after(self.sent, *waits), self.order[0])
-        self.going = True
+        if self.order and not self.going:
+            self.arriving = self.cube.swap(after(self.sent, *waits), self.order[0])
+            self.going = True
 
     def take(self, *waits):
+        self.send()
+        if not self.order:
+            return
         b, self.going = self.order.pop(0), False
         self.have.remove(b)
         total = self.keep + after(self.arriving, *waits).astype(jnp.float32)
@@ -520,29 +540,242 @@
 
     def rest(self):
         while self.order:
-            if not self.going:
-                self.send()
             self.take()
         return self.keep[0]
 
 
+def direct_sum(cube, total, have, bits, kind):
+    have, parts = list(have), {0: total}
+    for b in bits:
+        halves = {m: cube.halves(part, have, b) for m, part in parts.items()}
+        have.remove(b)
+        parts = {m | k << b: halves[m][k] for m in halves for k in range(2)}
+    keep = parts.pop(0)
+    return keep + sum(cube.trade(p.astype(kind), m).astype(jnp.float32) for m, p in parts.items())
+
+
 def after(block, *waits):
     return lax.optimization_barrier((block, *waits))[0] if waits else block
 
 
+def gelu_parts(a):
+    root = 0.7978845608028654
+    square = a * a
+    t = jnp.tanh(root * a * (1.0 + 0.044715 * square))
+    half = 0.5 * (1.0 + t)
+    slope = half + 0.5 * a * (1.0 - t * t) * root * (1.0 + 3.0 * 0.044715 * square)
+    return a * half, slope
+
+
+def gate_kernel(
+    split, core_ref, normed_ref, state_refs, grad_ref, up_refs, expand_refs, down_refs,
+    grad_out, up_out, gated_refs, state_outs, state_scratch, sum_scratch,
+):
+    step, last = pl.program_id(0), pl.num_programs(0) - 1
+    channels = state_refs[0].shape[0]
+    swapped = core_ref[0] == 1
+
+    @pl.when(step == 0)
+    def _():
+        for k in range(2):
+            turned = state_refs[k][...].astype(jnp.float32).T
+            state_scratch[:, channels * k : channels * (k + 1)] = turned.astype(jnp.bfloat16)
+        sum_scratch[...] = jnp.zeros_like(sum_scratch)
+
+    def pair(mine, other):
+        return jnp.where(swapped, other, mine), jnp.where(swapped, mine, other)
+
+    rows = normed_ref.shape[1] // 2
+    up_pre = nn(normed_ref[:, :rows], up_refs[0][...]) + nn(normed_ref[:, rows:], up_refs[1][...])
+    if split:
+        down = []
+        for s in range(down_refs[0].shape[0]):
+            down += pair(down_refs[0][s], down_refs[1][s])
+        down = jnp.concatenate(down, axis=0)
+    else:
+        down = down_refs[0][...]
+    gated_grad = nt(grad_ref[...], down)
+    expanded = nn(state_scratch[:, :channels], expand_refs[0][...]) + nn(
+        state_scratch[:, channels:], expand_refs[1][...]
+    )
+    upper, slope = gelu_parts(up_pre)
+    expanded_grad = (gated_grad * upper).astype(jnp.bfloat16)
+    grad_out[...] = expanded_grad
+    up_out[...] = (gated_grad * expanded * slope).astype(jnp.bfloat16)
+    gated = (upper * expanded).T.astype(jnp.bfloat16)
+    if split:
+        size = gated_refs[0].shape[1]
+        for s in range(gated_refs[0].shape[0]):
+            first = gated[2 * s * size : (2 * s + 1) * size]
+            second = gated[(2 * s + 1) * size : (2 * s + 2) * size]
+            mine, other = pair(first, second)
+            gated_refs[0][s] = mine
+            gated_refs[1][s] = other
+    else:
+        gated_refs[0][...] = gated
+    for k in range(2):
+        sum_scratch[:, channels * k : channels * (k + 1)] += nt(expanded_grad, expand_refs[k][...])
+
+    @pl.when(step == last)
+    def _():
+        for k in range(2):
+            total = sum_scratch[:, channels * k : channels * (k + 1)].T
+            state_outs[k][...] = total.astype(jnp.bfloat16)
+
+
+def gate(cube, normed, states, grad_rows, ups, expands, downs):
+    tokens, width = grad_rows.shape
+    hidden = ups[0].shape[1]
+    split = downs[0].shape[1] % 16 == 0
+    block = 2 * downs[0].shape[1] * max(1, 192 // downs[0].shape[1]) if split else 384
+    low, f32 = jnp.bfloat16, jnp.float32
+    full = lambda array: pl.BlockSpec(array.shape, lambda i: (0,) * array.ndim)
+    if split:
+        shards = block // (2 * downs[0].shape[1])
+        down_spec = pl.BlockSpec((shards,) + downs[0].shape[1:], lambda i: (i, 0, 0))
+        gated_shape = jax.ShapeDtypeStruct(downs[0].shape[:2] + (tokens,), low)
+        gated_spec = pl.BlockSpec((shards, downs[0].shape[1], tokens), lambda i: (i, 0, 0))
+        count = 2
+    else:
+        downs = [cube.merge(*downs)]
+        down_spec = pl.BlockSpec((block, width), lambda i: (i, 0))
+        gated_shape = jax.ShapeDtypeStruct((hidden, tokens), low)
+        gated_spec = pl.BlockSpec((block, tokens), lambda i: (i, 0))
+        count = 1
+    columns = lambda array: pl.BlockSpec((array.shape[0], block), lambda i: (0, i))
+    channels = states[0].shape[0]
+    row_spec = pl.BlockSpec((tokens, block), lambda i: (0, i))
+    state_shape = jax.ShapeDtypeStruct((channels, tokens), low)
+
+    def body(core, normed, s0, s1, grad, u0, u1, e0, e1, *refs):
+        down_refs, refs = refs[:count], refs[count:]
+        grad_out, up_out, gated_refs, refs = refs[0], refs[1], refs[2 : 2 + count], refs[2 + count :]
+        gate_kernel(
+            split, core, normed, (s0, s1), grad, (u0, u1), (e0, e1), down_refs,
+            grad_out, up_out, gated_refs, refs[:2], refs[2], refs[3],
+        )
+
+    outs = pl.pallas_call(
+        body,
+        grid=(hidden // block,),
+        in_specs=[pl.BlockSpec(memory_space=pltpu.SMEM), full(normed)]
+        + [full(s) for s in states]
+        + [full(grad_rows)]
+        + [columns(u) for u in ups]
+        + [columns(e) for e in expands]
+        + [down_spec] * count,
+        out_specs=[row_spec, row_spec] + [gated_spec] * count + [full(state_shape)] * 2,
+        out_shape=[jax.ShapeDtypeStruct((tokens, hidden), low)] * 2
+        + [gated_shape] * count
+        + [state_shape] * 2,
+        scratch_shapes=[
+            pltpu.VMEM((tokens, 2 * channels), low),
+            pltpu.VMEM((tokens, 2 * channels), f32),
+        ],
+        compiler_params=pltpu.CompilerParams(vmem_limit_bytes=48 * 2**20),
+        cost_estimate=pl.CostEstimate(
+            flops=10**6, bytes_accessed=2**10, transcendentals=0
+        ),
+        name="gate",
+    )(cube.bit(0).reshape(1), normed, *states, grad_rows, *ups, *expands, *downs)
+    grad_out, up_out = outs[:2]
+    gated = outs[2 : 2 + count]
+    gated = gated if split else cube.split(gated[0])
+    return grad_out, up_out, gated, outs[2 + count :]
+
+
+def value_kernel(
+    width, grad_ref, pre_ref, value_refs, normed_refs, hat_refs, part_refs, keep_ref, send_ref, out_refs
+):
+    slope = gelu_parts(pre_ref[...])[1]
+    grad = (grad_ref[...].astype(jnp.float32) * slope).astype(jnp.bfloat16)
+    for k, ref in ((1, send_ref), (0, keep_ref)):
+        total = part_refs[k][...] + nn(value_refs[k][:, :width], grad)
+        out_refs[k][...] = total
+        ref[:, :width] = nt(normed_refs[k][...], grad).astype(ref.dtype)
+        lane = lax.broadcasted_iota(jnp.int32, (total.shape[0], 128), 1)
+        gain = jnp.sum(total * hat_refs[k][...], axis=1, keepdims=True)
+        shift = jnp.sum(total, axis=1, keepdims=True)
+        columns = jnp.where(lane == 0, gain, jnp.where(lane == 1, shift, 0.0))
+        ref[:, width:] = columns.astype(ref.dtype)
+
+
+def value_grads(width, value_grad, value_pre, packs, normed, hats, parts):
+    rows, tokens = normed[0].shape
+    columns = packs[0].shape[1]
+
+    def body(grad, pre, p0, p1, n0, n1, h0, h1, a0, a1, keep, send, g0, g1):
+        value_kernel(
+            width, grad, pre, (p0, p1), (n0, n1), (h0, h1), (a0, a1), keep, send, (g0, g1)
+        )
+
+    operands = (value_grad, value_pre, *packs, *normed, *hats, *parts)
+    results = [((rows, columns), jnp.float32), ((rows, columns), jnp.bfloat16)]
+    results += [((rows, tokens), jnp.float32)] * 2
+    keep, send, first, second = pl.pallas_call(
+        body,
+        grid=(1,),
+        in_specs=[whole(a.shape) for a in operands],
+        out_specs=[whole(shape) for shape, _ in results],
+        out_shape=[jax.ShapeDtypeStruct(shape, kind) for shape, kind in results],
+        compiler_params=pltpu.CompilerParams(vmem_limit_bytes=48 * 2**20),
+        cost_estimate=pl.CostEstimate(flops=10**6, bytes_accessed=2**10, transcendentals=0),
+        name="value_grads",
+    )(*operands)
+    return keep, send, (first, second)
+
+
+def products_kernel(bit_ref, own_send, own_keep, got_send, got_keep, own, got, send_ref, keep_ref):
+    def product(a, b):
+        flat = lambda ref: ref[...].reshape((-1, ref.shape[3]))
+        return nn(flat(a), own[...]) + nn(flat(b), got[...])
+
+    send_ref[...] = product(own_send, got_send).astype(jnp.bfloat16)
+    keep_ref[...] = product(own_keep, got_keep)
+
+
 def products(cube, lefts, rights, first, have):
-    sides = [cube.halves(left, have, first) for left in lefts]
-
-    def product(side):
-        parts = []
-        for pair, right in zip(sides, rights):
-            left = pair[side]
-            parts.append(dot(left.reshape((-1, left.shape[2])), right, 1, 1))
-        shape = (-1, lefts[0].shape[1], rights[0].shape[0])
-        return (parts[0] + parts[1]).reshape(shape)
-
-    send = product(1).astype(jnp.bfloat16)
-    return product(0), send
+    shards, rows, tokens = lefts[0].shape
+    columns = rights[0].shape[1]
+    above = 1 << sum(1 for k in have if k > first)
+    shape = (shards // 2, rows, columns)
+    if rows % 16:
+        sides = [cube.halves(left, have, first) for left in lefts]
+        keep, send = [
+            sum(
+                dot(pair[k].reshape((-1, tokens)), right, 1, 0)
+                for pair, right in zip(sides, rights)
+            ).reshape(shape)
+            for k in range(2)
+        ]
+        return keep, send.astype(jnp.bfloat16)
+    lefts = [left.reshape((above, 2, -1, tokens)) for left in lefts]
+    side = (above, 1) + lefts[0].shape[2:]
+    send_spec = pl.BlockSpec(side, lambda j, bit: (0, 1 - bit[0], 0, 0))
+    keep_spec = pl.BlockSpec(side, lambda j, bit: (0, bit[0], 0, 0))
+    block = min(columns, 1024)
+    count = shards * rows // 2
+    right_spec = pl.BlockSpec((tokens, block), lambda j, bit: (0, j))
+    out_spec = pl.BlockSpec((count, block), lambda j, bit: (0, j))
+    send, keep = pl.pallas_call(
+        products_kernel,
+        grid_spec=pltpu.PrefetchScalarGridSpec(
+            num_scalar_prefetch=1,
+            grid=(columns // block,),
+            in_specs=[send_spec, keep_spec] * 2 + [right_spec] * 2,
+            out_specs=[out_spec] * 2,
+        ),
+        out_shape=[
+            jax.ShapeDtypeStruct((count, columns), jnp.bfloat16),
+            jax.ShapeDtypeStruct((count, columns), jnp.float32),
+        ],
+        compiler_params=pltpu.CompilerParams(vmem_limit_bytes=48 * 2**20),
+        cost_estimate=pl.CostEstimate(
+            flops=10**6, bytes_accessed=2**10, transcendentals=0
+        ),
+        name="weight_grad",
+    )(cube.bit(first).reshape(1), lefts[0], lefts[0], lefts[1], lefts[1], *rights)
+    return keep.reshape(shape), send.reshape(shape)
 
 
 def dot(a, b, a_dim, b_dim):
@@ -608,30 +841,26 @@
         (part.astype(jnp.float32) - average) * scale for part in cube.split(tokens[0].T)
     ]
 
+    expand.send()
+    pack.direct(zs)
+    up.send(pack.block)
+    down.send(pack.block)
+    if expand.order[1:]:
+        expand.take(pack.block)
+        expand.send()
+    pack.direct(xs + ys)
+    packs = pack.both()
+    up.take()
+    down.take()
     up.send()
     down.send()
-    expand.send()
-    for _ in range(2 * nx):
-        pack.send()
-        pack.take()
-    up.take()
-    down.take()
-    for _ in range(nz):
-        pack.send(up.block, down.block)
-        pack.take()
-    up.send(pack.block)
-    down.send(pack.block)
-    expand.take(pack.block)
-    if expand.order:
-        expand.send()
-    packs = pack.both()
     values = [pack[:, :, :inner] for pack in packs]
     gains = [pack[:, :, inner : inner + 1].astype(jnp.float32) for pack in packs]
     shifts = [pack[:, :, inner + 1 : inner + 2].astype(jnp.float32) for pack in packs]
     normed = [(h * g + b).astype(low) for h, g, b in zip(hats, gains, shifts)]
     value_preactivation = dots(values, normed, 0, 0)
-    value_act, value_back = jax.vjp(gelu_curve, value_preactivation)
-    value_low = value_act.astype(low)
+    value_act = gelu_curve(value_preactivation)
+    value_low = after(value_act.astype(low), up.block, down.block)
     channel_values = lax.all_to_all(value_low, "tok", split_axis=0, concat_axis=1, tiled=True)
 
     for _ in range(nz - 2):
@@ -648,9 +877,9 @@
     pieces = pieces_of(lengths[0], length)
     powers, lams, coefs = mixer_inputs(poles, coefs)
     channel_values = channel_values.reshape(blocked)
-    grad_columns = grad_rows.T
+    normed_rows = jnp.concatenate([flat(side).T for side in normed], axis=1)
     normed_swapped = cube.swap(normed[1], 0)
-    columns_swapped = cube.swap(grad_columns, 0)
+    columns_swapped = cube.swap(grad_rows, 0)
     mixer = mix_forward(channel_values, pieces, powers, lams, coefs)
 
     def run(*waits):
@@ -669,67 +898,67 @@
         down.take(*token)
         up.send()
         down.send()
-    token = run(up.block, down.block)
     expand.take(*token)
     if expand.order:
         expand.send()
-    token = run(*token, expand.block, normed_swapped, columns_swapped)
-    mixer.last()
+    token = run(up.block, down.block, expand.block)
+    token = run(*token)
+    if expand.order:
+        expand.take(*token)
+    mixer.last(*token, expand.block, normed_swapped, columns_swapped, normed_rows)
     state_out, starts, taps = mixer.outs
+    for part in (up, down):
+        part.arriving = after(part.arriving, state_out)
     token_states = lax.all_to_all(
         state_out.reshape(channels, length), "tok", split_axis=1, concat_axis=0, tiled=True
     )
     state_sides = cube.split(token_states)
-    expand.rest(token_states)
-    up.rest(token_states)
-    down.rest(token_states)
+    expand.rest()
+    up.rest()
+    down.rest()
     ups, downs, expands = up.both(), down.both(), expand.both()
 
-    upper, upper_back = jax.vjp(gelu_curve, dots(ups, normed, 0, 0))
-    gated_grad = cube.merge(
-        *[dot(flat(down), grad_rows, 1, 1).reshape(down.shape[:2] + (-1,)) for down in downs]
-    )
-    expanded = dots(expands, state_sides, 0, 0)
-    expanded_grad = (gated_grad * upper).astype(low)
-    state_grad = cube.merge(
-        *[
-            dot(flat(expand), expanded_grad, 1, 0).astype(low).reshape(expand.shape[:2] + (-1,))
-            for expand in expands
-        ]
-    )
+    expanded_grad, up_pre_grad, gated_sides, state_grads = gate(
+        cube,
+        normed_rows,
+        [flat(side) for side in state_sides],
+        grad_rows,
+        [flat(side) for side in ups],
+        [flat(side) for side in expands],
+        downs,
+    )
+    state_grad = cube.merge(*[g.reshape(state_sides[0].shape) for g in state_grads])
     channel_grad = lax.all_to_all(state_grad, "tok", split_axis=0, concat_axis=1, tiled=True)
-    gated = (upper * expanded).astype(low)
-    gated_sides = cube.split(gated)
-    up_pre_grad = upper_back(gated_grad * expanded)[0].astype(low)
-
-    def both(block):
-        return block, cube.swap(block, 0)
+    channel_grad = channel_grad.reshape(blocked)
+    gated_swapped = cube.swap(gated_sides[1], 0)
+    expanded_swapped = cube.swap(expanded_grad, 0)
+    up_pre_swapped = cube.swap(after(up_pre_grad, gated_swapped), 0)
+    state_swapped = cube.swap(state_sides[1], 0)
 
     def scatter(lefts, rights, order):
         keep, send = products(cube, lefts, rights, order[0], tok_bits)
-        sums = Scatter(cube, keep, send, order, tok_bits)
-        sums.send()
-        return sums
+        return Scatter(cube, keep, send, order, tok_bits)
 
     down_sums = scatter(
-        (gated_sides[0], cube.swap(gated_sides[1], 0)),
-        (grad_columns, columns_swapped),
+        (gated_sides[0], gated_swapped),
+        (grad_rows, columns_swapped),
         xs + ys + zs,
     )
-    up_sums = scatter((normed[0], normed_swapped), both(up_pre_grad), ys + xs + zs)
+    up_sums = scatter((normed[0], normed_swapped), (up_pre_grad, up_pre_swapped), ys + xs + zs)
     expand_sums = scatter(
-        (state_sides[0], cube.swap(state_sides[1], 0)), both(expanded_grad), zs + ys + xs
-    )
-    layer_out = (token_rows + dots(gated_sides, downs, 0, 0)).astype(low)[None]
-
+        (state_sides[0], state_swapped), (expanded_grad, expanded_swapped), zs + ys + xs
+    )
+    down_sums.send()
+    up_sums.send()
+    expand_sums.send(channel_grad)
     mixer = mix_backward(
-        channel_values, channel_grad.reshape(blocked), pieces, powers, lams, coefs, starts, taps
+        channel_values, channel_grad, pieces, powers, lams, coefs, starts, taps
     )
     token = run(up_sums.sent, down_sums.sent, expand_sums.sent)
-    token = run()
+    token = run(*token)
     expand_sums.take(*token)
     expand_sums.send()
-    token = run(expand_sums.sent)
+    token = run(*token, expand_sums.sent)
     for _ in range(nx):
         up_sums.take(*token)
         down_sums.take(*token)
@@ -737,7 +966,7 @@
         down_sums.send()
     expand_sums.take(*token)
     expand_sums.send()
-    mixer.last(up_sums.sent, down_sums.sent, expand_sums.sent)
+    mixer.last(*token, up_sums.sent, down_sums.sent, expand_sums.sent)
     value_grad_channels, param_grad = mixer.outs
     states = param_grad.shape[1] // 2
     param_grad = jnp.stack([param_grad[:channels, :states], param_grad[:channels, states:]])
@@ -752,38 +981,38 @@
         concat_axis=0,
         tiled=True,
     )
-    value_pre_grad = value_back(value_grad.astype(jnp.float32))[0].astype(low)
-    ups_grads = [dot(flat(up), up_pre_grad, 1, 0) for up in ups]
-    normed_grads = [
-        (g + dot(flat(value), value_pre_grad, 1, 0)).reshape(h.shape)
-        for g, value, h in zip(ups_grads, values, hats)
-    ]
-    packed_grads = []
-    for side, h, g in zip(normed, hats, normed_grads):
-        weight_grad = dot(flat(side), value_pre_grad, 1, 1).reshape(side.shape[:2] + (-1,))
-        norm_grad = jnp.stack([jnp.sum(g * h, axis=2), jnp.sum(g, axis=2)], axis=2)
-        norm_grad = jnp.pad(norm_grad, ((0, 0), (0, 0), (0, 126)))
-        packed_grads.append(jnp.concatenate([weight_grad, norm_grad], axis=2))
-    packed_sums = Scatter(
-        cube, packed_grads[0], packed_grads[1].astype(low), [0] + tok_bits, [0] + tok_bits, ys + zs
-    )
     for sums in (up_sums, down_sums):
         sums.take()
         sums.send()
-    expand_sums.take(value_pre_grad)
+    expand_sums.take(value_grad)
     if expand_sums.order:
         expand_sums.send()
-    packed_sums.send()
-    packed_sums.take(up_sums.arriving, down_sums.arriving)
+    up_pre_late = after(up_pre_grad, value_grad_channels)
+    ups_grads = [dot(flat(part), up_pre_late, 1, 1) for part in ups]
+    keep, send, normed_grads = value_grads(
+        inner,
+        value_grad,
+        value_preactivation,
+        [flat(part) for part in packs],
+        [flat(part) for part in normed],
+        [flat(part) for part in hats],
+        ups_grads,
+    )
+    normed_grads = [g.reshape(h.shape) for g, h in zip(normed_grads, hats)]
+    keep, send = [part.reshape(hats[0].shape[:2] + (-1,)) for part in (keep, send)]
+    packed_sum = keep + cube.swap(send, 0).astype(jnp.float32)
+    core_sum = packed_sum
+    normed_grads = [after(g, core_sum) for g in normed_grads]
+    gated_late = after(gated_sides[0], packed_sum), gated_sides[1]
+    layer_out = (token_rows + dots(gated_late, downs, 0, 0)).astype(low)[None]
+    packed_sum = direct_sum(cube, packed_sum, tok_bits, xs + ys, low)
     for sums in (up_sums, down_sums, expand_sums):
         if sums.order:
-            sums.take(value_pre_grad)
+            sums.take(core_sum)
         if sums.order:
             sums.send()
-    packed_sums.send()
-    packed_sums.take()
-    packed_sums.send(up_sums.arriving, down_sums.arriving)
-    packed_sum = packed_sums.rest()
+            sums.arriving = after(sums.arriving, packed_sum)
+    packed_sum = direct_sum(cube, packed_sum, zs, zs, jnp.float32)[0]
     up_sum, down_sum, expand_sum = [
         sums.rest() for sums in (up_sums, down_sums, expand_sums)
     ]

time: 420 us -> 349 us (0.83)
  matrix products: 75.6 us -> 18.4 us
  waiting for transfers between devices: 81.6 us -> 26.9 us
  Pallas kernels: 87.8 us -> 117 us
  blocking collectives: 0 us -> 14 us
  local copies, waits for them, and re-layouts: 48.4 us -> 40.2 us
    dot_general x30 -> x6, matrix products: 75.6 us -> 18.4 us  [dot(): lax.dot_general(a, b, (((a_dim,), (b_dim,)), ((), ())), preferred_element...]
    ppermute x44 -> x48, waiting for transfers between devices: 67 us -> 23.8 us  [trade(): return lax.ppermute(block, ('tok', 'rep'), pairs)]
    pallas_call x0 -> x5, Pallas kernels: none -> 30.2 us  [the longest x1 13.6 us: gate(): pl.pallas_call(body, grid=(hidden // block,), in_specs=[pl.BlockSpec(memo...]
    all_to_all x0 -> x1, blocking collectives: none -> 14 us  [per_device(): lax.all_to_all(state_out.reshape(channels, length), 'tok', split_axis=1,...]
    unnamed x214 -> x210, local copies, waits for them, and re-layouts: 18.1 us -> 10.6 us
    ppermute x44 -> x48, starting transfers between devices: 41.7 us -> 48.6 us  [trade(): return lax.ppermute(block, ('tok', 'rep'), pairs)]
    all_to_all x1, waiting for transfers between devices: 5.91 us -> 0.01 us  [per_device(): lax.all_to_all(value_low, 'tok', split_axis=0, concat_axis=1, tiled=True)]
    dynamic_slice x7 -> x2, local copies, waits for them, and re-layouts: 6.01 us -> 0.71 us  [halves(): other = lax.dynamic_index_in_dim(split, 1 - index, 1, keepdims=False)]
  transfers between devices with their start and end apart: 48 -> 51, of which waited for: 18 -> 14; matrix products, arithmetic and copies ran while one was open for 37% -> 31% of each run, Pallas kernels for 21% -> 30%
where the time goes in v2:
time: 349 us; the launch traced here: 343 us
  Pallas kernels  117 us (34%)
  starting transfers between devices  63.5 us (18%)
  other arithmetic  59.9 us (17%)
  local copies, waits for them, and re-layouts  40.2 us (12%)
  waiting for transfers between devices  26.9 us (8%)
  matrix products  18.4 us (5%)
  blocking collectives  14 us (4%)
    pallas_call x8, Pallas kernels, call(): pl.pallas_call(body, grid=(1,), in_specs=specs + [pl.BlockSpec(memory_spa...  87.3 us
    ppermute x48, starting transfers between devices, trade(): return lax.ppermute(block, ('tok', 'rep'), pairs)  48.6 us
    ppermute x48, waiting for transfers between devices, trade(): return lax.ppermute(block, ('tok', 'rep'), pairs)  23.8 us
    dot_general x6, matrix products, dot(): lax.dot_general(a, b, (((a_dim,), (b_dim,)), ((), ())), preferred_element...  18.4 us
    select_n x23, other arithmetic, join(): jnp.where(self.cube.bit(b) == 1, jnp.concatenate([second, first], axis=1)...  17 us
    all_to_all x1, blocking collectives, per_device(): lax.all_to_all(state_out.reshape(channels, length), 'tok', split_axis=1,...  14 us
    pallas_call x1, Pallas kernels, gate(): pl.pallas_call(body, grid=(hidden // block,), in_specs=[pl.BlockSpec(memo...  13.6 us
    pallas_call x3, Pallas kernels, products(): pl.pallas_call(products_kernel, grid_spec=pltpu.PrefetchScalarGridSpec(nu...  13.4 us
  transfers between devices with their start and end apart: 51, of which 14 were waited for; matrix products, arithmetic and copies ran while one was open for 31% of the time, Pallas kernels for 30%

profile of v2, /device:TPU:0, one launch (start us, length us, event | category | flops | bytes accessed | tf_op | source)
XLA Modules:
  0.0 342.9 jit_solution(13272726409993813587)
XLA Ops:
  2.4 5.1 %collective-permute-start = (bf16[1,32,640]{2,1,0:T(8,128)(2,1)S(1)}, bf16[1,32,640]{2,1,0:T(8,128)(2,1)S(1)}, u32[]{:S(2)}, u32[]{:S(2)}) collective-permute-start(bf16[1,32,640]{2,1,0:T(8,128)(2,1)S(1)} %get-tuple-element.358), channel_id=1, source_target_pairs={{0,24},{1,25},{2,26},{3,27},{4,28},{5,29},{6,30},{7,31},{8,16},{9,... | collective-permute-start | bytes 122888 | tf_op jit(solution)/shard_map/ppermute | solution.py:449
  9.1 1.7 collective-permute-start.12
  15.3 1.6 collective-permute-start.3
  17.2 1.6 collective-permute-start.5
  18.9 2.1 collective-permute-start.7
  23.3 2.1 collective-permute-start.8
  29.2 6.5 %collective-permute-done.7 = bf16[1,32,3072]{2,1,0:T(8,128)(2,1)S(1)} collective-permute-done((bf16[1,32,3072]{2,1,0:T(8,128)(2,1)S(1)}, bf16[1,32,3072]{2,1,0:T(8,128)(2,1)S(1)}, u32[]{:S(2)}, u32[]{:S(2)}) %collective-permute-start.7) | collective-permute-done | bytes 196640 | tf_op jit(solution)/shard_map/ppermute | solution.py:449
  36.5 2.5 collective-permute-done.8
  39.1 1.8 maximum_select_fusion.12
  40.9 1.8 maximum_select_fusion.14
  44.9 2.4 fusion.18
  47.4 6.3 %all-to-all-start = ((bf16[16,32,256]{2,1,0:T(8,128)(2,1)}), bf16[16,32,256]{2,1,0:T(8,128)(2,1)S(1)}, u32[]{:S(2)}, u32[]{:S(2)}) async-start(bf16[16,32,256]{2,1,0:T(8,128)(2,1)} %bitcast.30), calls=%async_computation | async-start | bytes 524288 | tf_op jit(solution)/shard_map/all_to_all | solution.py:864
  54.4 3.9 %fusion.4 = (f32[32,16,512]{2,0,1:T(8,128)S(1)}, f32[32,16,512]{2,0,1:T(8,128)S(1)}) fusion(f32[32,512]{1,0:T(8,128)S(1)} %get-tuple-element.362, f32[16]{0:T(128)S(1)} %copy-done.102, f32[32,512]{1,0:T(8,128)S(1)} %get-tuple-element.363), kind=kLoop, calls=%fused_computation.31 | loop fusion | flops 1048576 | bytes 2228288 | tf_op jit(solution)/shard_map/mul | solution.py:61
  60.7 2.5 copy.327.refs_4_.refs_5_
  69.1 3.0 collective-permute-start.15
  73.4 1.5 collective-permute-start.14
  76.2 1.5 collective-permute-start.10
  77.7 11.3 %mix_forward.4 = (bf16[32,32,128]{2,1,0:T(8,128)(2,1)S(1)}, f32[1536,1024]{1,0:T(8,128)}, bf16[32,128,128]{2,1,0:T(8,128)(2,1)S(1)}, f32[8,128]{1,0:T(8,128)}) custom-call(f32[48]{0:T(128)S(1)} %add_convert_fusion.6.refs_0_, bf16[48,32]{1,0:T(8,128)(2,1)S(1)} %fusion.53.refs_1_, bf16[48,128]{1,0:T(8,128)(2,1)S(1)} %fusion.55.refs_2_, ...), custom_call_target="tpu_custom_call" | custom-call | flops 8000000000 | bytes 4194304 | tf_op jit(solution)/shard_map/mix_forward/pallas_call | solution.py:298
  90.8 1.8 collective-permute-done.14
  93.0 2.1 collective-permute-done.10
  95.4 1.5 collective-permute-start.22
  97.5 11.4 %mix_forward.5 = (bf16[32,32,128]{2,1,0:T(8,128)(2,1)S(1)}, f32[1536,1024]{1,0:T(8,128)}, bf16[32,128,128]{2,1,0:T(8,128)(2,1)S(1)}, f32[8,128]{1,0:T(8,128)S(1)}) custom-call(f32[48]{0:T(128)S(1)} %add_convert_fusion.6.refs_0_, bf16[48,32]{1,0:T(8,128)(2,1)S(1)} %fusion.53.refs_1_, ...), custom_call_target="tpu_custom_call", output_to_operand_aliasing={{0}: (10, {}), {1}: (11, {}), {2}: (12, {})} | custom-call | flops 8000000000 | bytes 4194304 | tf_op jit(solution)/shard_map/mix_forward/pallas_call | solution.py:298
  109.0 10.9 %mix_forward.6 = (bf16[32,32,128]{2,1,0:T(8,128)(2,1)S(1)}, f32[1536,1024]{1,0:T(8,128)}, bf16[32,128,128]{2,1,0:T(8,128)(2,1)S(1)}, f32[8,128]{1,0:T(8,128)S(1)}) custom-call(f32[48]{0:T(128)S(1)} %add_convert_fusion.6.refs_0_, bf16[48,32]{1,0:T(8,128)(2,1)S(1)} %fusion.53.refs_1_, ...), custom_call_target="tpu_custom_call", output_to_operand_aliasing={{0}: (8, {}), {1}: (9, {}), {2}: (10, {})} | custom-call | flops 8000000000 | bytes 4194304 | tf_op jit(solution)/shard_map/mix_forward/pallas_call | solution.py:298
  121.2 11.3 %mix_forward.7 = (bf16[32,32,128]{2,1,0:T(8,128)(2,1)S(1)}, f32[1536,1024]{1,0:T(8,128)}, bf16[32,128,128]{2,1,0:T(8,128)(2,1)S(1)}, f32[8,128]{1,0:T(8,128)}) custom-call(f32[48]{0:T(128)S(1)} %add_convert_fusion.6.refs_0_, bf16[48,32]{1,0:T(8,128)(2,1)S(1)} %fusion.53.refs_1_, ...), custom_call_target="tpu_custom_call", output_to_operand_aliasing={{0}: (12, {}), {1}: (13, {}), {2}: (14, {})} | custom-call | flops 8000000000 | bytes 4194304 | tf_op jit(solution)/shard_map/mix_forward/pallas_call | solution.py:298
  132.5 2.6 maximum_select_fusion.1
  135.1 2.2 copy.335
  137.3 2.3 maximum_select_fusion
  139.6 1.9 copy.332
  144.0 14.0 %all_to_all.67 = bf16[32,16,256]{2,0,1:T(8,128)(2,1)S(1)} all-to-all(bf16[32,16,256]{2,0,1:T(8,128)(2,1)S(1)} %copy.329), channel_id=1, replica_groups=mesh['tok'=16,'rep'=2] {'tok'}, dimensions={1} | all-to-all | bytes 524288 | tf_op jit(solution)/shard_map/all_to_all | solution.py:912
  158.8 13.6 %gate.1 = (bf16[256,3072]{1,0:T(8,128)(2,1)}, bf16[256,3072]{1,0:T(8,128)(2,1)}, bf16[16,96,256]{2,1,0:T(8,128)(2,1)S(1)}, bf16[16,96,256]{2,1,0:T(8,128)(2,1)S(...) custom-call(s32[1]{0:T(128)} %bitcast.1.core, bf16[256,1024]{1,0:T(8,128)(2,1)S(1)} %copy-done.7, ...), custom_call_target="tpu_custom_call" | custom-call | flops 1000000 | bytes 1024 | tf_op jit(solution)/shard_map/gate/pallas_call | solution.py:658
  172.9 2.1 collective-permute-done.24
  179.9 4.4 %all-to-all-start.2 = ((bf16[16,32,256]{2,1,0:T(8,128)(2,1)}), bf16[16,32,256]{2,1,0:T(8,128)(2,1)}, u32[]{:S(2)}, u32[]{:S(2)}) async-start(bf16[16,32,256]{2,1,0:T(8,128)(2,1)} %bitcast.81), calls=%async_computation.2 | async-start | bytes 524288 | tf_op jit(solution)/shard_map/all_to_all | solution.py:931
  185.7 1.8 bitcast_convert_fusion.6
  192.0 3.1 all-to-all-done.2
  195.0 1.8 copy.338
  196.8 1.7 reshape.1737.refs_4_
  198.6 4.6 %weight_grad.4 = (bf16[768,1024]{1,0:T(8,128)(2,1)S(1)}, f32[768,1024]{1,0:T(8,128)}) custom-call(s32[1]{0:T(128)} %bitcast.87.bit_ref, bf16[8,2,96,256]{3,2,1,0:T(8,128)(2,1)S(1)} %bitcast.369, bf16[8,2,96,256]{3,2,1,0:T(8,128)(2,1)S(1)} %bitcast.370, bf16[8,2,96,256]{3,2,1,0:T(8,128)(2,1)S(1)} %bitcast.372, bf16[8,2,96,256]{3,2,1,0:T(8,128)(2,1)S(1)} %bitcast.373, ...), custom_call_target="tpu_custom_call" | custom-call | flops 1000000 | bytes 1024 | tf_op jit(solution)/shard_map/weight_grad/pallas_call | solution.py:760
  204.0 3.6 %weight_grad.5 = (bf16[128,3072]{1,0:T(8,128)(2,1)S(1)}, f32[128,3072]{1,0:T(8,128)S(1)}) custom-call(s32[1]{0:T(128)} %bitcast.91.bit_ref, bf16[2,2,64,256]{3,2,1,0:T(8,128)(2,1)S(1)} %bitcast.380, bf16[2,2,64,256]{3,2,1,0:T(8,128)(2,1)S(1)} %bitcast.381, bf16[2,2,64,256]{3,2,1,0:T(8,128)(2,1)} %bitcast.94.got_send.got_keep, ...), custom_call_target="tpu_custom_call" | custom-call | flops 1000000 | bytes 1024 | tf_op jit(solution)/shard_map/weight_grad/pallas_call | solution.py:760
  208.7 5.2 %weight_grad.3 = (bf16[256,3072]{1,0:T(8,128)(2,1)S(1)}, f32[256,3072]{1,0:T(8,128)}) custom-call(s32[1]{0:T(128)} %bitcast.83.bit_ref, bf16[4,2,64,256]{3,2,1,0:T(8,128)(2,1)S(1)} %add_convert_fusion.own_send.own_keep, bf16[4,2,64,256]{3,2,1,0:T(8,128)(2,1)S(1)} %add_convert_fusion.own_send.own_keep, bf16[4,2,64,256]{3,2,1,0:T(8,128)(2,1)S(1)} %bitcast.389, ...), custom_call_target="tpu_custom_call" | custom-call | flops 1000000 | bytes 1024 | tf_op jit(solution)/shard_map/weight_grad/pallas_call | solution.py:760
  214.6 10.7 %mix_backward.4 = (bf16[32,32,128]{2,1,0:T(8,128)(2,1)S(1)}, f32[32,1024]{1,0:T(8,128)S(1)}, f32[8,128]{1,0:T(8,128)S(1)}) custom-call(f32[48]{0:T(128)S(1)} %add_convert_fusion.6.refs_0_, bf16[48,32]{1,0:T(8,128)(2,1)S(1)} %fusion.53.refs_1_, bf16[48,128]{1,0:T(8,128)(2,1)S(1)} %copy-done.32, bf16[32,32,128]{2,1,0:T(8,128)(2,1)S(1)} %copy-done.23, ...), custom_call_target="tpu_custom_call" | custom-call | flops 10700000256 | bytes 4194304 | tf_op jit(solution)/shard_map/mix_backward/pallas_call | solution.py:298
  225.3 10.8 %mix_backward.5 = (bf16[32,32,128]{2,1,0:T(8,128)(2,1)S(1)}, f32[32,1024]{1,0:T(8,128)S(1)}, f32[8,128]{1,0:T(8,128)S(1)}) custom-call(f32[48]{0:T(128)S(1)} %add_convert_fusion.6.refs_0_, bf16[48,32]{1,0:T(8,128)(2,1)S(1)} %fusion.53.refs_1_, bf16[48,128]{1,0:T(8,128)(2,1)S(1)} %copy-done.32, ...), custom_call_target="tpu_custom_call", output_to_operand_aliasing={{0}: (11, {}), {1}: (12, {})} | custom-call | flops 10700000256 | bytes 4194304 | tf_op jit(solution)/shard_map/mix_backward/pallas_call | solution.py:298
  236.3 1.6 collective-permute-start.31
  237.9 10.4 %mix_backward.6 = (bf16[32,32,128]{2,1,0:T(8,128)(2,1)S(1)}, f32[32,1024]{1,0:T(8,128)S(1)}, f32[8,128]{1,0:T(8,128)S(1)}) custom-call(f32[48]{0:T(128)S(1)} %add_convert_fusion.6.refs_0_, bf16[48,32]{1,0:T(8,128)(2,1)S(1)} %fusion.53.refs_1_, bf16[48,128]{1,0:T(8,128)(2,1)S(1)} %copy-done.32, ...), custom_call_target="tpu_custom_call", output_to_operand_aliasing={{0}: (12, {}), {1}: (13, {})} | custom-call | flops 10700000256 | bytes 4194304 | tf_op jit(solution)/shard_map/mix_backward/pallas_call | solution.py:298
  248.3 3.0 convert_add_fusion
  252.4 3.0 collective-permute-done.31
  256.3 1.8 convert_add_fusion.1
  260.2 10.6 %mix_backward.7 = (bf16[32,32,128]{2,1,0:T(8,128)(2,1)S(1)}, f32[32,1024]{1,0:T(8,128)S(1)}, f32[8,128]{1,0:T(8,128)}) custom-call(f32[48]{0:T(128)S(1)} %add_convert_fusion.6.refs_0_, bf16[48,32]{1,0:T(8,128)(2,1)S(1)} %fusion.53.refs_1_, bf16[48,128]{1,0:T(8,128)(2,1)S(1)} %copy-done.32, ...), custom_call_target="tpu_custom_call", output_to_operand_aliasing={{0}: (14, {}), {1}: (15, {})} | custom-call | flops 10700000256 | bytes 4194304 | tf_op jit(solution)/shard_map/mix_backward/pallas_call | solution.py:298
  272.0 1.8 bitcast_add_fusion
  277.4 4.2 %fusion.69.a1 = f32[512,256]{1,0:T(8,128)} fusion(bf16[512,3072]{1,0:T(8,128)(2,1)} %bitcast.73.u1, bf16[256,3072]{1,0:T(8,128)(2,1)} %get-tuple-element.158.own), kind=kOutput, calls=%fused_computation.227 | convolution fusion | flops 805306368 | bytes 5242880 | tf_op jit(solution)/shard_map/dot_general | solution.py:782
  282.3 4.2 %all-to-all-start.3 = ((bf16[32,16,256]{2,0,1:T(8,128)(2,1)}), bf16[32,16,256]{2,0,1:T(8,128)(2,1)S(1)}, u32[]{:S(2)}, u32[]{:S(2)}) async-start(bf16[32,16,256]{2,0,1:T(8,128)(2,1)} %copy.345), calls=%async_computation.3 | async-start | bytes 524288 | tf_op jit(solution)/shard_map/all_to_all | solution.py:977
  286.6 1.9 bitcast_add_fusion.1
  290.5 1.7 collective-permute-start.35
  292.2 3.7 %fusion.68.a0 = f32[512,256]{1,0:T(8,128)} fusion(bf16[512,3072]{1,0:T(8,128)(2,1)} %bitcast.71.u0, bf16[256,3072]{1,0:T(8,128)(2,1)S(1)} %copy-done.12), kind=kOutput, calls=%fused_computation.226 | convolution fusion | flops 805306368 | bytes 5242880 | tf_op jit(solution)/shard_map/dot_general | solution.py:782
  300.1 3.2 value_grads.1
  303.4 1.5 collective-permute-start.44
  305.5 1.6 convert_add_fusion.4
  309.2 2.4 collective-permute-start.46
  312.3 1.5 collective-permute-start.38
  313.8 1.5 collective-permute-start.39
  320.3 3.0 fusion.70
  324.4 3.7 %fusion.2 = bf16[1,256,1024]{2,1,0:T(8,128)(2,1)} fusion(f32[256,1024]{1,0:T(8,128)S(1)} %fusion.70, bf16[16,96,256]{2,1,0:T(8,128)(2,1)S(1)} %copy-done.35, bf16[16,96,1024]{2,1,0:T(8,128)(2,1)} %collective-permute-done.23.refs_1_, bf16[1,256,1024]{2,1,0:T(8,128)(2,1)S(1)} %copy-done.51), kind=kOutput, calls=%fused_computation.27 | convolution fusion | flops 806354944 | bytes 6029312 | tf_op jit(solution)/shard_map/dot_general | solution.py:782
  330.5 2.4 collective-permute-start.40
  334.9 2.1 multiply_subtract_fusion.1
  337.2 2.2 multiply_subtract_fusion
  (410 shorter events, 82.3 us)
Async XLA Ops:
  0.7 13.8 %copy-start.61 = (f32[32,3072]{1,0:T(8,128)S(1)}, f32[32,3072]{1,0:T(8,128)}, u32[]{:S(2)}) copy-start(f32[32,3072]{1,0:T(8,128)} %param.26) | copy-start | bytes 1179652
  0.7 13.8 %copy-start.63 = (f32[96,1024]{1,0:T(8,128)S(1)}, f32[96,1024]{1,0:T(8,128)}, u32[]{:S(2)}) copy-start(f32[96,1024]{1,0:T(8,128)} %param.29) | copy-start | bytes 1179652
  2.4 12.8 %collective-permute-start = (bf16[1,32,640]{2,1,0:T(8,128)(2,1)S(1)}, bf16[1,32,640]{2,1,0:T(8,128)(2,1)S(1)}, u32[]{:S(2)}, u32[]{:S(2)}) collective-permute-start(bf16[1,32,640]{2,1,0:T(8,128)(2,1)S(1)} %get-tuple-element.358), channel_id=1, source_target_pairs={{0,24},{1,25},{2,26},{3,27},{4,28},{5,29},{6,30},{7,31},{8,16},{9,... | collective-permute-start | bytes 122888 | tf_op jit(solution)/shard_map/ppermute | solution.py:449
  7.5 7.7 %collective-permute-start.1 = (bf16[1,32,640]{2,1,0:T(8,128)(2,1)S(1)}, bf16[1,32,640]{2,1,0:T(8,128)(2,1)S(1)}, u32[]{:S(2)}, u32[]{:S(2)}) collective-permute-start(bf16[1,32,640]{2,1,0:T(8,128)(2,1)S(1)} %get-tuple-element.358), channel_id=1, source_target_pairs={{0,16},{1,17},{2,18},{3,19},{4,20},{5,21},{6,22},{7,23},{8,24},{9,... | collective-permute-start | bytes 122888 | tf_op jit(solution)/shard_map/ppermute | solution.py:449
  7.5 7.7 %collective-permute-start.2 = (bf16[1,32,640]{2,1,0:T(8,128)(2,1)S(1)}, bf16[1,32,640]{2,1,0:T(8,128)(2,1)S(1)}, u32[]{:S(2)}, u32[]{:S(2)}) collective-permute-start(bf16[1,32,640]{2,1,0:T(8,128)(2,1)S(1)} %get-tuple-element.358), channel_id=1, source_target_pairs={{0,8},{1,9},{2,10},{3,11},{4,12},{5,13},{6,14},{7,15},{8,0},{9,1},... | collective-permute-start | bytes 122888 | tf_op jit(solution)/shard_map/ppermute | solution.py:449
  9.1 9.7 %collective-permute-start.12 = (bf16[1,16,3072]{2,1,0:T(8,128)(2,1)S(1)}, bf16[1,16,3072]{2,1,0:T(8,128)(2,1)S(1)}, u32[]{:S(2)}, u32[]{:S(2)}) collective-permute-start(bf16[1,16,3072]{2,1,0:T(8,128)(2,1)S(1)} %get-tuple-element.348), channel_id=1, source_target_pairs={{0,2},{1,3},{2,0},{3,1},{4,6},{5,7},{6,4},{7,5},{8,10},{9,11},{10,... | collective-permute-start | bytes 294920 | tf_op jit(solution)/shard_map/ppermute | solution.py:449
  10.8 109.7 %collective-permute-start.18 = (bf16[256,1024]{1,0:T(8,128)(2,1)}, bf16[256,1024]{1,0:T(8,128)(2,1)}, u32[]{:S(2)}, u32[]{:S(2)}) collective-permute-start(bf16[256,1024]{1,0:T(8,128)(2,1)} %bitcast.358), channel_id=1, source_target_pairs={{0,1},{1,0},{2,3},{3,2},{4,5},{5,4},{6,7},{7,6},{8,9},{9,8},{10,11... | collective-permute-start | bytes 1572872 | tf_op jit(solution)/shard_map/ppermute | solution.py:449
  13.6 30.4 %copy-start.95 = (f32[256]{0:T(256)}, f32[256]{0:T(256)S(1)}, u32[]{:S(2)}) copy-start(f32[256]{0:T(256)S(1)} %broadcast_multiply_fusion.2) | copy-start | bytes 3076
  14.9 94.1 %copy-start.30 = (bf16[48,128]{1,0:T(8,128)(2,1)}, bf16[48,128]{1,0:T(8,128)(2,1)S(1)}, u32[]{:S(2)}) copy-start(bf16[48,128]{1,0:T(8,128)(2,1)S(1)} %fusion.55.refs_2_) | copy-start | bytes 36868
  15.2 43.1 %copy-start.39 = (bf16[1024,256]{1,0:T(8,128)(2,1)}, bf16[1024,256]{1,0:T(8,128)(2,1)S(1)}, u32[]{:S(2)}) copy-start(bf16[1024,256]{1,0:T(8,128)(2,1)S(1)} %copy.310) | copy-start | bytes 1572868
  15.3 8.0 %collective-permute-start.3 = (bf16[4,32,640]{2,1,0:T(8,128)(2,1)S(1)}, bf16[4,32,640]{2,1,0:T(8,128)(2,1)S(1)}, u32[]{:S(2)}, u32[]{:S(2)}) collective-permute-start(bf16[4,32,640]{2,1,0:T(8,128)(2,1)S(1)} %bitcast.442), channel_id=1, source_target_pairs={{0,6},{1,7},{2,4},{3,5},{4,2},{5,3},{6,0},{7,1},{8,14},{9,15},{10,... | collective-permute-start | bytes 491528 | tf_op jit(solution)/shard_map/ppermute | solution.py:449
  16.9 9.5 %collective-permute-start.4 = (bf16[4,32,640]{2,1,0:T(8,128)(2,1)S(1)}, bf16[4,32,640]{2,1,0:T(8,128)(2,1)S(1)}, u32[]{:S(2)}, u32[]{:S(2)}) collective-permute-start(bf16[4,32,640]{2,1,0:T(8,128)(2,1)S(1)} %bitcast.443), channel_id=1, source_target_pairs={{0,4},{1,5},{2,6},{3,7},{4,0},{5,1},{6,2},{7,3},{8,12},{9,13},{10,... | collective-permute-start | bytes 491528 | tf_op jit(solution)/shard_map/ppermute | solution.py:449
  17.2 10.0 %collective-permute-start.5 = (bf16[4,32,640]{2,1,0:T(8,128)(2,1)S(1)}, bf16[4,32,640]{2,1,0:T(8,128)(2,1)S(1)}, u32[]{:S(2)}, u32[]{:S(2)}) collective-permute-start(bf16[4,32,640]{2,1,0:T(8,128)(2,1)S(1)} %bitcast.444), channel_id=1, source_target_pairs={{0,2},{1,3},{2,0},{3,1},{4,6},{5,7},{6,4},{7,5},{8,10},{9,11},{10,... | collective-permute-start | bytes 491528 | tf_op jit(solution)/shard_map/ppermute | solution.py:449
  18.9 16.9 %collective-permute-start.7 = (bf16[1,32,3072]{2,1,0:T(8,128)(2,1)S(1)}, bf16[1,32,3072]{2,1,0:T(8,128)(2,1)S(1)}, u32[]{:S(2)}, u32[]{:S(2)}) collective-permute-start(bf16[1,32,3072]{2,1,0:T(8,128)(2,1)S(1)} %get-tuple-element.97), channel_id=1, source_target_pairs={{0,16},{1,17},{2,18},{3,19},{4,20},{5,21},{6,22},{7,23},{8,24},{9,... | collective-permute-start | bytes 589832 | tf_op jit(solution)/shard_map/ppermute | solution.py:449
  23.3 15.8 %collective-permute-start.8 = (bf16[1,96,1024]{2,1,0:T(8,128)(2,1)S(1)}, bf16[1,96,1024]{2,1,0:T(8,128)(2,1)}, u32[]{:S(2)}, u32[]{:S(2)}) collective-permute-start(bf16[1,96,1024]{2,1,0:T(8,128)(2,1)S(1)} %get-tuple-element.98), channel_id=1, source_target_pairs={{0,16},{1,17},{2,18},{3,19},{4,20},{5,21},{6,22},{7,23},{8,24},{9,... | collective-permute-start | bytes 589832 | tf_op jit(solution)/shard_map/ppermute | solution.py:449
  26.4 41.3 %collective-permute-start.13 = (bf16[2,16,3072]{2,1,0:T(8,128)(2,1)}, bf16[2,16,3072]{2,1,0:T(8,128)(2,1)}, u32[]{:S(2)}, u32[]{:S(2)}) collective-permute-start(bf16[2,16,3072]{2,1,0:T(8,128)(2,1)} %maximum_select_fusion.17), channel_id=1, source_target_pairs={{0,4},{1,5},{2,6},{3,7},{4,0},{5,1},{6,2},{7,3},{8,12},{9,13},{10,... | collective-permute-start | bytes 589832 | tf_op jit(solution)/shard_map/ppermute | solution.py:449
  27.4 16.2 %collective-permute-start.6 = (bf16[16,32,640]{2,1,0:T(8,128)(2,1)S(1)}, bf16[16,32,640]{2,1,0:T(8,128)(2,1)S(1)}, u32[]{:S(2)}, u32[]{:S(2)}) collective-permute-start(bf16[16,32,640]{2,1,0:T(8,128)(2,1)S(1)} %bitcast.361), channel_id=1, source_target_pairs={{0,1},{1,0},{2,3},{3,2},{4,5},{5,4},{6,7},{7,6},{8,9},{9,8},{10,11... | collective-permute-start | bytes 1966088 | tf_op jit(solution)/shard_map/ppermute | solution.py:449
  36.5 31.2 %collective-permute-start.9 = (bf16[2,32,3072]{2,1,0:T(8,128)(2,1)}, bf16[2,32,3072]{2,1,0:T(8,128)(2,1)}, u32[]{:S(2)}, u32[]{:S(2)}) collective-permute-start(bf16[2,32,3072]{2,1,0:T(8,128)(2,1)} %maximum_select_fusion.11), channel_id=1, source_target_pairs={{0,8},{1,9},{2,10},{3,11},{4,12},{5,13},{6,14},{7,15},{8,0},{9,1},... | collective-permute-start | bytes 1179656 | tf_op jit(solution)/shard_map/ppermute | solution.py:449
  40.9 26.8 %collective-permute-start.11 = (bf16[2,96,1024]{2,1,0:T(8,128)(2,1)}, bf16[2,96,1024]{2,1,0:T(8,128)(2,1)}, u32[]{:S(2)}, u32[]{:S(2)}) collective-permute-start(bf16[2,96,1024]{2,1,0:T(8,128)(2,1)} %maximum_select_fusion.12), channel_id=1, source_target_pairs={{0,8},{1,9},{2,10},{3,11},{4,12},{5,13},{6,14},{7,15},{8,0},{9,1},... | collective-permute-start | bytes 1179656 | tf_op jit(solution)/shard_map/ppermute | solution.py:449
  44.9 75.6 %collective-permute-start.17 = (bf16[16,32,256]{2,1,0:T(8,128)(2,1)}, bf16[16,32,256]{2,1,0:T(8,128)(2,1)S(1)}, u32[]{:S(2)}, u32[]{:S(2)}) collective-permute-start(bf16[16,32,256]{2,1,0:T(8,128)(2,1)} %add_convert_fusion.1), channel_id=1, source_target_pairs={{0,1},{1,0},{2,3},{3,2},{4,5},{5,4},{6,7},{7,6},{8,9},{9,8},{10,11... | collective-permute-start | bytes 786440 | tf_op jit(solution)/shard_map/ppermute | solution.py:449
  47.4 18.4 %all-to-all-start = ((bf16[16,32,256]{2,1,0:T(8,128)(2,1)}), bf16[16,32,256]{2,1,0:T(8,128)(2,1)S(1)}, u32[]{:S(2)}, u32[]{:S(2)}) async-start(bf16[16,32,256]{2,1,0:T(8,128)(2,1)} %bitcast.30), calls=%async_computation | async-start | bytes 524288 | tf_op jit(solution)/shard_map/all_to_all | solution.py:864
  64.5 56.0 %copy-start.6 = (bf16[256,1024]{1,0:T(8,128)(2,1)}, bf16[256,1024]{1,0:T(8,128)(2,1)S(1)}, u32[]{:S(2)}) copy-start(bf16[256,1024]{1,0:T(8,128)(2,1)S(1)} %copy.336.refs_11_.normed) | copy-start | bytes 1572868
  65.7 43.3 %copy-start.27 = (f32[32,1024]{1,0:T(8,128)}, f32[32,1024]{1,0:T(8,128)S(1)}, u32[]{:S(2)}) copy-start(f32[32,1024]{1,0:T(8,128)S(1)} %pad_maximum_fusion.7.refs_6_.refs_7_) | copy-start | bytes 393220
  65.7 43.2 %copy-start.18 = (f32[2,32,1024]{2,1,0:T(8,128)}, f32[2,32,1024]{2,1,0:T(8,128)S(1)}, u32[]{:S(2)}) copy-start(f32[2,32,1024]{2,1,0:T(8,128)S(1)} %pad_maximum_fusion.5.refs_5_.refs_6_) | copy-start | bytes 786436
  67.7 41.3 %copy-start.21 = (bf16[32,32,128]{2,1,0:T(8,128)(2,1)}, bf16[32,32,128]{2,1,0:T(8,128)(2,1)S(1)}, u32[]{:S(2)}) copy-start(bf16[32,32,128]{2,1,0:T(8,128)(2,1)S(1)} %reshape.1732.refs_3_) | copy-start | bytes 786436
  69.1 20.6 %collective-permute-start.15 = (bf16[4,16,3072]{2,1,0:T(8,128)(2,1)S(1)}, bf16[4,16,3072]{2,1,0:T(8,128)(2,1)S(1)}, u32[]{:S(2)}, u32[]{:S(2)}) collective-permute-start(bf16[4,16,3072]{2,1,0:T(8,128)(2,1)S(1)} %bitcast.365), channel_id=1, source_target_pairs={{0,16},{1,17},{2,18},{3,19},{4,20},{5,21},{6,22},{7,23},{8,24},{9,... | collective-permute-start | bytes 1179656 | tf_op jit(solution)/shard_map/ppermute | solution.py:449
  73.4 19.1 %collective-permute-start.14 = (bf16[4,96,1024]{2,1,0:T(8,128)(2,1)S(1)}, bf16[4,96,1024]{2,1,0:T(8,128)(2,1)S(1)}, u32[]{:S(2)}, u32[]{:S(2)}) collective-permute-start(bf16[4,96,1024]{2,1,0:T(8,128)(2,1)S(1)} %bitcast.374), channel_id=1, source_target_pairs={{0,4},{1,5},{2,6},{3,7},{4,0},{5,1},{6,2},{7,3},{8,12},{9,13},{10,... | collective-permute-start | bytes 2359304 | tf_op jit(solution)/shard_map/ppermute | solution.py:449
  76.2 18.9 %collective-permute-start.10 = (bf16[4,32,3072]{2,1,0:T(8,128)(2,1)S(1)}, bf16[4,32,3072]{2,1,0:T(8,128)(2,1)S(1)}, u32[]{:S(2)}, u32[]{:S(2)}) collective-permute-start(bf16[4,32,3072]{2,1,0:T(8,128)(2,1)S(1)} %bitcast.348), channel_id=1, source_target_pairs={{0,2},{1,3},{2,0},{3,1},{4,6},{5,7},{6,4},{7,5},{8,10},{9,11},{10,... | collective-permute-start | bytes 2359304 | tf_op jit(solution)/shard_map/ppermute | solution.py:449
  89.8 30.4 %collective-permute-start.16 = (bf16[8,16,3072]{2,1,0:T(8,128)(2,1)S(1)}, bf16[8,16,3072]{2,1,0:T(8,128)(2,1)S(1)}, u32[]{:S(2)}, u32[]{:S(2)}) collective-permute-start(bf16[8,16,3072]{2,1,0:T(8,128)(2,1)S(1)} %bitcast.392), channel_id=1, source_target_pairs={{0,8},{1,9},{2,10},{3,11},{4,12},{5,13},{6,14},{7,15},{8,0},{9,1},... | collective-permute-start | bytes 2359304 | tf_op jit(solution)/shard_map/ppermute | solution.py:449
  95.4 37.1 %collective-permute-start.22 = (bf16[8,96,1024]{2,1,0:T(8,128)(2,1)S(1)}, bf16[8,96,1024]{2,1,0:T(8,128)(2,1)}, u32[]{:S(2)}, u32[]{:S(2)}) collective-permute-start(bf16[8,96,1024]{2,1,0:T(8,128)(2,1)S(1)} %bitcast.355), channel_id=1, source_target_pairs={{0,2},{1,3},{2,0},{3,1},{4,6},{5,7},{6,4},{7,5},{8,10},{9,11},{10,... | collective-permute-start | bytes 4718600 | tf_op jit(solution)/shard_map/ppermute | solution.py:449
  97.0 40.3 %collective-permute-start.19 = (bf16[8,32,3072]{2,1,0:T(8,128)(2,1)S(1)}, bf16[8,32,3072]{2,1,0:T(8,128)(2,1)}, u32[]{:S(2)}, u32[]{:S(2)}) collective-permute-start(bf16[8,32,3072]{2,1,0:T(8,128)(2,1)S(1)} %bitcast.386), channel_id=1, source_target_pairs={{0,4},{1,5},{2,6},{3,7},{4,0},{5,1},{6,2},{7,3},{8,12},{9,13},{10,... | collective-permute-start | bytes 4718600 | tf_op jit(solution)/shard_map/ppermute | solution.py:449
  120.5 21.6 %copy-start = (bf16[2,2,4,16,3072]{4,3,2,1,0:T(8,128)(2,1)}, bf16[2,2,4,16,3072]{4,3,2,1,0:T(8,128)(2,1)S(1)}, u32[]{:S(2)}) copy-start(bf16[2,2,4,16,3072]{4,3,2,1,0:T(8,128)(2,1)S(1)} %maximum_select_fusion.4) | copy-start | bytes 4718596
  137.3 21.5 %collective-permute-start.23 = (bf16[16,96,1024]{2,1,0:T(8,128)(2,1)}, bf16[16,96,1024]{2,1,0:T(8,128)(2,1)}, u32[]{:S(2)}, u32[]{:S(2)}) collective-permute-start(bf16[16,96,1024]{2,1,0:T(8,128)(2,1)} %bitcast.78.refs_0_), channel_id=1, source_target_pairs={{0,1},{1,0},{2,3},{3,2},{4,5},{5,4},{6,7},{7,6},{8,9},{9,8},{10,11... | collective-permute-start | bytes 9437192 | tf_op jit(solution)/shard_map/ppermute | solution.py:449
  141.6 17.2 %copy-start.1 = (bf16[1,256,1024]{2,1,0:T(8,128)(2,1)S(1)}, bf16[1,256,1024]{2,1,0:T(8,128)(2,1)}, u32[]{:S(2)}) copy-start(bf16[1,256,1024]{2,1,0:T(8,128)(2,1)} %param.24) | copy-start | bytes 1572868
  141.6 17.2 %collective-permute-start.20 = (bf16[16,32,3072]{2,1,0:T(8,128)(2,1)}, bf16[16,32,3072]{2,1,0:T(8,128)(2,1)}, u32[]{:S(2)}, u32[]{:S(2)}) collective-permute-start(bf16[16,32,3072]{2,1,0:T(8,128)(2,1)} %bitcast.72), channel_id=1, source_target_pairs={{0,1},{1,0},{2,3},{3,2},{4,5},{5,4},{6,7},{7,6},{8,9},{9,8},{10,11... | collective-permute-start | bytes 9437192 | tf_op jit(solution)/shard_map/ppermute | solution.py:449
  142.1 16.7 %collective-permute-start.21 = (bf16[16,16,3072]{2,1,0:T(8,128)(2,1)S(1)}, bf16[16,16,3072]{2,1,0:T(8,128)(2,1)}, u32[]{:S(2)}, u32[]{:S(2)}) collective-permute-start(bf16[16,16,3072]{2,1,0:T(8,128)(2,1)S(1)} %bitcast.353), channel_id=1, source_target_pairs={{0,1},{1,0},{2,3},{3,2},{4,5},{5,4},{6,7},{7,6},{8,9},{9,8},{10,11... | collective-permute-start | bytes 4718600 | tf_op jit(solution)/shard_map/ppermute | solution.py:449
  142.9 15.8 %copy-start.7 = (bf16[256,1024]{1,0:T(8,128)(2,1)S(1)}, bf16[256,1024]{1,0:T(8,128)(2,1)}, u32[]{:S(2)}) copy-start(bf16[256,1024]{1,0:T(8,128)(2,1)} %copy-done.6) | copy-start | bytes 1572868
  158.7 13.6 %copy-start.2 = (bf16[16,1,1,16,256]{4,3,1,0,2:T(8,128)(2,1)}, bf16[16,1,1,16,256]{4,3,1,0,2:T(8,128)(2,1)S(1)}, u32[]{:S(2)}) copy-start(bf16[16,1,1,16,256]{4,3,1,0,2:T(8,128)(2,1)S(1)} %get-tuple-element.347) | copy-start | bytes 393220
  172.3 2.7 collective-permute-start.24
  172.4 31.6 %collective-permute-start.27 = (bf16[256,3072]{1,0:T(8,128)(2,1)}, bf16[256,3072]{1,0:T(8,128)(2,1)}, u32[]{:S(2)}, u32[]{:S(2)}) collective-permute-start(bf16[256,3072]{1,0:T(8,128)(2,1)} %get-tuple-element.135.own), channel_id=1, source_target_pairs={{0,1},{1,0},{2,3},{3,2},{4,5},{5,4},{6,7},{7,6},{8,9},{9,8},{10,11... | collective-permute-start | bytes 4718600 | tf_op jit(solution)/shard_map/ppermute | solution.py:449
  175.0 33.5 %collective-permute-start.25 = (bf16[256,3072]{1,0:T(8,128)(2,1)}, bf16[256,3072]{1,0:T(8,128)(2,1)}, u32[]{:S(2)}, u32[]{:S(2)}) collective-permute-start(bf16[256,3072]{1,0:T(8,128)(2,1)} %get-tuple-element.158.own), channel_id=1, source_target_pairs={{0,1},{1,0},{2,3},{3,2},{4,5},{5,4},{6,7},{7,6},{8,9},{9,8},{10,11... | collective-permute-start | bytes 4718600 | tf_op jit(solution)/shard_map/ppermute | solution.py:449
  179.9 15.1 %all-to-all-start.2 = ((bf16[16,32,256]{2,1,0:T(8,128)(2,1)}), bf16[16,32,256]{2,1,0:T(8,128)(2,1)}, u32[]{:S(2)}, u32[]{:S(2)}) async-start(bf16[16,32,256]{2,1,0:T(8,128)(2,1)} %bitcast.81), calls=%async_computation.2 | async-start | bytes 524288 | tf_op jit(solution)/shard_map/all_to_all | solution.py:931
  190.3 13.7 %collective-permute-start.26 = (bf16[16,16,256]{2,1,0:T(8,128)(2,1)}, bf16[16,16,256]{2,1,0:T(8,128)(2,1)}, u32[]{:S(2)}, u32[]{:S(2)}) collective-permute-start(bf16[16,16,256]{2,1,0:T(8,128)(2,1)} %bitcast.93), channel_id=1, source_target_pairs={{0,1},{1,0},{2,3},{3,2},{4,5},{5,4},{6,7},{7,6},{8,9},{9,8},{10,11... | collective-permute-start | bytes 393224 | tf_op jit(solution)/shard_map/ppermute | solution.py:449
  203.2 45.1 %collective-permute-start.30 = (bf16[8,96,1024]{2,1,0:T(8,128)(2,1)S(1)}, bf16[8,96,1024]{2,1,0:T(8,128)(2,1)}, u32[]{:S(2)}, u32[]{:S(2)}) collective-permute-start(bf16[8,96,1024]{2,1,0:T(8,128)(2,1)S(1)} %bitcast.394), channel_id=1, source_target_pairs={{0,2},{1,3},{2,0},{3,1},{4,6},{5,7},{6,4},{7,5},{8,10},{9,11},{10,... | collective-permute-start | bytes 4718600 | tf_op jit(solution)/shard_map/ppermute | solution.py:449
  207.6 28.4 %collective-permute-start.28 = (bf16[8,16,3072]{2,1,0:T(8,128)(2,1)S(1)}, bf16[8,16,3072]{2,1,0:T(8,128)(2,1)S(1)}, u32[]{:S(2)}, u32[]{:S(2)}) collective-permute-start(bf16[8,16,3072]{2,1,0:T(8,128)(2,1)S(1)} %bitcast.398), channel_id=1, source_target_pairs={{0,8},{1,9},{2,10},{3,11},{4,12},{5,13},{6,14},{7,15},{8,0},{9,1},... | collective-permute-start | bytes 2359304 | tf_op jit(solution)/shard_map/ppermute | solution.py:449
  213.8 42.5 %collective-permute-start.29 = (bf16[8,32,3072]{2,1,0:T(8,128)(2,1)S(1)}, bf16[8,32,3072]{2,1,0:T(8,128)(2,1)}, u32[]{:S(2)}, u32[]{:S(2)}) collective-permute-start(bf16[8,32,3072]{2,1,0:T(8,128)(2,1)S(1)} %bitcast.396), channel_id=1, source_target_pairs={{0,4},{1,5},{2,6},{3,7},{4,0},{5,1},{6,2},{7,3},{8,12},{9,13},{10,... | collective-permute-start | bytes 4718600 | tf_op jit(solution)/shard_map/ppermute | solution.py:449
  236.3 19.2 %collective-permute-start.31 = (bf16[4,16,3072]{2,1,0:T(8,128)(2,1)S(1)}, bf16[4,16,3072]{2,1,0:T(8,128)(2,1)S(1)}, u32[]{:S(2)}, u32[]{:S(2)}) collective-permute-start(bf16[4,16,3072]{2,1,0:T(8,128)(2,1)S(1)} %fusion.27.refs_11_), channel_id=1, source_target_pairs={{0,16},{1,17},{2,18},{3,19},{4,20},{5,21},{6,22},{7,23},{8,24},{9,... | collective-permute-start | bytes 1179656 | tf_op jit(solution)/shard_map/ppermute | solution.py:449
  251.5 20.5 %collective-permute-start.33 = (bf16[4,96,1024]{2,1,0:T(8,128)(2,1)S(1)}, bf16[4,96,1024]{2,1,0:T(8,128)(2,1)S(1)}, u32[]{:S(2)}, u32[]{:S(2)}) collective-permute-start(bf16[4,96,1024]{2,1,0:T(8,128)(2,1)S(1)} %fusion.10.refs_12_), channel_id=1, source_target_pairs={{0,4},{1,5},{2,6},{3,7},{4,0},{5,1},{6,2},{7,3},{8,12},{9,13},{10,... | collective-permute-start | bytes 2359304 | tf_op jit(solution)/shard_map/ppermute | solution.py:449
  255.5 19.7 %collective-permute-start.43 = (bf16[2,16,3072]{2,1,0:T(8,128)(2,1)S(1)}, bf16[2,16,3072]{2,1,0:T(8,128)(2,1)S(1)}, u32[]{:S(2)}, u32[]{:S(2)}) collective-permute-start(bf16[2,16,3072]{2,1,0:T(8,128)(2,1)S(1)} %fusion.38.refs_13_), channel_id=1, source_target_pairs={{0,4},{1,5},{2,6},{3,7},{4,0},{5,1},{6,2},{7,3},{8,12},{9,13},{10,... | collective-permute-start | bytes 589832 | tf_op jit(solution)/shard_map/ppermute | solution.py:449
  258.3 19.0 %collective-permute-start.32 = (bf16[4,32,3072]{2,1,0:T(8,128)(2,1)S(1)}, bf16[4,32,3072]{2,1,0:T(8,128)(2,1)}, u32[]{:S(2)}, u32[]{:S(2)}) collective-permute-start(bf16[4,32,3072]{2,1,0:T(8,128)(2,1)S(1)} %fusion.9.refs_11_), channel_id=1, source_target_pairs={{0,2},{1,3},{2,0},{3,1},{4,6},{5,7},{6,4},{7,5},{8,10},{9,11},{10,... | collective-permute-start | bytes 2359304 | tf_op jit(solution)/shard_map/ppermute | solution.py:449
  270.9 4.4 %collective-permute-start.47 = (f32[2,32,512]{2,1,0:T(8,128)S(1)}, f32[2,32,512]{2,1,0:T(8,128)S(1)}, u32[]{:S(2)}, u32[]{:S(2)}) collective-permute-start(f32[2,32,512]{2,1,0:T(8,128)S(1)} %pad_maximum_fusion.8), channel_id=1, source_target_pairs={{0,1},{1,0},{2,3},{3,2},{4,5},{5,4},{6,7},{7,6},{8,9},{9,8},{10,11... | collective-permute-start | bytes 393224 | tf_op jit(solution)/shard_map/ppermute | solution.py:449
  274.7 32.3 %collective-permute-start.45 = (bf16[2,96,1024]{2,1,0:T(8,128)(2,1)}, bf16[2,96,1024]{2,1,0:T(8,128)(2,1)}, u32[]{:S(2)}, u32[]{:S(2)}) collective-permute-start(bf16[2,96,1024]{2,1,0:T(8,128)(2,1)} %fusion.29), channel_id=1, source_target_pairs={{0,8},{1,9},{2,10},{3,11},{4,12},{5,13},{6,14},{7,15},{8,0},{9,1},... | collective-permute-start | bytes 1179656 | tf_op jit(solution)/shard_map/ppermute | solution.py:449
  282.3 13.6 %all-to-all-start.3 = ((bf16[32,16,256]{2,0,1:T(8,128)(2,1)}), bf16[32,16,256]{2,0,1:T(8,128)(2,1)S(1)}, u32[]{:S(2)}, u32[]{:S(2)}) async-start(bf16[32,16,256]{2,0,1:T(8,128)(2,1)} %copy.345), calls=%async_computation.3 | async-start | bytes 524288 | tf_op jit(solution)/shard_map/all_to_all | solution.py:977
  290.5 26.2 %collective-permute-start.35 = (bf16[2,32,3072]{2,1,0:T(8,128)(2,1)}, bf16[2,32,3072]{2,1,0:T(8,128)(2,1)}, u32[]{:S(2)}, u32[]{:S(2)}) collective-permute-start(bf16[2,32,3072]{2,1,0:T(8,128)(2,1)} %fusion.28), channel_id=1, source_target_pairs={{0,8},{1,9},{2,10},{3,11},{4,12},{5,13},{6,14},{7,15},{8,0},{9,1},... | collective-permute-start | bytes 1179656 | tf_op jit(solution)/shard_map/ppermute | solution.py:449
  303.3 2.1 collective-permute-start.34
  303.4 12.6 %collective-permute-start.44 = (bf16[1,16,3072]{2,1,0:T(8,128)(2,1)S(1)}, bf16[1,16,3072]{2,1,0:T(8,128)(2,1)S(1)}, u32[]{:S(2)}, u32[]{:S(2)}) collective-permute-start(bf16[1,16,3072]{2,1,0:T(8,128)(2,1)S(1)} %dynamic-slice_convert_fusion.5), channel_id=1, source_target_pairs={{0,2},{1,3},{2,0},{3,1},{4,6},{5,7},{6,4},{7,5},{8,10},{9,11},{10,... | collective-permute-start | bytes 294920 | tf_op jit(solution)/shard_map/ppermute | solution.py:449
  309.2 25.8 %collective-permute-start.46 = (bf16[1,96,1024]{2,1,0:T(8,128)(2,1)}, bf16[1,96,1024]{2,1,0:T(8,128)(2,1)}, u32[]{:S(2)}, u32[]{:S(2)}) collective-permute-start(bf16[1,96,1024]{2,1,0:T(8,128)(2,1)} %dynamic-slice_convert_fusion.1), channel_id=1, source_target_pairs={{0,16},{1,17},{2,18},{3,19},{4,20},{5,21},{6,22},{7,23},{8,24},{9,... | collective-permute-start | bytes 589832 | tf_op jit(solution)/shard_map/ppermute | solution.py:449
  312.3 16.8 %collective-permute-start.38 = (bf16[4,32,640]{2,1,0:T(8,128)(2,1)}, bf16[4,32,640]{2,1,0:T(8,128)(2,1)}, u32[]{:S(2)}, u32[]{:S(2)}) collective-permute-start(bf16[4,32,640]{2,1,0:T(8,128)(2,1)} %get-tuple-element.340), channel_id=1, source_target_pairs={{0,2},{1,3},{2,0},{3,1},{4,6},{5,7},{6,4},{7,5},{8,10},{9,11},{10,... | collective-permute-start | bytes 491528 | tf_op jit(solution)/shard_map/ppermute | solution.py:449
  313.8 15.4 %collective-permute-start.39 = (bf16[4,32,640]{2,1,0:T(8,128)(2,1)}, bf16[4,32,640]{2,1,0:T(8,128)(2,1)}, u32[]{:S(2)}, u32[]{:S(2)}) collective-permute-start(bf16[4,32,640]{2,1,0:T(8,128)(2,1)} %get-tuple-element.341), channel_id=1, source_target_pairs={{0,6},{1,7},{2,4},{3,5},{4,2},{5,3},{6,0},{7,1},{8,14},{9,15},{10,... | collective-permute-start | bytes 491528 | tf_op jit(solution)/shard_map/ppermute | solution.py:449
  316.1 13.1 %collective-permute-start.37 = (bf16[4,32,640]{2,1,0:T(8,128)(2,1)}, bf16[4,32,640]{2,1,0:T(8,128)(2,1)}, u32[]{:S(2)}, u32[]{:S(2)}) collective-permute-start(bf16[4,32,640]{2,1,0:T(8,128)(2,1)} %fusion.40), channel_id=1, source_target_pairs={{0,4},{1,5},{2,6},{3,7},{4,0},{5,1},{6,2},{7,3},{8,12},{9,13},{10,... | collective-permute-start | bytes 491528 | tf_op jit(solution)/shard_map/ppermute | solution.py:449
  318.5 16.4 %collective-permute-start.36 = (bf16[1,32,3072]{2,1,0:T(8,128)(2,1)}, bf16[1,32,3072]{2,1,0:T(8,128)(2,1)}, u32[]{:S(2)}, u32[]{:S(2)}) collective-permute-start(bf16[1,32,3072]{2,1,0:T(8,128)(2,1)} %dynamic-slice_convert_fusion.2), channel_id=1, source_target_pairs={{0,16},{1,17},{2,18},{3,19},{4,20},{5,21},{6,22},{7,23},{8,24},{9,... | collective-permute-start | bytes 589832 | tf_op jit(solution)/shard_map/ppermute | solution.py:449
  330.5 9.0 %collective-permute-start.40 = (f32[1,32,640]{2,1,0:T(8,128)S(1)}, f32[1,32,640]{2,1,0:T(8,128)S(1)}, u32[]{:S(2)}, u32[]{:S(2)}) collective-permute-start(f32[1,32,640]{2,1,0:T(8,128)S(1)} %get-tuple-element.339), channel_id=1, source_target_pairs={{0,16},{1,17},{2,18},{3,19},{4,20},{5,21},{6,22},{7,23},{8,24},{9,... | collective-permute-start | bytes 245768 | tf_op jit(solution)/shard_map/ppermute | solution.py:449
  332.9 6.5 %collective-permute-start.41 = (f32[1,32,640]{2,1,0:T(8,128)S(1)}, f32[1,32,640]{2,1,0:T(8,128)S(1)}, u32[]{:S(2)}, u32[]{:S(2)}) collective-permute-start(f32[1,32,640]{2,1,0:T(8,128)S(1)} %get-tuple-element.337), channel_id=1, source_target_pairs={{0,8},{1,9},{2,10},{3,11},{4,12},{5,13},{6,14},{7,15},{8,0},{9,1},... | collective-permute-start | bytes 245768 | tf_op jit(solution)/shard_map/ppermute | solution.py:449
  333.4 6.3 %collective-permute-start.42 = (f32[1,32,640]{2,1,0:T(8,128)S(1)}, f32[1,32,640]{2,1,0:T(8,128)S(1)}, u32[]{:S(2)}, u32[]{:S(2)}) collective-permute-start(f32[1,32,640]{2,1,0:T(8,128)S(1)} %get-tuple-element.338), channel_id=1, source_target_pairs={{0,24},{1,25},{2,26},{3,27},{4,28},{5,29},{6,30},{7,31},{8,16},{9,... | collective-permute-start | bytes 245768 | tf_op jit(solution)/shard_map/ppermute | solution.py:449
  (90 other events, 415.8 us)

commit v3 on v2

--- a/solution.py
+++ b/solution.py
@@ -21,8 +21,9 @@
     return jax.nn.gelu(values, approximate=True)
 
 
-def pieces_of(lengths_row, length):
+def pieces_of(lengths_row, length, shares):
     blocks = length // BLOCK
+    each = blocks // shares
     items = lengths_row.shape[0]
     ends = jnp.cumsum(lengths_row, dtype=jnp.int32)
     heads = BLOCK * jnp.arange(blocks, dtype=jnp.int32)
@@ -41,7 +42,9 @@
     segment = jnp.sum((ends[None, :] <= starts[:, None]).astype(jnp.int32), axis=1)
     positions = owner[:, None] * BLOCK + jnp.arange(BLOCK, dtype=jnp.int32)[None, :]
     mask = (positions >= starts[:, None]) & (positions < stops[:, None])
-    pick = owner[:, None] == jnp.arange(blocks, dtype=jnp.int32)[None, :]
+    heads = each * jnp.arange(shares, dtype=jnp.int32)[None, None, :]
+    heads = heads + jnp.arange(each, dtype=jnp.int32)[:, None, None]
+    pick = owner[None, :, None] == heads
     follows = (segment[1:] == segment[:-1]) & (owner[1:] != owner[:-1])
     follows = jnp.concatenate([jnp.zeros((1,), bool), follows])
     return (
@@ -143,21 +146,35 @@
         ref[half * count + k, rows, :] = block[:, 128 * k : 128 * (k + 1)]
 
 
+def gather_rows(pick, ref, c, mask):
+    rows = [nn(p, ref[c, :, BLOCK * h : BLOCK * (h + 1)]) for h, p in enumerate(pick)]
+    return sum(rows).astype(jnp.bfloat16) * mask
+
+
+def scatter_rows(pick, ref, c, result, mask):
+    low = result.astype(jnp.bfloat16) * mask
+    for h, p in enumerate(pick):
+        ref[c, :, BLOCK * h : BLOCK * (h + 1)] = tn(p, low).astype(jnp.bfloat16)
+
+
 def forward_kernel(
     active, follows_ref, pick_ref, mask_ref, values_ref, low_ref, lam_ref, coef_ref,
     out_ref, start_ref, taps_ref, token_ref, up_ref, down_ref, work_ref,
 ):
     token_ref[...] = jnp.zeros_like(token_ref)
-    places = pick_ref.shape[0]
+    places = pick_ref.shape[1]
     group, states = coef_ref.shape[0], coef_ref.shape[1] // 2
     if active < group:
         work_ref[...] = jnp.zeros_like(work_ref)
     mask = mask_ref[...]
-    pick = pick_ref[...]
-    for c in range(active):
+    pick = [pick_ref[h] for h in range(pick_ref.shape[0])]
+    each = range(active)
+    spread = [gather_rows(pick, values_ref, c, mask) for c in each]
+    for c in each:
         fill_tables(c, states, low_ref, up_ref, down_ref)
-        spread = nn(pick, values_ref[c]).astype(jnp.bfloat16) * mask
-        put_rows(work_ref, c, places, group, nn(spread, down_ref[c, 0]) + nn(spread, down_ref[c, 1]))
+    for c in each:
+        ends = nn(spread[c], down_ref[c, 0]) + nn(spread[c], down_ref[c, 1])
+        put_rows(work_ref, c, places, group, ends)
     lam_re, lam_im = lam_ref[0, :, :states], lam_ref[0, :, states:]
     far_re, far_im = lam_ref[1, :, :states], lam_ref[1, :, states:]
     coef_re, coef_im = coef_ref[:, :states], coef_ref[:, states:]
@@ -180,23 +197,24 @@
 
     zero = jnp.zeros((group, states), jnp.float32)
     lax.fori_loop(0, places, advance, (zero, zero), unroll=4)
-    for c in range(active):
+    carried, taps = [], []
+    for c in each:
         row = jnp.concatenate([coef_ref[c : c + 1, :states], -coef_ref[c : c + 1, states:]], axis=1)
         high, rest = split_rows(row)
         rows = jnp.concatenate([high, rest, jnp.zeros((14, 2 * states), jnp.bfloat16)], axis=0)
         mixed = split_rows(get_rows(work_ref, c, places, group))
         stack = jnp.concatenate([mixed[0], rows, mixed[1]], axis=0)
-        carried = nt(stack, up_ref[c, 0])
+        coarse = nt(stack, up_ref[c, 0])
         finer = nt(stack[: places + 16], up_ref[c, 1])
-        carried = jnp.concatenate(
-            [carried[:places] + carried[places + 16 :], carried[places : places + 16]], axis=0
-        ) + finer
-        kernel_row = carried[places : places + 1] + carried[places + 1 : places + 2]
-        taps = split_rows(toeplitz(kernel_row))
-        taps_ref[c] = taps[0]
-        spread = nn(pick, values_ref[c]).astype(jnp.bfloat16) * mask
-        result = (carried[:places] + nn(spread, taps[0]) + nn(spread, taps[1])).astype(jnp.bfloat16) * mask
-        out_ref[c] = tn(pick, result).astype(jnp.bfloat16)
+        carried.append(coarse[:places] + coarse[places + 16 :] + finer[:places])
+        kernel_row = coarse[places : places + 16] + finer[places:]
+        taps.append(split_rows(toeplitz(kernel_row[0:1] + kernel_row[1:2])))
+        taps_ref[c] = taps[c][0]
+    results = [
+        carried[c] + nn(spread[c], taps[c][0]) + nn(spread[c], taps[c][1]) for c in each
+    ]
+    for c in each:
+        scatter_rows(pick, out_ref, c, results[c], mask)
 
 
 def backward_kernel(
@@ -204,26 +222,32 @@
     start_ref, taps_ref, out_ref, sum_ref, token_ref, up_ref, down_ref, work_ref,
 ):
     token_ref[...] = jnp.zeros_like(token_ref)
-    places = pick_ref.shape[0]
+    places = pick_ref.shape[1]
     group, states = coef_ref.shape[0], coef_ref.shape[1] // 2
     if active < group:
         work_ref[...] = jnp.zeros_like(work_ref)
         sum_ref[...] = jnp.zeros_like(sum_ref)
     mask = mask_ref[...]
-    pick = pick_ref[...]
+    pick = [pick_ref[h] for h in range(pick_ref.shape[0])]
     rows = lax.broadcasted_iota(jnp.int32, (BLOCK, BLOCK), 0)
     columns = lax.broadcasted_iota(jnp.int32, (BLOCK, BLOCK), 1)
     turn = (rows + columns == BLOCK - 1).astype(jnp.bfloat16)
-    for c in range(active):
+    each = range(active)
+    values = [gather_rows(pick, values_ref, c, mask) for c in each]
+    grads = [gather_rows(pick, grads_ref, c, mask) for c in each]
+    turned = [nn(values[c], turn).astype(jnp.bfloat16) for c in each]
+    pairs = [tn(turned[c], grads[c]) for c in each]
+    for c in each:
         fill_tables(c, states, low_ref, up_ref, down_ref)
-        values = nn(pick, values_ref[c]).astype(jnp.bfloat16) * mask
-        grads = nn(pick, grads_ref[c]).astype(jnp.bfloat16) * mask
-        pairs = tn(nn(values, turn).astype(jnp.bfloat16), grads)
-        skewed = pltpu.roll(pairs, 1, 1, stride=1, stride_axis=0)
+    stacks = []
+    for c in each:
+        skewed = pltpu.roll(pairs[c], 1, 1, stride=1, stride_axis=0)
         lag_sum = jnp.sum(jnp.where(columns <= rows, skewed, 0.0), axis=0, keepdims=True)
         high, rest = split_rows(lag_sum)
         extra = jnp.concatenate([high, rest, jnp.zeros((14, BLOCK), jnp.bfloat16)], axis=0)
-        folded = nn(jnp.concatenate([grads, extra], axis=0), up_ref[c, 0])
+        stacks.append(jnp.concatenate([grads[c], extra], axis=0))
+    for c in each:
+        folded = nn(stacks[c], up_ref[c, 0])
         put_rows(work_ref, c, places, group, folded[:places])
         sum_ref[c : c + 1, :] = folded[places : places + 1] + folded[places + 1 : places + 2]
     lam_re, lam_im = lam_ref[0, :, :states], lam_ref[0, :, states:]
@@ -253,11 +277,13 @@
     _, _, total_re, total_im = lax.fori_loop(0, places, retreat, (zero, zero, zero, zero), unroll=4)
     sum_ref[:, :states] = sum_ref[:, :states] + total_re
     sum_ref[:, states:] = -(sum_ref[:, states:] + total_im)
-    for c in range(active):
+    near = [nt(grads[c], taps_ref[c]) for c in each]
+    results = []
+    for c in each:
         mixed = get_rows(work_ref, c, places, group).astype(jnp.bfloat16)
-        grads = nn(pick, grads_ref[c]).astype(jnp.bfloat16) * mask
-        result = nt(mixed, down_ref[c, 0]) + nt(grads, taps_ref[c])
-        out_ref[c] = tn(pick, result.astype(jnp.bfloat16) * mask).astype(jnp.bfloat16)
+        results.append(nt(mixed, down_ref[c, 0]) + near[c])
+    for c in each:
+        scatter_rows(pick, out_ref, c, results[c], mask)
 
 
 def whole(shape):
@@ -331,16 +357,16 @@
 
 
 def mix_forward(values, pieces, powers, lams, coefs):
-    channels, blocks = values.shape[0], values.shape[1]
+    channels, shares, width = values.shape
     pick, mask, follows = pieces
-    places, states = pick.shape[0], coefs.shape[1] // 2
+    places, states = pick.shape[1], coefs.shape[1] // 2
     group, active, spare, lams, coefs = padded(values, lams, coefs)
     full = lambda shape: lambda k: whole(shape)
     inputs = [
         (follows, lambda k: pl.BlockSpec(memory_space=pltpu.SMEM)),
-        (pick, full((places, blocks))),
+        (pick, full(pick.shape)),
         (mask, full((places, BLOCK))),
-        (values, lambda k: part((active, blocks, BLOCK), k)),
+        (values, lambda k: part((active, shares, width), k)),
         (powers, lambda k: part((active, 16, 2 * states), k)),
         (lams, lambda k: part((2, group, 2 * states), k, 1)),
         (coefs, lambda k: part((group, 2 * states), k)),
@@ -348,8 +374,8 @@
     f32 = jnp.float32
     results = [
         (
-            jax.ShapeDtypeStruct((channels, blocks, BLOCK), jnp.bfloat16),
-            lambda k: part((active, blocks, BLOCK), k),
+            jax.ShapeDtypeStruct(values.shape, jnp.bfloat16),
+            lambda k: part((active, shares, width), k),
         ),
         (
             jax.ShapeDtypeStruct((places * (channels + spare), 2 * states), f32),
@@ -372,17 +398,17 @@
 
 
 def mix_backward(values, grads, pieces, powers, lams, coefs, starts, taps):
-    channels, blocks = values.shape[0], values.shape[1]
+    channels, shares, width = values.shape
     pick, mask, follows = pieces
-    places, states = pick.shape[0], coefs.shape[1] // 2
+    places, states = pick.shape[1], coefs.shape[1] // 2
     group, active, spare, lams, coefs = padded(values, lams, coefs)
     full = lambda shape: lambda k: whole(shape)
     inputs = [
         (follows, lambda k: pl.BlockSpec(memory_space=pltpu.SMEM)),
-        (pick, full((places, blocks))),
+        (pick, full(pick.shape)),
         (mask, full((places, BLOCK))),
-        (values, lambda k: part((active, blocks, BLOCK), k)),
-        (grads, lambda k: part((active, blocks, BLOCK), k)),
+        (values, lambda k: part((active, shares, width), k)),
+        (grads, lambda k: part((active, shares, width), k)),
         (powers, lambda k: part((active, 16, 2 * states), k)),
         (lams, lambda k: part((2, group, 2 * states), k, 1)),
         (coefs, lambda k: part((group, 2 * states), k)),
@@ -391,8 +417,8 @@
     ]
     results = [
         (
-            jax.ShapeDtypeStruct((channels, blocks, BLOCK), jnp.bfloat16),
-            lambda k: part((active, blocks, BLOCK), k),
+            jax.ShapeDtypeStruct(values.shape, jnp.bfloat16),
+            lambda k: part((active, shares, width), k),
         ),
         (
             jax.ShapeDtypeStruct((channels + spare, 2 * states), jnp.float32),
@@ -569,7 +595,7 @@
 
 def gate_kernel(
     split, core_ref, normed_ref, state_refs, grad_ref, up_refs, expand_refs, down_refs,
-    grad_out, up_out, gated_refs, state_outs, state_scratch, sum_scratch,
+    grad_out, up_out, gated_refs, state_outs, norm_outs, state_scratch, sum_scratch, norm_scratch,
 ):
     step, last = pl.program_id(0), pl.num_programs(0) - 1
     channels = state_refs[0].shape[0]
@@ -581,6 +607,7 @@
             turned = state_refs[k][...].astype(jnp.float32).T
             state_scratch[:, channels * k : channels * (k + 1)] = turned.astype(jnp.bfloat16)
         sum_scratch[...] = jnp.zeros_like(sum_scratch)
+        norm_scratch[...] = jnp.zeros_like(norm_scratch)
 
     def pair(mine, other):
         return jnp.where(swapped, other, mine), jnp.where(swapped, mine, other)
@@ -601,7 +628,8 @@
     upper, slope = gelu_parts(up_pre)
     expanded_grad = (gated_grad * upper).astype(jnp.bfloat16)
     grad_out[...] = expanded_grad
-    up_out[...] = (gated_grad * expanded * slope).astype(jnp.bfloat16)
+    up_pre_grad = (gated_grad * expanded * slope).astype(jnp.bfloat16)
+    up_out[...] = up_pre_grad
     gated = (upper * expanded).T.astype(jnp.bfloat16)
     if split:
         size = gated_refs[0].shape[1]
@@ -615,12 +643,14 @@
         gated_refs[0][...] = gated
     for k in range(2):
         sum_scratch[:, channels * k : channels * (k + 1)] += nt(expanded_grad, expand_refs[k][...])
+        norm_scratch[:, rows * k : rows * (k + 1)] += nt(up_pre_grad, up_refs[k][...])
 
     @pl.when(step == last)
     def _():
         for k in range(2):
             total = sum_scratch[:, channels * k : channels * (k + 1)].T
             state_outs[k][...] = total.astype(jnp.bfloat16)
+            norm_outs[k][...] = norm_scratch[:, rows * k : rows * (k + 1)].T
 
 
 def gate(cube, normed, states, grad_rows, ups, expands, downs):
@@ -646,13 +676,14 @@
     channels = states[0].shape[0]
     row_spec = pl.BlockSpec((tokens, block), lambda i: (0, i))
     state_shape = jax.ShapeDtypeStruct((channels, tokens), low)
+    norm_shape = jax.ShapeDtypeStruct((width // 2, tokens), f32)
 
     def body(core, normed, s0, s1, grad, u0, u1, e0, e1, *refs):
         down_refs, refs = refs[:count], refs[count:]
         grad_out, up_out, gated_refs, refs = refs[0], refs[1], refs[2 : 2 + count], refs[2 + count :]
         gate_kernel(
             split, core, normed, (s0, s1), grad, (u0, u1), (e0, e1), down_refs,
-            grad_out, up_out, gated_refs, refs[:2], refs[2], refs[3],
+            grad_out, up_out, gated_refs, refs[:2], refs[2:4], *refs[4:],
         )
 
     outs = pl.pallas_call(
@@ -664,13 +695,18 @@
         + [columns(u) for u in ups]
         + [columns(e) for e in expands]
         + [down_spec] * count,
-        out_specs=[row_spec, row_spec] + [gated_spec] * count + [full(state_shape)] * 2,
+        out_specs=[row_spec, row_spec]
+        + [gated_spec] * count
+        + [full(state_shape)] * 2
+        + [full(norm_shape)] * 2,
         out_shape=[jax.ShapeDtypeStruct((tokens, hidden), low)] * 2
         + [gated_shape] * count
-        + [state_shape] * 2,
+        + [state_shape] * 2
+        + [norm_shape] * 2,
         scratch_shapes=[
             pltpu.VMEM((tokens, 2 * channels), low),
             pltpu.VMEM((tokens, 2 * channels), f32),
+            pltpu.VMEM((tokens, width), f32),
         ],
         compiler_params=pltpu.CompilerParams(vmem_limit_bytes=48 * 2**20),
         cost_estimate=pl.CostEstimate(
@@ -681,7 +717,7 @@
     grad_out, up_out = outs[:2]
     gated = outs[2 : 2 + count]
     gated = gated if split else cube.split(gated[0])
-    return grad_out, up_out, gated, outs[2 + count :]
+    return grad_out, up_out, gated, outs[2 + count : 4 + count], outs[4 + count :]
 
 
 def value_kernel(
@@ -873,8 +909,8 @@
         expand.send()
     poles, coefs = lax.optimization_barrier((state_poles, state_params, value_low))[:2]
     channels, length = channel_values.shape
-    blocked = (channels, length // BLOCK, BLOCK)
-    pieces = pieces_of(lengths[0], length)
+    blocked = (channels, tok_size, length // tok_size)
+    pieces = pieces_of(lengths[0], length, tok_size)
     powers, lams, coefs = mixer_inputs(poles, coefs)
     channel_values = channel_values.reshape(blocked)
     normed_rows = jnp.concatenate([flat(side).T for side in normed], axis=1)
@@ -918,7 +954,7 @@
     down.rest()
     ups, downs, expands = up.both(), down.both(), expand.both()
 
-    expanded_grad, up_pre_grad, gated_sides, state_grads = gate(
+    expanded_grad, up_pre_grad, gated_sides, state_grads, ups_grads = gate(
         cube,
         normed_rows,
         [flat(side) for side in state_sides],
@@ -928,8 +964,6 @@
         downs,
     )
     state_grad = cube.merge(*[g.reshape(state_sides[0].shape) for g in state_grads])
-    channel_grad = lax.all_to_all(state_grad, "tok", split_axis=0, concat_axis=1, tiled=True)
-    channel_grad = channel_grad.reshape(blocked)
     gated_swapped = cube.swap(gated_sides[1], 0)
     expanded_swapped = cube.swap(expanded_grad, 0)
     up_pre_swapped = cube.swap(after(up_pre_grad, gated_swapped), 0)
@@ -948,6 +982,8 @@
     expand_sums = scatter(
         (state_sides[0], state_swapped), (expanded_grad, expanded_swapped), zs + ys + xs
     )
+    channel_grad = lax.all_to_all(state_grad, "tok", split_axis=0, concat_axis=1, tiled=True)
+    channel_grad = channel_grad.reshape(blocked)
     down_sums.send()
     up_sums.send()
     expand_sums.send(channel_grad)
@@ -956,24 +992,18 @@
     )
     token = run(up_sums.sent, down_sums.sent, expand_sums.sent)
     token = run(*token)
+    token = run(*token)
     expand_sums.take(*token)
     expand_sums.send()
-    token = run(*token, expand_sums.sent)
-    for _ in range(nx):
-        up_sums.take(*token)
-        down_sums.take(*token)
-        up_sums.send()
-        down_sums.send()
-    expand_sums.take(*token)
-    expand_sums.send()
-    mixer.last(*token, up_sums.sent, down_sums.sent, expand_sums.sent)
+    mixer.last(*token, expand_sums.sent)
     value_grad_channels, param_grad = mixer.outs
     states = param_grad.shape[1] // 2
     param_grad = jnp.stack([param_grad[:channels, :states], param_grad[:channels, states:]])
     param_sum = param_grad + cube.swap(param_grad, 0)
-    for sums in (up_sums, down_sums, expand_sums):
-        sums.arriving = after(sums.arriving, value_grad_channels)
-    value_grad_channels = after(value_grad_channels, up_sums.arriving, down_sums.arriving)
+    for _ in range(nx):
+        for sums in (down_sums, up_sums):
+            sums.take(value_grad_channels)
+            sums.send()
     value_grad = lax.all_to_all(
         value_grad_channels.reshape(channels, length),
         "tok",
@@ -981,14 +1011,7 @@
         concat_axis=0,
         tiled=True,
     )
-    for sums in (up_sums, down_sums):
-        sums.take()
-        sums.send()
-    expand_sums.take(value_grad)
-    if expand_sums.order:
-        expand_sums.send()
-    up_pre_late = after(up_pre_grad, value_grad_channels)
-    ups_grads = [dot(flat(part), up_pre_late, 1, 1) for part in ups]
+    value_grad = after(value_grad, up_sums.sent, down_sums.sent)
     keep, send, normed_grads = value_grads(
         inner,
         value_grad,
@@ -1002,16 +1025,18 @@
     keep, send = [part.reshape(hats[0].shape[:2] + (-1,)) for part in (keep, send)]
     packed_sum = keep + cube.swap(send, 0).astype(jnp.float32)
     core_sum = packed_sum
+    for _ in range(nx):
+        for sums in (down_sums, up_sums, expand_sums):
+            sums.take(send)
+            sums.send()
+    packed_sum = after(packed_sum, up_sums.sent, down_sums.sent)
     normed_grads = [after(g, core_sum) for g in normed_grads]
     gated_late = after(gated_sides[0], packed_sum), gated_sides[1]
     layer_out = (token_rows + dots(gated_late, downs, 0, 0)).astype(low)[None]
     packed_sum = direct_sum(cube, packed_sum, tok_bits, xs + ys, low)
-    for sums in (up_sums, down_sums, expand_sums):
-        if sums.order:
-            sums.take(core_sum)
-        if sums.order:
-            sums.send()
-            sums.arriving = after(sums.arriving, packed_sum)
+    for sums in (down_sums, up_sums, expand_sums):
+        sums.take(packed_sum)
+        sums.send()
     packed_sum = direct_sum(cube, packed_sum, zs, zs, jnp.float32)[0]
     up_sum, down_sum, expand_sum = [
         sums.rest() for sums in (up_sums, down_sums, expand_sums)

time: 349 us -> 335 us (0.960)
  Pallas kernels: 117 us -> 88.8 us
  waiting for transfers between devices: 26.9 us -> 47.9 us
  matrix products: 18.4 us -> 6.5 us
    pallas_call x8, Pallas kernels: 87.3 us -> 57.6 us  [call(): pl.pallas_call(body, grid=(1,), in_specs=specs + [pl.BlockSpec(memory_spa...]
    ppermute x48, waiting for transfers between devices: 23.8 us -> 43.4 us  [trade(): return lax.ppermute(block, ('tok', 'rep'), pairs)]
    dot_general x6 -> x4, matrix products: 18.4 us -> 6.5 us  [dot(): lax.dot_general(a, b, (((a_dim,), (b_dim,)), ((), ())), preferred_element...]
    unnamed x210 -> x196, local copies, waits for them, and re-layouts: 10.6 us -> 19.9 us
  transfers between devices with their start and end apart: 51 -> 51, of which waited for: 14 -> 14; matrix products, arithmetic and copies ran while one was open for 31% -> 27% of each run, Pallas kernels for 30% -> 22%
where the time goes in v3:
time: 335 us; the launch traced here: 329 us
  Pallas kernels  88.8 us (27%)
  starting transfers between devices  65.1 us (19%)
  other arithmetic  59.7 us (18%)
  waiting for transfers between devices  47.9 us (14%)
  local copies, waits for them, and re-layouts  43.6 us (13%)
  blocking collectives  14.8 us (4%)
  matrix products  6.5 us (2%)
    pallas_call x8, Pallas kernels, call(): pl.pallas_call(body, grid=(1,), in_specs=specs + [pl.BlockSpec(memory_spa...  57.6 us
    ppermute x48, starting transfers between devices, trade(): return lax.ppermute(block, ('tok', 'rep'), pairs)  50.9 us
    ppermute x48, waiting for transfers between devices, trade(): return lax.ppermute(block, ('tok', 'rep'), pairs)  43.4 us
    unnamed x196, local copies, waits for them, and re-layouts  19.9 us
    pallas_call x1, Pallas kernels, gate(): pl.pallas_call(body, grid=(hidden // block,), in_specs=[pl.BlockSpec(memo...  15.2 us
    all_to_all x1, blocking collectives, per_device(): lax.all_to_all(state_out.reshape(channels, length), 'tok', split_axis=1,...  14.8 us
    select_n x23, other arithmetic, join(): jnp.where(self.cube.bit(b) == 1, jnp.concatenate([second, first], axis=1)...  14.1 us
    add x9, other arithmetic, take(): total = self.keep + after(self.arriving, *waits).astype(jnp.float32)  12.7 us
  transfers between devices with their start and end apart: 51, of which 14 were waited for; matrix products, arithmetic and copies ran while one was open for 27% of the time, Pallas kernels for 22%

profile of v3, /device:TPU:0, one launch (start us, length us, event | category | flops | bytes accessed | tf_op | source)
XLA Modules:
  0.0 328.7 jit_solution(6548190932829610162)
XLA Ops:
  2.4 3.1 collective-permute-start.2
  5.5 2.6 collective-permute-start.1
  9.1 1.8 collective-permute-start.12
  15.9 1.7 collective-permute-start.4
  19.0 1.7 collective-permute-start.7
  22.5 1.7 collective-permute-start.8
  25.0 2.4 collective-permute-start.13
  30.6 5.5 %collective-permute-done.7 = bf16[1,32,3072]{2,1,0:T(8,128)(2,1)S(1)} collective-permute-done((bf16[1,32,3072]{2,1,0:T(8,128)(2,1)}, bf16[1,32,3072]{2,1,0:T(8,128)(2,1)S(1)}, u32[]{:S(2)}, u32[]{:S(2)}) %collective-permute-start.7) | collective-permute-done | bytes 196640 | tf_op jit(solution)/shard_map/ppermute | solution.py:475
  36.1 1.8 maximum_select_fusion.11
  43.8 2.4 fusion.18
  46.2 4.9 %all-to-all-start = ((bf16[16,32,256]{2,1,0:T(8,128)(2,1)}), bf16[16,32,256]{2,1,0:T(8,128)(2,1)S(1)}, u32[]{:S(2)}, u32[]{:S(2)}) async-start(bf16[16,32,256]{2,1,0:T(8,128)(2,1)} %bitcast.30), calls=%async_computation | async-start | bytes 524288 | tf_op jit(solution)/shard_map/all_to_all | solution.py:900
  53.4 3.9 %fusion.4 = (f32[32,16,512]{2,0,1:T(8,128)S(1)}, f32[32,16,512]{2,0,1:T(8,128)S(1)}) fusion(f32[32,512]{1,0:T(8,128)S(1)} %get-tuple-element.358, f32[16]{0:T(128)S(1)} %copy-done.95, f32[32,512]{1,0:T(8,128)S(1)} %get-tuple-element.359), kind=kLoop, calls=%fused_computation.31 | loop fusion | flops 1048576 | bytes 2228288 | tf_op jit(solution)/shard_map/mul | solution.py:64
  57.3 1.5 pad_maximum_fusion
  60.1 4.1 %copy.328.refs_4_.refs_5_ = f32[32,16,1024]{2,1,0:T(8,128)} copy(f32[32,16,1024]{2,0,1:T(8,128)} %pad_maximum_fusion) | data formatting | bytes 4194304 | tf_op jit(solution)/shard_map/concatenate | solution.py:64
  64.4 1.6 maximum_select_fusion.6
  66.0 2.1 collective-permute-start.10
  69.4 1.5 collective-permute-start.14
  72.0 2.4 collective-permute-start.15
  74.5 7.7 %mix_forward.4 = (bf16[32,16,256]{2,1,0:T(8,128)(2,1)S(1)}, f32[1536,1024]{1,0:T(8,128)}, bf16[32,128,128]{2,1,0:T(8,128)(2,1)S(1)}, f32[8,128]{1,0:T(8,128)}) custom-call(f32[48]{0:T(128)S(1)} %add_convert_fusion.6.refs_0_, bf16[2,48,16]{2,1,0:T(8,128)(2,1)S(1)} %compare_convert_fusion.refs_1_, bf16[48,128]{1,0:T(8,128)(2,1)S(1)} %fusion.54.refs_2_, ...), custom_call_target="tpu_custom_call" | custom-call | flops 8000000000 | bytes 4194304 | tf_op jit(solution)/shard_map/mix_forward/pallas_call | solution.py:324
  82.2 9.6 %collective-permute-done.15 = bf16[4,16,3072]{2,1,0:T(8,128)(2,1)S(1)} collective-permute-done((bf16[4,16,3072]{2,1,0:T(8,128)(2,1)S(1)}, bf16[4,16,3072]{2,1,0:T(8,128)(2,1)S(1)}, u32[]{:S(2)}, u32[]{:S(2)}) %collective-permute-start.15) | collective-permute-done | bytes 393248 | tf_op jit(solution)/shard_map/ppermute | solution.py:475
  95.0 8.2 %mix_forward.5 = (bf16[32,16,256]{2,1,0:T(8,128)(2,1)S(1)}, f32[1536,1024]{1,0:T(8,128)}, bf16[32,128,128]{2,1,0:T(8,128)(2,1)S(1)}, f32[8,128]{1,0:T(8,128)S(1)}) custom-call(f32[48]{0:T(128)S(1)} %add_convert_fusion.6.refs_0_, bf16[2,48,16]{2,1,0:T(8,128)(2,1)S(1)} %copy-done.27, ...), custom_call_target="tpu_custom_call", output_to_operand_aliasing={{0}: (10, {}), {1}: (11, {}), {2}: (12, {})} | custom-call | flops 8000000000 | bytes 4194304 | tf_op jit(solution)/shard_map/mix_forward/pallas_call | solution.py:324
  103.2 8.0 %mix_forward.6 = (bf16[32,16,256]{2,1,0:T(8,128)(2,1)S(1)}, f32[1536,1024]{1,0:T(8,128)}, bf16[32,128,128]{2,1,0:T(8,128)(2,1)S(1)}, f32[8,128]{1,0:T(8,128)S(1)}) custom-call(f32[48]{0:T(128)S(1)} %add_convert_fusion.6.refs_0_, bf16[2,48,16]{2,1,0:T(8,128)(2,1)S(1)} %copy-done.27, ...), custom_call_target="tpu_custom_call", output_to_operand_aliasing={{0}: (8, {}), {1}: (9, {}), {2}: (10, {})} | custom-call | flops 8000000000 | bytes 4194304 | tf_op jit(solution)/shard_map/mix_forward/pallas_call | solution.py:324
  112.2 2.0 copy-done.32
  114.2 8.1 %mix_forward.7 = (bf16[32,16,256]{2,1,0:T(8,128)(2,1)S(1)}, f32[1536,1024]{1,0:T(8,128)}, bf16[32,128,128]{2,1,0:T(8,128)(2,1)S(1)}, f32[8,128]{1,0:T(8,128)}) custom-call(f32[48]{0:T(128)S(1)} %add_convert_fusion.6.refs_0_, bf16[2,48,16]{2,1,0:T(8,128)(2,1)S(1)} %copy-done.27, ...), custom_call_target="tpu_custom_call", output_to_operand_aliasing={{0}: (12, {}), {1}: (13, {}), {2}: (14, {})} | custom-call | flops 8000000000 | bytes 4194304 | tf_op jit(solution)/shard_map/mix_forward/pallas_call | solution.py:324
  122.3 7.6 %collective-permute-done.19 = bf16[8,32,3072]{2,1,0:T(8,128)(2,1)} collective-permute-done((bf16[8,32,3072]{2,1,0:T(8,128)(2,1)S(1)}, bf16[8,32,3072]{2,1,0:T(8,128)(2,1)}, u32[]{:S(2)}, u32[]{:S(2)}) %collective-permute-start.19) | collective-permute-done | bytes 1572896 | tf_op jit(solution)/shard_map/ppermute | solution.py:475
  129.9 2.4 maximum_select_fusion
  135.3 14.8 %all_to_all.61 = bf16[32,16,256]{2,0,1:T(8,128)(2,1)S(1)} all-to-all(bf16[32,16,256]{2,0,1:T(8,128)(2,1)S(1)} %copy.330), channel_id=1, replica_groups=mesh['tok'=16,'rep'=2] {'tok'}, dimensions={1} | all-to-all | bytes 524288 | tf_op jit(solution)/shard_map/all_to_all | solution.py:948
  150.9 1.6 copy-done.52
  154.0 15.2 %gate.1 = (bf16[256,3072]{1,0:T(8,128)(2,1)}, bf16[256,3072]{1,0:T(8,128)(2,1)}, bf16[16,96,256]{2,1,0:T(8,128)(2,1)S(1)}, bf16[16,96,256]{2,1,0:T(8,128)(2,1)S(...) custom-call(s32[1]{0:T(128)} %bitcast.1.core, ...), custom_call_target="tpu_custom_call" | custom-call | flops 1000000 | bytes 1024 | tf_op jit(solution)/shard_map/gate/pallas_call | solution.py:689
  171.3 2.9 collective-permute-done.24
  179.1 4.4 %all-to-all-start.2 = ((bf16[16,32,256]{2,1,0:T(8,128)(2,1)}), bf16[16,32,256]{2,1,0:T(8,128)(2,1)}, u32[]{:S(2)}, u32[]{:S(2)}) async-start(bf16[16,32,256]{2,1,0:T(8,128)(2,1)} %bitcast.81), calls=%async_computation.2 | async-start | bytes 524288 | tf_op jit(solution)/shard_map/all_to_all | solution.py:985
  184.8 1.8 bitcast_convert_fusion.4
  189.7 4.5 %all-to-all-done.2 = bf16[16,32,256]{2,1,0:T(8,128)(2,1)} async-done(((bf16[16,32,256]{2,1,0:T(8,128)(2,1)}), bf16[16,32,256]{2,1,0:T(8,128)(2,1)}, u32[]{:S(2)}, u32[]{:S(2)}) %all-to-all-start.2) | async-done | bytes 262176 | tf_op jit(solution)/shard_map/all_to_all | solution.py:985
  196.3 3.8 %weight_grad.4 = (bf16[768,1024]{1,0:T(8,128)(2,1)}, f32[768,1024]{1,0:T(8,128)}) custom-call(s32[1]{0:T(128)} %bitcast.87.bit_ref, bf16[8,2,96,256]{3,2,1,0:T(8,128)(2,1)S(1)} %bitcast.367, bf16[8,2,96,256]{3,2,1,0:T(8,128)(2,1)S(1)} %bitcast.368, bf16[8,2,96,256]{3,2,1,0:T(8,128)(2,1)S(1)} %bitcast.370, bf16[8,2,96,256]{3,2,1,0:T(8,128)(2,1)S(1)} %bitcast.371, ...), custom_call_target="tpu_custom_call" | custom-call | flops 1000000 | bytes 1024 | tf_op jit(solution)/shard_map/weight_grad/pallas_call | solution.py:796
  200.9 3.6 %weight_grad.5 = (bf16[128,3072]{1,0:T(8,128)(2,1)S(1)}, f32[128,3072]{1,0:T(8,128)S(1)}) custom-call(s32[1]{0:T(128)} %bitcast.91.bit_ref, bf16[2,2,64,256]{3,2,1,0:T(8,128)(2,1)S(1)} %bitcast.378, bf16[2,2,64,256]{3,2,1,0:T(8,128)(2,1)S(1)} %bitcast.379, bf16[2,2,64,256]{3,2,1,0:T(8,128)(2,1)} %bitcast.94.got_send.got_keep, ...), custom_call_target="tpu_custom_call" | custom-call | flops 1000000 | bytes 1024 | tf_op jit(solution)/shard_map/weight_grad/pallas_call | solution.py:796
  205.5 5.3 %weight_grad.3 = (bf16[256,3072]{1,0:T(8,128)(2,1)}, f32[256,3072]{1,0:T(8,128)}) custom-call(s32[1]{0:T(128)} %bitcast.83.bit_ref, bf16[4,2,64,256]{3,2,1,0:T(8,128)(2,1)S(1)} %add_convert_fusion.own_send.own_keep, bf16[4,2,64,256]{3,2,1,0:T(8,128)(2,1)S(1)} %add_convert_fusion.own_send.own_keep, bf16[4,2,64,256]{3,2,1,0:T(8,128)(2,1)S(1)} %bitcast.387, ...), custom_call_target="tpu_custom_call" | custom-call | flops 1000000 | bytes 1024 | tf_op jit(solution)/shard_map/weight_grad/pallas_call | solution.py:796
  211.5 6.6 %mix_backward.4 = (bf16[32,16,256]{2,1,0:T(8,128)(2,1)S(1)}, f32[32,1024]{1,0:T(8,128)S(1)}, f32[8,128]{1,0:T(8,128)S(1)}) custom-call(f32[48]{0:T(128)S(1)} %add_convert_fusion.6.refs_0_, bf16[2,48,16]{2,1,0:T(8,128)(2,1)S(1)} %copy-done.28, bf16[48,128]{1,0:T(8,128)(2,1)S(1)} %fusion.54.refs_2_, bf16[32,16,256]{2,1,0:T(8,128)(2,1)S(1)} %bitcast.395, ...), custom_call_target="tpu_custom_call" | custom-call | flops 10700000256 | bytes 4194304 | tf_op jit(solution)/shard_map/mix_backward/pallas_call | solution.py:324
  218.1 6.3 %mix_backward.5 = (bf16[32,16,256]{2,1,0:T(8,128)(2,1)S(1)}, f32[32,1024]{1,0:T(8,128)S(1)}, f32[8,128]{1,0:T(8,128)S(1)}) custom-call(f32[48]{0:T(128)S(1)} %add_convert_fusion.6.refs_0_, bf16[2,48,16]{2,1,0:T(8,128)(2,1)S(1)} %copy-done.28, bf16[48,128]{1,0:T(8,128)(2,1)S(1)} %fusion.54.refs_2_, ...), custom_call_target="tpu_custom_call", output_to_operand_aliasing={{0}: (11, {}), {1}: (12, {})} | custom-call | flops 10700000256 | bytes 4194304 | tf_op jit(solution)/shard_map/mix_backward/pallas_call | solution.py:324
  224.4 6.5 %mix_backward.6 = (bf16[32,16,256]{2,1,0:T(8,128)(2,1)S(1)}, f32[32,1024]{1,0:T(8,128)S(1)}, f32[8,128]{1,0:T(8,128)S(1)}) custom-call(f32[48]{0:T(128)S(1)} %add_convert_fusion.6.refs_0_, bf16[2,48,16]{2,1,0:T(8,128)(2,1)S(1)} %copy-done.28, bf16[48,128]{1,0:T(8,128)(2,1)S(1)} %fusion.54.refs_2_, ...), custom_call_target="tpu_custom_call", output_to_operand_aliasing={{0}: (11, {}), {1}: (12, {})} | custom-call | flops 10700000256 | bytes 4194304 | tf_op jit(solution)/shard_map/mix_backward/pallas_call | solution.py:324
  233.4 6.3 %mix_backward.7 = (bf16[32,16,256]{2,1,0:T(8,128)(2,1)S(1)}, f32[32,1024]{1,0:T(8,128)S(1)}, f32[8,128]{1,0:T(8,128)}) custom-call(f32[48]{0:T(128)S(1)} %add_convert_fusion.6.refs_0_, bf16[2,48,16]{2,1,0:T(8,128)(2,1)S(1)} %copy-done.28, bf16[48,128]{1,0:T(8,128)(2,1)S(1)} %fusion.54.refs_2_, ...), custom_call_target="tpu_custom_call", output_to_operand_aliasing={{0}: (12, {}), {1}: (13, {})} | custom-call | flops 10700000256 | bytes 4194304 | tf_op jit(solution)/shard_map/mix_backward/pallas_call | solution.py:324
  240.5 4.9 %all-to-all-start.3 = ((bf16[32,16,256]{2,0,1:T(8,128)(2,1)}), bf16[32,16,256]{2,0,1:T(8,128)(2,1)}, u32[]{:S(2)}, u32[]{:S(2)}) async-start(bf16[32,16,256]{2,0,1:T(8,128)(2,1)} %copy.346), calls=%async_computation.3 | async-start | bytes 524288 | tf_op jit(solution)/shard_map/all_to_all | solution.py:1007
  245.5 3.0 convert_add_fusion
  249.6 1.9 collective-permute-start.33
  252.4 1.9 convert_add_fusion.1
  254.3 1.6 copy-done.40
  257.0 1.5 collective-permute-start.32
  261.6 3.4 %value_grads.1 = (f32[512,640]{1,0:T(8,128)}, bf16[512,640]{1,0:T(8,128)(2,1)S(1)}, f32[512,256]{1,0:T(8,128)S(1)}, f32[512,256]{1,0:T(8,128)S(1)}) custom-call(bf16[512,256]{1,0:T(8,128)(2,1)} %bitcast.100.grad, f32[512,256]{1,0:T(8,128)S(1)} %copy-done.14, bf16[512,640]{1,0:T(8,128)(2,1)S(1)} %bitcast.362, bf16[512,640]{1,0:T(8,128)(2,1)} %bitcast.449, ...), custom_call_target="tpu_custom_call" | custom-call | flops 1000000 | bytes 1024 | tf_op jit(solution)/shard_map/value_grads/pallas_call | solution.py:751
  264.9 6.1 %collective-permute-done.33 = bf16[4,96,1024]{2,1,0:T(8,128)(2,1)} collective-permute-done((bf16[4,96,1024]{2,1,0:T(8,128)(2,1)}, bf16[4,96,1024]{2,1,0:T(8,128)(2,1)}, u32[]{:S(2)}, u32[]{:S(2)}) %collective-permute-start.33) | collective-permute-done | bytes 786464 | tf_op jit(solution)/shard_map/ppermute | solution.py:475
  272.9 1.5 collective-permute-start.43
  274.4 1.4 bitcast_add_fusion
  281.6 2.4 fusion.8
  284.0 1.9 bitcast_add_fusion.1
  286.9 1.5 collective-permute-start.37
  288.8 1.7 collective-permute-start.35
  292.8 1.8 fusion.2
  296.8 2.3 collective-permute-start.41
  299.1 2.2 collective-permute-start.40
  303.1 1.5 collective-permute-start.44
  306.4 4.1 %collective-permute-done.41 = f32[1,32,640]{2,1,0:T(8,128)S(1)} collective-permute-done((f32[1,32,640]{2,1,0:T(8,128)S(1)}, f32[1,32,640]{2,1,0:T(8,128)S(1)}, u32[]{:S(2)}, u32[]{:S(2)}) %collective-permute-start.41) | collective-permute-done | bytes 81952 | tf_op jit(solution)/shard_map/ppermute | solution.py:475
  310.7 1.6 multiply_subtract_fusion.4
  315.0 2.1 multiply_subtract_fusion.2
  318.2 3.3 %collective-permute-start.38 = (bf16[1,32,3072]{2,1,0:T(8,128)(2,1)S(1)}, bf16[1,32,3072]{2,1,0:T(8,128)(2,1)S(1)}, u32[]{:S(2)}, u32[]{:S(2)}) collective-permute-start(bf16[1,32,3072]{2,1,0:T(8,128)(2,1)S(1)} %dynamic-slice_convert_fusion.5), channel_id=1, source_target_pairs={{0,16},{1,17},{2,18},{3,19},{4,20},{5,21},{6,22},{7,23},{8,24},{9,... | collective-permute-start | bytes 589832 | tf_op jit(solution)/shard_map/ppermute | solution.py:475
  321.7 2.1 multiply_subtract_fusion
  323.9 3.4 %collective-permute-done.38 = bf16[1,32,3072]{2,1,0:T(8,128)(2,1)S(1)} collective-permute-done((bf16[1,32,3072]{2,1,0:T(8,128)(2,1)S(1)}, bf16[1,32,3072]{2,1,0:T(8,128)(2,1)S(1)}, u32[]{:S(2)}, u32[]{:S(2)}) %collective-permute-start.38) | collective-permute-done | bytes 196640 | tf_op jit(solution)/shard_map/ppermute | solution.py:475
  (392 shorter events, 83.4 us)
Async XLA Ops:
  0.7 13.4 %copy-start.59 = (f32[32,3072]{1,0:T(8,128)S(1)}, f32[32,3072]{1,0:T(8,128)}, u32[]{:S(2)}) copy-start(f32[32,3072]{1,0:T(8,128)} %param.26) | copy-start | bytes 1179652
  0.7 14.1 %copy-start.57 = (f32[96,1024]{1,0:T(8,128)S(1)}, f32[96,1024]{1,0:T(8,128)}, u32[]{:S(2)}) copy-start(f32[96,1024]{1,0:T(8,128)} %param.29) | copy-start | bytes 1179652
  2.4 12.9 %collective-permute-start.2 = (bf16[1,32,640]{2,1,0:T(8,128)(2,1)S(1)}, bf16[1,32,640]{2,1,0:T(8,128)(2,1)S(1)}, u32[]{:S(2)}, u32[]{:S(2)}) collective-permute-start(bf16[1,32,640]{2,1,0:T(8,128)(2,1)S(1)} %get-tuple-element.354), channel_id=1, source_target_pairs={{0,8},{1,9},{2,10},{3,11},{4,12},{5,13},{6,14},{7,15},{8,0},{9,1},... | collective-permute-start | bytes 122888 | tf_op jit(solution)/shard_map/ppermute | solution.py:475
  5.5 9.9 %collective-permute-start.1 = (bf16[1,32,640]{2,1,0:T(8,128)(2,1)S(1)}, bf16[1,32,640]{2,1,0:T(8,128)(2,1)S(1)}, u32[]{:S(2)}, u32[]{:S(2)}) collective-permute-start(bf16[1,32,640]{2,1,0:T(8,128)(2,1)S(1)} %get-tuple-element.354), channel_id=1, source_target_pairs={{0,16},{1,17},{2,18},{3,19},{4,20},{5,21},{6,22},{7,23},{8,24},{9,... | collective-permute-start | bytes 122888 | tf_op jit(solution)/shard_map/ppermute | solution.py:475
  8.1 7.3 %collective-permute-start = (bf16[1,32,640]{2,1,0:T(8,128)(2,1)S(1)}, bf16[1,32,640]{2,1,0:T(8,128)(2,1)S(1)}, u32[]{:S(2)}, u32[]{:S(2)}) collective-permute-start(bf16[1,32,640]{2,1,0:T(8,128)(2,1)S(1)} %get-tuple-element.354), channel_id=1, source_target_pairs={{0,24},{1,25},{2,26},{3,27},{4,28},{5,29},{6,30},{7,31},{8,16},{9,... | collective-permute-start | bytes 122888 | tf_op jit(solution)/shard_map/ppermute | solution.py:475
  9.1 10.0 %collective-permute-start.12 = (bf16[1,16,3072]{2,1,0:T(8,128)(2,1)S(1)}, bf16[1,16,3072]{2,1,0:T(8,128)(2,1)S(1)}, u32[]{:S(2)}, u32[]{:S(2)}) collective-permute-start(bf16[1,16,3072]{2,1,0:T(8,128)(2,1)S(1)} %get-tuple-element.344), channel_id=1, source_target_pairs={{0,2},{1,3},{2,0},{3,1},{4,6},{5,7},{6,4},{7,5},{8,10},{9,11},{10,... | collective-permute-start | bytes 294920 | tf_op jit(solution)/shard_map/ppermute | solution.py:475
  10.8 101.3 %collective-permute-start.18 = (bf16[256,1024]{1,0:T(8,128)(2,1)}, bf16[256,1024]{1,0:T(8,128)(2,1)S(1)}, u32[]{:S(2)}, u32[]{:S(2)}) collective-permute-start(bf16[256,1024]{1,0:T(8,128)(2,1)} %bitcast.356), channel_id=1, source_target_pairs={{0,1},{1,0},{2,3},{3,2},{4,5},{5,4},{6,7},{7,6},{8,9},{9,8},{10,11... | collective-permute-start | bytes 1572872 | tf_op jit(solution)/shard_map/ppermute | solution.py:475
  13.6 29.2 %copy-start.87 = (f32[256]{0:T(256)}, f32[256]{0:T(256)S(1)}, u32[]{:S(2)}) copy-start(f32[256]{0:T(256)S(1)} %broadcast_multiply_fusion.2) | copy-start | bytes 3076
  13.9 28.9 %copy-start.90 = (f32[256]{0:T(256)}, f32[256]{0:T(256)S(1)}, u32[]{:S(2)}) copy-start(f32[256]{0:T(256)S(1)} %add_rsqrt_fusion) | copy-start | bytes 3076
  14.1 60.4 %copy-start.26 = (bf16[2,48,16]{2,1,0:T(8,128)(2,1)}, bf16[2,48,16]{2,1,0:T(8,128)(2,1)S(1)}, u32[]{:S(2)}) copy-start(bf16[2,48,16]{2,1,0:T(8,128)(2,1)S(1)} %compare_convert_fusion.refs_1_) | copy-start | bytes 9220
  15.3 35.9 %copy-start.35 = (bf16[1024,256]{1,0:T(8,128)(2,1)}, bf16[1024,256]{1,0:T(8,128)(2,1)S(1)}, u32[]{:S(2)}) copy-start(bf16[1024,256]{1,0:T(8,128)(2,1)S(1)} %copy.311) | copy-start | bytes 1572868
  15.5 7.1 %collective-permute-start.5 = (bf16[4,32,640]{2,1,0:T(8,128)(2,1)S(1)}, bf16[4,32,640]{2,1,0:T(8,128)(2,1)S(1)}, u32[]{:S(2)}, u32[]{:S(2)}) collective-permute-start(bf16[4,32,640]{2,1,0:T(8,128)(2,1)S(1)} %bitcast.455), channel_id=1, source_target_pairs={{0,2},{1,3},{2,0},{3,1},{4,6},{5,7},{6,4},{7,5},{8,10},{9,11},{10,... | collective-permute-start | bytes 491528 | tf_op jit(solution)/shard_map/ppermute | solution.py:475
  15.9 9.1 %collective-permute-start.4 = (bf16[4,32,640]{2,1,0:T(8,128)(2,1)S(1)}, bf16[4,32,640]{2,1,0:T(8,128)(2,1)S(1)}, u32[]{:S(2)}, u32[]{:S(2)}) collective-permute-start(bf16[4,32,640]{2,1,0:T(8,128)(2,1)S(1)} %bitcast.456), channel_id=1, source_target_pairs={{0,4},{1,5},{2,6},{3,7},{4,0},{5,1},{6,2},{7,3},{8,12},{9,13},{10,... | collective-permute-start | bytes 491528 | tf_op jit(solution)/shard_map/ppermute | solution.py:475
  17.6 9.8 %collective-permute-start.3 = (bf16[4,32,640]{2,1,0:T(8,128)(2,1)S(1)}, bf16[4,32,640]{2,1,0:T(8,128)(2,1)S(1)}, u32[]{:S(2)}, u32[]{:S(2)}) collective-permute-start(bf16[4,32,640]{2,1,0:T(8,128)(2,1)S(1)} %bitcast.457), channel_id=1, source_target_pairs={{0,6},{1,7},{2,4},{3,5},{4,2},{5,3},{6,0},{7,1},{8,14},{9,15},{10,... | collective-permute-start | bytes 491528 | tf_op jit(solution)/shard_map/ppermute | solution.py:475
  19.0 17.1 %collective-permute-start.7 = (bf16[1,32,3072]{2,1,0:T(8,128)(2,1)}, bf16[1,32,3072]{2,1,0:T(8,128)(2,1)S(1)}, u32[]{:S(2)}, u32[]{:S(2)}) collective-permute-start(bf16[1,32,3072]{2,1,0:T(8,128)(2,1)} %get-tuple-element.95), channel_id=1, source_target_pairs={{0,16},{1,17},{2,18},{3,19},{4,20},{5,21},{6,22},{7,23},{8,24},{9,... | collective-permute-start | bytes 589832 | tf_op jit(solution)/shard_map/ppermute | solution.py:475
  22.5 16.8 %collective-permute-start.8 = (bf16[1,96,1024]{2,1,0:T(8,128)(2,1)S(1)}, bf16[1,96,1024]{2,1,0:T(8,128)(2,1)S(1)}, u32[]{:S(2)}, u32[]{:S(2)}) collective-permute-start(bf16[1,96,1024]{2,1,0:T(8,128)(2,1)S(1)} %get-tuple-element.96), channel_id=1, source_target_pairs={{0,16},{1,17},{2,18},{3,19},{4,20},{5,21},{6,22},{7,23},{8,24},{9,... | collective-permute-start | bytes 589832 | tf_op jit(solution)/shard_map/ppermute | solution.py:475
  25.0 43.2 %collective-permute-start.13 = (bf16[2,16,3072]{2,1,0:T(8,128)(2,1)}, bf16[2,16,3072]{2,1,0:T(8,128)(2,1)}, u32[]{:S(2)}, u32[]{:S(2)}) collective-permute-start(bf16[2,16,3072]{2,1,0:T(8,128)(2,1)} %maximum_select_fusion.17), channel_id=1, source_target_pairs={{0,4},{1,5},{2,6},{3,7},{4,0},{5,1},{6,2},{7,3},{8,12},{9,13},{10,... | collective-permute-start | bytes 589832 | tf_op jit(solution)/shard_map/ppermute | solution.py:475
  27.6 14.7 %collective-permute-start.6 = (bf16[16,32,640]{2,1,0:T(8,128)(2,1)S(1)}, bf16[16,32,640]{2,1,0:T(8,128)(2,1)S(1)}, u32[]{:S(2)}, u32[]{:S(2)}) collective-permute-start(bf16[16,32,640]{2,1,0:T(8,128)(2,1)S(1)} %bitcast.359), channel_id=1, source_target_pairs={{0,1},{1,0},{2,3},{3,2},{4,5},{5,4},{6,7},{7,6},{8,9},{9,8},{10,11... | collective-permute-start | bytes 1966088 | tf_op jit(solution)/shard_map/ppermute | solution.py:475
  38.0 26.4 %collective-permute-start.9 = (bf16[2,32,3072]{2,1,0:T(8,128)(2,1)}, bf16[2,32,3072]{2,1,0:T(8,128)(2,1)}, u32[]{:S(2)}, u32[]{:S(2)}) collective-permute-start(bf16[2,32,3072]{2,1,0:T(8,128)(2,1)} %maximum_select_fusion.11), channel_id=1, source_target_pairs={{0,8},{1,9},{2,10},{3,11},{4,12},{5,13},{6,14},{7,15},{8,0},{9,1},... | collective-permute-start | bytes 1179656 | tf_op jit(solution)/shard_map/ppermute | solution.py:475
  40.1 28.0 %collective-permute-start.11 = (bf16[2,96,1024]{2,1,0:T(8,128)(2,1)}, bf16[2,96,1024]{2,1,0:T(8,128)(2,1)}, u32[]{:S(2)}, u32[]{:S(2)}) collective-permute-start(bf16[2,96,1024]{2,1,0:T(8,128)(2,1)} %maximum_select_fusion.12), channel_id=1, source_target_pairs={{0,8},{1,9},{2,10},{3,11},{4,12},{5,13},{6,14},{7,15},{8,0},{9,1},... | collective-permute-start | bytes 1179656 | tf_op jit(solution)/shard_map/ppermute | solution.py:475
  43.7 68.4 %collective-permute-start.17 = (bf16[16,32,256]{2,1,0:T(8,128)(2,1)}, bf16[16,32,256]{2,1,0:T(8,128)(2,1)S(1)}, u32[]{:S(2)}, u32[]{:S(2)}) collective-permute-start(bf16[16,32,256]{2,1,0:T(8,128)(2,1)} %add_convert_fusion.1), channel_id=1, source_target_pairs={{0,1},{1,0},{2,3},{3,2},{4,5},{5,4},{6,7},{7,6},{8,9},{9,8},{10,11... | collective-permute-start | bytes 786440 | tf_op jit(solution)/shard_map/ppermute | solution.py:475
  46.2 18.0 %all-to-all-start = ((bf16[16,32,256]{2,1,0:T(8,128)(2,1)}), bf16[16,32,256]{2,1,0:T(8,128)(2,1)S(1)}, u32[]{:S(2)}, u32[]{:S(2)}) async-start(bf16[16,32,256]{2,1,0:T(8,128)(2,1)} %bitcast.30), calls=%async_computation | async-start | bytes 524288 | tf_op jit(solution)/shard_map/all_to_all | solution.py:900
  57.3 54.9 %copy-start.19 = (f32[2,32,1024]{2,1,0:T(8,128)}, f32[2,32,1024]{2,1,0:T(8,128)S(1)}, u32[]{:S(2)}) copy-start(f32[2,32,1024]{2,1,0:T(8,128)S(1)} %pad_maximum_fusion.5.refs_5_.refs_6_) | copy-start | bytes 786436
  58.8 15.7 %copy-start.23 = (f32[32,1024]{1,0:T(8,128)}, f32[32,1024]{1,0:T(8,128)S(1)}, u32[]{:S(2)}) copy-start(f32[32,1024]{1,0:T(8,128)S(1)} %pad_maximum_fusion.7.refs_6_.refs_7_) | copy-start | bytes 393220
  64.4 47.8 %copy-start.21 = (bf16[16,32,256]{2,0,1:T(8,128)(2,1)}, bf16[16,32,256]{2,0,1:T(8,128)(2,1)S(1)}, u32[]{:S(2)}) copy-start(bf16[16,32,256]{2,0,1:T(8,128)(2,1)S(1)} %copy.390) | copy-start | bytes 786436
  66.0 26.6 %collective-permute-start.10 = (bf16[4,32,3072]{2,1,0:T(8,128)(2,1)S(1)}, bf16[4,32,3072]{2,1,0:T(8,128)(2,1)S(1)}, u32[]{:S(2)}, u32[]{:S(2)}) collective-permute-start(bf16[4,32,3072]{2,1,0:T(8,128)(2,1)S(1)} %bitcast.346), channel_id=1, source_target_pairs={{0,2},{1,3},{2,0},{3,1},{4,6},{5,7},{6,4},{7,5},{8,10},{9,11},{10,... | collective-permute-start | bytes 2359304 | tf_op jit(solution)/shard_map/ppermute | solution.py:475
  69.4 23.8 %collective-permute-start.14 = (bf16[4,96,1024]{2,1,0:T(8,128)(2,1)S(1)}, bf16[4,96,1024]{2,1,0:T(8,128)(2,1)S(1)}, u32[]{:S(2)}, u32[]{:S(2)}) collective-permute-start(bf16[4,96,1024]{2,1,0:T(8,128)(2,1)S(1)} %bitcast.372), channel_id=1, source_target_pairs={{0,4},{1,5},{2,6},{3,7},{4,0},{5,1},{6,2},{7,3},{8,12},{9,13},{10,... | collective-permute-start | bytes 2359304 | tf_op jit(solution)/shard_map/ppermute | solution.py:475
  72.0 19.8 %collective-permute-start.15 = (bf16[4,16,3072]{2,1,0:T(8,128)(2,1)S(1)}, bf16[4,16,3072]{2,1,0:T(8,128)(2,1)S(1)}, u32[]{:S(2)}, u32[]{:S(2)}) collective-permute-start(bf16[4,16,3072]{2,1,0:T(8,128)(2,1)S(1)} %bitcast.363), channel_id=1, source_target_pairs={{0,16},{1,17},{2,18},{3,19},{4,20},{5,21},{6,22},{7,23},{8,24},{9,... | collective-permute-start | bytes 1179656 | tf_op jit(solution)/shard_map/ppermute | solution.py:475
  92.1 19.1 %collective-permute-start.16 = (bf16[8,16,3072]{2,1,0:T(8,128)(2,1)S(1)}, bf16[8,16,3072]{2,1,0:T(8,128)(2,1)S(1)}, u32[]{:S(2)}, u32[]{:S(2)}) collective-permute-start(bf16[8,16,3072]{2,1,0:T(8,128)(2,1)S(1)} %bitcast.389), channel_id=1, source_target_pairs={{0,8},{1,9},{2,10},{3,11},{4,12},{5,13},{6,14},{7,15},{8,0},{9,1},... | collective-permute-start | bytes 2359304 | tf_op jit(solution)/shard_map/ppermute | solution.py:475
  93.7 36.2 %collective-permute-start.19 = (bf16[8,32,3072]{2,1,0:T(8,128)(2,1)S(1)}, bf16[8,32,3072]{2,1,0:T(8,128)(2,1)}, u32[]{:S(2)}, u32[]{:S(2)}) collective-permute-start(bf16[8,32,3072]{2,1,0:T(8,128)(2,1)S(1)} %bitcast.384), channel_id=1, source_target_pairs={{0,4},{1,5},{2,6},{3,7},{4,0},{5,1},{6,2},{7,3},{8,12},{9,13},{10,... | collective-permute-start | bytes 4718600 | tf_op jit(solution)/shard_map/ppermute | solution.py:475
  94.3 38.4 %collective-permute-start.22 = (bf16[8,96,1024]{2,1,0:T(8,128)(2,1)S(1)}, bf16[8,96,1024]{2,1,0:T(8,128)(2,1)S(1)}, u32[]{:S(2)}, u32[]{:S(2)}) collective-permute-start(bf16[8,96,1024]{2,1,0:T(8,128)(2,1)S(1)} %bitcast.353), channel_id=1, source_target_pairs={{0,2},{1,3},{2,0},{3,1},{4,6},{5,7},{6,4},{7,5},{8,10},{9,11},{10,... | collective-permute-start | bytes 4718600 | tf_op jit(solution)/shard_map/ppermute | solution.py:475
  112.1 22.6 %copy-start = (bf16[2,2,4,16,3072]{4,3,2,1,0:T(8,128)(2,1)}, bf16[2,2,4,16,3072]{4,3,2,1,0:T(8,128)(2,1)S(1)}, u32[]{:S(2)}) copy-start(bf16[2,2,4,16,3072]{4,3,2,1,0:T(8,128)(2,1)S(1)} %maximum_select_fusion.4) | copy-start | bytes 4718596
  132.6 18.2 %collective-permute-start.20 = (bf16[16,32,3072]{2,1,0:T(8,128)(2,1)S(1)}, bf16[16,32,3072]{2,1,0:T(8,128)(2,1)S(1)}, u32[]{:S(2)}, u32[]{:S(2)}) collective-permute-start(bf16[16,32,3072]{2,1,0:T(8,128)(2,1)S(1)} %bitcast.415), channel_id=1, source_target_pairs={{0,1},{1,0},{2,3},{3,2},{4,5},{5,4},{6,7},{7,6},{8,9},{9,8},{10,11... | collective-permute-start | bytes 9437192 | tf_op jit(solution)/shard_map/ppermute | solution.py:475
  134.6 19.0 %copy-start.37 = (bf16[8,2,1,96,1024]{4,3,1,0,2:T(8,128)(2,1)}, bf16[8,2,1,96,1024]{4,3,1,0,2:T(8,128)(2,1)S(1)}, u32[]{:S(2)}) copy-start(bf16[8,2,1,96,1024]{4,3,1,0,2:T(8,128)(2,1)S(1)} %copy.338) | copy-start | bytes 9437188
  134.6 19.3 %copy-start.1 = (bf16[1,256,1024]{2,1,0:T(8,128)(2,1)S(1)}, bf16[1,256,1024]{2,1,0:T(8,128)(2,1)}, u32[]{:S(2)}) copy-start(bf16[1,256,1024]{2,1,0:T(8,128)(2,1)} %param.24) | copy-start | bytes 1572868
  134.7 16.2 %collective-permute-start.23 = (bf16[16,96,1024]{2,1,0:T(8,128)(2,1)S(1)}, bf16[16,96,1024]{2,1,0:T(8,128)(2,1)S(1)}, u32[]{:S(2)}, u32[]{:S(2)}) collective-permute-start(bf16[16,96,1024]{2,1,0:T(8,128)(2,1)S(1)} %bitcast.412), channel_id=1, source_target_pairs={{0,1},{1,0},{2,3},{3,2},{4,5},{5,4},{6,7},{7,6},{8,9},{9,8},{10,11... | collective-permute-start | bytes 9437192 | tf_op jit(solution)/shard_map/ppermute | solution.py:475
  134.7 16.1 %collective-permute-start.21 = (bf16[16,16,3072]{2,1,0:T(8,128)(2,1)S(1)}, bf16[16,16,3072]{2,1,0:T(8,128)(2,1)S(1)}, u32[]{:S(2)}, u32[]{:S(2)}) collective-permute-start(bf16[16,16,3072]{2,1,0:T(8,128)(2,1)S(1)} %bitcast.351), channel_id=1, source_target_pairs={{0,1},{1,0},{2,3},{3,2},{4,5},{5,4},{6,7},{7,6},{8,9},{9,8},{10,11... | collective-permute-start | bytes 4718600 | tf_op jit(solution)/shard_map/ppermute | solution.py:475
  150.8 18.3 %copy-start.2 = (bf16[16,1,1,16,256]{4,3,1,0,2:T(8,128)(2,1)}, bf16[16,1,1,16,256]{4,3,1,0,2:T(8,128)(2,1)S(1)}, u32[]{:S(2)}) copy-start(bf16[16,1,1,16,256]{4,3,1,0,2:T(8,128)(2,1)S(1)} %get-tuple-element.343) | copy-start | bytes 393220
  170.8 3.4 %collective-permute-start.24 = (bf16[16,96,256]{2,1,0:T(8,128)(2,1)S(1)}, bf16[16,96,256]{2,1,0:T(8,128)(2,1)S(1)}, u32[]{:S(2)}, u32[]{:S(2)}) collective-permute-start(bf16[16,96,256]{2,1,0:T(8,128)(2,1)S(1)} %get-tuple-element.129), channel_id=1, source_target_pairs={{0,1},{1,0},{2,3},{3,2},{4,5},{5,4},{6,7},{7,6},{8,9},{9,8},{10,11... | collective-permute-start | bytes 2359304 | tf_op jit(solution)/shard_map/ppermute | solution.py:475
  170.8 30.0 %collective-permute-start.27 = (bf16[256,3072]{1,0:T(8,128)(2,1)}, bf16[256,3072]{1,0:T(8,128)(2,1)}, u32[]{:S(2)}, u32[]{:S(2)}) collective-permute-start(bf16[256,3072]{1,0:T(8,128)(2,1)} %get-tuple-element.133.own), channel_id=1, source_target_pairs={{0,1},{1,0},{2,3},{3,2},{4,5},{5,4},{6,7},{7,6},{8,9},{9,8},{10,11... | collective-permute-start | bytes 4718600 | tf_op jit(solution)/shard_map/ppermute | solution.py:475
  174.2 31.2 %collective-permute-start.25 = (bf16[256,3072]{1,0:T(8,128)(2,1)}, bf16[256,3072]{1,0:T(8,128)(2,1)}, u32[]{:S(2)}, u32[]{:S(2)}) collective-permute-start(bf16[256,3072]{1,0:T(8,128)(2,1)} %get-tuple-element.130.own), channel_id=1, source_target_pairs={{0,1},{1,0},{2,3},{3,2},{4,5},{5,4},{6,7},{7,6},{8,9},{9,8},{10,11... | collective-permute-start | bytes 4718600 | tf_op jit(solution)/shard_map/ppermute | solution.py:475
  179.1 15.0 %all-to-all-start.2 = ((bf16[16,32,256]{2,1,0:T(8,128)(2,1)}), bf16[16,32,256]{2,1,0:T(8,128)(2,1)}, u32[]{:S(2)}, u32[]{:S(2)}) async-start(bf16[16,32,256]{2,1,0:T(8,128)(2,1)} %bitcast.81), calls=%async_computation.2 | async-start | bytes 524288 | tf_op jit(solution)/shard_map/all_to_all | solution.py:985
  188.0 12.8 %collective-permute-start.26 = (bf16[16,16,256]{2,1,0:T(8,128)(2,1)}, bf16[16,16,256]{2,1,0:T(8,128)(2,1)}, u32[]{:S(2)}, u32[]{:S(2)}) collective-permute-start(bf16[16,16,256]{2,1,0:T(8,128)(2,1)} %bitcast.93), channel_id=1, source_target_pairs={{0,1},{1,0},{2,3},{3,2},{4,5},{5,4},{6,7},{7,6},{8,9},{9,8},{10,11... | collective-permute-start | bytes 393224 | tf_op jit(solution)/shard_map/ppermute | solution.py:475
  200.0 45.4 %collective-permute-start.30 = (bf16[8,96,1024]{2,1,0:T(8,128)(2,1)}, bf16[8,96,1024]{2,1,0:T(8,128)(2,1)}, u32[]{:S(2)}, u32[]{:S(2)}) collective-permute-start(bf16[8,96,1024]{2,1,0:T(8,128)(2,1)} %bitcast.90.refs_11_), channel_id=1, source_target_pairs={{0,2},{1,3},{2,0},{3,1},{4,6},{5,7},{6,4},{7,5},{8,10},{9,11},{10,... | collective-permute-start | bytes 4718600 | tf_op jit(solution)/shard_map/ppermute | solution.py:475
  204.5 26.4 %collective-permute-start.28 = (bf16[8,16,3072]{2,1,0:T(8,128)(2,1)S(1)}, bf16[8,16,3072]{2,1,0:T(8,128)(2,1)S(1)}, u32[]{:S(2)}, u32[]{:S(2)}) collective-permute-start(bf16[8,16,3072]{2,1,0:T(8,128)(2,1)S(1)} %bitcast.403), channel_id=1, source_target_pairs={{0,8},{1,9},{2,10},{3,11},{4,12},{5,13},{6,14},{7,15},{8,0},{9,1},... | collective-permute-start | bytes 2359304 | tf_op jit(solution)/shard_map/ppermute | solution.py:475
  210.7 41.6 %collective-permute-start.29 = (bf16[8,32,3072]{2,1,0:T(8,128)(2,1)}, bf16[8,32,3072]{2,1,0:T(8,128)(2,1)}, u32[]{:S(2)}, u32[]{:S(2)}) collective-permute-start(bf16[8,32,3072]{2,1,0:T(8,128)(2,1)} %bitcast.86.refs_10_), channel_id=1, source_target_pairs={{0,4},{1,5},{2,6},{3,7},{4,0},{5,1},{6,2},{7,3},{8,12},{9,13},{10,... | collective-permute-start | bytes 4718600 | tf_op jit(solution)/shard_map/ppermute | solution.py:475
  232.0 39.1 %collective-permute-start.42 = (bf16[4,16,3072]{2,1,0:T(8,128)(2,1)}, bf16[4,16,3072]{2,1,0:T(8,128)(2,1)}, u32[]{:S(2)}, u32[]{:S(2)}) collective-permute-start(bf16[4,16,3072]{2,1,0:T(8,128)(2,1)} %fusion.27.refs_11_), channel_id=1, source_target_pairs={{0,16},{1,17},{2,18},{3,19},{4,20},{5,21},{6,22},{7,23},{8,24},{9,... | collective-permute-start | bytes 1179656 | tf_op jit(solution)/shard_map/ppermute | solution.py:475
  240.5 17.9 %all-to-all-start.3 = ((bf16[32,16,256]{2,0,1:T(8,128)(2,1)}), bf16[32,16,256]{2,0,1:T(8,128)(2,1)}, u32[]{:S(2)}, u32[]{:S(2)}) async-start(bf16[32,16,256]{2,0,1:T(8,128)(2,1)} %copy.346), calls=%async_computation.3 | async-start | bytes 524288 | tf_op jit(solution)/shard_map/all_to_all | solution.py:1007
  245.5 6.1 %collective-permute-start.47 = (f32[2,32,512]{2,1,0:T(8,128)S(1)}, f32[2,32,512]{2,1,0:T(8,128)S(1)}, u32[]{:S(2)}, u32[]{:S(2)}) collective-permute-start(f32[2,32,512]{2,1,0:T(8,128)S(1)} %pad_maximum_fusion.8), channel_id=1, source_target_pairs={{0,1},{1,0},{2,3},{3,2},{4,5},{5,4},{6,7},{7,6},{8,9},{9,8},{10,11... | collective-permute-start | bytes 393224 | tf_op jit(solution)/shard_map/ppermute | solution.py:475
  249.6 21.4 %collective-permute-start.33 = (bf16[4,96,1024]{2,1,0:T(8,128)(2,1)}, bf16[4,96,1024]{2,1,0:T(8,128)(2,1)}, u32[]{:S(2)}, u32[]{:S(2)}) collective-permute-start(bf16[4,96,1024]{2,1,0:T(8,128)(2,1)} %fusion.10), channel_id=1, source_target_pairs={{0,4},{1,5},{2,6},{3,7},{4,0},{5,1},{6,2},{7,3},{8,12},{9,13},{10,... | collective-permute-start | bytes 2359304 | tf_op jit(solution)/shard_map/ppermute | solution.py:475
  257.0 27.1 %collective-permute-start.32 = (bf16[4,32,3072]{2,1,0:T(8,128)(2,1)}, bf16[4,32,3072]{2,1,0:T(8,128)(2,1)}, u32[]{:S(2)}, u32[]{:S(2)}) collective-permute-start(bf16[4,32,3072]{2,1,0:T(8,128)(2,1)} %fusion.9), channel_id=1, source_target_pairs={{0,2},{1,3},{2,0},{3,1},{4,6},{5,7},{6,4},{7,5},{8,10},{9,11},{10,... | collective-permute-start | bytes 2359304 | tf_op jit(solution)/shard_map/ppermute | solution.py:475
  264.9 13.3 %collective-permute-start.31 = (bf16[16,32,640]{2,1,0:T(8,128)(2,1)S(1)}, bf16[16,32,640]{2,1,0:T(8,128)(2,1)S(1)}, u32[]{:S(2)}, u32[]{:S(2)}) collective-permute-start(bf16[16,32,640]{2,1,0:T(8,128)(2,1)S(1)} %bitcast.405), channel_id=1, source_target_pairs={{0,1},{1,0},{2,3},{3,2},{4,5},{5,4},{6,7},{7,6},{8,9},{9,8},{10,11... | collective-permute-start | bytes 1966088 | tf_op jit(solution)/shard_map/ppermute | solution.py:475
  272.9 26.2 %collective-permute-start.43 = (bf16[2,16,3072]{2,1,0:T(8,128)(2,1)}, bf16[2,16,3072]{2,1,0:T(8,128)(2,1)}, u32[]{:S(2)}, u32[]{:S(2)}) collective-permute-start(bf16[2,16,3072]{2,1,0:T(8,128)(2,1)} %fusion.38), channel_id=1, source_target_pairs={{0,4},{1,5},{2,6},{3,7},{4,0},{5,1},{6,2},{7,3},{8,12},{9,13},{10,... | collective-permute-start | bytes 589832 | tf_op jit(solution)/shard_map/ppermute | solution.py:475
  276.8 25.5 %collective-permute-start.45 = (bf16[2,96,1024]{2,1,0:T(8,128)(2,1)}, bf16[2,96,1024]{2,1,0:T(8,128)(2,1)S(1)}, u32[]{:S(2)}, u32[]{:S(2)}) collective-permute-start(bf16[2,96,1024]{2,1,0:T(8,128)(2,1)} %fusion.29), channel_id=1, source_target_pairs={{0,8},{1,9},{2,10},{3,11},{4,12},{5,13},{6,14},{7,15},{8,0},{9,1},... | collective-permute-start | bytes 1179656 | tf_op jit(solution)/shard_map/ppermute | solution.py:475
  286.9 8.1 %collective-permute-start.37 = (bf16[4,32,640]{2,1,0:T(8,128)(2,1)S(1)}, bf16[4,32,640]{2,1,0:T(8,128)(2,1)S(1)}, u32[]{:S(2)}, u32[]{:S(2)}) collective-permute-start(bf16[4,32,640]{2,1,0:T(8,128)(2,1)S(1)} %get-tuple-element.337), channel_id=1, source_target_pairs={{0,6},{1,7},{2,4},{3,5},{4,2},{5,3},{6,0},{7,1},{8,14},{9,15},{10,... | collective-permute-start | bytes 491528 | tf_op jit(solution)/shard_map/ppermute | solution.py:475
  288.4 7.3 %collective-permute-start.36 = (bf16[4,32,640]{2,1,0:T(8,128)(2,1)S(1)}, bf16[4,32,640]{2,1,0:T(8,128)(2,1)S(1)}, u32[]{:S(2)}, u32[]{:S(2)}) collective-permute-start(bf16[4,32,640]{2,1,0:T(8,128)(2,1)S(1)} %get-tuple-element.336), channel_id=1, source_target_pairs={{0,2},{1,3},{2,0},{3,1},{4,6},{5,7},{6,4},{7,5},{8,10},{9,11},{10,... | collective-permute-start | bytes 491528 | tf_op jit(solution)/shard_map/ppermute | solution.py:475
  288.8 7.9 %collective-permute-start.35 = (bf16[4,32,640]{2,1,0:T(8,128)(2,1)S(1)}, bf16[4,32,640]{2,1,0:T(8,128)(2,1)S(1)}, u32[]{:S(2)}, u32[]{:S(2)}) collective-permute-start(bf16[4,32,640]{2,1,0:T(8,128)(2,1)S(1)} %fusion.40), channel_id=1, source_target_pairs={{0,4},{1,5},{2,6},{3,7},{4,0},{5,1},{6,2},{7,3},{8,12},{9,13},{10,... | collective-permute-start | bytes 491528 | tf_op jit(solution)/shard_map/ppermute | solution.py:475
  295.0 22.1 %collective-permute-start.34 = (bf16[2,32,3072]{2,1,0:T(8,128)(2,1)}, bf16[2,32,3072]{2,1,0:T(8,128)(2,1)}, u32[]{:S(2)}, u32[]{:S(2)}) collective-permute-start(bf16[2,32,3072]{2,1,0:T(8,128)(2,1)} %fusion.28), channel_id=1, source_target_pairs={{0,8},{1,9},{2,10},{3,11},{4,12},{5,13},{6,14},{7,15},{8,0},{9,1},... | collective-permute-start | bytes 1179656 | tf_op jit(solution)/shard_map/ppermute | solution.py:475
  296.8 13.7 %collective-permute-start.41 = (f32[1,32,640]{2,1,0:T(8,128)S(1)}, f32[1,32,640]{2,1,0:T(8,128)S(1)}, u32[]{:S(2)}, u32[]{:S(2)}) collective-permute-start(f32[1,32,640]{2,1,0:T(8,128)S(1)} %get-tuple-element.334), channel_id=1, source_target_pairs={{0,24},{1,25},{2,26},{3,27},{4,28},{5,29},{6,30},{7,31},{8,16},{9,... | collective-permute-start | bytes 245768 | tf_op jit(solution)/shard_map/ppermute | solution.py:475
  299.1 11.4 %collective-permute-start.39 = (f32[1,32,640]{2,1,0:T(8,128)S(1)}, f32[1,32,640]{2,1,0:T(8,128)S(1)}, u32[]{:S(2)}, u32[]{:S(2)}) collective-permute-start(f32[1,32,640]{2,1,0:T(8,128)S(1)} %get-tuple-element.335), channel_id=1, source_target_pairs={{0,16},{1,17},{2,18},{3,19},{4,20},{5,21},{6,22},{7,23},{8,24},{9,... | collective-permute-start | bytes 245768 | tf_op jit(solution)/shard_map/ppermute | solution.py:475
  299.1 11.4 %collective-permute-start.40 = (f32[1,32,640]{2,1,0:T(8,128)S(1)}, f32[1,32,640]{2,1,0:T(8,128)S(1)}, u32[]{:S(2)}, u32[]{:S(2)}) collective-permute-start(f32[1,32,640]{2,1,0:T(8,128)S(1)} %get-tuple-element.333), channel_id=1, source_target_pairs={{0,8},{1,9},{2,10},{3,11},{4,12},{5,13},{6,14},{7,15},{8,0},{9,1},... | collective-permute-start | bytes 245768 | tf_op jit(solution)/shard_map/ppermute | solution.py:475
  303.1 11.9 %collective-permute-start.44 = (bf16[1,16,3072]{2,1,0:T(8,128)(2,1)S(1)}, bf16[1,16,3072]{2,1,0:T(8,128)(2,1)}, u32[]{:S(2)}, u32[]{:S(2)}) collective-permute-start(bf16[1,16,3072]{2,1,0:T(8,128)(2,1)S(1)} %dynamic-slice_convert_fusion.7), channel_id=1, source_target_pairs={{0,2},{1,3},{2,0},{3,1},{4,6},{5,7},{6,4},{7,5},{8,10},{9,11},{10,... | collective-permute-start | bytes 294920 | tf_op jit(solution)/shard_map/ppermute | solution.py:475
  310.5 11.2 %collective-permute-start.46 = (bf16[1,96,1024]{2,1,0:T(8,128)(2,1)}, bf16[1,96,1024]{2,1,0:T(8,128)(2,1)}, u32[]{:S(2)}, u32[]{:S(2)}) collective-permute-start(bf16[1,96,1024]{2,1,0:T(8,128)(2,1)} %dynamic-slice_convert_fusion.3), channel_id=1, source_target_pairs={{0,16},{1,17},{2,18},{3,19},{4,20},{5,21},{6,22},{7,23},{8,24},{9,... | collective-permute-start | bytes 589832 | tf_op jit(solution)/shard_map/ppermute | solution.py:475
  318.2 9.1 %collective-permute-start.38 = (bf16[1,32,3072]{2,1,0:T(8,128)(2,1)S(1)}, bf16[1,32,3072]{2,1,0:T(8,128)(2,1)S(1)}, u32[]{:S(2)}, u32[]{:S(2)}) collective-permute-start(bf16[1,32,3072]{2,1,0:T(8,128)(2,1)S(1)} %dynamic-slice_convert_fusion.5), channel_id=1, source_target_pairs={{0,16},{1,17},{2,18},{3,19},{4,20},{5,21},{6,22},{7,23},{8,24},{9,... | collective-permute-start | bytes 589832 | tf_op jit(solution)/shard_map/ppermute | solution.py:475
  (83 other events, 417.5 us)

commit v4 on v3

--- a/solution.py
+++ b/solution.py
@@ -922,9 +922,9 @@
         token = mixer.run(*waits)
         return [] if token is None else [token]
 
-    up.take(channel_values)
-    down.take(channel_values)
-    expand.take(channel_values)
+    up.take(powers)
+    down.take(powers)
+    expand.take(powers)
     up.send()
     down.send()
     expand.send()
@@ -1000,10 +1000,12 @@
     states = param_grad.shape[1] // 2
     param_grad = jnp.stack([param_grad[:channels, :states], param_grad[:channels, states:]])
     param_sum = param_grad + cube.swap(param_grad, 0)
+    mixed = value_grad_channels
     for _ in range(nx):
         for sums in (down_sums, up_sums):
-            sums.take(value_grad_channels)
+            sums.take(mixed)
             sums.send()
+    value_grad_channels = after(value_grad_channels, down_sums.sent, up_sums.sent)
     value_grad = lax.all_to_all(
         value_grad_channels.reshape(channels, length),
         "tok",
@@ -1011,7 +1013,10 @@
         concat_axis=0,
         tiled=True,
     )
-    value_grad = after(value_grad, up_sums.sent, down_sums.sent)
+    for _ in range(nx):
+        down_sums.take(value_grad_channels)
+        down_sums.send()
+    value_grad = after(value_grad, down_sums.sent)
     keep, send, normed_grads = value_grads(
         inner,
         value_grad,
@@ -1026,15 +1031,17 @@
     packed_sum = keep + cube.swap(send, 0).astype(jnp.float32)
     core_sum = packed_sum
     for _ in range(nx):
-        for sums in (down_sums, up_sums, expand_sums):
+        for sums in (up_sums, expand_sums):
             sums.take(send)
             sums.send()
     packed_sum = after(packed_sum, up_sums.sent, down_sums.sent)
-    normed_grads = [after(g, core_sum) for g in normed_grads]
+    packed_sum = direct_sum(cube, packed_sum, tok_bits, xs + ys, low)
     gated_late = after(gated_sides[0], packed_sum), gated_sides[1]
     layer_out = (token_rows + dots(gated_late, downs, 0, 0)).astype(low)[None]
-    packed_sum = direct_sum(cube, packed_sum, tok_bits, xs + ys, low)
-    for sums in (down_sums, up_sums, expand_sums):
+    normed_grads = [after(g, packed_sum) for g in normed_grads]
+    down_sums.take(core_sum)
+    down_sums.send()
+    for sums in (up_sums, expand_sums):
         sums.take(packed_sum)
         sums.send()
     packed_sum = direct_sum(cube, packed_sum, zs, zs, jnp.float32)[0]
@@ -1061,6 +1068,9 @@
     down_next, down_mean_next, down_square_next = adam_step(
         down_weight, down_sum, down_mean, down_square, step_value, 0.08, 0.1
     )
+    norm_params, norm_mean, norm_square = lax.optimization_barrier(
+        (norm_params, norm_mean, norm_square, core_sum)
+    )[:3]
     norm_next, norm_mean_next, norm_square_next = adam_step(
         norm_params, norm_sum, norm_mean, norm_square, step_value, 1.0, 0.0
     )

time: 335 us -> 331 us (0.988)
  waiting for transfers between devices: 47.9 us -> 39.6 us
    ppermute x48, waiting for transfers between devices: 43.4 us -> 33.8 us  [trade(): return lax.ppermute(block, ('tok', 'rep'), pairs)]
    unnamed x196 -> x217, local copies, waits for them, and re-layouts: 19.9 us -> 21.9 us
  transfers between devices with their start and end apart: 51 -> 51, of which waited for: 14 -> 14; matrix products, arithmetic and copies ran while one was open for 27% -> 28% of each run, Pallas kernels for 22% -> 23%
where the time goes in v4:
time: 331 us; the launch traced here: 325 us
  Pallas kernels  90 us (27%)
  starting transfers between devices  64.3 us (19%)
  other arithmetic  58.7 us (18%)
  local copies, waits for them, and re-layouts  46.1 us (14%)
  waiting for transfers between devices  39.6 us (12%)
  blocking collectives  14.8 us (4%)
  matrix products  8.57 us (3%)
    pallas_call x8, Pallas kernels, call(): pl.pallas_call(body, grid=(1,), in_specs=specs + [pl.BlockSpec(memory_spa...  57.5 us
    ppermute x48, starting transfers between devices, trade(): return lax.ppermute(block, ('tok', 'rep'), pairs)  49.3 us
    ppermute x48, waiting for transfers between devices, trade(): return lax.ppermute(block, ('tok', 'rep'), pairs)  33.8 us
    unnamed x217, local copies, waits for them, and re-layouts  21.9 us
    select_n x23, other arithmetic, join(): jnp.where(self.cube.bit(b) == 1, jnp.concatenate([second, first], axis=1)...  17.4 us
    pallas_call x1, Pallas kernels, gate(): pl.pallas_call(body, grid=(hidden // block,), in_specs=[pl.BlockSpec(memo...  15.2 us
    all_to_all x1, blocking collectives, per_device(): lax.all_to_all(state_out.reshape(channels, length), 'tok', split_axis=1,...  14.8 us
    pallas_call x3, Pallas kernels, products(): pl.pallas_call(products_kernel, grid_spec=pltpu.PrefetchScalarGridSpec(nu...  14.1 us
  transfers between devices with their start and end apart: 51, of which 14 were waited for; matrix products, arithmetic and copies ran while one was open for 28% of the time, Pallas kernels for 23%

profile of v4, /device:TPU:0, one launch (start us, length us, event | category | flops | bytes accessed | tf_op | source)
XLA Modules:
  0.0 324.6 jit_solution(15505369802914208646)
XLA Ops:
  2.4 3.1 collective-permute-start.2
  5.5 2.6 collective-permute-start.1
  9.1 1.8 collective-permute-start.12
  15.8 1.7 collective-permute-start.4
  17.5 1.4 collective-permute-start.3
  19.0 1.7 collective-permute-start.7
  22.5 1.7 collective-permute-start.8
  24.9 2.4 collective-permute-start.13
  30.6 5.3 %collective-permute-done.7 = bf16[1,32,3072]{2,1,0:T(8,128)(2,1)S(1)} collective-permute-done((bf16[1,32,3072]{2,1,0:T(8,128)(2,1)S(1)}, bf16[1,32,3072]{2,1,0:T(8,128)(2,1)S(1)}, u32[]{:S(2)}, u32[]{:S(2)}) %collective-permute-start.7) | collective-permute-done | bytes 196640 | tf_op jit(solution)/shard_map/ppermute | solution.py:475
  36.7 2.4 collective-permute-done.8
  41.4 1.9 fusion.23
  44.4 2.4 fusion.18
  46.8 5.7 %all-to-all-start = ((bf16[16,32,256]{2,1,0:T(8,128)(2,1)}), bf16[16,32,256]{2,1,0:T(8,128)(2,1)}, u32[]{:S(2)}, u32[]{:S(2)}) async-start(bf16[16,32,256]{2,1,0:T(8,128)(2,1)} %bitcast.30), calls=%async_computation | async-start | bytes 524288 | tf_op jit(solution)/shard_map/all_to_all | solution.py:900
  52.6 3.9 %fusion.4 = (f32[32,16,512]{2,0,1:T(8,128)S(1)}, f32[32,16,512]{2,0,1:T(8,128)S(1)}) fusion(f32[32,512]{1,0:T(8,128)S(1)} %get-tuple-element.366, f32[16]{0:T(128)S(1)} %copy-done.106, f32[32,512]{1,0:T(8,128)S(1)} %get-tuple-element.367), kind=kLoop, calls=%fused_computation.31 | loop fusion | flops 1048576 | bytes 2228288 | tf_op jit(solution)/shard_map/mul | solution.py:64
  56.6 2.7 copy.328.refs_4_.refs_5_
  60.7 2.1 collective-permute-start.10
  64.0 1.5 collective-permute-start.14
  66.6 2.4 collective-permute-start.15
  70.9 1.7 copy-done.7
  74.3 7.7 %mix_forward.4 = (bf16[32,16,256]{2,1,0:T(8,128)(2,1)S(1)}, f32[1536,1024]{1,0:T(8,128)}, bf16[32,128,128]{2,1,0:T(8,128)(2,1)S(1)}, f32[8,128]{1,0:T(8,128)}) custom-call(f32[48]{0:T(128)S(1)} %add_convert_fusion.6.refs_0_, bf16[2,48,16]{2,1,0:T(8,128)(2,1)S(1)} %copy-done.28, bf16[48,128]{1,0:T(8,128)(2,1)S(1)} %fusion.54.refs_2_, ...), custom_call_target="tpu_custom_call" | custom-call | flops 8000000000 | bytes 4194304 | tf_op jit(solution)/shard_map/mix_forward/pallas_call | solution.py:324
  82.0 4.4 %collective-permute-done.15 = bf16[4,16,3072]{2,1,0:T(8,128)(2,1)} collective-permute-done((bf16[4,16,3072]{2,1,0:T(8,128)(2,1)S(1)}, bf16[4,16,3072]{2,1,0:T(8,128)(2,1)}, u32[]{:S(2)}, u32[]{:S(2)}) %collective-permute-start.15) | collective-permute-done | bytes 393248 | tf_op jit(solution)/shard_map/ppermute | solution.py:475
  89.3 1.6 maximum_select_fusion.2
  91.1 1.6 maximum_select_fusion.5
  92.7 1.6 maximum_select_fusion.3
  95.6 8.2 %mix_forward.5 = (bf16[32,16,256]{2,1,0:T(8,128)(2,1)S(1)}, f32[1536,1024]{1,0:T(8,128)}, bf16[32,128,128]{2,1,0:T(8,128)(2,1)S(1)}, f32[8,128]{1,0:T(8,128)S(1)}) custom-call(f32[48]{0:T(128)S(1)} %add_convert_fusion.6.refs_0_, bf16[2,48,16]{2,1,0:T(8,128)(2,1)S(1)} %copy-done.28, ...), custom_call_target="tpu_custom_call", output_to_operand_aliasing={{0}: (10, {}), {1}: (11, {}), {2}: (12, {})} | custom-call | flops 8000000000 | bytes 4194304 | tf_op jit(solution)/shard_map/mix_forward/pallas_call | solution.py:324
  103.8 7.9 %mix_forward.6 = (bf16[32,16,256]{2,1,0:T(8,128)(2,1)S(1)}, f32[1536,1024]{1,0:T(8,128)}, bf16[32,128,128]{2,1,0:T(8,128)(2,1)S(1)}, f32[8,128]{1,0:T(8,128)S(1)}) custom-call(f32[48]{0:T(128)S(1)} %add_convert_fusion.6.refs_0_, bf16[2,48,16]{2,1,0:T(8,128)(2,1)S(1)} %copy-done.28, ...), custom_call_target="tpu_custom_call", output_to_operand_aliasing={{0}: (8, {}), {1}: (9, {}), {2}: (10, {})} | custom-call | flops 8000000000 | bytes 4194304 | tf_op jit(solution)/shard_map/mix_forward/pallas_call | solution.py:324
  114.6 8.1 %mix_forward.7 = (bf16[32,16,256]{2,1,0:T(8,128)(2,1)S(1)}, f32[1536,1024]{1,0:T(8,128)}, bf16[32,128,128]{2,1,0:T(8,128)(2,1)S(1)}, f32[8,128]{1,0:T(8,128)}) custom-call(f32[48]{0:T(128)S(1)} %add_convert_fusion.6.refs_0_, bf16[2,48,16]{2,1,0:T(8,128)(2,1)S(1)} %copy-done.28, ...), custom_call_target="tpu_custom_call", output_to_operand_aliasing={{0}: (12, {}), {1}: (13, {}), {2}: (14, {})} | custom-call | flops 8000000000 | bytes 4194304 | tf_op jit(solution)/shard_map/mix_forward/pallas_call | solution.py:324
  122.6 8.0 %collective-permute-done.19 = bf16[8,32,3072]{2,1,0:T(8,128)(2,1)} collective-permute-done((bf16[8,32,3072]{2,1,0:T(8,128)(2,1)S(1)}, bf16[8,32,3072]{2,1,0:T(8,128)(2,1)}, u32[]{:S(2)}, u32[]{:S(2)}) %collective-permute-start.19) | collective-permute-done | bytes 1572896 | tf_op jit(solution)/shard_map/ppermute | solution.py:475
  130.6 2.3 maximum_select_fusion
  135.8 14.8 %all_to_all.61 = bf16[32,16,256]{2,0,1:T(8,128)(2,1)S(1)} all-to-all(bf16[32,16,256]{2,0,1:T(8,128)(2,1)S(1)} %copy.330), channel_id=1, replica_groups=mesh['tok'=16,'rep'=2] {'tok'}, dimensions={1} | all-to-all | bytes 524288 | tf_op jit(solution)/shard_map/all_to_all | solution.py:948
  151.3 1.6 copy-done.53
  154.5 15.2 %gate.1 = (bf16[256,3072]{1,0:T(8,128)(2,1)}, bf16[256,3072]{1,0:T(8,128)(2,1)}, bf16[16,96,256]{2,1,0:T(8,128)(2,1)S(1)}, bf16[16,96,256]{2,1,0:T(8,128)(2,1)S(...) custom-call(s32[1]{0:T(128)} %bitcast.1.core, ...), custom_call_target="tpu_custom_call" | custom-call | flops 1000000 | bytes 1024 | tf_op jit(solution)/shard_map/gate/pallas_call | solution.py:689
  171.8 2.9 collective-permute-done.24
  175.6 4.4 %all-to-all-start.2 = ((bf16[16,32,256]{2,1,0:T(8,128)(2,1)}), bf16[16,32,256]{2,1,0:T(8,128)(2,1)}, u32[]{:S(2)}, u32[]{:S(2)}) async-start(bf16[16,32,256]{2,1,0:T(8,128)(2,1)} %bitcast.81), calls=%async_computation.2 | async-start | bytes 524288 | tf_op jit(solution)/shard_map/all_to_all | solution.py:985
  180.1 1.8 bitcast_convert_fusion.4
  184.9 5.8 %all-to-all-done.2 = bf16[16,32,256]{2,1,0:T(8,128)(2,1)} async-done(((bf16[16,32,256]{2,1,0:T(8,128)(2,1)}), bf16[16,32,256]{2,1,0:T(8,128)(2,1)}, u32[]{:S(2)}, u32[]{:S(2)}) %all-to-all-start.2) | async-done | bytes 262176 | tf_op jit(solution)/shard_map/all_to_all | solution.py:985
  191.8 4.7 %weight_grad.4 = (bf16[768,1024]{1,0:T(8,128)(2,1)S(1)}, f32[768,1024]{1,0:T(8,128)}) custom-call(s32[1]{0:T(128)} %bitcast.87.bit_ref, bf16[8,2,96,256]{3,2,1,0:T(8,128)(2,1)S(1)} %bitcast.367, bf16[8,2,96,256]{3,2,1,0:T(8,128)(2,1)S(1)} %bitcast.368, bf16[8,2,96,256]{3,2,1,0:T(8,128)(2,1)S(1)} %bitcast.370, bf16[8,2,96,256]{3,2,1,0:T(8,128)(2,1)S(1)} %bitcast.371, ...), custom_call_target="tpu_custom_call" | custom-call | flops 1000000 | bytes 1024 | tf_op jit(solution)/shard_map/weight_grad/pallas_call | solution.py:796
  197.3 4.1 %weight_grad.5 = (bf16[128,3072]{1,0:T(8,128)(2,1)}, f32[128,3072]{1,0:T(8,128)S(1)}) custom-call(s32[1]{0:T(128)} %bitcast.91.bit_ref, bf16[2,2,64,256]{3,2,1,0:T(8,128)(2,1)S(1)} %bitcast.378, bf16[2,2,64,256]{3,2,1,0:T(8,128)(2,1)S(1)} %bitcast.379, bf16[2,2,64,256]{3,2,1,0:T(8,128)(2,1)} %bitcast.94.got_send.got_keep, ...), custom_call_target="tpu_custom_call" | custom-call | flops 1000000 | bytes 1024 | tf_op jit(solution)/shard_map/weight_grad/pallas_call | solution.py:796
  202.3 5.3 %weight_grad.3 = (bf16[256,3072]{1,0:T(8,128)(2,1)S(1)}, f32[256,3072]{1,0:T(8,128)}) custom-call(s32[1]{0:T(128)} %bitcast.83.bit_ref, bf16[4,2,64,256]{3,2,1,0:T(8,128)(2,1)S(1)} %add_convert_fusion.own_send.own_keep, bf16[4,2,64,256]{3,2,1,0:T(8,128)(2,1)S(1)} %add_convert_fusion.own_send.own_keep, bf16[4,2,64,256]{3,2,1,0:T(8,128)(2,1)S(1)} %bitcast.387, ...), custom_call_target="tpu_custom_call" | custom-call | flops 1000000 | bytes 1024 | tf_op jit(solution)/shard_map/weight_grad/pallas_call | solution.py:796
  208.4 6.6 %mix_backward.4 = (bf16[32,16,256]{2,1,0:T(8,128)(2,1)S(1)}, f32[32,1024]{1,0:T(8,128)S(1)}, f32[8,128]{1,0:T(8,128)S(1)}) custom-call(f32[48]{0:T(128)S(1)} %add_convert_fusion.6.refs_0_, bf16[2,48,16]{2,1,0:T(8,128)(2,1)S(1)} %copy-done.29, bf16[48,128]{1,0:T(8,128)(2,1)S(1)} %fusion.54.refs_2_, bf16[32,16,256]{2,1,0:T(8,128)(2,1)S(1)} %bitcast.396, ...), custom_call_target="tpu_custom_call" | custom-call | flops 10700000256 | bytes 4194304 | tf_op jit(solution)/shard_map/mix_backward/pallas_call | solution.py:324
  215.0 6.3 %mix_backward.5 = (bf16[32,16,256]{2,1,0:T(8,128)(2,1)S(1)}, f32[32,1024]{1,0:T(8,128)S(1)}, f32[8,128]{1,0:T(8,128)S(1)}) custom-call(f32[48]{0:T(128)S(1)} %add_convert_fusion.6.refs_0_, bf16[2,48,16]{2,1,0:T(8,128)(2,1)S(1)} %copy-done.29, bf16[48,128]{1,0:T(8,128)(2,1)S(1)} %fusion.54.refs_2_, ...), custom_call_target="tpu_custom_call", output_to_operand_aliasing={{0}: (11, {}), {1}: (12, {})} | custom-call | flops 10700000256 | bytes 4194304 | tf_op jit(solution)/shard_map/mix_backward/pallas_call | solution.py:324
  221.2 6.5 %mix_backward.6 = (bf16[32,16,256]{2,1,0:T(8,128)(2,1)S(1)}, f32[32,1024]{1,0:T(8,128)S(1)}, f32[8,128]{1,0:T(8,128)S(1)}) custom-call(f32[48]{0:T(128)S(1)} %add_convert_fusion.6.refs_0_, bf16[2,48,16]{2,1,0:T(8,128)(2,1)S(1)} %copy-done.29, bf16[48,128]{1,0:T(8,128)(2,1)S(1)} %fusion.54.refs_2_, ...), custom_call_target="tpu_custom_call", output_to_operand_aliasing={{0}: (11, {}), {1}: (12, {})} | custom-call | flops 10700000256 | bytes 4194304 | tf_op jit(solution)/shard_map/mix_backward/pallas_call | solution.py:324
  228.8 1.4 collective-permute-start.42
  230.2 6.3 %mix_backward.7 = (bf16[32,16,256]{2,1,0:T(8,128)(2,1)S(1)}, f32[32,1024]{1,0:T(8,128)S(1)}, f32[8,128]{1,0:T(8,128)}) custom-call(f32[48]{0:T(128)S(1)} %add_convert_fusion.6.refs_0_, bf16[2,48,16]{2,1,0:T(8,128)(2,1)S(1)} %copy-done.29, bf16[48,128]{1,0:T(8,128)(2,1)S(1)} %fusion.54.refs_2_, ...), custom_call_target="tpu_custom_call", output_to_operand_aliasing={{0}: (12, {}), {1}: (13, {})} | custom-call | flops 10700000256 | bytes 4194304 | tf_op jit(solution)/shard_map/mix_backward/pallas_call | solution.py:324
  236.5 2.8 convert_add_fusion.1
  243.0 1.9 convert_add_fusion
  244.9 1.6 copy-done.41
  248.3 5.0 %all-to-all-start.3 = ((bf16[32,16,256]{2,0,1:T(8,128)(2,1)}), bf16[32,16,256]{2,0,1:T(8,128)(2,1)S(1)}, u32[]{:S(2)}, u32[]{:S(2)}) async-start(bf16[32,16,256]{2,0,1:T(8,128)(2,1)} %copy.348), calls=%async_computation.3 | async-start | bytes 524288 | tf_op jit(solution)/shard_map/all_to_all | solution.py:1009
  254.2 1.9 collective-permute-start.33
  256.1 5.3 %collective-permute-done.31 = bf16[4,96,1024]{2,1,0:T(8,128)(2,1)} collective-permute-done((bf16[4,96,1024]{2,1,0:T(8,128)(2,1)}, bf16[4,96,1024]{2,1,0:T(8,128)(2,1)}, u32[]{:S(2)}, u32[]{:S(2)}) %collective-permute-start.31) | collective-permute-done | bytes 786464 | tf_op jit(solution)/shard_map/ppermute | solution.py:475
  261.4 1.9 bitcast_add_fusion.1
  264.6 2.2 collective-permute-start.45
  271.0 3.2 %value_grads.1 = (f32[512,640]{1,0:T(8,128)}, bf16[512,640]{1,0:T(8,128)(2,1)S(1)}, f32[512,256]{1,0:T(8,128)S(1)}, f32[512,256]{1,0:T(8,128)S(1)}) custom-call(bf16[512,256]{1,0:T(8,128)(2,1)S(1)} %bitcast.389, f32[512,256]{1,0:T(8,128)S(1)} %copy-done.17, bf16[512,640]{1,0:T(8,128)(2,1)S(1)} %bitcast.362, bf16[512,640]{1,0:T(8,128)(2,1)} %bitcast.448, ...), custom_call_target="tpu_custom_call" | custom-call | flops 1000000 | bytes 1024 | tf_op jit(solution)/shard_map/value_grads/pallas_call | solution.py:751
  280.2 1.4 collective-permute-start.36
  288.4 1.8 collective-permute-start.46
  292.1 1.4 bitcast_add_fusion.5
  297.0 1.6 copy.353
  298.6 1.6 collective-permute-start.38
  300.2 1.9 collective-permute-start.41
  302.3 2.4 collective-permute-start.40
  306.4 3.0 fusion.67
  309.7 1.8 fusion.2
  314.1 2.1 multiply_subtract_fusion
  322.3 2.1 multiply_subtract_fusion.1
  (414 shorter events, 87.4 us)
Async XLA Ops:
  0.7 12.9 %copy-start.49 = (bf16[1,256,1024]{2,1,0:T(8,128)(2,1)S(1)}, bf16[1,256,1024]{2,1,0:T(8,128)(2,1)}, u32[]{:S(2)}) copy-start(bf16[1,256,1024]{2,1,0:T(8,128)(2,1)} %param.23) | copy-start | bytes 1572868
  0.7 14.0 %copy-start.64 = (f32[32,3072]{1,0:T(8,128)S(1)}, f32[32,3072]{1,0:T(8,128)}, u32[]{:S(2)}) copy-start(f32[32,3072]{1,0:T(8,128)} %param.26) | copy-start | bytes 1179652
  0.7 14.0 %copy-start.62 = (f32[96,1024]{1,0:T(8,128)S(1)}, f32[96,1024]{1,0:T(8,128)}, u32[]{:S(2)}) copy-start(f32[96,1024]{1,0:T(8,128)} %param.29) | copy-start | bytes 1179652
  2.4 12.9 %collective-permute-start.2 = (bf16[1,32,640]{2,1,0:T(8,128)(2,1)S(1)}, bf16[1,32,640]{2,1,0:T(8,128)(2,1)S(1)}, u32[]{:S(2)}, u32[]{:S(2)}) collective-permute-start(bf16[1,32,640]{2,1,0:T(8,128)(2,1)S(1)} %get-tuple-element.362), channel_id=1, source_target_pairs={{0,8},{1,9},{2,10},{3,11},{4,12},{5,13},{6,14},{7,15},{8,0},{9,1},... | collective-permute-start | bytes 122888 | tf_op jit(solution)/shard_map/ppermute | solution.py:475
  5.5 9.8 %collective-permute-start.1 = (bf16[1,32,640]{2,1,0:T(8,128)(2,1)S(1)}, bf16[1,32,640]{2,1,0:T(8,128)(2,1)S(1)}, u32[]{:S(2)}, u32[]{:S(2)}) collective-permute-start(bf16[1,32,640]{2,1,0:T(8,128)(2,1)S(1)} %get-tuple-element.362), channel_id=1, source_target_pairs={{0,16},{1,17},{2,18},{3,19},{4,20},{5,21},{6,22},{7,23},{8,24},{9,... | collective-permute-start | bytes 122888 | tf_op jit(solution)/shard_map/ppermute | solution.py:475
  8.1 7.2 %collective-permute-start = (bf16[1,32,640]{2,1,0:T(8,128)(2,1)S(1)}, bf16[1,32,640]{2,1,0:T(8,128)(2,1)S(1)}, u32[]{:S(2)}, u32[]{:S(2)}) collective-permute-start(bf16[1,32,640]{2,1,0:T(8,128)(2,1)S(1)} %get-tuple-element.362), channel_id=1, source_target_pairs={{0,24},{1,25},{2,26},{3,27},{4,28},{5,29},{6,30},{7,31},{8,16},{9,... | collective-permute-start | bytes 122888 | tf_op jit(solution)/shard_map/ppermute | solution.py:475
  9.1 9.9 %collective-permute-start.12 = (bf16[1,16,3072]{2,1,0:T(8,128)(2,1)S(1)}, bf16[1,16,3072]{2,1,0:T(8,128)(2,1)S(1)}, u32[]{:S(2)}, u32[]{:S(2)}) collective-permute-start(bf16[1,16,3072]{2,1,0:T(8,128)(2,1)S(1)} %get-tuple-element.352), channel_id=1, source_target_pairs={{0,2},{1,3},{2,0},{3,1},{4,6},{5,7},{6,4},{7,5},{8,10},{9,11},{10,... | collective-permute-start | bytes 294920 | tf_op jit(solution)/shard_map/ppermute | solution.py:475
  10.8 102.1 %collective-permute-start.18 = (bf16[256,1024]{1,0:T(8,128)(2,1)}, bf16[256,1024]{1,0:T(8,128)(2,1)}, u32[]{:S(2)}, u32[]{:S(2)}) collective-permute-start(bf16[256,1024]{1,0:T(8,128)(2,1)} %bitcast.356), channel_id=1, source_target_pairs={{0,1},{1,0},{2,3},{3,2},{4,5},{5,4},{6,7},{7,6},{8,9},{9,8},{10,11... | collective-permute-start | bytes 1572872 | tf_op jit(solution)/shard_map/ppermute | solution.py:475
  13.6 15.7 %copy-start.96 = (f32[256]{0:T(256)}, f32[256]{0:T(256)S(1)}, u32[]{:S(2)}) copy-start(f32[256]{0:T(256)S(1)} %broadcast_multiply_fusion.2) | copy-start | bytes 3076
  13.9 15.4 %copy-start.99 = (f32[256]{0:T(256)}, f32[256]{0:T(256)S(1)}, u32[]{:S(2)}) copy-start(f32[256]{0:T(256)S(1)} %add_rsqrt_fusion) | copy-start | bytes 3076
  15.2 26.1 %copy-start.37 = (bf16[1024,256]{1,0:T(8,128)(2,1)}, bf16[1024,256]{1,0:T(8,128)(2,1)S(1)}, u32[]{:S(2)}) copy-start(bf16[1024,256]{1,0:T(8,128)(2,1)S(1)} %copy.311) | copy-start | bytes 1572868
  15.4 7.1 %collective-permute-start.5 = (bf16[4,32,640]{2,1,0:T(8,128)(2,1)S(1)}, bf16[4,32,640]{2,1,0:T(8,128)(2,1)S(1)}, u32[]{:S(2)}, u32[]{:S(2)}) collective-permute-start(bf16[4,32,640]{2,1,0:T(8,128)(2,1)S(1)} %bitcast.453), channel_id=1, source_target_pairs={{0,2},{1,3},{2,0},{3,1},{4,6},{5,7},{6,4},{7,5},{8,10},{9,11},{10,... | collective-permute-start | bytes 491528 | tf_op jit(solution)/shard_map/ppermute | solution.py:475
  15.8 9.1 %collective-permute-start.4 = (bf16[4,32,640]{2,1,0:T(8,128)(2,1)S(1)}, bf16[4,32,640]{2,1,0:T(8,128)(2,1)S(1)}, u32[]{:S(2)}, u32[]{:S(2)}) collective-permute-start(bf16[4,32,640]{2,1,0:T(8,128)(2,1)S(1)} %bitcast.454), channel_id=1, source_target_pairs={{0,4},{1,5},{2,6},{3,7},{4,0},{5,1},{6,2},{7,3},{8,12},{9,13},{10,... | collective-permute-start | bytes 491528 | tf_op jit(solution)/shard_map/ppermute | solution.py:475
  17.5 9.8 %collective-permute-start.3 = (bf16[4,32,640]{2,1,0:T(8,128)(2,1)S(1)}, bf16[4,32,640]{2,1,0:T(8,128)(2,1)S(1)}, u32[]{:S(2)}, u32[]{:S(2)}) collective-permute-start(bf16[4,32,640]{2,1,0:T(8,128)(2,1)S(1)} %bitcast.455), channel_id=1, source_target_pairs={{0,6},{1,7},{2,4},{3,5},{4,2},{5,3},{6,0},{7,1},{8,14},{9,15},{10,... | collective-permute-start | bytes 491528 | tf_op jit(solution)/shard_map/ppermute | solution.py:475
  19.0 16.9 %collective-permute-start.7 = (bf16[1,32,3072]{2,1,0:T(8,128)(2,1)S(1)}, bf16[1,32,3072]{2,1,0:T(8,128)(2,1)S(1)}, u32[]{:S(2)}, u32[]{:S(2)}) collective-permute-start(bf16[1,32,3072]{2,1,0:T(8,128)(2,1)S(1)} %get-tuple-element.99), channel_id=1, source_target_pairs={{0,16},{1,17},{2,18},{3,19},{4,20},{5,21},{6,22},{7,23},{8,24},{9,... | collective-permute-start | bytes 589832 | tf_op jit(solution)/shard_map/ppermute | solution.py:475
  22.5 16.6 %collective-permute-start.8 = (bf16[1,96,1024]{2,1,0:T(8,128)(2,1)S(1)}, bf16[1,96,1024]{2,1,0:T(8,128)(2,1)S(1)}, u32[]{:S(2)}, u32[]{:S(2)}) collective-permute-start(bf16[1,96,1024]{2,1,0:T(8,128)(2,1)S(1)} %get-tuple-element.100), channel_id=1, source_target_pairs={{0,16},{1,17},{2,18},{3,19},{4,20},{5,21},{6,22},{7,23},{8,24},{9,... | collective-permute-start | bytes 589832 | tf_op jit(solution)/shard_map/ppermute | solution.py:475
  24.9 37.8 %collective-permute-start.13 = (bf16[2,16,3072]{2,1,0:T(8,128)(2,1)}, bf16[2,16,3072]{2,1,0:T(8,128)(2,1)}, u32[]{:S(2)}, u32[]{:S(2)}) collective-permute-start(bf16[2,16,3072]{2,1,0:T(8,128)(2,1)} %maximum_select_fusion.17), channel_id=1, source_target_pairs={{0,4},{1,5},{2,6},{3,7},{4,0},{5,1},{6,2},{7,3},{8,12},{9,13},{10,... | collective-permute-start | bytes 589832 | tf_op jit(solution)/shard_map/ppermute | solution.py:475
  27.6 12.4 %collective-permute-start.6 = (bf16[16,32,640]{2,1,0:T(8,128)(2,1)S(1)}, bf16[16,32,640]{2,1,0:T(8,128)(2,1)S(1)}, u32[]{:S(2)}, u32[]{:S(2)}) collective-permute-start(bf16[16,32,640]{2,1,0:T(8,128)(2,1)S(1)} %bitcast.359), channel_id=1, source_target_pairs={{0,1},{1,0},{2,3},{3,2},{4,5},{5,4},{6,7},{7,6},{8,9},{9,8},{10,11... | collective-permute-start | bytes 1966088 | tf_op jit(solution)/shard_map/ppermute | solution.py:475
  36.6 22.7 %collective-permute-start.9 = (bf16[2,32,3072]{2,1,0:T(8,128)(2,1)}, bf16[2,32,3072]{2,1,0:T(8,128)(2,1)}, u32[]{:S(2)}, u32[]{:S(2)}) collective-permute-start(bf16[2,32,3072]{2,1,0:T(8,128)(2,1)} %maximum_select_fusion.11), channel_id=1, source_target_pairs={{0,8},{1,9},{2,10},{3,11},{4,12},{5,13},{6,14},{7,15},{8,0},{9,1},... | collective-permute-start | bytes 1179656 | tf_op jit(solution)/shard_map/ppermute | solution.py:475
  39.9 22.9 %collective-permute-start.11 = (bf16[2,96,1024]{2,1,0:T(8,128)(2,1)}, bf16[2,96,1024]{2,1,0:T(8,128)(2,1)}, u32[]{:S(2)}, u32[]{:S(2)}) collective-permute-start(bf16[2,96,1024]{2,1,0:T(8,128)(2,1)} %maximum_select_fusion.12), channel_id=1, source_target_pairs={{0,8},{1,9},{2,10},{3,11},{4,12},{5,13},{6,14},{7,15},{8,0},{9,1},... | collective-permute-start | bytes 1179656 | tf_op jit(solution)/shard_map/ppermute | solution.py:475
  44.4 68.6 %collective-permute-start.17 = (bf16[16,32,256]{2,1,0:T(8,128)(2,1)}, bf16[16,32,256]{2,1,0:T(8,128)(2,1)S(1)}, u32[]{:S(2)}, u32[]{:S(2)}) collective-permute-start(bf16[16,32,256]{2,1,0:T(8,128)(2,1)} %add_convert_fusion.1), channel_id=1, source_target_pairs={{0,1},{1,0},{2,3},{3,2},{4,5},{5,4},{6,7},{7,6},{8,9},{9,8},{10,11... | collective-permute-start | bytes 786440 | tf_op jit(solution)/shard_map/ppermute | solution.py:475
  46.8 23.0 %all-to-all-start = ((bf16[16,32,256]{2,1,0:T(8,128)(2,1)}), bf16[16,32,256]{2,1,0:T(8,128)(2,1)}, u32[]{:S(2)}, u32[]{:S(2)}) async-start(bf16[16,32,256]{2,1,0:T(8,128)(2,1)} %bitcast.30), calls=%async_computation | async-start | bytes 524288 | tf_op jit(solution)/shard_map/all_to_all | solution.py:900
  60.7 28.7 %collective-permute-start.10 = (bf16[4,32,3072]{2,1,0:T(8,128)(2,1)S(1)}, bf16[4,32,3072]{2,1,0:T(8,128)(2,1)}, u32[]{:S(2)}, u32[]{:S(2)}) collective-permute-start(bf16[4,32,3072]{2,1,0:T(8,128)(2,1)S(1)} %bitcast.346), channel_id=1, source_target_pairs={{0,2},{1,3},{2,0},{3,1},{4,6},{5,7},{6,4},{7,5},{8,10},{9,11},{10,... | collective-permute-start | bytes 2359304 | tf_op jit(solution)/shard_map/ppermute | solution.py:475
  64.0 28.7 %collective-permute-start.14 = (bf16[4,96,1024]{2,1,0:T(8,128)(2,1)S(1)}, bf16[4,96,1024]{2,1,0:T(8,128)(2,1)}, u32[]{:S(2)}, u32[]{:S(2)}) collective-permute-start(bf16[4,96,1024]{2,1,0:T(8,128)(2,1)S(1)} %bitcast.372), channel_id=1, source_target_pairs={{0,4},{1,5},{2,6},{3,7},{4,0},{5,1},{6,2},{7,3},{8,12},{9,13},{10,... | collective-permute-start | bytes 2359304 | tf_op jit(solution)/shard_map/ppermute | solution.py:475
  66.6 19.9 %collective-permute-start.15 = (bf16[4,16,3072]{2,1,0:T(8,128)(2,1)S(1)}, bf16[4,16,3072]{2,1,0:T(8,128)(2,1)}, u32[]{:S(2)}, u32[]{:S(2)}) collective-permute-start(bf16[4,16,3072]{2,1,0:T(8,128)(2,1)S(1)} %bitcast.363), channel_id=1, source_target_pairs={{0,16},{1,17},{2,18},{3,19},{4,20},{5,21},{6,22},{7,23},{8,24},{9,... | collective-permute-start | bytes 1179656 | tf_op jit(solution)/shard_map/ppermute | solution.py:475
  69.0 44.0 %copy-start.26 = (f32[32,1024]{1,0:T(8,128)}, f32[32,1024]{1,0:T(8,128)S(1)}, u32[]{:S(2)}) copy-start(f32[32,1024]{1,0:T(8,128)S(1)} %pad_maximum_fusion.7.refs_6_.refs_7_) | copy-start | bytes 393220
  70.9 42.1 %copy-start.24 = (bf16[16,32,256]{2,0,1:T(8,128)(2,1)}, bf16[16,32,256]{2,0,1:T(8,128)(2,1)S(1)}, u32[]{:S(2)}) copy-start(bf16[16,32,256]{2,0,1:T(8,128)(2,1)S(1)} %copy.390) | copy-start | bytes 786436
  88.9 23.8 %collective-permute-start.16 = (bf16[8,16,3072]{2,1,0:T(8,128)(2,1)S(1)}, bf16[8,16,3072]{2,1,0:T(8,128)(2,1)S(1)}, u32[]{:S(2)}, u32[]{:S(2)}) collective-permute-start(bf16[8,16,3072]{2,1,0:T(8,128)(2,1)S(1)} %bitcast.390), channel_id=1, source_target_pairs={{0,8},{1,9},{2,10},{3,11},{4,12},{5,13},{6,14},{7,15},{8,0},{9,1},... | collective-permute-start | bytes 2359304 | tf_op jit(solution)/shard_map/ppermute | solution.py:475
  94.4 36.2 %collective-permute-start.19 = (bf16[8,32,3072]{2,1,0:T(8,128)(2,1)S(1)}, bf16[8,32,3072]{2,1,0:T(8,128)(2,1)}, u32[]{:S(2)}, u32[]{:S(2)}) collective-permute-start(bf16[8,32,3072]{2,1,0:T(8,128)(2,1)S(1)} %bitcast.384), channel_id=1, source_target_pairs={{0,4},{1,5},{2,6},{3,7},{4,0},{5,1},{6,2},{7,3},{8,12},{9,13},{10,... | collective-permute-start | bytes 4718600 | tf_op jit(solution)/shard_map/ppermute | solution.py:475
  95.1 38.2 %collective-permute-start.22 = (bf16[8,96,1024]{2,1,0:T(8,128)(2,1)S(1)}, bf16[8,96,1024]{2,1,0:T(8,128)(2,1)S(1)}, u32[]{:S(2)}, u32[]{:S(2)}) collective-permute-start(bf16[8,96,1024]{2,1,0:T(8,128)(2,1)S(1)} %bitcast.353), channel_id=1, source_target_pairs={{0,2},{1,3},{2,0},{3,1},{4,6},{5,7},{6,4},{7,5},{8,10},{9,11},{10,... | collective-permute-start | bytes 4718600 | tf_op jit(solution)/shard_map/ppermute | solution.py:475
  113.0 22.3 %copy-start = (bf16[2,2,4,16,3072]{4,3,2,1,0:T(8,128)(2,1)}, bf16[2,2,4,16,3072]{4,3,2,1,0:T(8,128)(2,1)S(1)}, u32[]{:S(2)}) copy-start(bf16[2,2,4,16,3072]{4,3,2,1,0:T(8,128)(2,1)S(1)} %maximum_select_fusion.4) | copy-start | bytes 4718596
  133.2 18.1 %collective-permute-start.20 = (bf16[16,32,3072]{2,1,0:T(8,128)(2,1)S(1)}, bf16[16,32,3072]{2,1,0:T(8,128)(2,1)S(1)}, u32[]{:S(2)}, u32[]{:S(2)}) collective-permute-start(bf16[16,32,3072]{2,1,0:T(8,128)(2,1)S(1)} %bitcast.418), channel_id=1, source_target_pairs={{0,1},{1,0},{2,3},{3,2},{4,5},{5,4},{6,7},{7,6},{8,9},{9,8},{10,11... | collective-permute-start | bytes 9437192 | tf_op jit(solution)/shard_map/ppermute | solution.py:475
  135.2 18.9 %copy-start.39 = (bf16[8,2,1,96,1024]{4,3,1,0,2:T(8,128)(2,1)}, bf16[8,2,1,96,1024]{4,3,1,0,2:T(8,128)(2,1)S(1)}, u32[]{:S(2)}) copy-start(bf16[8,2,1,96,1024]{4,3,1,0,2:T(8,128)(2,1)S(1)} %copy.338) | copy-start | bytes 9437188
  135.2 19.3 %copy-start.1 = (bf16[1,256,1024]{2,1,0:T(8,128)(2,1)S(1)}, bf16[1,256,1024]{2,1,0:T(8,128)(2,1)}, u32[]{:S(2)}) copy-start(bf16[1,256,1024]{2,1,0:T(8,128)(2,1)} %param.24) | copy-start | bytes 1572868
  135.2 16.1 %collective-permute-start.23 = (bf16[16,96,1024]{2,1,0:T(8,128)(2,1)S(1)}, bf16[16,96,1024]{2,1,0:T(8,128)(2,1)S(1)}, u32[]{:S(2)}, u32[]{:S(2)}) collective-permute-start(bf16[16,96,1024]{2,1,0:T(8,128)(2,1)S(1)} %bitcast.415), channel_id=1, source_target_pairs={{0,1},{1,0},{2,3},{3,2},{4,5},{5,4},{6,7},{7,6},{8,9},{9,8},{10,11... | collective-permute-start | bytes 9437192 | tf_op jit(solution)/shard_map/ppermute | solution.py:475
  135.3 16.0 %collective-permute-start.21 = (bf16[16,16,3072]{2,1,0:T(8,128)(2,1)S(1)}, bf16[16,16,3072]{2,1,0:T(8,128)(2,1)S(1)}, u32[]{:S(2)}, u32[]{:S(2)}) collective-permute-start(bf16[16,16,3072]{2,1,0:T(8,128)(2,1)S(1)} %bitcast.351), channel_id=1, source_target_pairs={{0,1},{1,0},{2,3},{3,2},{4,5},{5,4},{6,7},{7,6},{8,9},{9,8},{10,11... | collective-permute-start | bytes 4718600 | tf_op jit(solution)/shard_map/ppermute | solution.py:475
  151.3 18.4 %copy-start.2 = (bf16[16,1,1,16,256]{4,3,1,0,2:T(8,128)(2,1)}, bf16[16,1,1,16,256]{4,3,1,0,2:T(8,128)(2,1)S(1)}, u32[]{:S(2)}) copy-start(bf16[16,1,1,16,256]{4,3,1,0,2:T(8,128)(2,1)S(1)} %get-tuple-element.351) | copy-start | bytes 393220
  171.3 3.4 %collective-permute-start.24 = (bf16[16,96,256]{2,1,0:T(8,128)(2,1)S(1)}, bf16[16,96,256]{2,1,0:T(8,128)(2,1)S(1)}, u32[]{:S(2)}, u32[]{:S(2)}) collective-permute-start(bf16[16,96,256]{2,1,0:T(8,128)(2,1)S(1)} %get-tuple-element.133), channel_id=1, source_target_pairs={{0,1},{1,0},{2,3},{3,2},{4,5},{5,4},{6,7},{7,6},{8,9},{9,8},{10,11... | collective-permute-start | bytes 2359304 | tf_op jit(solution)/shard_map/ppermute | solution.py:475
  171.3 26.0 %collective-permute-start.27 = (bf16[256,3072]{1,0:T(8,128)(2,1)}, bf16[256,3072]{1,0:T(8,128)(2,1)}, u32[]{:S(2)}, u32[]{:S(2)}) collective-permute-start(bf16[256,3072]{1,0:T(8,128)(2,1)} %get-tuple-element.137.own), channel_id=1, source_target_pairs={{0,1},{1,0},{2,3},{3,2},{4,5},{5,4},{6,7},{7,6},{8,9},{9,8},{10,11... | collective-permute-start | bytes 4718600 | tf_op jit(solution)/shard_map/ppermute | solution.py:475
  174.7 27.6 %collective-permute-start.25 = (bf16[256,3072]{1,0:T(8,128)(2,1)}, bf16[256,3072]{1,0:T(8,128)(2,1)}, u32[]{:S(2)}, u32[]{:S(2)}) collective-permute-start(bf16[256,3072]{1,0:T(8,128)(2,1)} %get-tuple-element.134.own), channel_id=1, source_target_pairs={{0,1},{1,0},{2,3},{3,2},{4,5},{5,4},{6,7},{7,6},{8,9},{9,8},{10,11... | collective-permute-start | bytes 4718600 | tf_op jit(solution)/shard_map/ppermute | solution.py:475
  175.6 15.1 %all-to-all-start.2 = ((bf16[16,32,256]{2,1,0:T(8,128)(2,1)}), bf16[16,32,256]{2,1,0:T(8,128)(2,1)}, u32[]{:S(2)}, u32[]{:S(2)}) async-start(bf16[16,32,256]{2,1,0:T(8,128)(2,1)} %bitcast.81), calls=%async_computation.2 | async-start | bytes 524288 | tf_op jit(solution)/shard_map/all_to_all | solution.py:985
  183.2 14.0 %collective-permute-start.26 = (bf16[16,16,256]{2,1,0:T(8,128)(2,1)}, bf16[16,16,256]{2,1,0:T(8,128)(2,1)}, u32[]{:S(2)}, u32[]{:S(2)}) collective-permute-start(bf16[16,16,256]{2,1,0:T(8,128)(2,1)} %bitcast.93), channel_id=1, source_target_pairs={{0,1},{1,0},{2,3},{3,2},{4,5},{5,4},{6,7},{7,6},{8,9},{9,8},{10,11... | collective-permute-start | bytes 393224 | tf_op jit(solution)/shard_map/ppermute | solution.py:475
  196.5 40.0 %collective-permute-start.29 = (bf16[8,96,1024]{2,1,0:T(8,128)(2,1)S(1)}, bf16[8,96,1024]{2,1,0:T(8,128)(2,1)S(1)}, u32[]{:S(2)}, u32[]{:S(2)}) collective-permute-start(bf16[8,96,1024]{2,1,0:T(8,128)(2,1)S(1)} %bitcast.404), channel_id=1, source_target_pairs={{0,2},{1,3},{2,0},{3,1},{4,6},{5,7},{6,4},{7,5},{8,10},{9,11},{10,... | collective-permute-start | bytes 4718600 | tf_op jit(solution)/shard_map/ppermute | solution.py:475
  201.4 26.3 %collective-permute-start.28 = (bf16[8,16,3072]{2,1,0:T(8,128)(2,1)}, bf16[8,16,3072]{2,1,0:T(8,128)(2,1)S(1)}, u32[]{:S(2)}, u32[]{:S(2)}) collective-permute-start(bf16[8,16,3072]{2,1,0:T(8,128)(2,1)} %bitcast.95.refs_12_), channel_id=1, source_target_pairs={{0,8},{1,9},{2,10},{3,11},{4,12},{5,13},{6,14},{7,15},{8,0},{9,1},... | collective-permute-start | bytes 2359304 | tf_op jit(solution)/shard_map/ppermute | solution.py:475
  207.6 35.3 %collective-permute-start.30 = (bf16[8,32,3072]{2,1,0:T(8,128)(2,1)S(1)}, bf16[8,32,3072]{2,1,0:T(8,128)(2,1)}, u32[]{:S(2)}, u32[]{:S(2)}) collective-permute-start(bf16[8,32,3072]{2,1,0:T(8,128)(2,1)S(1)} %bitcast.406), channel_id=1, source_target_pairs={{0,4},{1,5},{2,6},{3,7},{4,0},{5,1},{6,2},{7,3},{8,12},{9,13},{10,... | collective-permute-start | bytes 4718600 | tf_op jit(solution)/shard_map/ppermute | solution.py:475
  228.8 45.5 %collective-permute-start.42 = (bf16[4,16,3072]{2,1,0:T(8,128)(2,1)}, bf16[4,16,3072]{2,1,0:T(8,128)(2,1)}, u32[]{:S(2)}, u32[]{:S(2)}) collective-permute-start(bf16[4,16,3072]{2,1,0:T(8,128)(2,1)} %fusion.27.refs_11_), channel_id=1, source_target_pairs={{0,16},{1,17},{2,18},{3,19},{4,20},{5,21},{6,22},{7,23},{8,24},{9,... | collective-permute-start | bytes 1179656 | tf_op jit(solution)/shard_map/ppermute | solution.py:475
  240.5 20.9 %collective-permute-start.31 = (bf16[4,96,1024]{2,1,0:T(8,128)(2,1)}, bf16[4,96,1024]{2,1,0:T(8,128)(2,1)}, u32[]{:S(2)}, u32[]{:S(2)}) collective-permute-start(bf16[4,96,1024]{2,1,0:T(8,128)(2,1)} %fusion.9), channel_id=1, source_target_pairs={{0,4},{1,5},{2,6},{3,7},{4,0},{5,1},{6,2},{7,3},{8,12},{9,13},{10,... | collective-permute-start | bytes 2359304 | tf_op jit(solution)/shard_map/ppermute | solution.py:475
  241.5 11.8 %collective-permute-start.47 = (f32[2,32,512]{2,1,0:T(8,128)S(1)}, f32[2,32,512]{2,1,0:T(8,128)S(1)}, u32[]{:S(2)}, u32[]{:S(2)}) collective-permute-start(f32[2,32,512]{2,1,0:T(8,128)S(1)} %pad_maximum_fusion.8), channel_id=1, source_target_pairs={{0,1},{1,0},{2,3},{3,2},{4,5},{5,4},{6,7},{7,6},{8,9},{9,8},{10,11... | collective-permute-start | bytes 393224 | tf_op jit(solution)/shard_map/ppermute | solution.py:475
  248.3 18.5 %all-to-all-start.3 = ((bf16[32,16,256]{2,0,1:T(8,128)(2,1)}), bf16[32,16,256]{2,0,1:T(8,128)(2,1)S(1)}, u32[]{:S(2)}, u32[]{:S(2)}) async-start(bf16[32,16,256]{2,0,1:T(8,128)(2,1)} %copy.348), calls=%async_computation.3 | async-start | bytes 524288 | tf_op jit(solution)/shard_map/all_to_all | solution.py:1009
  254.2 12.7 %copy-start.4 = (f32[512,256]{1,0:T(8,128)S(1)}, f32[512,256]{1,0:T(8,128)}, u32[]{:S(2)}) copy-start(f32[512,256]{1,0:T(8,128)} %get-tuple-element.333.h1) | copy-start | bytes 1572868
  254.2 22.3 %collective-permute-start.33 = (bf16[4,32,3072]{2,1,0:T(8,128)(2,1)}, bf16[4,32,3072]{2,1,0:T(8,128)(2,1)}, u32[]{:S(2)}, u32[]{:S(2)}) collective-permute-start(bf16[4,32,3072]{2,1,0:T(8,128)(2,1)} %fusion.10), channel_id=1, source_target_pairs={{0,2},{1,3},{2,0},{3,1},{4,6},{5,7},{6,4},{7,5},{8,10},{9,11},{10,... | collective-permute-start | bytes 2359304 | tf_op jit(solution)/shard_map/ppermute | solution.py:475
  264.6 18.2 %collective-permute-start.45 = (bf16[2,96,1024]{2,1,0:T(8,128)(2,1)}, bf16[2,96,1024]{2,1,0:T(8,128)(2,1)}, u32[]{:S(2)}, u32[]{:S(2)}) collective-permute-start(bf16[2,96,1024]{2,1,0:T(8,128)(2,1)} %fusion.28), channel_id=1, source_target_pairs={{0,8},{1,9},{2,10},{3,11},{4,12},{5,13},{6,14},{7,15},{8,0},{9,1},... | collective-permute-start | bytes 1179656 | tf_op jit(solution)/shard_map/ppermute | solution.py:475
  274.3 5.7 %collective-permute-start.32 = (bf16[16,32,640]{2,1,0:T(8,128)(2,1)S(1)}, bf16[16,32,640]{2,1,0:T(8,128)(2,1)S(1)}, u32[]{:S(2)}, u32[]{:S(2)}) collective-permute-start(bf16[16,32,640]{2,1,0:T(8,128)(2,1)S(1)} %bitcast.408), channel_id=1, source_target_pairs={{0,1},{1,0},{2,3},{3,2},{4,5},{5,4},{6,7},{7,6},{8,9},{9,8},{10,11... | collective-permute-start | bytes 1966088 | tf_op jit(solution)/shard_map/ppermute | solution.py:475
  276.4 25.9 %collective-permute-start.43 = (bf16[2,16,3072]{2,1,0:T(8,128)(2,1)}, bf16[2,16,3072]{2,1,0:T(8,128)(2,1)S(1)}, u32[]{:S(2)}, u32[]{:S(2)}) collective-permute-start(bf16[2,16,3072]{2,1,0:T(8,128)(2,1)} %fusion.38), channel_id=1, source_target_pairs={{0,4},{1,5},{2,6},{3,7},{4,0},{5,1},{6,2},{7,3},{8,12},{9,13},{10,... | collective-permute-start | bytes 589832 | tf_op jit(solution)/shard_map/ppermute | solution.py:475
  278.8 13.3 %collective-permute-start.37 = (bf16[2,32,3072]{2,1,0:T(8,128)(2,1)}, bf16[2,32,3072]{2,1,0:T(8,128)(2,1)}, u32[]{:S(2)}, u32[]{:S(2)}) collective-permute-start(bf16[2,32,3072]{2,1,0:T(8,128)(2,1)} %fusion.29), channel_id=1, source_target_pairs={{0,8},{1,9},{2,10},{3,11},{4,12},{5,13},{6,14},{7,15},{8,0},{9,1},... | collective-permute-start | bytes 1179656 | tf_op jit(solution)/shard_map/ppermute | solution.py:475
  280.2 8.2 %collective-permute-start.36 = (bf16[4,32,640]{2,1,0:T(8,128)(2,1)S(1)}, bf16[4,32,640]{2,1,0:T(8,128)(2,1)}, u32[]{:S(2)}, u32[]{:S(2)}) collective-permute-start(bf16[4,32,640]{2,1,0:T(8,128)(2,1)S(1)} %get-tuple-element.345), channel_id=1, source_target_pairs={{0,6},{1,7},{2,4},{3,5},{4,2},{5,3},{6,0},{7,1},{8,14},{9,15},{10,... | collective-permute-start | bytes 491528 | tf_op jit(solution)/shard_map/ppermute | solution.py:475
  281.7 8.6 %collective-permute-start.35 = (bf16[4,32,640]{2,1,0:T(8,128)(2,1)S(1)}, bf16[4,32,640]{2,1,0:T(8,128)(2,1)}, u32[]{:S(2)}, u32[]{:S(2)}) collective-permute-start(bf16[4,32,640]{2,1,0:T(8,128)(2,1)S(1)} %get-tuple-element.344), channel_id=1, source_target_pairs={{0,2},{1,3},{2,0},{3,1},{4,6},{5,7},{6,4},{7,5},{8,10},{9,11},{10,... | collective-permute-start | bytes 491528 | tf_op jit(solution)/shard_map/ppermute | solution.py:475
  282.8 8.0 %collective-permute-start.34 = (bf16[4,32,640]{2,1,0:T(8,128)(2,1)S(1)}, bf16[4,32,640]{2,1,0:T(8,128)(2,1)}, u32[]{:S(2)}, u32[]{:S(2)}) collective-permute-start(bf16[4,32,640]{2,1,0:T(8,128)(2,1)S(1)} %fusion.40), channel_id=1, source_target_pairs={{0,4},{1,5},{2,6},{3,7},{4,0},{5,1},{6,2},{7,3},{8,12},{9,13},{10,... | collective-permute-start | bytes 491528 | tf_op jit(solution)/shard_map/ppermute | solution.py:475
  288.4 24.3 %collective-permute-start.46 = (bf16[1,96,1024]{2,1,0:T(8,128)(2,1)}, bf16[1,96,1024]{2,1,0:T(8,128)(2,1)}, u32[]{:S(2)}, u32[]{:S(2)}) collective-permute-start(bf16[1,96,1024]{2,1,0:T(8,128)(2,1)} %dynamic-slice_convert_fusion.3), channel_id=1, source_target_pairs={{0,16},{1,17},{2,18},{3,19},{4,20},{5,21},{6,22},{7,23},{8,24},{9,... | collective-permute-start | bytes 589832 | tf_op jit(solution)/shard_map/ppermute | solution.py:475
  298.6 23.7 %collective-permute-start.38 = (bf16[1,32,3072]{2,1,0:T(8,128)(2,1)}, bf16[1,32,3072]{2,1,0:T(8,128)(2,1)}, u32[]{:S(2)}, u32[]{:S(2)}) collective-permute-start(bf16[1,32,3072]{2,1,0:T(8,128)(2,1)} %dynamic-slice_convert_fusion.5), channel_id=1, source_target_pairs={{0,16},{1,17},{2,18},{3,19},{4,20},{5,21},{6,22},{7,23},{8,24},{9,... | collective-permute-start | bytes 589832 | tf_op jit(solution)/shard_map/ppermute | solution.py:475
  300.2 16.0 %collective-permute-start.41 = (f32[1,32,640]{2,1,0:T(8,128)S(1)}, f32[1,32,640]{2,1,0:T(8,128)S(1)}, u32[]{:S(2)}, u32[]{:S(2)}) collective-permute-start(f32[1,32,640]{2,1,0:T(8,128)S(1)} %get-tuple-element.342), channel_id=1, source_target_pairs={{0,24},{1,25},{2,26},{3,27},{4,28},{5,29},{6,30},{7,31},{8,16},{9,... | collective-permute-start | bytes 245768 | tf_op jit(solution)/shard_map/ppermute | solution.py:475
  302.1 15.4 %collective-permute-start.39 = (f32[1,32,640]{2,1,0:T(8,128)S(1)}, f32[1,32,640]{2,1,0:T(8,128)S(1)}, u32[]{:S(2)}, u32[]{:S(2)}) collective-permute-start(f32[1,32,640]{2,1,0:T(8,128)S(1)} %get-tuple-element.343), channel_id=1, source_target_pairs={{0,16},{1,17},{2,18},{3,19},{4,20},{5,21},{6,22},{7,23},{8,24},{9,... | collective-permute-start | bytes 245768 | tf_op jit(solution)/shard_map/ppermute | solution.py:475
  302.3 15.3 %collective-permute-start.40 = (f32[1,32,640]{2,1,0:T(8,128)S(1)}, f32[1,32,640]{2,1,0:T(8,128)S(1)}, u32[]{:S(2)}, u32[]{:S(2)}) collective-permute-start(f32[1,32,640]{2,1,0:T(8,128)S(1)} %get-tuple-element.341), channel_id=1, source_target_pairs={{0,8},{1,9},{2,10},{3,11},{4,12},{5,13},{6,14},{7,15},{8,0},{9,1},... | collective-permute-start | bytes 245768 | tf_op jit(solution)/shard_map/ppermute | solution.py:475
  312.7 8.6 %collective-permute-start.44 = (bf16[1,16,3072]{2,1,0:T(8,128)(2,1)S(1)}, bf16[1,16,3072]{2,1,0:T(8,128)(2,1)S(1)}, u32[]{:S(2)}, u32[]{:S(2)}) collective-permute-start(bf16[1,16,3072]{2,1,0:T(8,128)(2,1)S(1)} %dynamic-slice_convert_fusion.7), channel_id=1, source_target_pairs={{0,2},{1,3},{2,0},{3,1},{4,6},{5,7},{6,4},{7,5},{8,10},{9,11},{10,... | collective-permute-start | bytes 294920 | tf_op jit(solution)/shard_map/ppermute | solution.py:475
  (94 other events, 465.4 us)

commit v5 on v4

--- a/solution.py
+++ b/solution.py
@@ -299,6 +299,8 @@
     def __init__(self, kernel, name, inputs, results, scratch, parts, flops):
         self.kernel, self.name, self.inputs, self.results = kernel, name, inputs, results
         self.scratch, self.parts, self.flops = scratch, parts, flops
+        rows = scratch[-1].shape
+        self.room = 20 * 2**20 + 14 * rows[0] * rows[1] * rows[2]
         self.done, self.outs, self.waits = 0, [], []
 
     def run(self, *waits):
@@ -329,7 +331,7 @@
             out_shape=[shape for shape, _ in self.results] + [token],
             input_output_aliases={count + len(waits) + n: n for n in range(len(before))},
             scratch_shapes=self.scratch,
-            compiler_params=pltpu.CompilerParams(vmem_limit_bytes=48 * 2**20),
+            compiler_params=pltpu.CompilerParams(vmem_limit_bytes=self.room),
             cost_estimate=pl.CostEstimate(
                 flops=self.flops, bytes_accessed=4 * 2**20, transcendentals=0
             ),

time: 331 us -> 329 us (level)
  waiting for transfers between devices: 39.6 us -> 48.8 us
  Pallas kernels: 90 us -> 81 us
  other arithmetic: 58.7 us -> 55.1 us
    ppermute x48, waiting for transfers between devices: 33.8 us -> 43 us  [trade(): return lax.ppermute(block, ('tok', 'rep'), pairs)]
    pallas_call x8, Pallas kernels: 57.5 us -> 49.2 us  [call(): pl.pallas_call(body, grid=(1,), in_specs=specs + [pl.BlockSpec(memory_spa...]
    unnamed x217 -> x215, local copies, waits for them, and re-layouts: 21.9 us -> 24 us
  transfers between devices with their start and end apart: 51 -> 51, of which waited for: 14 -> 14; matrix products, arithmetic and copies ran while one was open for 28% -> 27% of each run, Pallas kernels for 23% -> 20%
where the time goes in v5:
time: 329 us; the launch traced here: 322 us
  Pallas kernels  81 us (25%)
  starting transfers between devices  63 us (19%)
  other arithmetic  55.1 us (17%)
  waiting for transfers between devices  48.8 us (15%)
  local copies, waits for them, and re-layouts  48.3 us (15%)
  blocking collectives  14.8 us (4%)
  matrix products  8.58 us (3%)
    pallas_call x8, Pallas kernels, call(): pl.pallas_call(body, grid=(1,), in_specs=specs + [pl.BlockSpec(memory_spa...  49.2 us
    ppermute x48, starting transfers between devices, trade(): return lax.ppermute(block, ('tok', 'rep'), pairs)  48.7 us
    ppermute x48, waiting for transfers between devices, trade(): return lax.ppermute(block, ('tok', 'rep'), pairs)  43 us
    unnamed x215, local copies, waits for them, and re-layouts  24 us
    select_n x23, other arithmetic, join(): jnp.where(self.cube.bit(b) == 1, jnp.concatenate([second, first], axis=1)...  15.7 us
    pallas_call x1, Pallas kernels, gate(): pl.pallas_call(body, grid=(hidden // block,), in_specs=[pl.BlockSpec(memo...  15.2 us
    all_to_all x1, blocking collectives, per_device(): lax.all_to_all(state_out.reshape(channels, length), 'tok', split_axis=1,...  14.8 us
    pallas_call x3, Pallas kernels, products(): pl.pallas_call(products_kernel, grid_spec=pltpu.PrefetchScalarGridSpec(nu...  13.4 us
  transfers between devices with their start and end apart: 51, of which 14 were waited for; matrix products, arithmetic and copies ran while one was open for 27% of the time, Pallas kernels for 20%

profile of v5, /device:TPU:0, one launch (start us, length us, event | category | flops | bytes accessed | tf_op | source)
XLA Modules:
  0.0 322.3 jit_solution(11736935214272562720)
XLA Ops:
  2.4 3.1 collective-permute-start.2
  5.5 2.6 collective-permute-start.1
  9.1 1.8 collective-permute-start.12
  15.8 1.7 collective-permute-start.4
  17.5 1.4 collective-permute-start.3
  19.0 1.7 collective-permute-start.7
  22.5 1.7 collective-permute-start.8
  24.9 2.4 collective-permute-start.13
  30.6 5.3 %collective-permute-done.7 = bf16[1,32,3072]{2,1,0:T(8,128)(2,1)S(1)} collective-permute-done((bf16[1,32,3072]{2,1,0:T(8,128)(2,1)S(1)}, bf16[1,32,3072]{2,1,0:T(8,128)(2,1)S(1)}, u32[]{:S(2)}, u32[]{:S(2)}) %collective-permute-start.7) | collective-permute-done | bytes 196640 | tf_op jit(solution)/shard_map/ppermute | solution.py:477
  36.7 2.4 collective-permute-done.8
  41.4 1.9 fusion.23
  44.4 2.4 fusion.18
  46.8 5.7 %all-to-all-start = ((bf16[16,32,256]{2,1,0:T(8,128)(2,1)}), bf16[16,32,256]{2,1,0:T(8,128)(2,1)}, u32[]{:S(2)}, u32[]{:S(2)}) async-start(bf16[16,32,256]{2,1,0:T(8,128)(2,1)} %bitcast.30), calls=%async_computation | async-start | bytes 524288 | tf_op jit(solution)/shard_map/all_to_all | solution.py:902
  52.6 3.9 %fusion.4 = (f32[32,16,512]{2,0,1:T(8,128)S(1)}, f32[32,16,512]{2,0,1:T(8,128)S(1)}) fusion(f32[32,512]{1,0:T(8,128)S(1)} %get-tuple-element.366, f32[16]{0:T(128)S(1)} %copy-done.105, f32[32,512]{1,0:T(8,128)S(1)} %get-tuple-element.367), kind=kLoop, calls=%fused_computation.31 | loop fusion | flops 1048576 | bytes 2228288 | tf_op jit(solution)/shard_map/mul | solution.py:64
  56.6 2.6 copy.328.refs_4_.refs_5_
  60.5 2.1 collective-permute-start.10
  63.8 1.5 collective-permute-start.14
  66.4 2.4 collective-permute-start.15
  70.8 1.7 copy-done.7
  74.1 6.9 %mix_forward.4 = (bf16[32,16,256]{2,1,0:T(8,128)(2,1)S(1)}, f32[1536,1024]{1,0:T(8,128)S(1)}, bf16[32,128,128]{2,1,0:T(8,128)(2,1)S(1)}, f32[8,128]{1,0:T(8,128)}) custom-call(f32[48]{0:T(128)S(1)} %add_convert_fusion.6.refs_0_, bf16[2,48,16]{2,1,0:T(8,128)(2,1)S(1)} %copy-done.27, bf16[48,128]{1,0:T(8,128)(2,1)S(1)} %fusion.54.refs_2_, ...), custom_call_target="tpu_custom_call" | custom-call | flops 8000000000 | bytes 4194304 | tf_op jit(solution)/shard_map/mix_forward/pallas_call | solution.py:326
  81.0 5.2 %collective-permute-done.15 = bf16[4,16,3072]{2,1,0:T(8,128)(2,1)} collective-permute-done((bf16[4,16,3072]{2,1,0:T(8,128)(2,1)S(1)}, bf16[4,16,3072]{2,1,0:T(8,128)(2,1)}, u32[]{:S(2)}, u32[]{:S(2)}) %collective-permute-start.15) | collective-permute-done | bytes 393248 | tf_op jit(solution)/shard_map/ppermute | solution.py:477
  89.2 1.6 maximum_select_fusion.2
  90.9 1.6 maximum_select_fusion.5
  92.5 1.6 maximum_select_fusion.3
  95.4 6.7 %mix_forward.5 = (bf16[32,16,256]{2,1,0:T(8,128)(2,1)S(1)}, f32[1536,1024]{1,0:T(8,128)S(1)}, bf16[32,128,128]{2,1,0:T(8,128)(2,1)S(1)}, f32[8,128]{1,0:T(8,128)S(1)}) custom-call(f32[48]{0:T(128)S(1)} %add_convert_fusion.6.refs_0_, bf16[2,48,16]{2,1,0:T(8,128)(2,1)S(1)} %copy-done.27, ...), custom_call_target="tpu_custom_call", output_to_operand_aliasing={{0}: (10, {}), {1}: (11, {}), {2}: (12, {})} | custom-call | flops 8000000000 | bytes 4194304 | tf_op jit(solution)/shard_map/mix_forward/pallas_call | solution.py:326
  102.2 7.1 %mix_forward.6 = (bf16[32,16,256]{2,1,0:T(8,128)(2,1)S(1)}, f32[1536,1024]{1,0:T(8,128)S(1)}, bf16[32,128,128]{2,1,0:T(8,128)(2,1)S(1)}, f32[8,128]{1,0:T(8,128)S(1)}) custom-call(f32[48]{0:T(128)S(1)} %add_convert_fusion.6.refs_0_, bf16[2,48,16]{2,1,0:T(8,128)(2,1)S(1)} %copy-done.27, ...), custom_call_target="tpu_custom_call", output_to_operand_aliasing={{0}: (8, {}), {1}: (9, {}), {2}: (10, {})} | custom-call | flops 8000000000 | bytes 4194304 | tf_op jit(solution)/shard_map/mix_forward/pallas_call | solution.py:326
  110.3 6.7 %mix_forward.7 = (bf16[32,16,256]{2,1,0:T(8,128)(2,1)S(1)}, f32[1536,1024]{1,0:T(8,128)S(1)}, bf16[32,128,128]{2,1,0:T(8,128)(2,1)S(1)}, f32[8,128]{1,0:T(8,128)}) custom-call(f32[48]{0:T(128)S(1)} %add_convert_fusion.6.refs_0_, bf16[2,48,16]{2,1,0:T(8,128)(2,1)S(1)} %copy-done.27, ...), custom_call_target="tpu_custom_call", output_to_operand_aliasing={{0}: (12, {}), {1}: (13, {}), {2}: (14, {})} | custom-call | flops 8000000000 | bytes 4194304 | tf_op jit(solution)/shard_map/mix_forward/pallas_call | solution.py:326
  118.0 12.3 %collective-permute-done.19 = bf16[8,32,3072]{2,1,0:T(8,128)(2,1)S(1)} collective-permute-done((bf16[8,32,3072]{2,1,0:T(8,128)(2,1)S(1)}, bf16[8,32,3072]{2,1,0:T(8,128)(2,1)S(1)}, u32[]{:S(2)}, u32[]{:S(2)}) %collective-permute-start.19) | collective-permute-done | bytes 1572896 | tf_op jit(solution)/shard_map/ppermute | solution.py:477
  134.1 14.8 %all_to_all.61 = bf16[32,16,256]{2,0,1:T(8,128)(2,1)S(1)} all-to-all(bf16[32,16,256]{2,0,1:T(8,128)(2,1)S(1)} %copy.330), channel_id=1, replica_groups=mesh['tok'=16,'rep'=2] {'tok'}, dimensions={1} | all-to-all | bytes 524288 | tf_op jit(solution)/shard_map/all_to_all | solution.py:950
  152.9 15.2 %gate.1 = (bf16[256,3072]{1,0:T(8,128)(2,1)}, bf16[256,3072]{1,0:T(8,128)(2,1)}, bf16[16,96,256]{2,1,0:T(8,128)(2,1)S(1)}, bf16[16,96,256]{2,1,0:T(8,128)(2,1)S(...) custom-call(s32[1]{0:T(128)} %bitcast.1.core, ...), custom_call_target="tpu_custom_call" | custom-call | flops 1000000 | bytes 1024 | tf_op jit(solution)/shard_map/gate/pallas_call | solution.py:691
  170.2 2.9 collective-permute-done.24
  174.0 4.4 %all-to-all-start.2 = ((bf16[16,32,256]{2,1,0:T(8,128)(2,1)}), bf16[16,32,256]{2,1,0:T(8,128)(2,1)}, u32[]{:S(2)}, u32[]{:S(2)}) async-start(bf16[16,32,256]{2,1,0:T(8,128)(2,1)} %bitcast.81), calls=%async_computation.2 | async-start | bytes 524288 | tf_op jit(solution)/shard_map/all_to_all | solution.py:987
  178.5 1.8 bitcast_convert_fusion.4
  183.3 5.8 %all-to-all-done.2 = bf16[16,32,256]{2,1,0:T(8,128)(2,1)} async-done(((bf16[16,32,256]{2,1,0:T(8,128)(2,1)}), bf16[16,32,256]{2,1,0:T(8,128)(2,1)}, u32[]{:S(2)}, u32[]{:S(2)}) %all-to-all-start.2) | async-done | bytes 262176 | tf_op jit(solution)/shard_map/all_to_all | solution.py:987
  190.2 4.6 %weight_grad.4 = (bf16[768,1024]{1,0:T(8,128)(2,1)S(1)}, f32[768,1024]{1,0:T(8,128)}) custom-call(s32[1]{0:T(128)} %bitcast.87.bit_ref, bf16[8,2,96,256]{3,2,1,0:T(8,128)(2,1)S(1)} %bitcast.367, bf16[8,2,96,256]{3,2,1,0:T(8,128)(2,1)S(1)} %bitcast.368, bf16[8,2,96,256]{3,2,1,0:T(8,128)(2,1)S(1)} %bitcast.370, bf16[8,2,96,256]{3,2,1,0:T(8,128)(2,1)S(1)} %bitcast.371, ...), custom_call_target="tpu_custom_call" | custom-call | flops 1000000 | bytes 1024 | tf_op jit(solution)/shard_map/weight_grad/pallas_call | solution.py:798
  195.6 3.6 %weight_grad.5 = (bf16[128,3072]{1,0:T(8,128)(2,1)S(1)}, f32[128,3072]{1,0:T(8,128)S(1)}) custom-call(s32[1]{0:T(128)} %bitcast.91.bit_ref, bf16[2,2,64,256]{3,2,1,0:T(8,128)(2,1)S(1)} %bitcast.378, bf16[2,2,64,256]{3,2,1,0:T(8,128)(2,1)S(1)} %bitcast.379, bf16[2,2,64,256]{3,2,1,0:T(8,128)(2,1)} %bitcast.94.got_send.got_keep, ...), custom_call_target="tpu_custom_call" | custom-call | flops 1000000 | bytes 1024 | tf_op jit(solution)/shard_map/weight_grad/pallas_call | solution.py:798
  200.2 5.2 %weight_grad.3 = (bf16[256,3072]{1,0:T(8,128)(2,1)S(1)}, f32[256,3072]{1,0:T(8,128)}) custom-call(s32[1]{0:T(128)} %bitcast.83.bit_ref, bf16[4,2,64,256]{3,2,1,0:T(8,128)(2,1)S(1)} %add_convert_fusion.own_send.own_keep, bf16[4,2,64,256]{3,2,1,0:T(8,128)(2,1)S(1)} %add_convert_fusion.own_send.own_keep, bf16[4,2,64,256]{3,2,1,0:T(8,128)(2,1)S(1)} %bitcast.387, ...), custom_call_target="tpu_custom_call" | custom-call | flops 1000000 | bytes 1024 | tf_op jit(solution)/shard_map/weight_grad/pallas_call | solution.py:798
  206.2 2.8 copy-done.32
  209.0 5.4 %mix_backward.4 = (bf16[32,16,256]{2,1,0:T(8,128)(2,1)S(1)}, f32[32,1024]{1,0:T(8,128)S(1)}, f32[8,128]{1,0:T(8,128)S(1)}) custom-call(f32[48]{0:T(128)S(1)} %add_convert_fusion.6.refs_0_, bf16[2,48,16]{2,1,0:T(8,128)(2,1)S(1)} %copy-done.28, bf16[48,128]{1,0:T(8,128)(2,1)S(1)} %fusion.54.refs_2_, bf16[32,16,256]{2,1,0:T(8,128)(2,1)S(1)} %bitcast.396, ...), custom_call_target="tpu_custom_call" | custom-call | flops 10700000256 | bytes 4194304 | tf_op jit(solution)/shard_map/mix_backward/pallas_call | solution.py:326
  214.3 5.4 %mix_backward.5 = (bf16[32,16,256]{2,1,0:T(8,128)(2,1)S(1)}, f32[32,1024]{1,0:T(8,128)S(1)}, f32[8,128]{1,0:T(8,128)S(1)}) custom-call(f32[48]{0:T(128)S(1)} %add_convert_fusion.6.refs_0_, bf16[2,48,16]{2,1,0:T(8,128)(2,1)S(1)} %copy-done.28, bf16[48,128]{1,0:T(8,128)(2,1)S(1)} %fusion.54.refs_2_, ...), custom_call_target="tpu_custom_call", output_to_operand_aliasing={{0}: (11, {}), {1}: (12, {})} | custom-call | flops 10700000256 | bytes 4194304 | tf_op jit(solution)/shard_map/mix_backward/pallas_call | solution.py:326
  219.7 5.6 %mix_backward.6 = (bf16[32,16,256]{2,1,0:T(8,128)(2,1)S(1)}, f32[32,1024]{1,0:T(8,128)S(1)}, f32[8,128]{1,0:T(8,128)S(1)}) custom-call(f32[48]{0:T(128)S(1)} %add_convert_fusion.6.refs_0_, bf16[2,48,16]{2,1,0:T(8,128)(2,1)S(1)} %copy-done.28, bf16[48,128]{1,0:T(8,128)(2,1)S(1)} %fusion.54.refs_2_, ...), custom_call_target="tpu_custom_call", output_to_operand_aliasing={{0}: (11, {}), {1}: (12, {})} | custom-call | flops 10700000256 | bytes 4194304 | tf_op jit(solution)/shard_map/mix_backward/pallas_call | solution.py:326
  226.4 1.4 collective-permute-start.42
  227.8 5.4 %mix_backward.7 = (bf16[32,16,256]{2,1,0:T(8,128)(2,1)S(1)}, f32[32,1024]{1,0:T(8,128)S(1)}, f32[8,128]{1,0:T(8,128)}) custom-call(f32[48]{0:T(128)S(1)} %add_convert_fusion.6.refs_0_, bf16[2,48,16]{2,1,0:T(8,128)(2,1)S(1)} %copy-done.28, bf16[48,128]{1,0:T(8,128)(2,1)S(1)} %fusion.54.refs_2_, ...), custom_call_target="tpu_custom_call", output_to_operand_aliasing={{0}: (12, {}), {1}: (13, {})} | custom-call | flops 10700000256 | bytes 4194304 | tf_op jit(solution)/shard_map/mix_backward/pallas_call | solution.py:326
  233.3 2.3 convert_add_fusion.1
  237.9 4.5 %collective-permute-done.30 = bf16[8,32,3072]{2,1,0:T(8,128)(2,1)S(1)} collective-permute-done((bf16[8,32,3072]{2,1,0:T(8,128)(2,1)S(1)}, bf16[8,32,3072]{2,1,0:T(8,128)(2,1)S(1)}, u32[]{:S(2)}, u32[]{:S(2)}) %collective-permute-start.30) | collective-permute-done | bytes 1572896 | tf_op jit(solution)/shard_map/ppermute | solution.py:477
  242.9 1.7 copy-done.39
  246.3 4.3 %all-to-all-start.3 = ((bf16[32,16,256]{2,0,1:T(8,128)(2,1)}), bf16[32,16,256]{2,0,1:T(8,128)(2,1)S(1)}, u32[]{:S(2)}, u32[]{:S(2)}) async-start(bf16[32,16,256]{2,0,1:T(8,128)(2,1)} %copy.348), calls=%async_computation.3 | async-start | bytes 524288 | tf_op jit(solution)/shard_map/all_to_all | solution.py:1011
  251.5 1.9 collective-permute-start.33
  253.4 6.3 %collective-permute-done.31 = bf16[4,96,1024]{2,1,0:T(8,128)(2,1)} collective-permute-done((bf16[4,96,1024]{2,1,0:T(8,128)(2,1)}, bf16[4,96,1024]{2,1,0:T(8,128)(2,1)}, u32[]{:S(2)}, u32[]{:S(2)}) %collective-permute-start.31) | collective-permute-done | bytes 786464 | tf_op jit(solution)/shard_map/ppermute | solution.py:477
  259.7 1.9 bitcast_add_fusion.1
  262.9 1.7 collective-permute-start.45
  268.8 3.3 %value_grads.1 = (f32[512,640]{1,0:T(8,128)}, bf16[512,640]{1,0:T(8,128)(2,1)S(1)}, f32[512,256]{1,0:T(8,128)S(1)}, f32[512,256]{1,0:T(8,128)S(1)}) custom-call(bf16[512,256]{1,0:T(8,128)(2,1)S(1)} %bitcast.389, f32[512,256]{1,0:T(8,128)S(1)} %copy-done.16, bf16[512,640]{1,0:T(8,128)(2,1)S(1)} %bitcast.362, bf16[512,640]{1,0:T(8,128)(2,1)} %bitcast.451, ...), custom_call_target="tpu_custom_call" | custom-call | flops 1000000 | bytes 1024 | tf_op jit(solution)/shard_map/value_grads/pallas_call | solution.py:753
  278.0 1.8 collective-permute-start.36
  286.2 1.6 collective-permute-start.46
  289.9 1.4 bitcast_add_fusion.5
  294.8 1.6 copy.353
  296.3 1.5 collective-permute-start.38
  297.8 2.1 collective-permute-start.41
  300.1 2.2 collective-permute-start.40
  304.1 3.0 fusion.67
  307.3 1.8 fusion.2
  310.3 1.5 collective-permute-start.44
  311.9 2.1 multiply_subtract_fusion
  319.9 2.1 multiply_subtract_fusion.1
  (412 shorter events, 86.7 us)
Async XLA Ops:
  0.7 14.0 %copy-start.63 = (f32[32,3072]{1,0:T(8,128)S(1)}, f32[32,3072]{1,0:T(8,128)}, u32[]{:S(2)}) copy-start(f32[32,3072]{1,0:T(8,128)} %param.26) | copy-start | bytes 1179652
  0.7 14.0 %copy-start.61 = (f32[96,1024]{1,0:T(8,128)S(1)}, f32[96,1024]{1,0:T(8,128)}, u32[]{:S(2)}) copy-start(f32[96,1024]{1,0:T(8,128)} %param.29) | copy-start | bytes 1179652
  2.4 12.9 %collective-permute-start.2 = (bf16[1,32,640]{2,1,0:T(8,128)(2,1)S(1)}, bf16[1,32,640]{2,1,0:T(8,128)(2,1)S(1)}, u32[]{:S(2)}, u32[]{:S(2)}) collective-permute-start(bf16[1,32,640]{2,1,0:T(8,128)(2,1)S(1)} %get-tuple-element.362), channel_id=1, source_target_pairs={{0,8},{1,9},{2,10},{3,11},{4,12},{5,13},{6,14},{7,15},{8,0},{9,1},... | collective-permute-start | bytes 122888 | tf_op jit(solution)/shard_map/ppermute | solution.py:477
  5.5 9.8 %collective-permute-start.1 = (bf16[1,32,640]{2,1,0:T(8,128)(2,1)S(1)}, bf16[1,32,640]{2,1,0:T(8,128)(2,1)S(1)}, u32[]{:S(2)}, u32[]{:S(2)}) collective-permute-start(bf16[1,32,640]{2,1,0:T(8,128)(2,1)S(1)} %get-tuple-element.362), channel_id=1, source_target_pairs={{0,16},{1,17},{2,18},{3,19},{4,20},{5,21},{6,22},{7,23},{8,24},{9,... | collective-permute-start | bytes 122888 | tf_op jit(solution)/shard_map/ppermute | solution.py:477
  8.1 7.2 %collective-permute-start = (bf16[1,32,640]{2,1,0:T(8,128)(2,1)S(1)}, bf16[1,32,640]{2,1,0:T(8,128)(2,1)S(1)}, u32[]{:S(2)}, u32[]{:S(2)}) collective-permute-start(bf16[1,32,640]{2,1,0:T(8,128)(2,1)S(1)} %get-tuple-element.362), channel_id=1, source_target_pairs={{0,24},{1,25},{2,26},{3,27},{4,28},{5,29},{6,30},{7,31},{8,16},{9,... | collective-permute-start | bytes 122888 | tf_op jit(solution)/shard_map/ppermute | solution.py:477
  9.1 9.9 %collective-permute-start.12 = (bf16[1,16,3072]{2,1,0:T(8,128)(2,1)S(1)}, bf16[1,16,3072]{2,1,0:T(8,128)(2,1)S(1)}, u32[]{:S(2)}, u32[]{:S(2)}) collective-permute-start(bf16[1,16,3072]{2,1,0:T(8,128)(2,1)S(1)} %get-tuple-element.352), channel_id=1, source_target_pairs={{0,2},{1,3},{2,0},{3,1},{4,6},{5,7},{6,4},{7,5},{8,10},{9,11},{10,... | collective-permute-start | bytes 294920 | tf_op jit(solution)/shard_map/ppermute | solution.py:477
  10.8 98.7 %collective-permute-start.18 = (bf16[256,1024]{1,0:T(8,128)(2,1)}, bf16[256,1024]{1,0:T(8,128)(2,1)}, u32[]{:S(2)}, u32[]{:S(2)}) collective-permute-start(bf16[256,1024]{1,0:T(8,128)(2,1)} %bitcast.356), channel_id=1, source_target_pairs={{0,1},{1,0},{2,3},{3,2},{4,5},{5,4},{6,7},{7,6},{8,9},{9,8},{10,11... | collective-permute-start | bytes 1572872 | tf_op jit(solution)/shard_map/ppermute | solution.py:477
  13.6 15.7 %copy-start.95 = (f32[256]{0:T(256)}, f32[256]{0:T(256)S(1)}, u32[]{:S(2)}) copy-start(f32[256]{0:T(256)S(1)} %broadcast_multiply_fusion.2) | copy-start | bytes 3076
  13.9 15.4 %copy-start.98 = (f32[256]{0:T(256)}, f32[256]{0:T(256)S(1)}, u32[]{:S(2)}) copy-start(f32[256]{0:T(256)S(1)} %add_rsqrt_fusion) | copy-start | bytes 3076
  15.2 26.1 %copy-start.35 = (bf16[1024,256]{1,0:T(8,128)(2,1)}, bf16[1024,256]{1,0:T(8,128)(2,1)S(1)}, u32[]{:S(2)}) copy-start(bf16[1024,256]{1,0:T(8,128)(2,1)S(1)} %copy.311) | copy-start | bytes 1572868
  15.4 7.1 %collective-permute-start.5 = (bf16[4,32,640]{2,1,0:T(8,128)(2,1)S(1)}, bf16[4,32,640]{2,1,0:T(8,128)(2,1)S(1)}, u32[]{:S(2)}, u32[]{:S(2)}) collective-permute-start(bf16[4,32,640]{2,1,0:T(8,128)(2,1)S(1)} %bitcast.456), channel_id=1, source_target_pairs={{0,2},{1,3},{2,0},{3,1},{4,6},{5,7},{6,4},{7,5},{8,10},{9,11},{10,... | collective-permute-start | bytes 491528 | tf_op jit(solution)/shard_map/ppermute | solution.py:477
  15.8 9.1 %collective-permute-start.4 = (bf16[4,32,640]{2,1,0:T(8,128)(2,1)S(1)}, bf16[4,32,640]{2,1,0:T(8,128)(2,1)S(1)}, u32[]{:S(2)}, u32[]{:S(2)}) collective-permute-start(bf16[4,32,640]{2,1,0:T(8,128)(2,1)S(1)} %bitcast.457), channel_id=1, source_target_pairs={{0,4},{1,5},{2,6},{3,7},{4,0},{5,1},{6,2},{7,3},{8,12},{9,13},{10,... | collective-permute-start | bytes 491528 | tf_op jit(solution)/shard_map/ppermute | solution.py:477
  17.5 9.8 %collective-permute-start.3 = (bf16[4,32,640]{2,1,0:T(8,128)(2,1)S(1)}, bf16[4,32,640]{2,1,0:T(8,128)(2,1)S(1)}, u32[]{:S(2)}, u32[]{:S(2)}) collective-permute-start(bf16[4,32,640]{2,1,0:T(8,128)(2,1)S(1)} %bitcast.458), channel_id=1, source_target_pairs={{0,6},{1,7},{2,4},{3,5},{4,2},{5,3},{6,0},{7,1},{8,14},{9,15},{10,... | collective-permute-start | bytes 491528 | tf_op jit(solution)/shard_map/ppermute | solution.py:477
  19.0 16.9 %collective-permute-start.7 = (bf16[1,32,3072]{2,1,0:T(8,128)(2,1)S(1)}, bf16[1,32,3072]{2,1,0:T(8,128)(2,1)S(1)}, u32[]{:S(2)}, u32[]{:S(2)}) collective-permute-start(bf16[1,32,3072]{2,1,0:T(8,128)(2,1)S(1)} %get-tuple-element.99), channel_id=1, source_target_pairs={{0,16},{1,17},{2,18},{3,19},{4,20},{5,21},{6,22},{7,23},{8,24},{9,... | collective-permute-start | bytes 589832 | tf_op jit(solution)/shard_map/ppermute | solution.py:477
  22.5 16.6 %collective-permute-start.8 = (bf16[1,96,1024]{2,1,0:T(8,128)(2,1)S(1)}, bf16[1,96,1024]{2,1,0:T(8,128)(2,1)S(1)}, u32[]{:S(2)}, u32[]{:S(2)}) collective-permute-start(bf16[1,96,1024]{2,1,0:T(8,128)(2,1)S(1)} %get-tuple-element.100), channel_id=1, source_target_pairs={{0,16},{1,17},{2,18},{3,19},{4,20},{5,21},{6,22},{7,23},{8,24},{9,... | collective-permute-start | bytes 589832 | tf_op jit(solution)/shard_map/ppermute | solution.py:477
  24.9 37.7 %collective-permute-start.13 = (bf16[2,16,3072]{2,1,0:T(8,128)(2,1)}, bf16[2,16,3072]{2,1,0:T(8,128)(2,1)}, u32[]{:S(2)}, u32[]{:S(2)}) collective-permute-start(bf16[2,16,3072]{2,1,0:T(8,128)(2,1)} %maximum_select_fusion.17), channel_id=1, source_target_pairs={{0,4},{1,5},{2,6},{3,7},{4,0},{5,1},{6,2},{7,3},{8,12},{9,13},{10,... | collective-permute-start | bytes 589832 | tf_op jit(solution)/shard_map/ppermute | solution.py:477
  27.6 12.4 %collective-permute-start.6 = (bf16[16,32,640]{2,1,0:T(8,128)(2,1)S(1)}, bf16[16,32,640]{2,1,0:T(8,128)(2,1)S(1)}, u32[]{:S(2)}, u32[]{:S(2)}) collective-permute-start(bf16[16,32,640]{2,1,0:T(8,128)(2,1)S(1)} %bitcast.359), channel_id=1, source_target_pairs={{0,1},{1,0},{2,3},{3,2},{4,5},{5,4},{6,7},{7,6},{8,9},{9,8},{10,11... | collective-permute-start | bytes 1966088 | tf_op jit(solution)/shard_map/ppermute | solution.py:477
  36.6 22.5 %collective-permute-start.9 = (bf16[2,32,3072]{2,1,0:T(8,128)(2,1)}, bf16[2,32,3072]{2,1,0:T(8,128)(2,1)}, u32[]{:S(2)}, u32[]{:S(2)}) collective-permute-start(bf16[2,32,3072]{2,1,0:T(8,128)(2,1)} %maximum_select_fusion.11), channel_id=1, source_target_pairs={{0,8},{1,9},{2,10},{3,11},{4,12},{5,13},{6,14},{7,15},{8,0},{9,1},... | collective-permute-start | bytes 1179656 | tf_op jit(solution)/shard_map/ppermute | solution.py:477
  39.9 22.7 %collective-permute-start.11 = (bf16[2,96,1024]{2,1,0:T(8,128)(2,1)}, bf16[2,96,1024]{2,1,0:T(8,128)(2,1)}, u32[]{:S(2)}, u32[]{:S(2)}) collective-permute-start(bf16[2,96,1024]{2,1,0:T(8,128)(2,1)} %maximum_select_fusion.12), channel_id=1, source_target_pairs={{0,8},{1,9},{2,10},{3,11},{4,12},{5,13},{6,14},{7,15},{8,0},{9,1},... | collective-permute-start | bytes 1179656 | tf_op jit(solution)/shard_map/ppermute | solution.py:477
  44.4 65.2 %collective-permute-start.17 = (bf16[16,32,256]{2,1,0:T(8,128)(2,1)}, bf16[16,32,256]{2,1,0:T(8,128)(2,1)S(1)}, u32[]{:S(2)}, u32[]{:S(2)}) collective-permute-start(bf16[16,32,256]{2,1,0:T(8,128)(2,1)} %add_convert_fusion.1), channel_id=1, source_target_pairs={{0,1},{1,0},{2,3},{3,2},{4,5},{5,4},{6,7},{7,6},{8,9},{9,8},{10,11... | collective-permute-start | bytes 786440 | tf_op jit(solution)/shard_map/ppermute | solution.py:477
  46.8 22.8 %all-to-all-start = ((bf16[16,32,256]{2,1,0:T(8,128)(2,1)}), bf16[16,32,256]{2,1,0:T(8,128)(2,1)}, u32[]{:S(2)}, u32[]{:S(2)}) async-start(bf16[16,32,256]{2,1,0:T(8,128)(2,1)} %bitcast.30), calls=%async_computation | async-start | bytes 524288 | tf_op jit(solution)/shard_map/all_to_all | solution.py:902
  60.5 28.7 %collective-permute-start.10 = (bf16[4,32,3072]{2,1,0:T(8,128)(2,1)S(1)}, bf16[4,32,3072]{2,1,0:T(8,128)(2,1)}, u32[]{:S(2)}, u32[]{:S(2)}) collective-permute-start(bf16[4,32,3072]{2,1,0:T(8,128)(2,1)S(1)} %bitcast.346), channel_id=1, source_target_pairs={{0,2},{1,3},{2,0},{3,1},{4,6},{5,7},{6,4},{7,5},{8,10},{9,11},{10,... | collective-permute-start | bytes 2359304 | tf_op jit(solution)/shard_map/ppermute | solution.py:477
  63.8 28.7 %collective-permute-start.14 = (bf16[4,96,1024]{2,1,0:T(8,128)(2,1)S(1)}, bf16[4,96,1024]{2,1,0:T(8,128)(2,1)}, u32[]{:S(2)}, u32[]{:S(2)}) collective-permute-start(bf16[4,96,1024]{2,1,0:T(8,128)(2,1)S(1)} %bitcast.372), channel_id=1, source_target_pairs={{0,4},{1,5},{2,6},{3,7},{4,0},{5,1},{6,2},{7,3},{8,12},{9,13},{10,... | collective-permute-start | bytes 2359304 | tf_op jit(solution)/shard_map/ppermute | solution.py:477
  66.4 19.9 %collective-permute-start.15 = (bf16[4,16,3072]{2,1,0:T(8,128)(2,1)S(1)}, bf16[4,16,3072]{2,1,0:T(8,128)(2,1)}, u32[]{:S(2)}, u32[]{:S(2)}) collective-permute-start(bf16[4,16,3072]{2,1,0:T(8,128)(2,1)S(1)} %bitcast.363), channel_id=1, source_target_pairs={{0,16},{1,17},{2,18},{3,19},{4,20},{5,21},{6,22},{7,23},{8,24},{9,... | collective-permute-start | bytes 1179656 | tf_op jit(solution)/shard_map/ppermute | solution.py:477
  68.9 40.7 %copy-start.25 = (f32[32,1024]{1,0:T(8,128)}, f32[32,1024]{1,0:T(8,128)S(1)}, u32[]{:S(2)}) copy-start(f32[32,1024]{1,0:T(8,128)S(1)} %pad_maximum_fusion.7.refs_6_.refs_7_) | copy-start | bytes 393220
  70.7 38.9 %copy-start.23 = (bf16[16,32,256]{2,0,1:T(8,128)(2,1)}, bf16[16,32,256]{2,0,1:T(8,128)(2,1)S(1)}, u32[]{:S(2)}) copy-start(bf16[16,32,256]{2,0,1:T(8,128)(2,1)S(1)} %copy.390) | copy-start | bytes 786436
  88.7 20.5 %collective-permute-start.16 = (bf16[8,16,3072]{2,1,0:T(8,128)(2,1)S(1)}, bf16[8,16,3072]{2,1,0:T(8,128)(2,1)S(1)}, u32[]{:S(2)}, u32[]{:S(2)}) collective-permute-start(bf16[8,16,3072]{2,1,0:T(8,128)(2,1)S(1)} %bitcast.390), channel_id=1, source_target_pairs={{0,8},{1,9},{2,10},{3,11},{4,12},{5,13},{6,14},{7,15},{8,0},{9,1},... | collective-permute-start | bytes 2359304 | tf_op jit(solution)/shard_map/ppermute | solution.py:477
  94.2 36.1 %collective-permute-start.19 = (bf16[8,32,3072]{2,1,0:T(8,128)(2,1)S(1)}, bf16[8,32,3072]{2,1,0:T(8,128)(2,1)S(1)}, u32[]{:S(2)}, u32[]{:S(2)}) collective-permute-start(bf16[8,32,3072]{2,1,0:T(8,128)(2,1)S(1)} %bitcast.384), channel_id=1, source_target_pairs={{0,4},{1,5},{2,6},{3,7},{4,0},{5,1},{6,2},{7,3},{8,12},{9,13},{10,... | collective-permute-start | bytes 4718600 | tf_op jit(solution)/shard_map/ppermute | solution.py:477
  94.9 36.6 %collective-permute-start.22 = (bf16[8,96,1024]{2,1,0:T(8,128)(2,1)S(1)}, bf16[8,96,1024]{2,1,0:T(8,128)(2,1)S(1)}, u32[]{:S(2)}, u32[]{:S(2)}) collective-permute-start(bf16[8,96,1024]{2,1,0:T(8,128)(2,1)S(1)} %bitcast.353), channel_id=1, source_target_pairs={{0,2},{1,3},{2,0},{3,1},{4,6},{5,7},{6,4},{7,5},{8,10},{9,11},{10,... | collective-permute-start | bytes 4718600 | tf_op jit(solution)/shard_map/ppermute | solution.py:477
  109.6 24.0 %copy-start = (bf16[2,2,4,16,3072]{4,3,2,1,0:T(8,128)(2,1)}, bf16[2,2,4,16,3072]{4,3,2,1,0:T(8,128)(2,1)S(1)}, u32[]{:S(2)}) copy-start(bf16[2,2,4,16,3072]{4,3,2,1,0:T(8,128)(2,1)S(1)} %maximum_select_fusion.4) | copy-start | bytes 4718596
  118.0 13.0 %copy-start.31 = (f32[1536,1024]{1,0:T(8,128)}, f32[1536,1024]{1,0:T(8,128)S(1)}, u32[]{:S(2)}) copy-start(f32[1536,1024]{1,0:T(8,128)S(1)} %get-tuple-element.130.refs_8_) | copy-start | bytes 18874372
  131.4 18.2 %collective-permute-start.20 = (bf16[16,32,3072]{2,1,0:T(8,128)(2,1)S(1)}, bf16[16,32,3072]{2,1,0:T(8,128)(2,1)S(1)}, u32[]{:S(2)}, u32[]{:S(2)}) collective-permute-start(bf16[16,32,3072]{2,1,0:T(8,128)(2,1)S(1)} %bitcast.420), channel_id=1, source_target_pairs={{0,1},{1,0},{2,3},{3,2},{4,5},{5,4},{6,7},{7,6},{8,9},{9,8},{10,11... | collective-permute-start | bytes 9437192 | tf_op jit(solution)/shard_map/ppermute | solution.py:477
  133.4 18.3 %copy-start.37 = (bf16[8,2,1,96,1024]{4,3,1,0,2:T(8,128)(2,1)}, bf16[8,2,1,96,1024]{4,3,1,0,2:T(8,128)(2,1)S(1)}, u32[]{:S(2)}) copy-start(bf16[8,2,1,96,1024]{4,3,1,0,2:T(8,128)(2,1)S(1)} %copy.338) | copy-start | bytes 9437188
  133.4 19.4 %copy-start.1 = (bf16[1,256,1024]{2,1,0:T(8,128)(2,1)S(1)}, bf16[1,256,1024]{2,1,0:T(8,128)(2,1)}, u32[]{:S(2)}) copy-start(bf16[1,256,1024]{2,1,0:T(8,128)(2,1)} %param.24) | copy-start | bytes 1572868
  133.4 16.1 %collective-permute-start.23 = (bf16[16,96,1024]{2,1,0:T(8,128)(2,1)S(1)}, bf16[16,96,1024]{2,1,0:T(8,128)(2,1)S(1)}, u32[]{:S(2)}, u32[]{:S(2)}) collective-permute-start(bf16[16,96,1024]{2,1,0:T(8,128)(2,1)S(1)} %bitcast.417), channel_id=1, source_target_pairs={{0,1},{1,0},{2,3},{3,2},{4,5},{5,4},{6,7},{7,6},{8,9},{9,8},{10,11... | collective-permute-start | bytes 9437192 | tf_op jit(solution)/shard_map/ppermute | solution.py:477
  133.5 16.0 %collective-permute-start.21 = (bf16[16,16,3072]{2,1,0:T(8,128)(2,1)S(1)}, bf16[16,16,3072]{2,1,0:T(8,128)(2,1)S(1)}, u32[]{:S(2)}, u32[]{:S(2)}) collective-permute-start(bf16[16,16,3072]{2,1,0:T(8,128)(2,1)S(1)} %bitcast.351), channel_id=1, source_target_pairs={{0,1},{1,0},{2,3},{3,2},{4,5},{5,4},{6,7},{7,6},{8,9},{9,8},{10,11... | collective-permute-start | bytes 4718600 | tf_op jit(solution)/shard_map/ppermute | solution.py:477
  149.6 18.5 %copy-start.2 = (bf16[16,1,1,16,256]{4,3,1,0,2:T(8,128)(2,1)}, bf16[16,1,1,16,256]{4,3,1,0,2:T(8,128)(2,1)S(1)}, u32[]{:S(2)}) copy-start(bf16[16,1,1,16,256]{4,3,1,0,2:T(8,128)(2,1)S(1)} %get-tuple-element.351) | copy-start | bytes 393220
  169.7 3.4 %collective-permute-start.24 = (bf16[16,96,256]{2,1,0:T(8,128)(2,1)S(1)}, bf16[16,96,256]{2,1,0:T(8,128)(2,1)S(1)}, u32[]{:S(2)}, u32[]{:S(2)}) collective-permute-start(bf16[16,96,256]{2,1,0:T(8,128)(2,1)S(1)} %get-tuple-element.133), channel_id=1, source_target_pairs={{0,1},{1,0},{2,3},{3,2},{4,5},{5,4},{6,7},{7,6},{8,9},{9,8},{10,11... | collective-permute-start | bytes 2359304 | tf_op jit(solution)/shard_map/ppermute | solution.py:477
  169.7 25.9 %collective-permute-start.27 = (bf16[256,3072]{1,0:T(8,128)(2,1)}, bf16[256,3072]{1,0:T(8,128)(2,1)}, u32[]{:S(2)}, u32[]{:S(2)}) collective-permute-start(bf16[256,3072]{1,0:T(8,128)(2,1)} %get-tuple-element.137.own), channel_id=1, source_target_pairs={{0,1},{1,0},{2,3},{3,2},{4,5},{5,4},{6,7},{7,6},{8,9},{9,8},{10,11... | collective-permute-start | bytes 4718600 | tf_op jit(solution)/shard_map/ppermute | solution.py:477
  173.1 27.1 %collective-permute-start.25 = (bf16[256,3072]{1,0:T(8,128)(2,1)}, bf16[256,3072]{1,0:T(8,128)(2,1)}, u32[]{:S(2)}, u32[]{:S(2)}) collective-permute-start(bf16[256,3072]{1,0:T(8,128)(2,1)} %get-tuple-element.134.own), channel_id=1, source_target_pairs={{0,1},{1,0},{2,3},{3,2},{4,5},{5,4},{6,7},{7,6},{8,9},{9,8},{10,11... | collective-permute-start | bytes 4718600 | tf_op jit(solution)/shard_map/ppermute | solution.py:477
  174.0 15.0 %all-to-all-start.2 = ((bf16[16,32,256]{2,1,0:T(8,128)(2,1)}), bf16[16,32,256]{2,1,0:T(8,128)(2,1)}, u32[]{:S(2)}, u32[]{:S(2)}) async-start(bf16[16,32,256]{2,1,0:T(8,128)(2,1)} %bitcast.81), calls=%async_computation.2 | async-start | bytes 524288 | tf_op jit(solution)/shard_map/all_to_all | solution.py:987
  181.6 13.9 %collective-permute-start.26 = (bf16[16,16,256]{2,1,0:T(8,128)(2,1)}, bf16[16,16,256]{2,1,0:T(8,128)(2,1)}, u32[]{:S(2)}, u32[]{:S(2)}) collective-permute-start(bf16[16,16,256]{2,1,0:T(8,128)(2,1)} %bitcast.93), channel_id=1, source_target_pairs={{0,1},{1,0},{2,3},{3,2},{4,5},{5,4},{6,7},{7,6},{8,9},{9,8},{10,11... | collective-permute-start | bytes 393224 | tf_op jit(solution)/shard_map/ppermute | solution.py:477
  194.8 38.5 %collective-permute-start.29 = (bf16[8,96,1024]{2,1,0:T(8,128)(2,1)S(1)}, bf16[8,96,1024]{2,1,0:T(8,128)(2,1)}, u32[]{:S(2)}, u32[]{:S(2)}) collective-permute-start(bf16[8,96,1024]{2,1,0:T(8,128)(2,1)S(1)} %bitcast.404), channel_id=1, source_target_pairs={{0,2},{1,3},{2,0},{3,1},{4,6},{5,7},{6,4},{7,5},{8,10},{9,11},{10,... | collective-permute-start | bytes 4718600 | tf_op jit(solution)/shard_map/ppermute | solution.py:477
  199.2 26.1 %collective-permute-start.28 = (bf16[8,16,3072]{2,1,0:T(8,128)(2,1)S(1)}, bf16[8,16,3072]{2,1,0:T(8,128)(2,1)S(1)}, u32[]{:S(2)}, u32[]{:S(2)}) collective-permute-start(bf16[8,16,3072]{2,1,0:T(8,128)(2,1)S(1)} %bitcast.408), channel_id=1, source_target_pairs={{0,8},{1,9},{2,10},{3,11},{4,12},{5,13},{6,14},{7,15},{8,0},{9,1},... | collective-permute-start | bytes 2359304 | tf_op jit(solution)/shard_map/ppermute | solution.py:477
  205.4 36.9 %collective-permute-start.30 = (bf16[8,32,3072]{2,1,0:T(8,128)(2,1)S(1)}, bf16[8,32,3072]{2,1,0:T(8,128)(2,1)S(1)}, u32[]{:S(2)}, u32[]{:S(2)}) collective-permute-start(bf16[8,32,3072]{2,1,0:T(8,128)(2,1)S(1)} %bitcast.406), channel_id=1, source_target_pairs={{0,4},{1,5},{2,6},{3,7},{4,0},{5,1},{6,2},{7,3},{8,12},{9,13},{10,... | collective-permute-start | bytes 4718600 | tf_op jit(solution)/shard_map/ppermute | solution.py:477
  226.4 45.6 %collective-permute-start.42 = (bf16[4,16,3072]{2,1,0:T(8,128)(2,1)}, bf16[4,16,3072]{2,1,0:T(8,128)(2,1)}, u32[]{:S(2)}, u32[]{:S(2)}) collective-permute-start(bf16[4,16,3072]{2,1,0:T(8,128)(2,1)} %fusion.27.refs_11_), channel_id=1, source_target_pairs={{0,16},{1,17},{2,18},{3,19},{4,20},{5,21},{6,22},{7,23},{8,24},{9,... | collective-permute-start | bytes 1179656 | tf_op jit(solution)/shard_map/ppermute | solution.py:477
  236.7 23.0 %collective-permute-start.31 = (bf16[4,96,1024]{2,1,0:T(8,128)(2,1)}, bf16[4,96,1024]{2,1,0:T(8,128)(2,1)}, u32[]{:S(2)}, u32[]{:S(2)}) collective-permute-start(bf16[4,96,1024]{2,1,0:T(8,128)(2,1)} %fusion.9), channel_id=1, source_target_pairs={{0,4},{1,5},{2,6},{3,7},{4,0},{5,1},{6,2},{7,3},{8,12},{9,13},{10,... | collective-permute-start | bytes 2359304 | tf_op jit(solution)/shard_map/ppermute | solution.py:477
  237.8 12.8 %collective-permute-start.47 = (f32[2,32,512]{2,1,0:T(8,128)S(1)}, f32[2,32,512]{2,1,0:T(8,128)S(1)}, u32[]{:S(2)}, u32[]{:S(2)}) collective-permute-start(f32[2,32,512]{2,1,0:T(8,128)S(1)} %pad_maximum_fusion.8), channel_id=1, source_target_pairs={{0,1},{1,0},{2,3},{3,2},{4,5},{5,4},{6,7},{7,6},{8,9},{9,8},{10,11... | collective-permute-start | bytes 393224 | tf_op jit(solution)/shard_map/ppermute | solution.py:477
  246.3 18.3 %all-to-all-start.3 = ((bf16[32,16,256]{2,0,1:T(8,128)(2,1)}), bf16[32,16,256]{2,0,1:T(8,128)(2,1)S(1)}, u32[]{:S(2)}, u32[]{:S(2)}) async-start(bf16[32,16,256]{2,0,1:T(8,128)(2,1)} %copy.348), calls=%async_computation.3 | async-start | bytes 524288 | tf_op jit(solution)/shard_map/all_to_all | solution.py:1011
  251.5 13.1 %copy-start.4 = (f32[512,256]{1,0:T(8,128)S(1)}, f32[512,256]{1,0:T(8,128)}, u32[]{:S(2)}) copy-start(f32[512,256]{1,0:T(8,128)} %get-tuple-element.333.h1) | copy-start | bytes 1572868
  251.5 23.0 %collective-permute-start.33 = (bf16[4,32,3072]{2,1,0:T(8,128)(2,1)}, bf16[4,32,3072]{2,1,0:T(8,128)(2,1)}, u32[]{:S(2)}, u32[]{:S(2)}) collective-permute-start(bf16[4,32,3072]{2,1,0:T(8,128)(2,1)} %fusion.10), channel_id=1, source_target_pairs={{0,2},{1,3},{2,0},{3,1},{4,6},{5,7},{6,4},{7,5},{8,10},{9,11},{10,... | collective-permute-start | bytes 2359304 | tf_op jit(solution)/shard_map/ppermute | solution.py:477
  262.9 17.8 %collective-permute-start.45 = (bf16[2,96,1024]{2,1,0:T(8,128)(2,1)}, bf16[2,96,1024]{2,1,0:T(8,128)(2,1)}, u32[]{:S(2)}, u32[]{:S(2)}) collective-permute-start(bf16[2,96,1024]{2,1,0:T(8,128)(2,1)} %fusion.28), channel_id=1, source_target_pairs={{0,8},{1,9},{2,10},{3,11},{4,12},{5,13},{6,14},{7,15},{8,0},{9,1},... | collective-permute-start | bytes 1179656 | tf_op jit(solution)/shard_map/ppermute | solution.py:477
  272.1 5.7 %collective-permute-start.32 = (bf16[16,32,640]{2,1,0:T(8,128)(2,1)S(1)}, bf16[16,32,640]{2,1,0:T(8,128)(2,1)S(1)}, u32[]{:S(2)}, u32[]{:S(2)}) collective-permute-start(bf16[16,32,640]{2,1,0:T(8,128)(2,1)S(1)} %bitcast.410), channel_id=1, source_target_pairs={{0,1},{1,0},{2,3},{3,2},{4,5},{5,4},{6,7},{7,6},{8,9},{9,8},{10,11... | collective-permute-start | bytes 1966088 | tf_op jit(solution)/shard_map/ppermute | solution.py:477
  274.2 25.8 %collective-permute-start.43 = (bf16[2,16,3072]{2,1,0:T(8,128)(2,1)}, bf16[2,16,3072]{2,1,0:T(8,128)(2,1)S(1)}, u32[]{:S(2)}, u32[]{:S(2)}) collective-permute-start(bf16[2,16,3072]{2,1,0:T(8,128)(2,1)} %fusion.38), channel_id=1, source_target_pairs={{0,4},{1,5},{2,6},{3,7},{4,0},{5,1},{6,2},{7,3},{8,12},{9,13},{10,... | collective-permute-start | bytes 589832 | tf_op jit(solution)/shard_map/ppermute | solution.py:477
  276.8 13.0 %collective-permute-start.37 = (bf16[2,32,3072]{2,1,0:T(8,128)(2,1)}, bf16[2,32,3072]{2,1,0:T(8,128)(2,1)}, u32[]{:S(2)}, u32[]{:S(2)}) collective-permute-start(bf16[2,32,3072]{2,1,0:T(8,128)(2,1)} %fusion.29), channel_id=1, source_target_pairs={{0,8},{1,9},{2,10},{3,11},{4,12},{5,13},{6,14},{7,15},{8,0},{9,1},... | collective-permute-start | bytes 1179656 | tf_op jit(solution)/shard_map/ppermute | solution.py:477
  278.0 8.2 %collective-permute-start.36 = (bf16[4,32,640]{2,1,0:T(8,128)(2,1)S(1)}, bf16[4,32,640]{2,1,0:T(8,128)(2,1)}, u32[]{:S(2)}, u32[]{:S(2)}) collective-permute-start(bf16[4,32,640]{2,1,0:T(8,128)(2,1)S(1)} %get-tuple-element.345), channel_id=1, source_target_pairs={{0,6},{1,7},{2,4},{3,5},{4,2},{5,3},{6,0},{7,1},{8,14},{9,15},{10,... | collective-permute-start | bytes 491528 | tf_op jit(solution)/shard_map/ppermute | solution.py:477
  279.8 8.3 %collective-permute-start.35 = (bf16[4,32,640]{2,1,0:T(8,128)(2,1)S(1)}, bf16[4,32,640]{2,1,0:T(8,128)(2,1)}, u32[]{:S(2)}, u32[]{:S(2)}) collective-permute-start(bf16[4,32,640]{2,1,0:T(8,128)(2,1)S(1)} %get-tuple-element.344), channel_id=1, source_target_pairs={{0,2},{1,3},{2,0},{3,1},{4,6},{5,7},{6,4},{7,5},{8,10},{9,11},{10,... | collective-permute-start | bytes 491528 | tf_op jit(solution)/shard_map/ppermute | solution.py:477
  280.7 7.9 %collective-permute-start.34 = (bf16[4,32,640]{2,1,0:T(8,128)(2,1)S(1)}, bf16[4,32,640]{2,1,0:T(8,128)(2,1)}, u32[]{:S(2)}, u32[]{:S(2)}) collective-permute-start(bf16[4,32,640]{2,1,0:T(8,128)(2,1)S(1)} %fusion.40), channel_id=1, source_target_pairs={{0,4},{1,5},{2,6},{3,7},{4,0},{5,1},{6,2},{7,3},{8,12},{9,13},{10,... | collective-permute-start | bytes 491528 | tf_op jit(solution)/shard_map/ppermute | solution.py:477
  286.2 24.1 %collective-permute-start.46 = (bf16[1,96,1024]{2,1,0:T(8,128)(2,1)}, bf16[1,96,1024]{2,1,0:T(8,128)(2,1)}, u32[]{:S(2)}, u32[]{:S(2)}) collective-permute-start(bf16[1,96,1024]{2,1,0:T(8,128)(2,1)} %dynamic-slice_convert_fusion.3), channel_id=1, source_target_pairs={{0,16},{1,17},{2,18},{3,19},{4,20},{5,21},{6,22},{7,23},{8,24},{9,... | collective-permute-start | bytes 589832 | tf_op jit(solution)/shard_map/ppermute | solution.py:477
  296.3 23.5 %collective-permute-start.38 = (bf16[1,32,3072]{2,1,0:T(8,128)(2,1)}, bf16[1,32,3072]{2,1,0:T(8,128)(2,1)}, u32[]{:S(2)}, u32[]{:S(2)}) collective-permute-start(bf16[1,32,3072]{2,1,0:T(8,128)(2,1)} %dynamic-slice_convert_fusion.5), channel_id=1, source_target_pairs={{0,16},{1,17},{2,18},{3,19},{4,20},{5,21},{6,22},{7,23},{8,24},{9,... | collective-permute-start | bytes 589832 | tf_op jit(solution)/shard_map/ppermute | solution.py:477
  297.8 16.2 %collective-permute-start.41 = (f32[1,32,640]{2,1,0:T(8,128)S(1)}, f32[1,32,640]{2,1,0:T(8,128)S(1)}, u32[]{:S(2)}, u32[]{:S(2)}) collective-permute-start(f32[1,32,640]{2,1,0:T(8,128)S(1)} %get-tuple-element.342), channel_id=1, source_target_pairs={{0,24},{1,25},{2,26},{3,27},{4,28},{5,29},{6,30},{7,31},{8,16},{9,... | collective-permute-start | bytes 245768 | tf_op jit(solution)/shard_map/ppermute | solution.py:477
  299.9 15.2 %collective-permute-start.39 = (f32[1,32,640]{2,1,0:T(8,128)S(1)}, f32[1,32,640]{2,1,0:T(8,128)S(1)}, u32[]{:S(2)}, u32[]{:S(2)}) collective-permute-start(f32[1,32,640]{2,1,0:T(8,128)S(1)} %get-tuple-element.343), channel_id=1, source_target_pairs={{0,16},{1,17},{2,18},{3,19},{4,20},{5,21},{6,22},{7,23},{8,24},{9,... | collective-permute-start | bytes 245768 | tf_op jit(solution)/shard_map/ppermute | solution.py:477
  300.1 15.1 %collective-permute-start.40 = (f32[1,32,640]{2,1,0:T(8,128)S(1)}, f32[1,32,640]{2,1,0:T(8,128)S(1)}, u32[]{:S(2)}, u32[]{:S(2)}) collective-permute-start(f32[1,32,640]{2,1,0:T(8,128)S(1)} %get-tuple-element.341), channel_id=1, source_target_pairs={{0,8},{1,9},{2,10},{3,11},{4,12},{5,13},{6,14},{7,15},{8,0},{9,1},... | collective-permute-start | bytes 245768 | tf_op jit(solution)/shard_map/ppermute | solution.py:477
  310.3 8.6 %collective-permute-start.44 = (bf16[1,16,3072]{2,1,0:T(8,128)(2,1)S(1)}, bf16[1,16,3072]{2,1,0:T(8,128)(2,1)S(1)}, u32[]{:S(2)}, u32[]{:S(2)}) collective-permute-start(bf16[1,16,3072]{2,1,0:T(8,128)(2,1)S(1)} %dynamic-slice_convert_fusion.7), channel_id=1, source_target_pairs={{0,2},{1,3},{2,0},{3,1},{4,6},{5,7},{6,4},{7,5},{8,10},{9,11},{10,... | collective-permute-start | bytes 294920 | tf_op jit(solution)/shard_map/ppermute | solution.py:477
  (93 other events, 458.2 us)
